TPU v7x, 256 devices: a whole 4x4x8 slice. The times are simulated.
256 devices in a mesh: gx: 32 (over z, y), gy: 4 (over x), gz: 2 (over core).
Axes of the slice: x: 4, y: 4, z: 8, core: 2. Of those that a mesh axis runs over, the one named last changes fastest.
Arguments:
- adjoint: float32 [22, 512, 32, 256], P(None, 'gx', 'gy', 'gz'), may hold values from -6 to 6
- log_conc: bfloat16 [32, 512, 32, 256], P(None, 'gx', 'gy', 'gz'), may hold values from -3 to 3
- levels: int32 [512, 32, 256], P('gx', 'gy', 'gz'), may hold values from 0 to 3, as said below
- conduct: float32 [512, 32, 256], P('gx', 'gy', 'gz'), may hold values from 6 to 20
- orders_fwd: bfloat16 [206, 32], replicated, may hold values from -1 to 1
- orders_rev: bfloat16 [206, 32], replicated, may hold values from -1 to 1
- stoich: bfloat16 [206, 22], replicated, may hold values from -1.25 to 1.25
- rate_fwd: float32 [206], replicated, may hold values from 0.1 to 1
- rate_rev: float32 [206], replicated, may hold values from 0.1 to 1
- diffusivity: float32 [22], replicated, may hold values from 0.1 to 1
Outputs:
- adjoint_next: float32 [22, 512, 32, 256], P(None, 'gx', 'gy', 'gz')
Inputs may be any that keep to these rules, and one draw needn't show every extreme that they name: `levels`: within each aligned block of 4 x-cells by 8 y-rows and all z, some cell holds the block's highest level.
All inputs are finite; a program needn't handle non-finite values.
Results may differ from a plain program's by a relative error of at most 0.0054.
Values sent between devices are 32-bit elements; how exact they have to be, the bound alone decides.
No kernel may reach another device: no remote copies, remote signals or barrier semaphores. Data moves between devices by JAX's collectives and lax.ppermute only.
A program may use at most 128 MiB of HBM per device.

v0:
```python
import jax
import jax.numpy as jnp
from jax import lax
from jax.sharding import PartitionSpec as P

XBAND = 4
YBAND = 8


section_weight = 0.02
step_size = 0.3
mass_weight = 0.001


def from_behind(value, axis, steps):
    count = lax.axis_size(axis)
    first, last = (max(0, -steps), min(count, count - steps))
    return lax.ppermute(value, axis, [(source, source + steps) for source in range(first, last)])


def with_halo(cells, sides, width):
    for axis, dim in sides:
        count = lax.axis_size(axis)
        ends = count - 1
        head = lax.slice_in_dim(cells, 0, width, axis=dim)
        tail = lax.slice_in_dim(cells, cells.shape[dim] - width, cells.shape[dim], axis=dim)
        cells = jnp.concatenate(
            [
                lax.ppermute(tail, axis, [(i, (i + 1) % count) for i in range(ends)]),
                cells,
                lax.ppermute(head, axis, [((i + 1) % count, i) for i in range(ends)]),
            ],
            axis=dim,
        )
    return cells


def carried_in(value, axis, join, neutral, backward):
    count, mine = (lax.axis_size(axis), lax.axis_index(axis))
    pieces = jax.tree.map(lambda part: lax.all_gather(part, axis), value)
    if backward:
        pieces = jax.tree.map(lambda part: part[::-1], pieces)
        mine = count - 1 - mine
    subtotal = jax.tree.map(
        lambda part, zero: jnp.full_like(part, 0) + jnp.asarray(zero, part.dtype), value, neutral
    )

    def hop(position, subtotal):
        longer = join(subtotal, jax.tree.map(lambda part: part[position], pieces))
        return jax.tree.map(lambda new, old: jnp.where(position < mine, new, old), longer, subtotal)

    return lax.fori_loop(0, count - 1, hop, subtotal)


def react_terms(operands, react_count):
    lam_flat, conc_flat, level_flat, orders_fwd, orders_rev, stoich, rate_fwd, rate_rev = operands
    carried = lam_flat.shape[0]
    tier_index = 4 * jnp.arange(react_count, dtype=jnp.int32) // orders_fwd.shape[0]
    active = tier_index[:, None] <= level_flat[None, :]
    weight = jnp.dot(stoich, lam_flat, preferred_element_type=jnp.float32)
    fwd_exp = jnp.dot(orders_fwd, conc_flat, preferred_element_type=jnp.float32)
    rev_exp = jnp.dot(orders_rev, conc_flat, preferred_element_type=jnp.float32)
    act_fwd = jnp.where(
        active, rate_fwd[:react_count, None] * jnp.exp(fwd_exp) * weight, 0.0
    ).astype(jnp.bfloat16)
    act_rev = jnp.where(
        active, rate_rev[:react_count, None] * jnp.exp(rev_exp) * weight, 0.0
    ).astype(jnp.bfloat16)
    gained = jnp.dot(orders_fwd[:, :carried].T, act_fwd, preferred_element_type=jnp.float32)
    lost = jnp.dot(orders_rev[:, :carried].T, act_rev, preferred_element_type=jnp.float32)
    return gained - lost


def chemistry(lam_low, log_conc, levels, orders_fwd, orders_rev, stoich, rate_fwd, rate_rev):
    carried, x_cells, y_cells, z_cells = lam_low.shape
    species = log_conc.shape[0]
    reactions = orders_fwd.shape[0]
    y_blocks = y_cells // YBAND
    block_count = x_cells // XBAND * y_blocks
    block_cells = XBAND * YBAND * z_cells

    def chemistry_advance(block_index, chem_acc):
        x_start = block_index // y_blocks * XBAND
        y_start = block_index % y_blocks * YBAND
        lam_block = lax.dynamic_slice(
            lam_low, (0, x_start, y_start, 0), (carried, XBAND, YBAND, z_cells)
        )
        conc_block = lax.dynamic_slice(
            log_conc, (0, x_start, y_start, 0), (species, XBAND, YBAND, z_cells)
        )
        level_block = lax.dynamic_slice(
            levels, (x_start, y_start, 0), (XBAND, YBAND, z_cells)
        ).reshape(block_cells)
        operands = (
            lam_block.reshape(carried, block_cells),
            conc_block.reshape(species, block_cells),
            level_block,
            orders_fwd,
            orders_rev,
            stoich,
            rate_fwd,
            rate_rev,
        )
        terms = react_terms(operands, reactions)
        return lax.dynamic_update_slice(
            chem_acc, terms.reshape(carried, XBAND, YBAND, z_cells), (0, x_start, y_start, 0)
        )

    return lax.fori_loop(0, block_count, chemistry_advance, jnp.zeros(lam_low.shape, jnp.float32))


def second_y(padded, y_len):
    inner = padded[:, :, :, 2:-2]
    return (
        -inner[:, :, 0:y_len]
        + 16.0 * inner[:, :, 1 : y_len + 1]
        - 30.0 * inner[:, :, 2 : y_len + 2]
        + 16.0 * inner[:, :, 3 : y_len + 3]
        - inner[:, :, 4 : y_len + 4]
    ) / 12.0


def second_z(padded, z_len):
    inner = padded[:, :, 2:-2, :]
    return (
        -inner[..., 0:z_len]
        + 16.0 * inner[..., 1 : z_len + 1]
        - 30.0 * inner[..., 2 : z_len + 2]
        + 16.0 * inner[..., 3 : z_len + 3]
        - inner[..., 4 : z_len + 4]
    ) / 12.0


def matrix_raw(first, second):
    top_left = second[0] * first[0] + second[1] * first[2]
    top_right = second[0] * first[1] + second[1] * first[3]
    low_left = second[2] * first[0] + second[3] * first[2]
    low_right = second[2] * first[1] + second[3] * first[3]
    return (top_left, top_right, low_left, low_right)


def largest(raw):
    return jnp.maximum(
        jnp.maximum(jnp.abs(raw[0]), jnp.abs(raw[1])), jnp.maximum(jnp.abs(raw[2]), jnp.abs(raw[3]))
    )


def joint_product(first, second):
    first_mat, first_gain, first_cross, first_source = first
    second_mat, second_gain, second_cross, second_source = second
    raw = matrix_raw(first_mat, second_mat)
    scale_max = largest(raw)
    gain = second_gain * first_gain
    cross = second_gain * first_cross + second_cross * first_mat[0] + second_source * first_mat[2]
    source = second_gain * first_source + second_cross * first_mat[1] + second_source * first_mat[3]
    return (
        (raw[0] / scale_max, raw[1] / scale_max, raw[2] / scale_max, raw[3] / scale_max),
        gain / scale_max,
        cross / scale_max,
        source / scale_max,
    )


def affine_product(first, second):
    return (second[0] + second[1] * first[0], second[1] * first[1])


def cell_plane(array, index):
    return lax.dynamic_index_in_dim(array, index, 0, keepdims=False)


def rhs_plane(array, index):
    return lax.dynamic_index_in_dim(array, index, 1, keepdims=False)


def joint_summary(lower, diag, upper, rhs):
    ones_plane = jnp.ones(lower.shape[1:], jnp.float32)
    zero_plane = jnp.zeros(lower.shape[1:], jnp.float32)
    zero_fields = jnp.zeros((rhs.shape[0],) + lower.shape[1:], jnp.float32)

    def joint_advance(index, carry):
        lower_cell = cell_plane(lower, index)
        cell = (
            (zero_plane, cell_plane(upper, index), -lower_cell, cell_plane(diag, index)),
            -lower_cell,
            zero_fields,
            rhs_plane(rhs, index),
        )
        return joint_product(carry, cell)

    start = ((ones_plane, zero_plane, zero_plane, ones_plane), ones_plane, zero_fields, zero_fields)
    return lax.fori_loop(0, lower.shape[0], joint_advance, start)


def forward_sweep(lower, diag, upper, rhs, c_in, d_in):
    x_cells = lower.shape[0]

    def forward_advance(index, carry):
        c_prev, d_prev, q_prev, c_all, d_all, q_all = carry
        lower_cell = cell_plane(lower, index)
        denom = cell_plane(diag, index) - lower_cell * c_prev
        c_next = cell_plane(upper, index) / denom
        d_next = (rhs_plane(rhs, index) - lower_cell * d_prev) / denom
        q_next = -lower_cell / denom * q_prev
        c_all = lax.dynamic_update_index_in_dim(c_all, c_next, index, 0)
        d_all = lax.dynamic_update_index_in_dim(d_all, d_next, index, 1)
        q_all = lax.dynamic_update_index_in_dim(q_all, q_next, index, 0)
        return (c_next, d_next, q_next, c_all, d_all, q_all)

    start = (
        c_in,
        d_in,
        jnp.ones(lower.shape[1:], jnp.float32),
        jnp.zeros(lower.shape, jnp.float32),
        jnp.zeros(rhs.shape, jnp.float32),
        jnp.zeros(lower.shape, jnp.float32),
    )
    result = lax.fori_loop(0, x_cells, forward_advance, start)
    return (result[3], result[4], result[5])


def back_sweep(c_all, d_all):
    x_cells = c_all.shape[0]

    def back_advance(turn, carry):
        w_prev, p_prev, w_all, p_all = carry
        index = x_cells - 1 - turn
        c_cell = cell_plane(c_all, index)
        w_cell = rhs_plane(d_all, index) - c_cell * w_prev
        p_cell = -c_cell * p_prev
        w_all = lax.dynamic_update_index_in_dim(w_all, w_cell, index, 1)
        p_all = lax.dynamic_update_index_in_dim(p_all, p_cell, index, 0)
        return (w_cell, p_cell, w_all, p_all)

    start = (
        jnp.zeros((d_all.shape[0],) + c_all.shape[1:], jnp.float32),
        jnp.ones(c_all.shape[1:], jnp.float32),
        jnp.zeros(d_all.shape, jnp.float32),
        jnp.zeros(c_all.shape, jnp.float32),
    )
    result = lax.fori_loop(0, x_cells, back_advance, start)
    return (result[2], result[3])


def shards(
    adjoint,
    log_conc,
    levels,
    conduct,
    orders_fwd,
    orders_rev,
    stoich,
    rate_fwd,
    rate_rev,
    diffusivity,
):
    carried, x_cells, y_cells, z_cells = adjoint.shape
    ones_plane = jnp.ones((y_cells, z_cells), jnp.float32)
    zero_plane = jnp.zeros((y_cells, z_cells), jnp.float32)
    zero_fields = jnp.zeros((carried, y_cells, z_cells), jnp.float32)
    left_face = from_behind(conduct[x_cells - 1 :], "gx", 1)
    kappa_prev = jnp.concatenate([left_face, conduct[:-1]], axis=0)
    lower = mass_weight / 3.0 - kappa_prev
    diag = mass_weight + kappa_prev + conduct
    upper = mass_weight / 3.0 - conduct
    lam_low = adjoint.astype(jnp.bfloat16)
    chem = chemistry(lam_low, log_conc, levels, orders_fwd, orders_rev, stoich, rate_fwd, rate_rev)
    padded = with_halo(adjoint, (("gy", 2), ("gz", 3)), 2)
    diffusion = diffusivity[:, None, None, None] * (
        second_y(padded, y_cells) + second_z(padded, z_cells)
    )
    rhs = section_weight * (adjoint + step_size * (chem + diffusion))
    summary_mat, summary_gain, summary_cross, summary_source = joint_summary(
        lower, diag, upper, rhs
    )
    entering = carried_in(
        (
            (summary_mat[0], summary_mat[1], summary_mat[2], summary_mat[3]),
            summary_gain,
            summary_cross,
            summary_source,
        ),
        "gx",
        joint_product,
        ((ones_plane, zero_plane, zero_plane, ones_plane), ones_plane, zero_fields, zero_fields),
        False,
    )
    c_in = entering[0][1] / entering[0][3]
    d_in = entering[3] / entering[0][3]
    c_all, d_all, q_all = forward_sweep(lower, diag, upper, rhs, c_in, d_in)
    w_zero, p_all = back_sweep(c_all, d_all)
    back_in = carried_in(
        (w_zero[:, 0], p_all[0]), "gx", affine_product, (zero_fields, ones_plane), True
    )
    return w_zero + p_all[None] * back_in[0][:, None]


def solution(mesh):
    in_specs = (
        P(None, "gx", "gy", "gz"),
        P(None, "gx", "gy", "gz"),
        P("gx", "gy", "gz"),
        P("gx", "gy", "gz"),
        P(),
        P(),
        P(),
        P(),
        P(),
        P(),
    )
    out_specs = P(None, "gx", "gy", "gz")
    return jax.shard_map(shards, mesh=mesh, in_specs=in_specs, out_specs=out_specs, check_vma=False)
```

profile of v0, /device:TPU:2, one launch (start us, length us, event | category | flops | bytes accessed | tf_op | source)
XLA Modules:
  0.0 544.5 jit_solution(18349887171840460560)
XLA Ops:
  9.7 3.4 collective-permute-start.1
  13.8 3.2 collective-permute-start.2
  17.1 3.6 collective-permute-start
  22.1 49.3 %while.119 = (s32[]{:T(128)}, f32[22,16,8,128]{3,1,2,0:T(8,128)}, s32[16,8,128]{2,1,0:T(8,128)}, f32[206]{0:T(256)S(1)}, bf16[32,16,8,128]{3,2,1,0:T(8,128)(2,1)...) while((s32[]{:T(128)}, f32[22,16,8,128]{3,1,2,0:T(8,128)}, ...), condition=%wide.region_1.2_spmd, body=%wide.region_0.1_spmd.sunk | while | flops 227911488 | bytes 21763604 | solution.py:109
  26.7 2.8 fusion.100
  29.5 3.0 convolution_subtract_fusion.2
  39.0 2.8 fusion.100
  41.8 3.0 convolution_subtract_fusion.2
  51.3 2.8 fusion.100
  54.1 3.0 convolution_subtract_fusion.2
  66.5 3.0 convolution_subtract_fusion.2
  71.5 5.7 %copy.58 = f32[22,16,8,128]{0,1,3,2:T(8,128)} copy(f32[22,16,8,128]{3,2,1,0:T(8,128)} %param.22) | data formatting | bytes 2883584 | tf_op args[0]
  79.9 3.1 copy.59
  83.0 5.0 pad_maximum_fusion
  88.1 4.6 copy-done
  100.4 9.8 %copy.61 = f32[22,16,12,128]{3,1,2,0:T(8,128)} copy(f32[22,16,12,128]{0,1,3,2:T(8,128)} %copy-done) | data formatting | bytes 4325376 | tf_op jit(solution)/shard_map/concatenate | solution.py:27
  110.2 4.2 copy.60
  114.3 4.2 copy.63
  118.5 7.5 %fusion.50 = f32[22,16,8,128]{3,1,2,0:T(8,128)S(1)} fusion(f32[22,16,8,128]{3,1,2,0:T(8,128)} %get-tuple-element.1144, f32[22,16,12,2]{3,1,2,0:T(8,128)} %copy.63, f32[22,16,12,128]{3,1,2,0:T(8,128)} %copy.61, f32[22,16,12,2]{3,1,2,0:T(8,128)} %copy.60, f32[22,16,10,128]{3,1,2,0:T(8,128)S(1)} %constant_dynamic-update-slice_fusion.2, ...), kind=kLoop, calls=%fused_computation.104 | loop fusion | flops 9011200 | bytes 12322904 | tf_op jit(solution)/shard_map/mul | solution.py:272
  126.4 13.4 %while.121 = (s32[]{:T(128)}, f32[8,128]{1,0:T(8,128)S(1)}, f32[8,128]{1,0:T(8,128)S(1)}, f32[8,128]{1,0:T(8,128)S(1)}, f32[8,128]{1,0:T(8,128)S(1)}, /*index=5*...) while((s32[]{:T(128)}, f32[8,128]{1,0:T(8,128)S(1)}, ...), condition=%wide.region_3.4_spmd.clone, body=%wide.region_2.3_spmd.clone.sunk | while | flops 302083 | bytes 589976 | solution.py:192
  141.4 46.0 %all-gather = f32[256,128]{1,0:T(8,128)S(1)} all-gather(f32[8,128]{1,0:T(8,128)S(1)} %get-tuple-element.1145), channel_id=2, replica_groups=mesh['gx'=32,'gy'=4,'gz'=2] {'gx'}, dimensions={0}, use_global_device_ids=true | all-gather | bytes 135168 | tf_op jit(solution)/shard_map/all_gather | solution.py:40
  187.4 41.4 %all-gather.1 = f32[256,128]{1,0:T(8,128)S(1)} all-gather(f32[8,128]{1,0:T(8,128)S(1)} %get-tuple-element.1146), channel_id=3, replica_groups=mesh['gx'=32,'gy'=4,'gz'=2] {'gx'}, dimensions={0}, use_global_device_ids=true | all-gather | bytes 135168 | tf_op jit(solution)/shard_map/all_gather | solution.py:40
  228.8 41.9 %all-gather.2 = f32[256,128]{1,0:T(8,128)S(1)} all-gather(f32[8,128]{1,0:T(8,128)S(1)} %get-tuple-element.1147), channel_id=4, replica_groups=mesh['gx'=32,'gy'=4,'gz'=2] {'gx'}, dimensions={0}, use_global_device_ids=true | all-gather | bytes 135168 | tf_op jit(solution)/shard_map/all_gather | solution.py:40
  270.7 41.3 %all-gather.3 = f32[256,128]{1,0:T(8,128)S(1)} all-gather(f32[8,128]{1,0:T(8,128)S(1)} %get-tuple-element.1148), channel_id=5, replica_groups=mesh['gx'=32,'gy'=4,'gz'=2] {'gx'}, dimensions={0}, use_global_device_ids=true | all-gather | bytes 135168 | tf_op jit(solution)/shard_map/all_gather | solution.py:40
  312.0 41.9 %all-gather.4 = f32[256,128]{1,0:T(8,128)S(1)} all-gather(f32[8,128]{1,0:T(8,128)S(1)} %get-tuple-element.1149), channel_id=6, replica_groups=mesh['gx'=32,'gy'=4,'gz'=2] {'gx'}, dimensions={0}, use_global_device_ids=true | all-gather | bytes 135168 | tf_op jit(solution)/shard_map/all_gather | solution.py:40
  353.9 33.8 %while.122 = (s32[]{:T(128)}, f32[8,128]{1,0:T(8,128)S(1)}, f32[8,128]{1,0:T(8,128)S(1)}, f32[8,128]{1,0:T(8,128)S(1)}, f32[8,128]{1,0:T(8,128)S(1)}, /*index=5*...) while((s32[]{:T(128)}, f32[8,128]{1,0:T(8,128)S(1)}, ...), condition=%wide.region_5.6_spmd.clone, body=%wide.region_4.5_spmd.clone.sunk | while | flops 214020 | bytes 512190 | solution.py:52
  387.8 21.8 %while.120 = (s32[]{:T(128)}, f32[8,128]{1,0:T(8,128)S(1)}, f32[22,8,128]{2,1,0:T(8,128)S(1)}, f32[16,8,128]{2,1,0:T(8,128)S(1)}, f32[22,16,8,128]{3,2,0,1:T(8,1...) while((s32[]{:T(128)}, f32[8,128]{1,0:T(8,128)S(1)}, ...), condition=%wide.region_7.8_spmd, body=%wide.region_6.7_spmd.sunk | while | flops 70658 | bytes 402025 | solution.py:218
  409.7 15.6 %while.123 = (s32[]{:T(128)}, f32[22,8,128]{2,1,0:T(8,128)S(1)}, f32[8,128]{1,0:T(8,128)S(1)}, f32[22,16,8,128]{3,2,1,0:T(8,128)S(1)}, f32[16,8,128]{2,1,0:T(8,1...) while((s32[]{:T(128)}, f32[22,8,128]{2,1,0:T(8,128)S(1)}, ...), condition=%wide.region_9.10_spmd.clone, body=%wide.region_8.9_spmd.clone.sunk | while | flops 70663 | bytes 385198 | solution.py:241
  426.0 41.2 %all_gather.63 = f32[32,8,128]{2,1,0:T(8,128)S(1)} all-gather(f32[1,8,128]{2,1,0:T(8,128)S(1)} %slice.101), channel_id=1, replica_groups=mesh['gx'=32,'gy'=4,'gz'=2] {'gx'}, dimensions={0}, use_global_device_ids=true | all-gather | bytes 135168 | tf_op jit(solution)/shard_map/all_gather | solution.py:40
  467.2 36.0 %all-gather.16.cloned.1.call-done = f32[704,1,8,128]{3,2,1,0:T(8,128)} async-done(((f32[22,1,8,128]{3,2,1,0:T(8,128)}), f32[704,1,8,128]{3,2,1,0:T(8,128)}) %all-gather.16.cloned.1.call-update) | async-done | bytes 2883600 | tf_op jit(solution)/shard_map/all_gather | solution.py:40
  503.3 3.6 rev.6
  506.8 29.8 %while.124 = (s32[]{:T(128)}, f32[22,8,128]{2,1,0:T(8,128)S(1)}, s32[]{:T(128)}, f32[32,22,8,128]{3,2,1,0:T(8,128)}, f32[32,8,128]{2,1,0:T(8,128)S(1)}, /*index=5*/s32[]{:T(128)}, s32[]{:T(128)}) while((s32[]{:T(128)}, f32[22,8,128]{2,1,0:T(8,128)S(1)}, s32[]{:T(128)}, f32[32,22,8,128]{3,2,1,0:T(8,128)}, ...), condition=%wide.region_11.12_spmd.clone, body=%wide.region_10.11_spmd.clone.sunk | while | flops 90116 | bytes 282729 | solution.py:52
  (467 shorter events, 159.5 us)
Async XLA Ops:
  6.5 14.2 %copy-start.1 = (f32[22,16,8,128]{3,2,1,0:T(8,128)S(1)}, f32[22,16,8,128]{3,2,1,0:T(8,128)}, u32[]{:S(2)}) copy-start(f32[22,16,8,128]{3,2,1,0:T(8,128)} %param.22) | copy-start | bytes 4325380
  6.5 10.5 %copy-start.9 = (f32[16,8,128]{2,1,0:T(8,128)S(1)}, f32[16,8,128]{2,1,0:T(8,128)}, u32[]{:S(2)}) copy-start(f32[16,8,128]{2,1,0:T(8,128)} %param.25) | copy-start | bytes 196612
  6.5 347.4 %all-gather.12.cloned.1.call-start = ((), (), s32[]{:S(2)}) async-start(), calls=%async_computation | async-start | bytes 2973696 | tf_op jit(solution)/shard_map/all_gather | solution.py:40
  9.7 68.2 %collective-permute-start.1 = (f32[22,16,2,128]{3,1,2,0:T(8,128)}, f32[22,16,2,128]{3,1,2,0:T(8,128)}, u32[]{:S(2)}, u32[]{:S(2)}) collective-permute-start(f32[22,16,2,128]{3,1,2,0:T(8,128)} %copy.92), channel_id=1, source_target_pairs={{0,2},{2,4},{4,6},{1,3},{3,5},{5,7},{8,10},{10,12},{12,14},{9,11},... | collective-permute-start | bytes 1081352 | tf_op jit(solution)/shard_map/ppermute | solution.py:29
  13.8 66.0 %collective-permute-start.2 = (f32[22,16,2,128]{3,1,2,0:T(8,128)}, f32[22,16,2,128]{3,1,2,0:T(8,128)}, u32[]{:S(2)}, u32[]{:S(2)}) collective-permute-start(f32[22,16,2,128]{3,1,2,0:T(8,128)} %copy.91), channel_id=1, source_target_pairs={{2,0},{4,2},{6,4},{3,1},{5,3},{7,5},{10,8},{12,10},{14,12},{11,9},... | collective-permute-start | bytes 1081352 | tf_op jit(solution)/shard_map/ppermute | solution.py:31
  17.0 5.1 copy-start.8
  17.0 5.1 copy-start.10
  17.0 5.1 copy-start.11
  17.1 5.0 copy-start.12
  17.1 5.0 copy-start.13
  17.1 60.1 %collective-permute-start = (f32[1,8,128]{2,1,0:T(8,128)S(1)}, f32[1,8,128]{2,1,0:T(8,128)S(1)}, u32[]{:S(2)}, u32[]{:S(2)}) collective-permute-start(f32[1,8,128]{2,1,0:T(8,128)S(1)} %slice.86), channel_id=1, source_target_pairs={{0,8},{8,16},{16,24},{24,32},{32,40},{40,48},{48,56},{56,64},{64,7... | collective-permute-start | bytes 12296 | tf_op jit(solution)/shard_map/ppermute | solution.py:18
  22.1 49.3 %copy-start.14 = (f32[22]{0:T(128)S(1)}, f32[22]{0:T(128)}, u32[]{:S(2)}) copy-start(f32[22]{0:T(128)} %param.31) | copy-start | bytes 268
  22.1 0.9 copy-start.4
  32.5 2.0 copy-start.5
  34.5 0.9 copy-start.4
  44.8 2.0 copy-start.5
  46.8 0.9 copy-start.4
  57.1 2.0 copy-start.5
  59.1 0.9 copy-start.4
  69.4 2.0 copy-start.5
  71.5 5.7 %slice-start = ((f32[16,8,128]{2,1,0:T(8,128)}), f32[15,8,128]{2,1,0:T(8,128)S(1)}, s32[]{:S(2)}) async-start(f32[16,8,128]{2,1,0:T(8,128)} %param.25), calls=%async_computation.3 | async-start | bytes 122880 | tf_op jit(solution)/shard_map/slice | solution.py:262
  88.1 4.6 copy-start
  92.6 5.2 copy-start.2
  93.4 16.8 %collective-permute-start.3 = (f32[22,16,12,2]{0,1,3,2:T(8,128)}, f32[22,16,12,2]{0,1,3,2:T(8,128)}, u32[]{:S(2)}, u32[]{:S(2)}) collective-permute-start(f32[22,16,12,2]{0,1,3,2:T(8,128)} %get-tuple-element.1542), channel_id=1, source_target_pairs={{0,1},{2,3},{4,5},{6,7},{8,9},{10,11},{12,13},{14,15},{16,17},{18,... | collective-permute-start | bytes 101384 | tf_op jit(solution)/shard_map/ppermute | solution.py:29
  95.4 19.0 %collective-permute-start.4 = (f32[22,16,12,2]{0,1,3,2:T(8,128)}, f32[22,16,12,2]{0,1,3,2:T(8,128)}, u32[]{:S(2)}, u32[]{:S(2)}) collective-permute-start(f32[22,16,12,2]{0,1,3,2:T(8,128)} %get-tuple-element.1543), channel_id=1, source_target_pairs={{1,0},{3,2},{5,4},{7,6},{9,8},{11,10},{13,12},{15,14},{17,16},{19,... | collective-permute-start | bytes 101384 | tf_op jit(solution)/shard_map/ppermute | solution.py:31
  98.2 1.2 copy-start.3
  139.9 0.6 copy-start.6
  139.9 0.7 copy-start.7
  140.5 213.4 %all-gather.14.cloned.1.call-start = ((), (), s32[]{:S(2)}) async-start(), calls=%async_computation.1 | async-start | bytes 2973696 | tf_op jit(solution)/shard_map/all_gather | solution.py:40
  141.3 362.0 %all-gather.16.cloned.1.call-start = ((), (), s32[]{:S(2)}) async-start(), calls=%async_computation.2 | async-start | bytes 2973696 | tf_op jit(solution)/shard_map/all_gather | solution.py:40
Sparse Core Ops, SparseCore 0:
  140.6 83.3 all-gather.11
  226.7 76.3 all-gather.13
  426.1 77.1 all-gather.15
where the time goes:
time: 550 us; the launch traced here: 544 us
  blocking collectives  254 us (46%)
  other arithmetic  127 us (23%)
  local copies, waits for them, and re-layouts  69.9 us (13%)
  waiting for transfers between devices  36.8 us (7%)
  matrix products  25.7 us (5%)
  starting transfers between devices  13.7 us (2%)
  between operations  13.6 us (2%)
    all_gather x6, blocking collectives, carried_in(): pieces = jax.tree.map(lambda part: lax.all_gather(part, axis), value)  254 us
    select_n x124, other arithmetic, hop(): jnp.where(position < mine, new, old)  60.3 us
    all_gather x3, waiting for transfers between devices, carried_in(): pieces = jax.tree.map(lambda part: lax.all_gather(part, axis), value)  36.1 us
    unnamed x31, local copies, waits for them, and re-layouts  15.1 us
    dynamic_update_slice x16, other arithmetic, back_advance(): w_all = lax.dynamic_update_index_in_dim(w_all, w_cell, index, 1)  14.9 us
    dot_general x4, matrix products, react_terms(): jnp.dot(orders_rev[:, :carried].T, act_rev, preferred_element_type=jnp.fl...  11.9 us
    div x16, other arithmetic, joint_product(): gain / scale_max  11.4 us
    dot_general x4, matrix products, react_terms(): jnp.dot(orders_fwd[:, :carried].T, act_fwd, preferred_element_type=jnp.fl...  11.3 us
  transfers between devices with their start and end apart: 8, of which 1 were waited for; matrix products, arithmetic and copies ran while one was open for 13% of the time, Pallas kernels for 0%

commit v1 on v0

v1 whole, which is shorter than its diff:
```python
import math

import jax
import jax.numpy as jnp
from jax import lax
from jax.experimental import pallas as pl
from jax.experimental.pallas import tpu as pltpu
from jax.sharding import PartitionSpec as P

SECTION = 0.02
STEP = 0.3
MASS = 0.001
LOG2E = math.log2(math.e)
OFF = -1024.0

K_ROWS = 96
R_PAD = 208
CHUNKS = ((0, 64), (64, 48), (112, 48), (160, 48))
TILE = 256
XB = 2
LIMIT = 12 * 1024 * 1024
F32 = jnp.float32
BF16 = jnp.bfloat16


def iota(shape, dim):
    return lax.broadcasted_iota(jnp.int32, shape, dim)


def dot(a, b):
    return lax.dot_general(a, b, (((1,), (0,)), ((), ())), preferred_element_type=F32)


def dot_nt(a, b):
    return lax.dot_general(a, b, (((1,), (1,)), ((), ())), preferred_element_type=F32)


def one_hot(mask):
    return jnp.where(mask, 1.0, 0.0).astype(BF16)


def build_weights(of_ref, or_ref, st_ref, rf_ref, rr_ref, wide_ref, w_ref, c_ref):
    species, react = of_ref.shape
    carried = st_ref.shape[0]
    eye = one_hot(iota((R_PAD, 256), 0) == iota((R_PAD, 256), 1))
    pick_row, pick_col = iota((32, 32), 0), iota((32, 32), 1)
    pick = one_hot(pick_col == jnp.where(pick_row < 16, pick_row, jnp.where(pick_row < 24, pick_row - 2, -1)))
    sub, tier = iota((8, 256), 0), 4 * iota((8, 256), 1) // react
    full = []
    for index, (orders, rate) in enumerate(((of_ref, rf_ref), (or_ref, rr_ref))):
        wide_ref[...] = jnp.zeros(wide_ref.shape, F32)
        wide_ref[0:species, 0:react] = orders[...].astype(F32)
        plain = wide_ref[0:32, :]
        sign = 1.0 if index == 0 else -1.0
        c_ref[index] = (sign * dot(pick, plain.astype(BF16)))[:, 0:R_PAD].astype(BF16)
        scaled = plain * LOG2E
        hi = scaled.astype(BF16).astype(F32)
        wide_ref[0:32, :] = hi
        wide_ref[32:64, :] = scaled - hi
        wide_ref[88:89, 0:react] = jnp.log(rate[...]) * LOG2E
        r = jnp.broadcast_to(wide_ref[88:89, :], (8, 256))
        r0 = r.astype(BF16).astype(F32)
        r1 = (r - r0).astype(BF16).astype(F32)
        parts = jnp.where(sub == 3, r0, jnp.where(sub == 4, r1, jnp.where(sub == 5, r - r0 - r1, 0.0)))
        wide_ref[88:96, :] = jnp.where(sub < 3, jnp.where(tier > sub, OFF, 0.0), parts)
        full.append(dot_nt(eye, wide_ref[...].astype(BF16)).astype(BF16))
    wide_ref[...] = jnp.zeros(wide_ref.shape, F32)
    wide_ref[64:80, 0:react] = st_ref[0:16, :].astype(F32)
    wide_ref[82 : 66 + carried, 0:react] = st_ref[16:carried, :].astype(F32)
    full.append(dot_nt(eye, wide_ref[...].astype(BF16)).astype(BF16))
    base = 0
    for start, size in CHUNKS:
        for part in full:
            w_ref[base : base + size, :] = part[start : start + size]
            base += size


def chem_kernel(
    adj_ref, conc_ref, lev_ref, of_ref, or_ref, st_ref, rf_ref, rr_ref, out_ref,
    wide_ref, w_ref, c_ref, conc32_ref, x_ref, act_ref,
):
    @pl.when(pl.program_id(0) == 0)
    def _():
        build_weights(of_ref, or_ref, st_ref, rf_ref, rr_ref, wide_ref, w_ref, c_ref)

    carried, xb, ny, nz = adj_ref.shape
    species = conc_ref.shape[0]
    adj_rows = adj_ref.reshape(carried * xb * ny, nz)
    out_rows = out_ref.reshape(carried * xb * ny, nz)
    pitch = xb * ny
    conc32_ref[...] = conc_ref[...].astype(F32).reshape(species * pitch, nz)
    sub = iota((8, nz), 0)
    for x in range(xb):
        for y in range(ny):
            row = x * ny + y
            cols = slice(y * nz, (y + 1) * nz)
            conc = jnp.concatenate(
                [conc32_ref[pl.ds(row + 8 * q * pitch, 8, stride=pitch), :] for q in range(4)], axis=0
            ).astype(BF16)
            x_ref[x, 0:32, cols] = conc
            x_ref[x, 32:64, cols] = conc
            lam = [adj_rows[pl.ds(row + first * pitch, 8, stride=pitch), :] for first in (0, 8, carried - 8)]
            level = jnp.broadcast_to(lev_ref[x, y : y + 1, :], (8, nz))
            marks = jnp.where(level <= sub, 1.0, 0.0)
            x_ref[x, 64:96, cols] = jnp.concatenate(lam + [marks], axis=0).astype(BF16)
    per_tile = TILE // nz
    for x in range(xb):
        for tile in range(ny // per_tile):
            slot = (x * (ny // per_tile) + tile) % act_ref.shape[0]
            data = x_ref[x, :, tile * TILE : (tile + 1) * TILE]
            base = 0
            for start, size in CHUNKS:
                got = dot(w_ref[base : base + 3 * size, :], data)
                base += 3 * size
                weight = got[2 * size :]
                act_ref[slot, 0, start : start + size, :] = (jnp.exp2(got[:size]) * weight).astype(BF16)
                act_ref[slot, 1, start : start + size, :] = (jnp.exp2(got[size : 2 * size]) * weight).astype(BF16)
            chem = dot(c_ref[0], act_ref[slot, 0]) + dot(c_ref[1], act_ref[slot, 1])
            for part in range(per_tile):
                row = x * ny + tile * per_tile + part
                for q, first in enumerate((0, 8, carried - 8)):
                    out_rows[pl.ds(row + first * pitch, 8, stride=pitch), :] = chem[
                        8 * q : 8 * q + 8, part * nz : (part + 1) * nz
                    ]


def chemistry(adjoint, log_conc, levels, orders_fwd, orders_rev, stoich, rate_fwd, rate_rev):
    carried, nx, ny, nz = adjoint.shape
    species, react = log_conc.shape[0], orders_fwd.shape[0]
    whole = lambda a: pl.BlockSpec(a.shape, lambda i: (0,) * len(a.shape))
    small = [orders_fwd.T, orders_rev.T, stoich.T, rate_fwd.reshape(1, react), rate_rev.reshape(1, react)]
    return pl.pallas_call(
        chem_kernel,
        grid=(nx // XB,),
        in_specs=[
            pl.BlockSpec((carried, XB, ny, nz), lambda i: (0, i, 0, 0)),
            pl.BlockSpec((species, XB, ny, nz), lambda i: (0, i, 0, 0)),
            pl.BlockSpec((XB, ny, nz), lambda i: (i, 0, 0)),
        ]
        + [whole(a) for a in small],
        out_specs=pl.BlockSpec((carried, XB, ny, nz), lambda i: (0, i, 0, 0)),
        out_shape=jax.ShapeDtypeStruct(adjoint.shape, F32),
        scratch_shapes=[
            pltpu.VMEM((K_ROWS, 256), F32),
            pltpu.VMEM((3 * R_PAD, K_ROWS), BF16),
            pltpu.VMEM((2, 32, R_PAD), BF16),
            pltpu.VMEM((species * XB * ny, nz), F32),
            pltpu.VMEM((XB, K_ROWS, ny * nz), BF16),
            pltpu.VMEM((4, 2, R_PAD, TILE), BF16),
        ],
        compiler_params=pltpu.CompilerParams(dimension_semantics=("arbitrary",), vmem_limit_bytes=LIMIT),
        cost_estimate=pl.CostEstimate(flops=12 * 10**9, bytes_accessed=4 * 10**6, transcendentals=6_750_000),
        name="chem",
    )(adjoint, log_conc, levels, *small)


GROUP = 6
GROUPS = 4
ROWS = 16
SB = 2
ANY = pl.BlockSpec(memory_space=pl.ANY)
WHOLE = pl.BlockSpec(memory_space=pltpu.VMEM)
SMALL = pltpu.CompilerParams(vmem_limit_bytes=LIMIT)


def place(s):
    return s // GROUP * ROWS + s % GROUP


def edges_kernel(adj_ref, low_ref, high_ref):
    carried, nx, ny, nz = adj_ref.shape

    @pl.loop(0, carried)
    def _(s):
        for x in range(nx):
            low_ref[s, x] = adj_ref[s, x, ny - 2 : ny, :]
            high_ref[s, x] = adj_ref[s, x, 0:2, :]


def edges(adjoint):
    carried, nx, ny, nz = adjoint.shape
    shape = pltpu.VMEM((carried, nx, 2, nz), F32)
    return pl.pallas_call(
        edges_kernel,
        in_specs=[WHOLE],
        out_specs=[WHOLE, WHOLE],
        out_shape=[shape, shape],
        compiler_params=SMALL,
        cost_estimate=pl.CostEstimate(flops=0, bytes_accessed=2 * 10**6, transcendentals=0),
        name="edges",
    )(adjoint)


def local_kernel(
    diff_ref, cond_ref, adj_ref, chem_ref, near_ref, low_ref, high_ref, part_ref, coef_ref, msg_ref, inv_ref
):
    nx, ny, nz = cond_ref.shape
    carried = adj_ref.shape[0]
    stride = GROUPS * ROWS
    third = MASS / 3.0
    body = MASS + 2.0 * third
    mass_first = jnp.where(lax.axis_index("gx") == 0, MASS + third, body) * jnp.ones((ny, nz), F32)
    gap = cond_ref[0] - third
    mass = jnp.full((ny, nz), body, F32)
    for p in range(1, nx - 1):
        after = cond_ref[p] - third
        inv = 1.0 / (gap + after + mass)
        alpha, beta = gap * inv, after * inv
        coef_ref[0, p], coef_ref[1, p], inv_ref[p] = alpha, beta, inv
        mass_first = mass_first + alpha * mass
        mass = body + beta * mass
        gap = alpha * after
    face = cond_ref[nx - 1] - third
    msg_ref[...] = jnp.zeros(msg_ref.shape, F32)
    for group in range(GROUPS):
        for r, value in ((6, gap), (7, mass_first), (14, face), (15, mass)):
            msg_ref[pl.ds(group * ROWS + r, ny, stride=stride), :] = value

    lane, row = iota((ny, nz), 1), iota((ny, nz), 0)
    keep_low = jnp.where(lax.axis_index("gz") == 0, 1.0, 0.0)
    keep_high = 1.0 - keep_low

    @pl.loop(0, carried)
    def _(s):
        scale = diff_ref[s] * (SECTION * STEP / 12.0)
        b_first, carry = None, None
        for p in range(nx):
            own = adj_ref[s, p]
            near = near_ref[s, p]
            from_high = near * keep_low
            from_low = near * keep_high
            z_up1 = pltpu.roll(jnp.where(lane < 1, from_high, own), nz - 1, 1)
            z_up2 = pltpu.roll(jnp.where(lane < 2, from_high, own), nz - 2, 1)
            z_dn1 = pltpu.roll(jnp.where(lane >= nz - 1, from_low, own), 1, 1)
            z_dn2 = pltpu.roll(jnp.where(lane >= nz - 2, from_low, own), 2, 1)
            low0, low1 = low_ref[s, p, 0:1, :], low_ref[s, p, 1:2, :]
            high0, high1 = high_ref[s, p, 0:1, :], high_ref[s, p, 1:2, :]
            y_up1 = jnp.where(row == ny - 1, high0, pltpu.roll(own, ny - 1, 0))
            y_up2 = jnp.where(row == ny - 1, high1, jnp.where(row == ny - 2, high0, pltpu.roll(own, ny - 2, 0)))
            y_dn1 = jnp.where(row == 0, low1, pltpu.roll(own, 1, 0))
            y_dn2 = jnp.where(row == 0, low0, jnp.where(row == 1, low1, pltpu.roll(own, 2, 0)))
            spread = 16.0 * ((z_up1 + z_dn1) + (y_up1 + y_dn1)) - ((z_up2 + z_dn2) + (y_up2 + y_dn2)) - 60.0 * own
            b = SECTION * own + (SECTION * STEP) * chem_ref[s, p] + scale * spread
            if p == 0:
                b_first = b
            elif p < nx - 1:
                full = b if carry is None else b + carry
                part_ref[s, p] = full * inv_ref[p]
                b_first = b_first + coef_ref[0, p] * full
                carry = coef_ref[1, p] * full
            else:
                b_last = b + carry
        msg_ref[pl.ds(place(s), ny, stride=stride), :] = b_first
        msg_ref[pl.ds(place(s) + 8, ny, stride=stride), :] = b_last


def local_part(diffusivity, adjoint, chem, near, low, high, conduct):
    carried, nx, ny, nz = adjoint.shape
    smem = pl.BlockSpec(memory_space=pltpu.SMEM)
    return pl.pallas_call(
        local_kernel,
        in_specs=[smem] + [WHOLE] * 6,
        out_specs=[WHOLE] * 3,
        out_shape=[
            pltpu.VMEM(adjoint.shape, F32),
            pltpu.VMEM((2, nx, ny, nz), F32),
            pltpu.VMEM((GROUPS * ny * ROWS, nz), F32),
        ],
        scratch_shapes=[pltpu.VMEM((nx, ny, nz), F32)],
        compiler_params=SMALL,
        cost_estimate=pl.CostEstimate(flops=20 * 10**6, bytes_accessed=7 * 10**6, transcendentals=0),
        name="local",
    )(diffusivity, conduct, adjoint, chem, near, low, high)


def chain_kernel(in_ref, out_ref):
    count, _, nz = in_ref.shape
    h, mass, rhs, ends = [], [], [], []
    passed_m = passed_b = None
    for i in range(count):
        low, high = in_ref[i, 0:8, :], in_ref[i, 8:16, :]
        g = jnp.broadcast_to(in_ref[i, 6:7, :], (8, nz))
        m_f = jnp.broadcast_to(in_ref[i, 7:8, :], (8, nz))
        face = jnp.broadcast_to(in_ref[i, 14:15, :], (8, nz))
        m_l = jnp.broadcast_to(in_ref[i, 15:16, :], (8, nz))
        inv = 1.0 / (g + face + m_l)
        a, c = g * inv, face * inv
        m, b = m_f + a * m_l, low + a * high
        if i > 0:
            m, b = m + passed_m, b + passed_b
        passed_m, passed_b = c * m_l, c * high
        h.append(a * face)
        mass.append(m)
        rhs.append(b)
        ends.append((a, c, high * inv))
    half = count // 2
    scale, ratio = [None] * count, [None] * count
    for i in range(half - 1):
        inv = 1.0 / (mass[i] + h[i])
        q = h[i] * inv
        scale[i], ratio[i] = rhs[i] * inv, q
        mass[i + 1] = mass[i + 1] + q * mass[i]
        rhs[i + 1] = rhs[i + 1] + q * rhs[i]
    mass[count - 1] = mass[count - 1] + h[count - 1]
    for i in range(count - 1, half, -1):
        inv = 1.0 / (mass[i] + h[i - 1])
        q = h[i - 1] * inv
        scale[i], ratio[i] = rhs[i] * inv, q
        mass[i - 1] = mass[i - 1] + q * mass[i]
        rhs[i - 1] = rhs[i - 1] + q * rhs[i]
    inv = 1.0 / (mass[half - 1] + h[half - 1])
    q = h[half - 1] * inv
    first = [None] * (count + 1)
    first[half] = (rhs[half] + q * rhs[half - 1]) / (mass[half] + q * mass[half - 1])
    first[half - 1] = rhs[half - 1] * inv + q * first[half]
    for i in range(half - 2, -1, -1):
        first[i] = scale[i] + ratio[i] * first[i + 1]
    for i in range(half + 1, count):
        first[i] = scale[i] + ratio[i] * first[i - 1]
    for i in range(count):
        a, c, part = ends[i]
        last = part + a * first[i]
        if i < count - 1:
            last = last + c * first[i + 1]
        out_ref[i, 0:8, :] = first[i]
        out_ref[i, 8:16, :] = last


def chain(message):
    return pl.pallas_call(
        chain_kernel,
        in_specs=[WHOLE],
        out_specs=WHOLE,
        out_shape=pltpu.VMEM(message.shape, F32),
        compiler_params=SMALL,
        cost_estimate=pl.CostEstimate(flops=10**6, bytes_accessed=10**6, transcendentals=0),
        name="chain",
    )(message)


def back_kernel(coef_ref, ends_ref, part_ref, out_hbm, out_ref, out_sem):
    carried, nx, ny, _ = part_ref.shape
    groups = carried // SB

    def put(g):
        return pltpu.make_async_copy(out_ref.at[pl.ds(g * SB, SB)], out_hbm.at[pl.ds(g * SB, SB)], out_sem.at[g])

    @pl.loop(0, groups)
    def _(g):
        for t in range(SB):
            s = g * SB + t
            first = ends_ref[pl.ds(place(s), ny, stride=GROUPS * ROWS), :]
            value = ends_ref[pl.ds(place(s) + 8, ny, stride=GROUPS * ROWS), :]
            out_ref[s, 0] = first
            out_ref[s, nx - 1] = value
            for p in range(nx - 2, 0, -1):
                value = part_ref[s, p] + coef_ref[0, p] * first + coef_ref[1, p] * value
                out_ref[s, p] = value
        put(g).start()

    @pl.loop(0, groups)
    def _(g):
        put(g).wait()


def back(part, coef, ends):
    groups = part.shape[0] // SB
    return pl.pallas_call(
        back_kernel,
        in_specs=[WHOLE, WHOLE, WHOLE],
        out_specs=ANY,
        out_shape=jax.ShapeDtypeStruct(part.shape, F32),
        scratch_shapes=[pltpu.VMEM(part.shape, F32), pltpu.SemaphoreType.DMA((groups,))],
        compiler_params=SMALL,
        cost_estimate=pl.CostEstimate(flops=2 * 10**6, bytes_accessed=3 * 10**6, transcendentals=0),
        name="back",
    )(coef, ends, part)


def resident(value):
    return pltpu.with_memory_space_constraint(value, pltpu.VMEM)


def shards(
    adjoint, log_conc, levels, conduct, orders_fwd, orders_rev, stoich, rate_fwd, rate_rev, diffusivity
):
    carried, nx, ny, nz = adjoint.shape
    rows_y, blocks = lax.axis_size("gy"), lax.axis_size("gx")
    near = lax.ppermute(adjoint, "gz", [(0, 1), (1, 0)])
    tail, head = edges(adjoint)
    low = lax.ppermute(tail, "gy", [(i, i + 1) for i in range(rows_y - 1)])
    high = lax.ppermute(head, "gy", [(i + 1, i) for i in range(rows_y - 1)])
    chem = chemistry(adjoint, log_conc, levels, orders_fwd, orders_rev, stoich, rate_fwd, rate_rev)
    part, coef, message = local_part(diffusivity, adjoint, chem, near, low, high, conduct)
    message = lax.all_to_all(message.reshape(blocks, ROWS, nz), "gx", 0, 0, tiled=True)
    ends = lax.all_to_all(chain(message), "gx", 0, 0, tiled=True)
    return back(part, coef, ends.reshape(blocks * ROWS, nz))


def solution(mesh):
    cells = P(None, "gx", "gy", "gz")
    planes = P("gx", "gy", "gz")
    in_specs = (cells, cells, planes, planes, P(), P(), P(), P(), P(), P())
    return jax.shard_map(shards, mesh=mesh, in_specs=in_specs, out_specs=cells, check_vma=False)
```

time: 550 us -> 71.8 us (0.13)
  blocking collectives: 254 us -> 40.4 us
  other arithmetic: 127 us -> 0 us
  local copies, waits for them, and re-layouts: 69.9 us -> 1.4 us
  waiting for transfers between devices: 36.8 us -> 0.01 us
  matrix products: 25.7 us -> 0 us
  Pallas kernels: 0 us -> 23.7 us
  between operations: 13.6 us -> 0.19 us
  starting transfers between devices: 13.7 us -> 5.86 us
    all_gather x6 -> x0, blocking collectives: 254 us -> none  [carried_in(): pieces = jax.tree.map(lambda part: lax.all_gather(part, axis), value)]
    select_n x128 -> x0, other arithmetic: 62.7 us -> none  [the longest x124 60.3 us: hop(): jnp.where(position < mine, new, old)]
    all_to_all x0 -> x2, blocking collectives: none -> 40.4 us  [the longest x1 24.1 us: shards(): lax.all_to_all(message.reshape(blocks, ROWS, nz), 'gx', 0, 0, tiled=True)]
    dynamic_update_slice x64 -> x0, other arithmetic: 36.9 us -> none  [the longest x16 14.9 us: back_advance(): w_all = lax.dynamic_update_index_in_dim(w_all, w_cell, index, 1)]
    all_gather x3 -> x0, waiting for transfers between devices: 36.1 us -> none  [carried_in(): pieces = jax.tree.map(lambda part: lax.all_gather(part, axis), value)]
    dot_general x12 -> x0, matrix products: 25.7 us -> none  [the longest x4 11.9 us: react_terms(): jnp.dot(orders_rev[:, :carried].T, act_rev, preferred_element_type=jnp.fl...]
    pallas_call x0 -> x5, Pallas kernels: none -> 23.7 us  [the longest x1 17.7 us: chemistry(): pl.pallas_call(chem_kernel, grid=(nx // XB,), in_specs=[pl.BlockSpec((car...]
    unnamed x31 -> x20, local copies, waits for them, and re-layouts: 15.1 us -> 1.4 us
  transfers between devices with their start and end apart: 8 -> 3, of which waited for: 1 -> 0; matrix products, arithmetic and copies ran while one was open for 13% -> 0% of each run, Pallas kernels for 0% -> 25%
where the time goes in v1:
time: 71.8 us; the launch traced here: 71.5 us
  blocking collectives  40.4 us (56%)
  Pallas kernels  23.7 us (33%)
  starting transfers between devices  5.86 us (8%)
  local copies, waits for them, and re-layouts  1.4 us (2%)
    all_to_all x1, blocking collectives, shards(): lax.all_to_all(message.reshape(blocks, ROWS, nz), 'gx', 0, 0, tiled=True)  24.1 us
    pallas_call x1, Pallas kernels, chemistry(): pl.pallas_call(chem_kernel, grid=(nx // XB,), in_specs=[pl.BlockSpec((car...  17.7 us
    all_to_all x1, blocking collectives, shards(): ends = lax.all_to_all(chain(message), 'gx', 0, 0, tiled=True)  16.3 us
    pallas_call x1, Pallas kernels, local_part(): pl.pallas_call(local_kernel, in_specs=[smem] + [WHOLE] * 6, out_specs=[WH...  4.02 us
    ppermute x1, starting transfers between devices, shards(): low = lax.ppermute(tail, 'gy', [(i, i + 1) for i in range(rows_y - 1)])  3.4 us
    ppermute x1, starting transfers between devices, shards(): high = lax.ppermute(head, 'gy', [(i + 1, i) for i in range(rows_y - 1)])  2.46 us
  transfers between devices with their start and end apart: 3, of which 0 were waited for; matrix products, arithmetic and copies ran while one was open for 0% of the time, Pallas kernels for 25%

profile of v1, /device:TPU:2, one launch (start us, length us, event | category | flops | bytes accessed | tf_op | source)
XLA Modules:
  0.0 71.5 jit_solution(17850082166845817187)
XLA Ops:
  0.0 0.0 collective-permute-start
  0.0 0.0 copy-start
  0.0 1.4 %copy-done = f32[22,16,8,128]{3,2,1,0:T(8,128)S(1)} copy-done((f32[22,16,8,128]{3,2,1,0:T(8,128)S(1)}, f32[22,16,8,128]{3,2,1,0:T(8,128)}, u32[]{:S(2)}) %copy-start) | copy-done | bytes 1441816
  1.4 0.0 copy-start.3
  1.4 0.0 copy-start.4
  1.4 0.0 copy-start.5
  1.4 0.0 copy-start.7
  1.4 0.0 copy-start.8
  1.4 0.0 copy-start.9
  1.4 0.4 edges.1
  1.8 3.4 %collective-permute-start.1 = (f32[22,16,2,128]{3,2,1,0:T(2,128)S(1)}, f32[22,16,2,128]{3,2,1,0:T(2,128)S(1)}, u32[]{:S(2)}, u32[]{:S(2)}) collective-permute-start(f32[22,16,2,128]{3,2,1,0:T(2,128)S(1)} %get-tuple-element.10), channel_id=1, source_target_pairs={{0,2},{2,4},{4,6},{1,3},{3,5},{5,7},{8,10},{10,12},{12,14},{9,11},... | collective-permute-start | bytes 1081352 | tf_op jit(solution)/shard_map/ppermute | solution.py:391
  5.2 2.5 %collective-permute-start.2 = (f32[22,16,2,128]{3,2,1,0:T(2,128)S(1)}, f32[22,16,2,128]{3,2,1,0:T(2,128)S(1)}, u32[]{:S(2)}, u32[]{:S(2)}) collective-permute-start(f32[22,16,2,128]{3,2,1,0:T(2,128)S(1)} %get-tuple-element.11), channel_id=1, source_target_pairs={{2,0},{4,2},{6,4},{3,1},{5,3},{7,5},{10,8},{12,10},{14,12},{11,9},... | collective-permute-start | bytes 1081352 | tf_op jit(solution)/shard_map/ppermute | solution.py:392
  7.7 0.0 copy-done.3
  7.7 0.0 copy-done.4
  7.7 0.0 copy-done.5
  7.7 0.0 copy-done.6
  7.7 0.0 copy-done.7
  7.7 0.0 copy-done.8
  7.7 0.0 copy-done.9
  7.7 0.0 copy-start.1
  7.7 0.0 copy-start.2
  7.8 17.7 %chem.1.chem_ref = f32[22,16,8,128]{3,2,1,0:T(8,128)S(1)} custom-call(f32[22,16,8,128]{3,2,1,0:T(8,128)S(1)} %copy-done, bf16[32,16,8,128]{3,2,1,0:T(8,128)(2,1)S(1)} %copy-done.3, s32[16,8,128]{2,1,0:T(8,128)S(1)} %copy-done.4, bf16[32,206]{1,0:T(8,128)(2,1)S(1)} %bitcast.9, bf16[32,206]{1,0:T(8,128)(2,1)S(1)} %bitcast.10, bf16[22,206]{1,0:T(8,128)(2,1)S(1)} %bitcast.11, ...), custom_call_target="tpu_custom_call" | custom-call | flops 12000000000 | bytes 4000000 | tf_op jit(solution)/shard_map/chem/pallas_call | solution.py:132
  25.4 0.0 collective-permute-done.1.low_ref
  25.5 0.0 collective-permute-done.2.high_ref
  25.5 0.0 collective-permute-done.near_ref
  25.5 0.0 copy-done.1
  25.5 0.0 copy-done.2
  25.5 4.0 %local.1 = (f32[22,16,8,128]{3,2,1,0:T(8,128)S(1)}, f32[2,16,8,128]{3,2,1,0:T(8,128)S(1)}, f32[512,128]{1,0:T(8,128)S(1)}) custom-call(f32[22]{0:T(128)S(1)} %copy-done.2, f32[16,8,128]{2,1,0:T(8,128)S(1)} %copy-done.1, f32[22,16,8,128]{3,2,1,0:T(8,128)S(1)} %copy-done, f32[22,16,8,128]{3,2,1,0:T(8,128)S(1)} %chem.1.chem_ref, ...), custom_call_target="tpu_custom_call" | custom-call | flops 20000000 | bytes 7000000 | tf_op jit(solution)/shard_map/local/pallas_call | solution.py:260
  29.5 24.1 %all_to_all.10.in_ref = f32[32,16,128]{2,1,0:T(8,128)S(1)} all-to-all(f32[32,16,128]{2,1,0:T(8,128)S(1)} %bitcast.8), channel_id=1, replica_groups=mesh['gx'=32,'gy'=4,'gz'=2] {'gx'}, dimensions={0} | all-to-all | bytes 524288 | tf_op jit(solution)/shard_map/all_to_all | solution.py:395
  53.6 0.2 chain.1
  53.8 16.3 %all_to_all.11 = f32[32,16,128]{2,1,0:T(8,128)S(1)} all-to-all(f32[32,16,128]{2,1,0:T(8,128)S(1)} %chain.1), channel_id=1, replica_groups=mesh['gx'=32,'gy'=4,'gz'=2] {'gx'}, dimensions={0} | all-to-all | bytes 524288 | tf_op jit(solution)/shard_map/all_to_all | solution.py:396
  70.1 1.4 %back.1 = f32[22,16,8,128]{3,2,1,0:T(8,128)} custom-call(f32[2,16,8,128]{3,2,1,0:T(8,128)S(1)} %get-tuple-element.12.coef_ref, f32[512,128]{1,0:T(8,128)S(1)} %bitcast.7, f32[22,16,8,128]{3,2,1,0:T(8,128)S(1)} %get-tuple-element.14.part_ref), custom_call_target="tpu_custom_call" | custom-call | flops 2000000 | bytes 3000000 | tf_op jit(solution)/shard_map/back/pallas_call | solution.py:368
  (1 shorter events, 0.0 us)
Async XLA Ops:
  0.0 25.5 %collective-permute-start = (f32[22,16,8,128]{3,2,1,0:T(8,128)}, f32[22,16,8,128]{3,2,1,0:T(8,128)S(1)}, u32[]{:S(2)}, u32[]{:S(2)}) collective-permute-start(f32[22,16,8,128]{3,2,1,0:T(8,128)} %adj_ref.5), channel_id=1, source_target_pairs={{0,1},{1,0},{2,3},{3,2},{4,5},{5,4},{6,7},{7,6},{8,9},{9,8},{10,11... | collective-permute-start | bytes 4325384 | tf_op jit(solution)/shard_map/ppermute | solution.py:389
  0.0 1.4 %copy-start = (f32[22,16,8,128]{3,2,1,0:T(8,128)S(1)}, f32[22,16,8,128]{3,2,1,0:T(8,128)}, u32[]{:S(2)}) copy-start(f32[22,16,8,128]{3,2,1,0:T(8,128)} %adj_ref.5) | copy-start | bytes 4325380
  1.4 6.3 %copy-start.3 = (bf16[32,16,8,128]{3,2,1,0:T(8,128)(2,1)S(1)}, bf16[32,16,8,128]{3,2,1,0:T(8,128)(2,1)}, u32[]{:S(2)}) copy-start(bf16[32,16,8,128]{3,2,1,0:T(8,128)(2,1)} %conc_ref.1) | copy-start | bytes 3145732
  1.4 6.3 %copy-start.4 = (s32[16,8,128]{2,1,0:T(8,128)S(1)}, s32[16,8,128]{2,1,0:T(8,128)}, u32[]{:S(2)}) copy-start(s32[16,8,128]{2,1,0:T(8,128)} %lev_ref.1) | copy-start | bytes 196612
  1.4 6.3 %copy-start.5 = (bf16[206,32]{0,1:T(8,128)(2,1)S(1)}, bf16[206,32]{0,1:T(8,128)(2,1)}, u32[]{:S(2)}) copy-start(bf16[206,32]{0,1:T(8,128)(2,1)} %param.14) | copy-start | bytes 39556
  1.4 6.3 %copy-start.6 = (bf16[206,32]{0,1:T(8,128)(2,1)S(1)}, bf16[206,32]{0,1:T(8,128)(2,1)}, u32[]{:S(2)}) copy-start(bf16[206,32]{0,1:T(8,128)(2,1)} %param.15) | copy-start | bytes 39556
  1.4 6.3 %copy-start.7 = (bf16[206,22]{0,1:T(8,128)(2,1)S(1)}, bf16[206,22]{0,1:T(8,128)(2,1)}, u32[]{:S(2)}) copy-start(bf16[206,22]{0,1:T(8,128)(2,1)} %param.16) | copy-start | bytes 27196
  1.4 6.3 %copy-start.8 = (f32[206]{0:T(256)S(1)}, f32[206]{0:T(256)}, u32[]{:S(2)}) copy-start(f32[206]{0:T(256)} %param.17) | copy-start | bytes 2476
  1.4 6.3 %copy-start.9 = (f32[206]{0:T(256)S(1)}, f32[206]{0:T(256)}, u32[]{:S(2)}) copy-start(f32[206]{0:T(256)} %param.18) | copy-start | bytes 2476
  1.8 23.7 %collective-permute-start.1 = (f32[22,16,2,128]{3,2,1,0:T(2,128)S(1)}, f32[22,16,2,128]{3,2,1,0:T(2,128)S(1)}, u32[]{:S(2)}, u32[]{:S(2)}) collective-permute-start(f32[22,16,2,128]{3,2,1,0:T(2,128)S(1)} %get-tuple-element.10), channel_id=1, source_target_pairs={{0,2},{2,4},{4,6},{1,3},{3,5},{5,7},{8,10},{10,12},{12,14},{9,11},... | collective-permute-start | bytes 1081352 | tf_op jit(solution)/shard_map/ppermute | solution.py:391
  5.2 20.3 %collective-permute-start.2 = (f32[22,16,2,128]{3,2,1,0:T(2,128)S(1)}, f32[22,16,2,128]{3,2,1,0:T(2,128)S(1)}, u32[]{:S(2)}, u32[]{:S(2)}) collective-permute-start(f32[22,16,2,128]{3,2,1,0:T(2,128)S(1)} %get-tuple-element.11), channel_id=1, source_target_pairs={{2,0},{4,2},{6,4},{3,1},{5,3},{7,5},{10,8},{12,10},{14,12},{11,9},... | collective-permute-start | bytes 1081352 | tf_op jit(solution)/shard_map/ppermute | solution.py:392
  7.7 17.7 %copy-start.1 = (f32[16,8,128]{2,1,0:T(8,128)S(1)}, f32[16,8,128]{2,1,0:T(8,128)}, u32[]{:S(2)}) copy-start(f32[16,8,128]{2,1,0:T(8,128)} %cond_ref.1) | copy-start | bytes 196612
  7.7 17.7 %copy-start.2 = (f32[22]{0:T(128)S(1)}, f32[22]{0:T(128)}, u32[]{:S(2)}) copy-start(f32[22]{0:T(128)} %diff_ref.1) | copy-start | bytes 268

commit v2 on v1

--- a/solution.py
+++ b/solution.py
@@ -15,8 +15,9 @@
 
 K_ROWS = 96
 R_PAD = 208
-CHUNKS = ((0, 64), (64, 48), (112, 48), (160, 48))
-TILE = 256
+STRIP = 16
+CHUNKS = tuple((start, STRIP) for start in range(0, R_PAD, STRIP))
+TILE = 512
 XB = 2
 LIMIT = 12 * 1024 * 1024
 F32 = jnp.float32
@@ -108,10 +109,9 @@
         for tile in range(ny // per_tile):
             slot = (x * (ny // per_tile) + tile) % act_ref.shape[0]
             data = x_ref[x, :, tile * TILE : (tile + 1) * TILE]
-            base = 0
+            every = dot(w_ref[...], data)
             for start, size in CHUNKS:
-                got = dot(w_ref[base : base + 3 * size, :], data)
-                base += 3 * size
+                got = every[3 * start : 3 * (start + size)]
                 weight = got[2 * size :]
                 act_ref[slot, 0, start : start + size, :] = (jnp.exp2(got[:size]) * weight).astype(BF16)
                 act_ref[slot, 1, start : start + size, :] = (jnp.exp2(got[size : 2 * size]) * weight).astype(BF16)
@@ -146,7 +146,7 @@
             pltpu.VMEM((2, 32, R_PAD), BF16),
             pltpu.VMEM((species * XB * ny, nz), F32),
             pltpu.VMEM((XB, K_ROWS, ny * nz), BF16),
-            pltpu.VMEM((4, 2, R_PAD, TILE), BF16),
+            pltpu.VMEM((2, 2, R_PAD, TILE), BF16),
         ],
         compiler_params=pltpu.CompilerParams(dimension_semantics=("arbitrary",), vmem_limit_bytes=LIMIT),
         cost_estimate=pl.CostEstimate(flops=12 * 10**9, bytes_accessed=4 * 10**6, transcendentals=6_750_000),
@@ -167,14 +167,25 @@
     return s // GROUP * ROWS + s % GROUP
 
 
-def edges_kernel(adj_ref, low_ref, high_ref):
+PACK = 4
+
+
+def edges_kernel(adj_ref, low_ref, high_ref, side_ref):
     carried, nx, ny, nz = adj_ref.shape
+    lane = iota((ny, nz), 1)
+    own_shift = jnp.where(lax.axis_index("gz") == 0, 2, 0)
+    side_ref[...] = jnp.zeros(side_ref.shape, F32)
 
     @pl.loop(0, carried)
     def _(s):
+        start = s % PACK * 2 * nx
+        packed = side_ref[s // PACK]
         for x in range(nx):
             low_ref[s, x] = adj_ref[s, x, ny - 2 : ny, :]
             high_ref[s, x] = adj_ref[s, x, 0:2, :]
+            moved = pltpu.roll(adj_ref[s, x], lax.rem(start + (2 * x + own_shift), nz), 1)
+            packed = jnp.where(lane // 2 == start // 2 + x, moved, packed)
+        side_ref[s // PACK] = packed
 
 
 def edges(adjoint):
@@ -183,8 +194,8 @@
     return pl.pallas_call(
         edges_kernel,
         in_specs=[WHOLE],
-        out_specs=[WHOLE, WHOLE],
-        out_shape=[shape, shape],
+        out_specs=[WHOLE] * 3,
+        out_shape=[shape, shape, pltpu.VMEM((-(-carried // PACK), ny, nz), F32)],
         compiler_params=SMALL,
         cost_estimate=pl.CostEstimate(flops=0, bytes_accessed=2 * 10**6, transcendentals=0),
         name="edges",
@@ -219,39 +230,44 @@
     lane, row = iota((ny, nz), 1), iota((ny, nz), 0)
     keep_low = jnp.where(lax.axis_index("gz") == 0, 1.0, 0.0)
     keep_high = 1.0 - keep_low
-
-    @pl.loop(0, carried)
-    def _(s):
-        scale = diff_ref[s] * (SECTION * STEP / 12.0)
-        b_first, carry = None, None
-        for p in range(nx):
-            own = adj_ref[s, p]
-            near = near_ref[s, p]
-            from_high = near * keep_low
-            from_low = near * keep_high
-            z_up1 = pltpu.roll(jnp.where(lane < 1, from_high, own), nz - 1, 1)
-            z_up2 = pltpu.roll(jnp.where(lane < 2, from_high, own), nz - 2, 1)
-            z_dn1 = pltpu.roll(jnp.where(lane >= nz - 1, from_low, own), 1, 1)
-            z_dn2 = pltpu.roll(jnp.where(lane >= nz - 2, from_low, own), 2, 1)
-            low0, low1 = low_ref[s, p, 0:1, :], low_ref[s, p, 1:2, :]
-            high0, high1 = high_ref[s, p, 0:1, :], high_ref[s, p, 1:2, :]
-            y_up1 = jnp.where(row == ny - 1, high0, pltpu.roll(own, ny - 1, 0))
-            y_up2 = jnp.where(row == ny - 1, high1, jnp.where(row == ny - 2, high0, pltpu.roll(own, ny - 2, 0)))
-            y_dn1 = jnp.where(row == 0, low1, pltpu.roll(own, 1, 0))
-            y_dn2 = jnp.where(row == 0, low0, jnp.where(row == 1, low1, pltpu.roll(own, 2, 0)))
-            spread = 16.0 * ((z_up1 + z_dn1) + (y_up1 + y_dn1)) - ((z_up2 + z_dn2) + (y_up2 + y_dn2)) - 60.0 * own
-            b = SECTION * own + (SECTION * STEP) * chem_ref[s, p] + scale * spread
-            if p == 0:
-                b_first = b
-            elif p < nx - 1:
-                full = b if carry is None else b + carry
-                part_ref[s, p] = full * inv_ref[p]
-                b_first = b_first + coef_ref[0, p] * full
-                carry = coef_ref[1, p] * full
-            else:
-                b_last = b + carry
-        msg_ref[pl.ds(place(s), ny, stride=stride), :] = b_first
-        msg_ref[pl.ds(place(s) + 8, ny, stride=stride), :] = b_last
+    near_shift = jnp.where(lax.axis_index("gz") == 0, 0, 2)
+
+    @pl.loop(0, carried // SB)
+    def _(g):
+        for t in range(SB):
+            s = g * SB + t
+            scale = diff_ref[s] * (SECTION * STEP / 12.0)
+            side = near_ref[s // PACK]
+            back_by = nz - s % PACK * 2 * nx - near_shift
+            b_first, carry = None, None
+            for p in range(nx):
+                own = adj_ref[s, p]
+                near = pltpu.roll(side, lax.rem(back_by + (nz - 2 * p), nz), 1)
+                from_high = near * keep_low
+                from_low = near * keep_high
+                z_up1 = pltpu.roll(jnp.where(lane < 1, from_high, own), nz - 1, 1)
+                z_up2 = pltpu.roll(jnp.where(lane < 2, from_high, own), nz - 2, 1)
+                z_dn1 = pltpu.roll(jnp.where(lane >= nz - 1, from_low, own), 1, 1)
+                z_dn2 = pltpu.roll(jnp.where(lane >= nz - 2, from_low, own), 2, 1)
+                low0, low1 = low_ref[s, p, 0:1, :], low_ref[s, p, 1:2, :]
+                high0, high1 = high_ref[s, p, 0:1, :], high_ref[s, p, 1:2, :]
+                y_up1 = jnp.where(row == ny - 1, high0, pltpu.roll(own, ny - 1, 0))
+                y_up2 = jnp.where(row == ny - 1, high1, jnp.where(row == ny - 2, high0, pltpu.roll(own, ny - 2, 0)))
+                y_dn1 = jnp.where(row == 0, low1, pltpu.roll(own, 1, 0))
+                y_dn2 = jnp.where(row == 0, low0, jnp.where(row == 1, low1, pltpu.roll(own, 2, 0)))
+                spread = 16.0 * ((z_up1 + z_dn1) + (y_up1 + y_dn1)) - ((z_up2 + z_dn2) + (y_up2 + y_dn2)) - 60.0 * own
+                b = SECTION * own + (SECTION * STEP) * chem_ref[s, p] + scale * spread
+                if p == 0:
+                    b_first = b
+                elif p < nx - 1:
+                    full = b if carry is None else b + carry
+                    part_ref[s, p] = full * inv_ref[p]
+                    b_first = b_first + coef_ref[0, p] * full
+                    carry = coef_ref[1, p] * full
+                else:
+                    b_last = b + carry
+            msg_ref[pl.ds(place(s), ny, stride=stride), :] = b_first
+            msg_ref[pl.ds(place(s) + 8, ny, stride=stride), :] = b_last
 
 
 def local_part(diffusivity, adjoint, chem, near, low, high, conduct):
@@ -386,10 +402,10 @@
 ):
     carried, nx, ny, nz = adjoint.shape
     rows_y, blocks = lax.axis_size("gy"), lax.axis_size("gx")
-    near = lax.ppermute(adjoint, "gz", [(0, 1), (1, 0)])
-    tail, head = edges(adjoint)
+    tail, head, side = edges(adjoint)
     low = lax.ppermute(tail, "gy", [(i, i + 1) for i in range(rows_y - 1)])
     high = lax.ppermute(head, "gy", [(i + 1, i) for i in range(rows_y - 1)])
+    near = lax.ppermute(side, "gz", [(0, 1), (1, 0)])
     chem = chemistry(adjoint, log_conc, levels, orders_fwd, orders_rev, stoich, rate_fwd, rate_rev)
     part, coef, message = local_part(diffusivity, adjoint, chem, near, low, high, conduct)
     message = lax.all_to_all(message.reshape(blocks, ROWS, nz), "gx", 0, 0, tiled=True)

time: 71.8 us -> 70.4 us (0.981)
  Pallas kernels: 23.7 us -> 22.3 us
    pallas_call x1, Pallas kernels: 17.7 us -> 13.5 us  [chemistry(): pl.pallas_call(chem_kernel, grid=(nx // XB,), in_specs=[pl.BlockSpec((car...]
    pallas_call x1, Pallas kernels: 0.37 us -> 2.5 us  [edges(): pl.pallas_call(edges_kernel, in_specs=[WHOLE], out_specs=[WHOLE] * 3, out...]
  transfers between devices with their start and end apart: 3 -> 3, of which waited for: 0 -> 0; matrix products, arithmetic and copies ran while one was open for 0% -> 0% of each run, Pallas kernels for 25% -> 19%
where the time goes in v2:
time: 70.4 us; the launch traced here: 70.2 us
  blocking collectives  40.3 us (57%)
  Pallas kernels  22.3 us (32%)
  starting transfers between devices  5.95 us (8%)
  local copies, waits for them, and re-layouts  1.4 us (2%)
    all_to_all x1, blocking collectives, shards(): lax.all_to_all(message.reshape(blocks, ROWS, nz), 'gx', 0, 0, tiled=True)  24.1 us
    all_to_all x1, blocking collectives, shards(): ends = lax.all_to_all(chain(message), 'gx', 0, 0, tiled=True)  16.3 us
    pallas_call x1, Pallas kernels, chemistry(): pl.pallas_call(chem_kernel, grid=(nx // XB,), in_specs=[pl.BlockSpec((car...  13.5 us
    pallas_call x1, Pallas kernels, local_part(): pl.pallas_call(local_kernel, in_specs=[smem] + [WHOLE] * 6, out_specs=[WH...  4.73 us
    ppermute x1, starting transfers between devices, shards(): low = lax.ppermute(tail, 'gy', [(i, i + 1) for i in range(rows_y - 1)])  3.4 us
    pallas_call x1, Pallas kernels, edges(): pl.pallas_call(edges_kernel, in_specs=[WHOLE], out_specs=[WHOLE] * 3, out...  2.5 us
    ppermute x1, starting transfers between devices, shards(): high = lax.ppermute(head, 'gy', [(i + 1, i) for i in range(rows_y - 1)])  2.46 us
  transfers between devices with their start and end apart: 3, of which 0 were waited for; matrix products, arithmetic and copies ran while one was open for 0% of the time, Pallas kernels for 19%

profile of v2, /device:TPU:2, one launch (start us, length us, event | category | flops | bytes accessed | tf_op | source)
XLA Modules:
  0.0 70.2 jit_solution(15790075703294447866)
XLA Ops:
  0.0 0.0 copy-start
  0.0 1.4 %copy-done = f32[22,16,8,128]{3,2,1,0:T(8,128)S(1)} copy-done((f32[22,16,8,128]{3,2,1,0:T(8,128)S(1)}, f32[22,16,8,128]{3,2,1,0:T(8,128)}, u32[]{:S(2)}) %copy-start) | copy-done | bytes 1441816
  1.4 0.0 copy-start.3
  1.4 0.0 copy-start.4
  1.4 0.0 copy-start.5
  1.4 0.0 copy-start.7
  1.4 0.0 copy-start.8
  1.4 0.0 copy-start.9
  1.4 2.5 %edges.1 = (f32[22,16,2,128]{3,2,1,0:T(2,128)S(1)}, f32[22,16,2,128]{3,2,1,0:T(2,128)S(1)}, f32[6,8,128]{2,1,0:T(8,128)S(1)}) custom-call(f32[22,16,8,128]{3,2,1,0:T(8,128)S(1)} %copy-done), custom_call_target="tpu_custom_call" | custom-call | bytes 2000000 | tf_op jit(solution)/shard_map/edges/pallas_call | solution.py:194
  3.9 0.1 collective-permute-start
  4.0 3.4 %collective-permute-start.1 = (f32[22,16,2,128]{3,2,1,0:T(2,128)S(1)}, f32[22,16,2,128]{3,2,1,0:T(2,128)S(1)}, u32[]{:S(2)}, u32[]{:S(2)}) collective-permute-start(f32[22,16,2,128]{3,2,1,0:T(2,128)S(1)} %get-tuple-element.12), channel_id=1, source_target_pairs={{0,2},{2,4},{4,6},{1,3},{3,5},{5,7},{8,10},{10,12},{12,14},{9,11},... | collective-permute-start | bytes 1081352 | tf_op jit(solution)/shard_map/ppermute | solution.py:406
  7.4 2.5 %collective-permute-start.2 = (f32[22,16,2,128]{3,2,1,0:T(2,128)S(1)}, f32[22,16,2,128]{3,2,1,0:T(2,128)S(1)}, u32[]{:S(2)}, u32[]{:S(2)}) collective-permute-start(f32[22,16,2,128]{3,2,1,0:T(2,128)S(1)} %get-tuple-element.13), channel_id=1, source_target_pairs={{2,0},{4,2},{6,4},{3,1},{5,3},{7,5},{10,8},{12,10},{14,12},{11,9},... | collective-permute-start | bytes 1081352 | tf_op jit(solution)/shard_map/ppermute | solution.py:407
  9.9 0.0 copy-done.3
  9.9 0.0 copy-done.4
  9.9 0.0 copy-done.5
  9.9 0.0 copy-done.6
  9.9 0.0 copy-done.7
  9.9 0.0 copy-done.8
  9.9 0.0 copy-done.9
  9.9 0.0 copy-start.1
  10.0 0.0 copy-start.2
  10.0 13.5 %chem.1.chem_ref = f32[22,16,8,128]{3,2,1,0:T(8,128)S(1)} custom-call(f32[22,16,8,128]{3,2,1,0:T(8,128)S(1)} %copy-done, bf16[32,16,8,128]{3,2,1,0:T(8,128)(2,1)S(1)} %copy-done.3, s32[16,8,128]{2,1,0:T(8,128)S(1)} %copy-done.4, bf16[32,206]{1,0:T(8,128)(2,1)S(1)} %bitcast.9, bf16[32,206]{1,0:T(8,128)(2,1)S(1)} %bitcast.10, bf16[22,206]{1,0:T(8,128)(2,1)S(1)} %bitcast.11, ...), custom_call_target="tpu_custom_call" | custom-call | flops 12000000000 | bytes 4000000 | tf_op jit(solution)/shard_map/chem/pallas_call | solution.py:132
  23.5 0.0 collective-permute-done.near_ref
  23.5 0.0 collective-permute-done.1.low_ref
  23.5 0.0 collective-permute-done.2.high_ref
  23.5 0.0 copy-done.1
  23.5 0.0 copy-done.2
  23.5 4.7 %local.1 = (f32[22,16,8,128]{3,2,1,0:T(8,128)S(1)}, f32[2,16,8,128]{3,2,1,0:T(8,128)S(1)}, f32[512,128]{1,0:T(8,128)S(1)}) custom-call(f32[22]{0:T(128)S(1)} %copy-done.2, f32[16,8,128]{2,1,0:T(8,128)S(1)} %copy-done.1, f32[22,16,8,128]{3,2,1,0:T(8,128)S(1)} %copy-done, f32[22,16,8,128]{3,2,1,0:T(8,128)S(1)} %chem.1.chem_ref, ...), custom_call_target="tpu_custom_call" | custom-call | flops 20000000 | bytes 7000000 | tf_op jit(solution)/shard_map/local/pallas_call | solution.py:276
  28.2 24.1 %all_to_all.10.in_ref = f32[32,16,128]{2,1,0:T(8,128)S(1)} all-to-all(f32[32,16,128]{2,1,0:T(8,128)S(1)} %bitcast.8), channel_id=1, replica_groups=mesh['gx'=32,'gy'=4,'gz'=2] {'gx'}, dimensions={0} | all-to-all | bytes 524288 | tf_op jit(solution)/shard_map/all_to_all | solution.py:411
  52.3 0.2 chain.1
  52.5 16.3 %all_to_all.11 = f32[32,16,128]{2,1,0:T(8,128)S(1)} all-to-all(f32[32,16,128]{2,1,0:T(8,128)S(1)} %chain.1), channel_id=1, replica_groups=mesh['gx'=32,'gy'=4,'gz'=2] {'gx'}, dimensions={0} | all-to-all | bytes 524288 | tf_op jit(solution)/shard_map/all_to_all | solution.py:412
  68.8 1.4 %back.1 = f32[22,16,8,128]{3,2,1,0:T(8,128)} custom-call(f32[2,16,8,128]{3,2,1,0:T(8,128)S(1)} %get-tuple-element.14.coef_ref, f32[512,128]{1,0:T(8,128)S(1)} %bitcast.7, f32[22,16,8,128]{3,2,1,0:T(8,128)S(1)} %get-tuple-element.16.part_ref), custom_call_target="tpu_custom_call" | custom-call | flops 2000000 | bytes 3000000 | tf_op jit(solution)/shard_map/back/pallas_call | solution.py:384
  (1 shorter events, 0.0 us)
Async XLA Ops:
  0.0 1.4 %copy-start = (f32[22,16,8,128]{3,2,1,0:T(8,128)S(1)}, f32[22,16,8,128]{3,2,1,0:T(8,128)}, u32[]{:S(2)}) copy-start(f32[22,16,8,128]{3,2,1,0:T(8,128)} %adj_ref.5) | copy-start | bytes 4325380
  1.4 8.5 %copy-start.3 = (bf16[32,16,8,128]{3,2,1,0:T(8,128)(2,1)S(1)}, bf16[32,16,8,128]{3,2,1,0:T(8,128)(2,1)}, u32[]{:S(2)}) copy-start(bf16[32,16,8,128]{3,2,1,0:T(8,128)(2,1)} %conc_ref.1) | copy-start | bytes 3145732
  1.4 8.5 %copy-start.4 = (s32[16,8,128]{2,1,0:T(8,128)S(1)}, s32[16,8,128]{2,1,0:T(8,128)}, u32[]{:S(2)}) copy-start(s32[16,8,128]{2,1,0:T(8,128)} %lev_ref.1) | copy-start | bytes 196612
  1.4 8.5 %copy-start.5 = (bf16[206,32]{0,1:T(8,128)(2,1)S(1)}, bf16[206,32]{0,1:T(8,128)(2,1)}, u32[]{:S(2)}) copy-start(bf16[206,32]{0,1:T(8,128)(2,1)} %param.14) | copy-start | bytes 39556
  1.4 8.5 %copy-start.6 = (bf16[206,32]{0,1:T(8,128)(2,1)S(1)}, bf16[206,32]{0,1:T(8,128)(2,1)}, u32[]{:S(2)}) copy-start(bf16[206,32]{0,1:T(8,128)(2,1)} %param.15) | copy-start | bytes 39556
  1.4 8.5 %copy-start.7 = (bf16[206,22]{0,1:T(8,128)(2,1)S(1)}, bf16[206,22]{0,1:T(8,128)(2,1)}, u32[]{:S(2)}) copy-start(bf16[206,22]{0,1:T(8,128)(2,1)} %param.16) | copy-start | bytes 27196
  1.4 8.5 %copy-start.8 = (f32[206]{0:T(256)S(1)}, f32[206]{0:T(256)}, u32[]{:S(2)}) copy-start(f32[206]{0:T(256)} %param.17) | copy-start | bytes 2476
  1.4 8.5 %copy-start.9 = (f32[206]{0:T(256)S(1)}, f32[206]{0:T(256)}, u32[]{:S(2)}) copy-start(f32[206]{0:T(256)} %param.18) | copy-start | bytes 2476
  3.9 19.6 %collective-permute-start = (f32[6,8,128]{2,1,0:T(8,128)S(1)}, f32[6,8,128]{2,1,0:T(8,128)S(1)}, u32[]{:S(2)}, u32[]{:S(2)}) collective-permute-start(f32[6,8,128]{2,1,0:T(8,128)S(1)} %get-tuple-element.11), channel_id=1, source_target_pairs={{0,1},{1,0},{2,3},{3,2},{4,5},{5,4},{6,7},{7,6},{8,9},{9,8},{10,11... | collective-permute-start | bytes 73736 | tf_op jit(solution)/shard_map/ppermute | solution.py:408
  4.0 19.5 %collective-permute-start.1 = (f32[22,16,2,128]{3,2,1,0:T(2,128)S(1)}, f32[22,16,2,128]{3,2,1,0:T(2,128)S(1)}, u32[]{:S(2)}, u32[]{:S(2)}) collective-permute-start(f32[22,16,2,128]{3,2,1,0:T(2,128)S(1)} %get-tuple-element.12), channel_id=1, source_target_pairs={{0,2},{2,4},{4,6},{1,3},{3,5},{5,7},{8,10},{10,12},{12,14},{9,11},... | collective-permute-start | bytes 1081352 | tf_op jit(solution)/shard_map/ppermute | solution.py:406
  7.4 16.1 %collective-permute-start.2 = (f32[22,16,2,128]{3,2,1,0:T(2,128)S(1)}, f32[22,16,2,128]{3,2,1,0:T(2,128)S(1)}, u32[]{:S(2)}, u32[]{:S(2)}) collective-permute-start(f32[22,16,2,128]{3,2,1,0:T(2,128)S(1)} %get-tuple-element.13), channel_id=1, source_target_pairs={{2,0},{4,2},{6,4},{3,1},{5,3},{7,5},{10,8},{12,10},{14,12},{11,9},... | collective-permute-start | bytes 1081352 | tf_op jit(solution)/shard_map/ppermute | solution.py:407
  9.9 13.5 %copy-start.1 = (f32[16,8,128]{2,1,0:T(8,128)S(1)}, f32[16,8,128]{2,1,0:T(8,128)}, u32[]{:S(2)}) copy-start(f32[16,8,128]{2,1,0:T(8,128)} %cond_ref.1) | copy-start | bytes 196612
  10.0 13.5 %copy-start.2 = (f32[22]{0:T(128)S(1)}, f32[22]{0:T(128)}, u32[]{:S(2)}) copy-start(f32[22]{0:T(128)} %diff_ref.1) | copy-start | bytes 268

commit v3 on v2

--- a/solution.py
+++ b/solution.py
@@ -10,6 +10,8 @@
 SECTION = 0.02
 STEP = 0.3
 MASS = 0.001
+THIRD = MASS / 3.0
+BODY = MASS + 2.0 * THIRD
 LOG2E = math.log2(math.e)
 OFF = -1024.0
 
@@ -17,7 +19,7 @@
 R_PAD = 208
 STRIP = 16
 CHUNKS = tuple((start, STRIP) for start in range(0, R_PAD, STRIP))
-TILE = 512
+TILE = 1024
 XB = 2
 LIMIT = 12 * 1024 * 1024
 F32 = jnp.float32
@@ -77,12 +79,31 @@
 
 
 def chem_kernel(
-    adj_ref, conc_ref, lev_ref, of_ref, or_ref, st_ref, rf_ref, rr_ref, out_ref,
-    wide_ref, w_ref, c_ref, conc32_ref, x_ref, act_ref,
+    adj_ref, conc_ref, lev_ref, cond_ref, of_ref, or_ref, st_ref, rf_ref, rr_ref,
+    out_ref, coef_ref, tail_ref,
+    wide_ref, w_ref, c_ref, conc32_ref, x_ref, act_ref, run_ref,
 ):
-    @pl.when(pl.program_id(0) == 0)
+    step = pl.program_id(0)
+
+    @pl.when(step == 0)
     def _():
+        run_ref[0] = cond_ref[0] - THIRD
+        run_ref[1] = jnp.where(lax.axis_index("gx") == 0, MASS + THIRD, BODY) * jnp.ones(run_ref.shape[1:], F32)
+        run_ref[2] = jnp.full(run_ref.shape[1:], BODY, F32)
         build_weights(of_ref, or_ref, st_ref, rf_ref, rr_ref, wide_ref, w_ref, c_ref)
+
+    gap, mass_first, mass = run_ref[0], run_ref[1], run_ref[2]
+    for q in range(1, XB + 1):
+        p = step * XB + q
+        after = cond_ref[jnp.minimum(p, cond_ref.shape[0] - 1)] - THIRD
+        inv = 1.0 / (gap + after + mass)
+        alpha, beta = gap * inv, after * inv
+        coef_ref[0, p], coef_ref[1, p], coef_ref[2, p] = alpha, beta, inv
+        mass_first = mass_first + alpha * mass
+        mass = BODY + beta * mass
+        gap = alpha * after
+    run_ref[0], run_ref[1], run_ref[2] = gap, mass_first, mass
+    tail_ref[step, 0], tail_ref[step, 1], tail_ref[step, 2] = gap, mass_first, mass
 
     carried, xb, ny, nz = adj_ref.shape
     species = conc_ref.shape[0]
@@ -124,7 +145,7 @@
                     ]
 
 
-def chemistry(adjoint, log_conc, levels, orders_fwd, orders_rev, stoich, rate_fwd, rate_rev):
+def chemistry(adjoint, log_conc, levels, conduct, orders_fwd, orders_rev, stoich, rate_fwd, rate_rev):
     carried, nx, ny, nz = adjoint.shape
     species, react = log_conc.shape[0], orders_fwd.shape[0]
     whole = lambda a: pl.BlockSpec(a.shape, lambda i: (0,) * len(a.shape))
@@ -136,10 +157,19 @@
             pl.BlockSpec((carried, XB, ny, nz), lambda i: (0, i, 0, 0)),
             pl.BlockSpec((species, XB, ny, nz), lambda i: (0, i, 0, 0)),
             pl.BlockSpec((XB, ny, nz), lambda i: (i, 0, 0)),
+            whole(conduct),
         ]
         + [whole(a) for a in small],
-        out_specs=pl.BlockSpec((carried, XB, ny, nz), lambda i: (0, i, 0, 0)),
-        out_shape=jax.ShapeDtypeStruct(adjoint.shape, F32),
+        out_specs=[
+            pl.BlockSpec((carried, XB, ny, nz), lambda i: (0, i, 0, 0)),
+            pl.BlockSpec((3, nx + 1, ny, nz), lambda i: (0, 0, 0, 0)),
+            pl.BlockSpec((nx // XB, 3, ny, nz), lambda i: (0, 0, 0, 0)),
+        ],
+        out_shape=[
+            jax.ShapeDtypeStruct(adjoint.shape, F32),
+            jax.ShapeDtypeStruct((3, nx + 1, ny, nz), F32),
+            jax.ShapeDtypeStruct((nx // XB, 3, ny, nz), F32),
+        ],
         scratch_shapes=[
             pltpu.VMEM((K_ROWS, 256), F32),
             pltpu.VMEM((3 * R_PAD, K_ROWS), BF16),
@@ -147,11 +177,12 @@
             pltpu.VMEM((species * XB * ny, nz), F32),
             pltpu.VMEM((XB, K_ROWS, ny * nz), BF16),
             pltpu.VMEM((2, 2, R_PAD, TILE), BF16),
+            pltpu.VMEM((3, ny, nz), F32),
         ],
         compiler_params=pltpu.CompilerParams(dimension_semantics=("arbitrary",), vmem_limit_bytes=LIMIT),
         cost_estimate=pl.CostEstimate(flops=12 * 10**9, bytes_accessed=4 * 10**6, transcendentals=6_750_000),
         name="chem",
-    )(adjoint, log_conc, levels, *small)
+    )(adjoint, log_conc, levels, conduct, *small)
 
 
 GROUP = 6
@@ -167,25 +198,14 @@
     return s // GROUP * ROWS + s % GROUP
 
 
-PACK = 4
-
-
-def edges_kernel(adj_ref, low_ref, high_ref, side_ref):
+def edges_kernel(adj_ref, low_ref, high_ref):
     carried, nx, ny, nz = adj_ref.shape
-    lane = iota((ny, nz), 1)
-    own_shift = jnp.where(lax.axis_index("gz") == 0, 2, 0)
-    side_ref[...] = jnp.zeros(side_ref.shape, F32)
 
     @pl.loop(0, carried)
     def _(s):
-        start = s % PACK * 2 * nx
-        packed = side_ref[s // PACK]
         for x in range(nx):
             low_ref[s, x] = adj_ref[s, x, ny - 2 : ny, :]
             high_ref[s, x] = adj_ref[s, x, 0:2, :]
-            moved = pltpu.roll(adj_ref[s, x], lax.rem(start + (2 * x + own_shift), nz), 1)
-            packed = jnp.where(lane // 2 == start // 2 + x, moved, packed)
-        side_ref[s // PACK] = packed
 
 
 def edges(adjoint):
@@ -194,74 +214,71 @@
     return pl.pallas_call(
         edges_kernel,
         in_specs=[WHOLE],
-        out_specs=[WHOLE] * 3,
-        out_shape=[shape, shape, pltpu.VMEM((-(-carried // PACK), ny, nz), F32)],
+        out_specs=[WHOLE, WHOLE],
+        out_shape=[shape, shape],
         compiler_params=SMALL,
         cost_estimate=pl.CostEstimate(flops=0, bytes_accessed=2 * 10**6, transcendentals=0),
         name="edges",
     )(adjoint)
 
 
+def split(value):
+    high = value.astype(BF16)
+    return high, (value - high.astype(F32)).astype(BF16)
+
+
 def local_kernel(
-    diff_ref, cond_ref, adj_ref, chem_ref, near_ref, low_ref, high_ref, part_ref, coef_ref, msg_ref, inv_ref
+    diff_ref, cond_ref, adj_ref, chem_ref, near_ref, low_ref, high_ref, coef_ref, tail_ref,
+    part_ref, msg_ref, band_ref, zz_ref,
 ):
     nx, ny, nz = cond_ref.shape
     carried = adj_ref.shape[0]
     stride = GROUPS * ROWS
-    third = MASS / 3.0
-    body = MASS + 2.0 * third
-    mass_first = jnp.where(lax.axis_index("gx") == 0, MASS + third, body) * jnp.ones((ny, nz), F32)
-    gap = cond_ref[0] - third
-    mass = jnp.full((ny, nz), body, F32)
-    for p in range(1, nx - 1):
-        after = cond_ref[p] - third
-        inv = 1.0 / (gap + after + mass)
-        alpha, beta = gap * inv, after * inv
-        coef_ref[0, p], coef_ref[1, p], inv_ref[p] = alpha, beta, inv
-        mass_first = mass_first + alpha * mass
-        mass = body + beta * mass
-        gap = alpha * after
-    face = cond_ref[nx - 1] - third
     msg_ref[...] = jnp.zeros(msg_ref.shape, F32)
+    at = nx // XB - 2
+    face = cond_ref[nx - 1] - THIRD
     for group in range(GROUPS):
-        for r, value in ((6, gap), (7, mass_first), (14, face), (15, mass)):
+        for r, value in ((6, tail_ref[at, 0]), (7, tail_ref[at, 1]), (14, face), (15, tail_ref[at, 2])):
             msg_ref[pl.ds(group * ROWS + r, ny, stride=stride), :] = value
 
-    lane, row = iota((ny, nz), 1), iota((ny, nz), 0)
-    keep_low = jnp.where(lax.axis_index("gz") == 0, 1.0, 0.0)
-    keep_high = 1.0 - keep_low
-    near_shift = jnp.where(lax.axis_index("gz") == 0, 0, 2)
+    k, z = iota((2 * nz, nz), 0), iota((2 * nz, nz), 1)
+    offset = jnp.where(lax.axis_index("gz") == 0, nz, -nz)
+    gap = jnp.abs(jnp.where(k < nz, k, k - nz + offset) - z)
+    band_ref[...] = jnp.where(
+        gap == 0, -60.0, jnp.where(gap == 1, 16.0, jnp.where(gap == 2, -1.0, 0.0))
+    ).astype(BF16)
+    row = iota((ny, nz), 0)
 
     @pl.loop(0, carried // SB)
     def _(g):
         for t in range(SB):
             s = g * SB + t
+            own_hi, own_lo = split(adj_ref[s].reshape(nx * ny, nz))
+            near_hi, near_lo = split(near_ref[s].reshape(nx * ny, nz))
+            sides = jnp.concatenate(
+                [jnp.concatenate([own_hi, near_hi], axis=1), jnp.concatenate([own_lo, near_lo], axis=1)], axis=0
+            )
+            spread_z = dot(sides, band_ref[...])
+            zz_ref[t] = spread_z[: nx * ny] + spread_z[nx * ny :]
+        for t in range(SB):
+            s = g * SB + t
             scale = diff_ref[s] * (SECTION * STEP / 12.0)
-            side = near_ref[s // PACK]
-            back_by = nz - s % PACK * 2 * nx - near_shift
             b_first, carry = None, None
             for p in range(nx):
                 own = adj_ref[s, p]
-                near = pltpu.roll(side, lax.rem(back_by + (nz - 2 * p), nz), 1)
-                from_high = near * keep_low
-                from_low = near * keep_high
-                z_up1 = pltpu.roll(jnp.where(lane < 1, from_high, own), nz - 1, 1)
-                z_up2 = pltpu.roll(jnp.where(lane < 2, from_high, own), nz - 2, 1)
-                z_dn1 = pltpu.roll(jnp.where(lane >= nz - 1, from_low, own), 1, 1)
-                z_dn2 = pltpu.roll(jnp.where(lane >= nz - 2, from_low, own), 2, 1)
                 low0, low1 = low_ref[s, p, 0:1, :], low_ref[s, p, 1:2, :]
                 high0, high1 = high_ref[s, p, 0:1, :], high_ref[s, p, 1:2, :]
                 y_up1 = jnp.where(row == ny - 1, high0, pltpu.roll(own, ny - 1, 0))
                 y_up2 = jnp.where(row == ny - 1, high1, jnp.where(row == ny - 2, high0, pltpu.roll(own, ny - 2, 0)))
                 y_dn1 = jnp.where(row == 0, low1, pltpu.roll(own, 1, 0))
                 y_dn2 = jnp.where(row == 0, low0, jnp.where(row == 1, low1, pltpu.roll(own, 2, 0)))
-                spread = 16.0 * ((z_up1 + z_dn1) + (y_up1 + y_dn1)) - ((z_up2 + z_dn2) + (y_up2 + y_dn2)) - 60.0 * own
+                spread = 16.0 * (y_up1 + y_dn1) - (y_up2 + y_dn2) + zz_ref[t, p * ny : (p + 1) * ny, :]
                 b = SECTION * own + (SECTION * STEP) * chem_ref[s, p] + scale * spread
                 if p == 0:
                     b_first = b
                 elif p < nx - 1:
                     full = b if carry is None else b + carry
-                    part_ref[s, p] = full * inv_ref[p]
+                    part_ref[s, p] = full * coef_ref[2, p]
                     b_first = b_first + coef_ref[0, p] * full
                     carry = coef_ref[1, p] * full
                 else:
@@ -270,23 +287,22 @@
             msg_ref[pl.ds(place(s) + 8, ny, stride=stride), :] = b_last
 
 
-def local_part(diffusivity, adjoint, chem, near, low, high, conduct):
+def local_part(diffusivity, adjoint, chem, near, low, high, conduct, coef, ends):
     carried, nx, ny, nz = adjoint.shape
     smem = pl.BlockSpec(memory_space=pltpu.SMEM)
     return pl.pallas_call(
         local_kernel,
-        in_specs=[smem] + [WHOLE] * 6,
-        out_specs=[WHOLE] * 3,
+        in_specs=[smem] + [WHOLE] * 8,
+        out_specs=[WHOLE] * 2,
         out_shape=[
             pltpu.VMEM(adjoint.shape, F32),
-            pltpu.VMEM((2, nx, ny, nz), F32),
             pltpu.VMEM((GROUPS * ny * ROWS, nz), F32),
         ],
-        scratch_shapes=[pltpu.VMEM((nx, ny, nz), F32)],
+        scratch_shapes=[pltpu.VMEM((2 * nz, nz), BF16), pltpu.VMEM((SB, nx * ny, nz), F32)],
         compiler_params=SMALL,
         cost_estimate=pl.CostEstimate(flops=20 * 10**6, bytes_accessed=7 * 10**6, transcendentals=0),
         name="local",
-    )(diffusivity, conduct, adjoint, chem, near, low, high)
+    )(diffusivity, conduct, adjoint, chem, near, low, high, coef, ends)
 
 
 def chain_kernel(in_ref, out_ref):
@@ -402,12 +418,12 @@
 ):
     carried, nx, ny, nz = adjoint.shape
     rows_y, blocks = lax.axis_size("gy"), lax.axis_size("gx")
-    tail, head, side = edges(adjoint)
+    near = lax.ppermute(adjoint, "gz", [(0, 1), (1, 0)])
+    tail, head = edges(adjoint)
     low = lax.ppermute(tail, "gy", [(i, i + 1) for i in range(rows_y - 1)])
     high = lax.ppermute(head, "gy", [(i + 1, i) for i in range(rows_y - 1)])
-    near = lax.ppermute(side, "gz", [(0, 1), (1, 0)])
-    chem = chemistry(adjoint, log_conc, levels, orders_fwd, orders_rev, stoich, rate_fwd, rate_rev)
-    part, coef, message = local_part(diffusivity, adjoint, chem, near, low, high, conduct)
+    chem, coef, ends_m = chemistry(adjoint, log_conc, levels, conduct, orders_fwd, orders_rev, stoich, rate_fwd, rate_rev)
+    part, message = local_part(diffusivity, adjoint, chem, near, low, high, conduct, coef, ends_m)
     message = lax.all_to_all(message.reshape(blocks, ROWS, nz), "gx", 0, 0, tiled=True)
     ends = lax.all_to_all(chain(message), "gx", 0, 0, tiled=True)
     return back(part, coef, ends.reshape(blocks * ROWS, nz))

time: 70.4 us -> 65.1 us (0.925)
  Pallas kernels: 22.3 us -> 16.9 us
    pallas_call x2, Pallas kernels: 7.23 us -> 3.86 us  [the longest x1 3.49 us: local_part(): pl.pallas_call(local_kernel, in_specs=[smem] + [WHOLE] * 8, out_specs=[WH...]
    pallas_call x1, Pallas kernels: 13.5 us -> 11.4 us  [chemistry(): pl.pallas_call(chem_kernel, grid=(nx // XB,), in_specs=[pl.BlockSpec((car...]
  transfers between devices with their start and end apart: 3 -> 3, of which waited for: 0 -> 0; matrix products, arithmetic and copies ran while one was open for 0% -> 0% of each run, Pallas kernels for 19% -> 18%
where the time goes in v3:
time: 65.1 us; the launch traced here: 64.9 us
  blocking collectives  40.4 us (62%)
  Pallas kernels  16.9 us (26%)
  starting transfers between devices  5.99 us (9%)
  local copies, waits for them, and re-layouts  1.4 us (2%)
    all_to_all x1, blocking collectives, shards(): lax.all_to_all(message.reshape(blocks, ROWS, nz), 'gx', 0, 0, tiled=True)  24.1 us
    all_to_all x1, blocking collectives, shards(): ends = lax.all_to_all(chain(message), 'gx', 0, 0, tiled=True)  16.3 us
    pallas_call x1, Pallas kernels, chemistry(): pl.pallas_call(chem_kernel, grid=(nx // XB,), in_specs=[pl.BlockSpec((car...  11.4 us
    ppermute x1, starting transfers between devices, shards(): low = lax.ppermute(tail, 'gy', [(i, i + 1) for i in range(rows_y - 1)])  3.53 us
    pallas_call x1, Pallas kernels, local_part(): pl.pallas_call(local_kernel, in_specs=[smem] + [WHOLE] * 8, out_specs=[WH...  3.49 us
    ppermute x1, starting transfers between devices, shards(): high = lax.ppermute(head, 'gy', [(i + 1, i) for i in range(rows_y - 1)])  2.46 us
    unnamed x20, local copies, waits for them, and re-layouts  1.4 us
    pallas_call x1, Pallas kernels, back(): pl.pallas_call(back_kernel, in_specs=[WHOLE, WHOLE, WHOLE], out_specs=ANY...  1.37 us
  transfers between devices with their start and end apart: 3, of which 0 were waited for; matrix products, arithmetic and copies ran while one was open for 0% of the time, Pallas kernels for 18%

profile of v3, /device:TPU:2, one launch (start us, length us, event | category | flops | bytes accessed | tf_op | source)
XLA Modules:
  0.0 64.9 jit_solution(3359638619526230354)
XLA Ops:
  0.0 0.0 collective-permute-start
  0.0 1.4 %copy-done = f32[22,16,8,128]{3,2,1,0:T(8,128)S(1)} copy-done((f32[22,16,8,128]{3,2,1,0:T(8,128)S(1)}, f32[22,16,8,128]{3,2,1,0:T(8,128)}, u32[]{:S(2)}) %copy-start) | copy-done | bytes 1441816
  1.4 0.0 copy-start.1
  1.4 0.0 copy-start.3
  1.4 0.0 copy-start.4
  1.4 0.0 copy-start.5
  1.4 0.0 copy-start.6
  1.4 0.0 copy-start.7
  1.4 0.0 copy-start.8
  1.4 0.0 copy-start.9
  1.4 0.4 edges.1
  1.8 3.5 %collective-permute-start.1 = (f32[22,16,2,128]{3,2,1,0:T(2,128)S(1)}, f32[22,16,2,128]{3,2,1,0:T(2,128)S(1)}, u32[]{:S(2)}, u32[]{:S(2)}) collective-permute-start(f32[22,16,2,128]{3,2,1,0:T(2,128)S(1)} %get-tuple-element.14), channel_id=1, source_target_pairs={{0,2},{2,4},{4,6},{1,3},{3,5},{5,7},{8,10},{10,12},{12,14},{9,11},... | collective-permute-start | bytes 1081352 | tf_op jit(solution)/shard_map/ppermute | solution.py:423
  5.3 2.5 %collective-permute-start.2 = (f32[22,16,2,128]{3,2,1,0:T(2,128)S(1)}, f32[22,16,2,128]{3,2,1,0:T(2,128)S(1)}, u32[]{:S(2)}, u32[]{:S(2)}) collective-permute-start(f32[22,16,2,128]{3,2,1,0:T(2,128)S(1)} %get-tuple-element.15), channel_id=1, source_target_pairs={{2,0},{4,2},{6,4},{3,1},{5,3},{7,5},{10,8},{12,10},{14,12},{11,9},... | collective-permute-start | bytes 1081352 | tf_op jit(solution)/shard_map/ppermute | solution.py:424
  7.8 0.0 copy-done.1
  7.8 0.0 copy-done.3
  7.8 0.0 copy-done.4
  7.8 0.0 copy-done.5
  7.8 0.0 copy-done.6
  7.9 0.0 copy-done.7
  7.9 0.0 copy-done.8
  7.9 0.0 copy-done.9
  7.9 0.0 copy-start.2
  7.9 11.4 %chem.1 = (f32[22,16,8,128]{3,2,1,0:T(8,128)S(1)}, f32[3,17,8,128]{3,2,1,0:T(8,128)S(1)}, f32[8,3,8,128]{3,2,1,0:T(8,128)S(1)}) custom-call(f32[22,16,8,128]{3,2,1,0:T(8,128)S(1)} %copy-done, bf16[32,16,8,128]{3,2,1,0:T(8,128)(2,1)S(1)} %copy-done.3, s32[16,8,128]{2,1,0:T(8,128)S(1)} %copy-done.4, f32[16,8,128]{2,1,0:T(8,128)S(1)} %copy-done.1, ...), custom_call_target="tpu_custom_call" | custom-call | flops 12000000000 | bytes 4000000 | tf_op jit(solution)/shard_map/chem/pallas_call | solution.py:153
  19.3 0.0 collective-permute-done.1.low_ref
  19.3 0.0 collective-permute-done.2.high_ref
  19.3 0.0 collective-permute-done.near_ref
  19.4 0.0 copy-done.2
  19.4 3.5 %local.1 = (f32[22,16,8,128]{3,2,1,0:T(8,128)S(1)}, f32[512,128]{1,0:T(8,128)S(1)}) custom-call(f32[22]{0:T(128)S(1)} %copy-done.2, f32[16,8,128]{2,1,0:T(8,128)S(1)} %copy-done.1, f32[22,16,8,128]{3,2,1,0:T(8,128)S(1)} %copy-done, f32[22,16,8,128]{3,2,1,0:T(8,128)S(1)} %get-tuple-element.13.chem_ref, f32[22,16,8,128]{3,2,1,0:T(8,128)S(1)} %collective-permute-done.near_ref, ...), custom_call_target="tpu_custom_call" | custom-call | flops 20000000 | bytes 7000000 | tf_op jit(solution)/shard_map/local/pallas_call | solution.py:293
  22.9 24.1 %all_to_all.10.in_ref = f32[32,16,128]{2,1,0:T(8,128)S(1)} all-to-all(f32[32,16,128]{2,1,0:T(8,128)S(1)} %bitcast.8), channel_id=1, replica_groups=mesh['gx'=32,'gy'=4,'gz'=2] {'gx'}, dimensions={0} | all-to-all | bytes 524288 | tf_op jit(solution)/shard_map/all_to_all | solution.py:427
  47.0 0.2 chain.1
  47.2 16.3 %all_to_all.11 = f32[32,16,128]{2,1,0:T(8,128)S(1)} all-to-all(f32[32,16,128]{2,1,0:T(8,128)S(1)} %chain.1), channel_id=1, replica_groups=mesh['gx'=32,'gy'=4,'gz'=2] {'gx'}, dimensions={0} | all-to-all | bytes 524288 | tf_op jit(solution)/shard_map/all_to_all | solution.py:428
  63.5 1.4 %back.1 = f32[22,16,8,128]{3,2,1,0:T(8,128)} custom-call(f32[3,17,8,128]{3,2,1,0:T(8,128)S(1)} %get-tuple-element.12.coef_ref, f32[512,128]{1,0:T(8,128)S(1)} %bitcast.7, f32[22,16,8,128]{3,2,1,0:T(8,128)S(1)} %get-tuple-element.18.part_ref), custom_call_target="tpu_custom_call" | custom-call | flops 2000000 | bytes 3000000 | tf_op jit(solution)/shard_map/back/pallas_call | solution.py:400
  (1 shorter events, 0.0 us)
Async XLA Ops:
  0.0 19.3 %collective-permute-start = (f32[22,16,8,128]{3,2,1,0:T(8,128)}, f32[22,16,8,128]{3,2,1,0:T(8,128)S(1)}, u32[]{:S(2)}, u32[]{:S(2)}) collective-permute-start(f32[22,16,8,128]{3,2,1,0:T(8,128)} %adj_ref.5), channel_id=1, source_target_pairs={{0,1},{1,0},{2,3},{3,2},{4,5},{5,4},{6,7},{7,6},{8,9},{9,8},{10,11... | collective-permute-start | bytes 4325384 | tf_op jit(solution)/shard_map/ppermute | solution.py:421
  0.0 1.4 %copy-start = (f32[22,16,8,128]{3,2,1,0:T(8,128)S(1)}, f32[22,16,8,128]{3,2,1,0:T(8,128)}, u32[]{:S(2)}) copy-start(f32[22,16,8,128]{3,2,1,0:T(8,128)} %adj_ref.5) | copy-start | bytes 4325380
  1.4 6.4 %copy-start.1 = (f32[16,8,128]{2,1,0:T(8,128)S(1)}, f32[16,8,128]{2,1,0:T(8,128)}, u32[]{:S(2)}) copy-start(f32[16,8,128]{2,1,0:T(8,128)} %cond_ref.3) | copy-start | bytes 196612
  1.4 6.5 %copy-start.3 = (bf16[32,16,8,128]{3,2,1,0:T(8,128)(2,1)S(1)}, bf16[32,16,8,128]{3,2,1,0:T(8,128)(2,1)}, u32[]{:S(2)}) copy-start(bf16[32,16,8,128]{3,2,1,0:T(8,128)(2,1)} %conc_ref.1) | copy-start | bytes 3145732
  1.4 6.5 %copy-start.4 = (s32[16,8,128]{2,1,0:T(8,128)S(1)}, s32[16,8,128]{2,1,0:T(8,128)}, u32[]{:S(2)}) copy-start(s32[16,8,128]{2,1,0:T(8,128)} %lev_ref.1) | copy-start | bytes 196612
  1.4 6.5 %copy-start.5 = (bf16[206,32]{0,1:T(8,128)(2,1)S(1)}, bf16[206,32]{0,1:T(8,128)(2,1)}, u32[]{:S(2)}) copy-start(bf16[206,32]{0,1:T(8,128)(2,1)} %param.14) | copy-start | bytes 39556
  1.4 6.5 %copy-start.6 = (bf16[206,32]{0,1:T(8,128)(2,1)S(1)}, bf16[206,32]{0,1:T(8,128)(2,1)}, u32[]{:S(2)}) copy-start(bf16[206,32]{0,1:T(8,128)(2,1)} %param.15) | copy-start | bytes 39556
  1.4 6.5 %copy-start.7 = (bf16[206,22]{0,1:T(8,128)(2,1)S(1)}, bf16[206,22]{0,1:T(8,128)(2,1)}, u32[]{:S(2)}) copy-start(bf16[206,22]{0,1:T(8,128)(2,1)} %param.16) | copy-start | bytes 27196
  1.4 6.5 %copy-start.8 = (f32[206]{0:T(256)S(1)}, f32[206]{0:T(256)}, u32[]{:S(2)}) copy-start(f32[206]{0:T(256)} %param.17) | copy-start | bytes 2476
  1.4 6.5 %copy-start.9 = (f32[206]{0:T(256)S(1)}, f32[206]{0:T(256)}, u32[]{:S(2)}) copy-start(f32[206]{0:T(256)} %param.18) | copy-start | bytes 2476
  1.8 17.5 %collective-permute-start.1 = (f32[22,16,2,128]{3,2,1,0:T(2,128)S(1)}, f32[22,16,2,128]{3,2,1,0:T(2,128)S(1)}, u32[]{:S(2)}, u32[]{:S(2)}) collective-permute-start(f32[22,16,2,128]{3,2,1,0:T(2,128)S(1)} %get-tuple-element.14), channel_id=1, source_target_pairs={{0,2},{2,4},{4,6},{1,3},{3,5},{5,7},{8,10},{10,12},{12,14},{9,11},... | collective-permute-start | bytes 1081352 | tf_op jit(solution)/shard_map/ppermute | solution.py:423
  5.3 14.0 %collective-permute-start.2 = (f32[22,16,2,128]{3,2,1,0:T(2,128)S(1)}, f32[22,16,2,128]{3,2,1,0:T(2,128)S(1)}, u32[]{:S(2)}, u32[]{:S(2)}) collective-permute-start(f32[22,16,2,128]{3,2,1,0:T(2,128)S(1)} %get-tuple-element.15), channel_id=1, source_target_pairs={{2,0},{4,2},{6,4},{3,1},{5,3},{7,5},{10,8},{12,10},{14,12},{11,9},... | collective-permute-start | bytes 1081352 | tf_op jit(solution)/shard_map/ppermute | solution.py:424
  7.9 11.5 %copy-start.2 = (f32[22]{0:T(128)S(1)}, f32[22]{0:T(128)}, u32[]{:S(2)}) copy-start(f32[22]{0:T(128)} %diff_ref.1) | copy-start | bytes 268

commit v4 on v3

--- a/solution.py
+++ b/solution.py
@@ -20,8 +20,8 @@
 STRIP = 16
 CHUNKS = tuple((start, STRIP) for start in range(0, R_PAD, STRIP))
 TILE = 1024
-XB = 2
-LIMIT = 12 * 1024 * 1024
+XB = 4
+LIMIT = 24 * 1024 * 1024
 F32 = jnp.float32
 BF16 = jnp.bfloat16
 
@@ -102,8 +102,8 @@
         mass_first = mass_first + alpha * mass
         mass = BODY + beta * mass
         gap = alpha * after
+        tail_ref[p, 0], tail_ref[p, 1], tail_ref[p, 2] = gap, mass_first, mass
     run_ref[0], run_ref[1], run_ref[2] = gap, mass_first, mass
-    tail_ref[step, 0], tail_ref[step, 1], tail_ref[step, 2] = gap, mass_first, mass
 
     carried, xb, ny, nz = adj_ref.shape
     species = conc_ref.shape[0]
@@ -163,12 +163,12 @@
         out_specs=[
             pl.BlockSpec((carried, XB, ny, nz), lambda i: (0, i, 0, 0)),
             pl.BlockSpec((3, nx + 1, ny, nz), lambda i: (0, 0, 0, 0)),
-            pl.BlockSpec((nx // XB, 3, ny, nz), lambda i: (0, 0, 0, 0)),
+            pl.BlockSpec((nx + 1, 3, ny, nz), lambda i: (0, 0, 0, 0)),
         ],
         out_shape=[
             jax.ShapeDtypeStruct(adjoint.shape, F32),
             jax.ShapeDtypeStruct((3, nx + 1, ny, nz), F32),
-            jax.ShapeDtypeStruct((nx // XB, 3, ny, nz), F32),
+            jax.ShapeDtypeStruct((nx + 1, 3, ny, nz), F32),
         ],
         scratch_shapes=[
             pltpu.VMEM((K_ROWS, 256), F32),
@@ -189,6 +189,7 @@
 GROUPS = 4
 ROWS = 16
 SB = 2
+LB = 11
 ANY = pl.BlockSpec(memory_space=pl.ANY)
 WHOLE = pl.BlockSpec(memory_space=pltpu.VMEM)
 SMALL = pltpu.CompilerParams(vmem_limit_bytes=LIMIT)
@@ -200,12 +201,15 @@
 
 def edges_kernel(adj_ref, low_ref, high_ref):
     carried, nx, ny, nz = adj_ref.shape
+    mine = lax.axis_index("gy")
+    to_high = jnp.where(mine == lax.axis_size("gy") - 1, 0.0, 1.0)
+    to_low = jnp.where(mine == 0, 0.0, 1.0)
 
     @pl.loop(0, carried)
     def _(s):
         for x in range(nx):
-            low_ref[s, x] = adj_ref[s, x, ny - 2 : ny, :]
-            high_ref[s, x] = adj_ref[s, x, 0:2, :]
+            low_ref[s, x] = adj_ref[s, x, ny - 2 : ny, :] * to_high
+            high_ref[s, x] = adj_ref[s, x, 0:2, :] * to_low
 
 
 def edges(adjoint):
@@ -235,7 +239,7 @@
     carried = adj_ref.shape[0]
     stride = GROUPS * ROWS
     msg_ref[...] = jnp.zeros(msg_ref.shape, F32)
-    at = nx // XB - 2
+    at = nx - 2
     face = cond_ref[nx - 1] - THIRD
     for group in range(GROUPS):
         for r, value in ((6, tail_ref[at, 0]), (7, tail_ref[at, 1]), (14, face), (15, tail_ref[at, 2])):
@@ -249,10 +253,10 @@
     ).astype(BF16)
     row = iota((ny, nz), 0)
 
-    @pl.loop(0, carried // SB)
+    @pl.loop(0, carried // LB)
     def _(g):
-        for t in range(SB):
-            s = g * SB + t
+        for t in range(LB):
+            s = g * LB + t
             own_hi, own_lo = split(adj_ref[s].reshape(nx * ny, nz))
             near_hi, near_lo = split(near_ref[s].reshape(nx * ny, nz))
             sides = jnp.concatenate(
@@ -260,8 +264,8 @@
             )
             spread_z = dot(sides, band_ref[...])
             zz_ref[t] = spread_z[: nx * ny] + spread_z[nx * ny :]
-        for t in range(SB):
-            s = g * SB + t
+        for t in range(LB):
+            s = g * LB + t
             scale = diff_ref[s] * (SECTION * STEP / 12.0)
             b_first, carry = None, None
             for p in range(nx):
@@ -298,7 +302,7 @@
             pltpu.VMEM(adjoint.shape, F32),
             pltpu.VMEM((GROUPS * ny * ROWS, nz), F32),
         ],
-        scratch_shapes=[pltpu.VMEM((2 * nz, nz), BF16), pltpu.VMEM((SB, nx * ny, nz), F32)],
+        scratch_shapes=[pltpu.VMEM((2 * nz, nz), BF16), pltpu.VMEM((LB, nx * ny, nz), F32)],
         compiler_params=SMALL,
         cost_estimate=pl.CostEstimate(flops=20 * 10**6, bytes_accessed=7 * 10**6, transcendentals=0),
         name="local",
@@ -420,8 +424,8 @@
     rows_y, blocks = lax.axis_size("gy"), lax.axis_size("gx")
     near = lax.ppermute(adjoint, "gz", [(0, 1), (1, 0)])
     tail, head = edges(adjoint)
-    low = lax.ppermute(tail, "gy", [(i, i + 1) for i in range(rows_y - 1)])
-    high = lax.ppermute(head, "gy", [(i + 1, i) for i in range(rows_y - 1)])
+    low = lax.ppermute(tail, "gy", [(i, (i + 1) % rows_y) for i in range(rows_y)])
+    high = lax.ppermute(head, "gy", [((i + 1) % rows_y, i) for i in range(rows_y)])
     chem, coef, ends_m = chemistry(adjoint, log_conc, levels, conduct, orders_fwd, orders_rev, stoich, rate_fwd, rate_rev)
     part, message = local_part(diffusivity, adjoint, chem, near, low, high, conduct, coef, ends_m)
     message = lax.all_to_all(message.reshape(blocks, ROWS, nz), "gx", 0, 0, tiled=True)

time: 65.1 us -> 60.3 us (0.926)
  starting transfers between devices: 5.99 us -> 2.44 us
  Pallas kernels: 16.9 us -> 16.1 us
    ppermute x2, starting transfers between devices: 5.99 us -> 2.44 us  [the longest x1 1.57 us: shards(): lax.ppermute(tail, 'gy', [(i, (i + 1) % rows_y) for i in range(rows_y)])]
    pallas_call x1, Pallas kernels: 3.49 us -> 2.74 us  [local_part(): pl.pallas_call(local_kernel, in_specs=[smem] + [WHOLE] * 8, out_specs=[WH...]
  transfers between devices with their start and end apart: 3 -> 3, of which waited for: 0 -> 0; matrix products, arithmetic and copies ran while one was open for 0% -> 0% of each run, Pallas kernels for 18% -> 19%
where the time goes in v4:
time: 60.3 us; the launch traced here: 60.1 us
  blocking collectives  40 us (66%)
  Pallas kernels  16.1 us (27%)
  starting transfers between devices  2.44 us (4%)
  local copies, waits for them, and re-layouts  1.4 us (2%)
    all_to_all x1, blocking collectives, shards(): lax.all_to_all(message.reshape(blocks, ROWS, nz), 'gx', 0, 0, tiled=True)  23.7 us
    all_to_all x1, blocking collectives, shards(): ends = lax.all_to_all(chain(message), 'gx', 0, 0, tiled=True)  16.3 us
    pallas_call x1, Pallas kernels, chemistry(): pl.pallas_call(chem_kernel, grid=(nx // XB,), in_specs=[pl.BlockSpec((car...  11.3 us
    pallas_call x1, Pallas kernels, local_part(): pl.pallas_call(local_kernel, in_specs=[smem] + [WHOLE] * 8, out_specs=[WH...  2.74 us
    ppermute x1, starting transfers between devices, shards(): lax.ppermute(tail, 'gy', [(i, (i + 1) % rows_y) for i in range(rows_y)])  1.57 us
    unnamed x20, local copies, waits for them, and re-layouts  1.4 us
    pallas_call x1, Pallas kernels, back(): pl.pallas_call(back_kernel, in_specs=[WHOLE, WHOLE, WHOLE], out_specs=ANY...  1.37 us
  transfers between devices with their start and end apart: 3, of which 0 were waited for; matrix products, arithmetic and copies ran while one was open for 0% of the time, Pallas kernels for 19%

profile of v4, /device:TPU:2, one launch (start us, length us, event | category | flops | bytes accessed | tf_op | source)
XLA Modules:
  0.0 60.1 jit_solution(18295125997775161715)
XLA Ops:
  0.0 0.0 collective-permute-start
  0.0 0.0 copy-start
  0.0 1.4 %copy-done = f32[22,16,8,128]{3,2,1,0:T(8,128)S(1)} copy-done((f32[22,16,8,128]{3,2,1,0:T(8,128)S(1)}, f32[22,16,8,128]{3,2,1,0:T(8,128)}, u32[]{:S(2)}) %copy-start) | copy-done | bytes 1441816
  1.4 0.0 copy-start.1
  1.4 0.0 copy-start.3
  1.4 0.0 copy-start.4
  1.4 0.0 copy-start.6
  1.4 0.0 copy-start.7
  1.4 0.0 copy-start.8
  1.4 0.0 copy-start.9
  1.4 0.4 edges.1
  1.8 1.6 %collective-permute-start.1 = (f32[22,16,2,128]{3,2,1,0:T(2,128)S(1)}, f32[22,16,2,128]{3,2,1,0:T(2,128)S(1)}, u32[]{:S(2)}, u32[]{:S(2)}) collective-permute-start(f32[22,16,2,128]{3,2,1,0:T(2,128)S(1)} %get-tuple-element.14), channel_id=1, source_target_pairs={{0,2},{2,4},{4,6},{6,0},{1,3},{3,5},{5,7},{7,1},{8,10},{10,12},{12... | collective-permute-start | bytes 1081352 | tf_op jit(solution)/shard_map/ppermute | solution.py:427
  3.4 0.9 %collective-permute-start.2 = (f32[22,16,2,128]{3,2,1,0:T(2,128)S(1)}, f32[22,16,2,128]{3,2,1,0:T(2,128)S(1)}, u32[]{:S(2)}, u32[]{:S(2)}) collective-permute-start(f32[22,16,2,128]{3,2,1,0:T(2,128)S(1)} %get-tuple-element.15), channel_id=1, source_target_pairs={{2,0},{4,2},{6,4},{0,6},{3,1},{5,3},{7,5},{1,7},{10,8},{12,10},{14... | collective-permute-start | bytes 1081352 | tf_op jit(solution)/shard_map/ppermute | solution.py:428
  4.2 0.0 copy-done.1
  4.2 0.0 copy-done.3
  4.2 0.0 copy-done.4
  4.2 0.0 copy-done.5
  4.3 0.0 copy-done.6
  4.3 0.0 copy-done.7
  4.3 0.0 copy-done.8
  4.3 0.0 copy-done.9
  4.3 0.0 copy-start.2
  4.3 11.3 %chem.1 = (f32[22,16,8,128]{3,2,1,0:T(8,128)S(1)}, f32[3,17,8,128]{3,2,1,0:T(8,128)S(1)}, f32[17,3,8,128]{3,2,1,0:T(8,128)S(1)}) custom-call(f32[22,16,8,128]{3,2,1,0:T(8,128)S(1)} %copy-done, bf16[32,16,8,128]{3,2,1,0:T(8,128)(2,1)S(1)} %copy-done.3, s32[16,8,128]{2,1,0:T(8,128)S(1)} %copy-done.4, f32[16,8,128]{2,1,0:T(8,128)S(1)} %copy-done.1, ...), custom_call_target="tpu_custom_call" | custom-call | flops 12000000000 | bytes 4000000 | tf_op jit(solution)/shard_map/chem/pallas_call | solution.py:153
  15.7 0.0 collective-permute-done.1.low_ref
  15.7 0.0 collective-permute-done.2.high_ref
  15.7 0.0 collective-permute-done.near_ref
  15.7 0.0 copy-done.2
  15.7 2.7 %local.1 = (f32[22,16,8,128]{3,2,1,0:T(8,128)S(1)}, f32[512,128]{1,0:T(8,128)S(1)}) custom-call(f32[22]{0:T(128)S(1)} %copy-done.2, f32[16,8,128]{2,1,0:T(8,128)S(1)} %copy-done.1, f32[22,16,8,128]{3,2,1,0:T(8,128)S(1)} %copy-done, f32[22,16,8,128]{3,2,1,0:T(8,128)S(1)} %get-tuple-element.13.chem_ref, f32[22,16,8,128]{3,2,1,0:T(8,128)S(1)} %collective-permute-done.near_ref, ...), custom_call_target="tpu_custom_call" | custom-call | flops 20000000 | bytes 7000000 | tf_op jit(solution)/shard_map/local/pallas_call | solution.py:297
  18.4 23.7 %all_to_all.10.in_ref = f32[32,16,128]{2,1,0:T(8,128)S(1)} all-to-all(f32[32,16,128]{2,1,0:T(8,128)S(1)} %bitcast.8), channel_id=1, replica_groups=mesh['gx'=32,'gy'=4,'gz'=2] {'gx'}, dimensions={0} | all-to-all | bytes 524288 | tf_op jit(solution)/shard_map/all_to_all | solution.py:431
  42.2 0.2 chain.1
  42.4 16.3 %all_to_all.11 = f32[32,16,128]{2,1,0:T(8,128)S(1)} all-to-all(f32[32,16,128]{2,1,0:T(8,128)S(1)} %chain.1), channel_id=1, replica_groups=mesh['gx'=32,'gy'=4,'gz'=2] {'gx'}, dimensions={0} | all-to-all | bytes 524288 | tf_op jit(solution)/shard_map/all_to_all | solution.py:432
  58.7 1.4 %back.1 = f32[22,16,8,128]{3,2,1,0:T(8,128)} custom-call(f32[3,17,8,128]{3,2,1,0:T(8,128)S(1)} %get-tuple-element.12.coef_ref, f32[512,128]{1,0:T(8,128)S(1)} %bitcast.7, f32[22,16,8,128]{3,2,1,0:T(8,128)S(1)} %get-tuple-element.18.part_ref), custom_call_target="tpu_custom_call" | custom-call | flops 2000000 | bytes 3000000 | tf_op jit(solution)/shard_map/back/pallas_call | solution.py:404
  (1 shorter events, 0.0 us)
Async XLA Ops:
  0.0 15.7 %collective-permute-start = (f32[22,16,8,128]{3,2,1,0:T(8,128)}, f32[22,16,8,128]{3,2,1,0:T(8,128)S(1)}, u32[]{:S(2)}, u32[]{:S(2)}) collective-permute-start(f32[22,16,8,128]{3,2,1,0:T(8,128)} %adj_ref.5), channel_id=1, source_target_pairs={{0,1},{1,0},{2,3},{3,2},{4,5},{5,4},{6,7},{7,6},{8,9},{9,8},{10,11... | collective-permute-start | bytes 4325384 | tf_op jit(solution)/shard_map/ppermute | solution.py:425
  0.0 1.4 %copy-start = (f32[22,16,8,128]{3,2,1,0:T(8,128)S(1)}, f32[22,16,8,128]{3,2,1,0:T(8,128)}, u32[]{:S(2)}) copy-start(f32[22,16,8,128]{3,2,1,0:T(8,128)} %adj_ref.5) | copy-start | bytes 4325380
  1.4 2.9 %copy-start.1 = (f32[16,8,128]{2,1,0:T(8,128)S(1)}, f32[16,8,128]{2,1,0:T(8,128)}, u32[]{:S(2)}) copy-start(f32[16,8,128]{2,1,0:T(8,128)} %cond_ref.3) | copy-start | bytes 196612
  1.4 2.9 %copy-start.3 = (bf16[32,16,8,128]{3,2,1,0:T(8,128)(2,1)S(1)}, bf16[32,16,8,128]{3,2,1,0:T(8,128)(2,1)}, u32[]{:S(2)}) copy-start(bf16[32,16,8,128]{3,2,1,0:T(8,128)(2,1)} %conc_ref.1) | copy-start | bytes 3145732
  1.4 2.9 %copy-start.4 = (s32[16,8,128]{2,1,0:T(8,128)S(1)}, s32[16,8,128]{2,1,0:T(8,128)}, u32[]{:S(2)}) copy-start(s32[16,8,128]{2,1,0:T(8,128)} %lev_ref.1) | copy-start | bytes 196612
  1.4 2.9 %copy-start.5 = (bf16[206,32]{0,1:T(8,128)(2,1)S(1)}, bf16[206,32]{0,1:T(8,128)(2,1)}, u32[]{:S(2)}) copy-start(bf16[206,32]{0,1:T(8,128)(2,1)} %param.14) | copy-start | bytes 39556
  1.4 2.9 %copy-start.6 = (bf16[206,32]{0,1:T(8,128)(2,1)S(1)}, bf16[206,32]{0,1:T(8,128)(2,1)}, u32[]{:S(2)}) copy-start(bf16[206,32]{0,1:T(8,128)(2,1)} %param.15) | copy-start | bytes 39556
  1.4 2.9 %copy-start.7 = (bf16[206,22]{0,1:T(8,128)(2,1)S(1)}, bf16[206,22]{0,1:T(8,128)(2,1)}, u32[]{:S(2)}) copy-start(bf16[206,22]{0,1:T(8,128)(2,1)} %param.16) | copy-start | bytes 27196
  1.4 2.9 %copy-start.8 = (f32[206]{0:T(256)S(1)}, f32[206]{0:T(256)}, u32[]{:S(2)}) copy-start(f32[206]{0:T(256)} %param.17) | copy-start | bytes 2476
  1.4 2.9 %copy-start.9 = (f32[206]{0:T(256)S(1)}, f32[206]{0:T(256)}, u32[]{:S(2)}) copy-start(f32[206]{0:T(256)} %param.18) | copy-start | bytes 2476
  1.8 13.9 %collective-permute-start.1 = (f32[22,16,2,128]{3,2,1,0:T(2,128)S(1)}, f32[22,16,2,128]{3,2,1,0:T(2,128)S(1)}, u32[]{:S(2)}, u32[]{:S(2)}) collective-permute-start(f32[22,16,2,128]{3,2,1,0:T(2,128)S(1)} %get-tuple-element.14), channel_id=1, source_target_pairs={{0,2},{2,4},{4,6},{6,0},{1,3},{3,5},{5,7},{7,1},{8,10},{10,12},{12... | collective-permute-start | bytes 1081352 | tf_op jit(solution)/shard_map/ppermute | solution.py:427
  3.4 12.3 %collective-permute-start.2 = (f32[22,16,2,128]{3,2,1,0:T(2,128)S(1)}, f32[22,16,2,128]{3,2,1,0:T(2,128)S(1)}, u32[]{:S(2)}, u32[]{:S(2)}) collective-permute-start(f32[22,16,2,128]{3,2,1,0:T(2,128)S(1)} %get-tuple-element.15), channel_id=1, source_target_pairs={{2,0},{4,2},{6,4},{0,6},{3,1},{5,3},{7,5},{1,7},{10,8},{12,10},{14... | collective-permute-start | bytes 1081352 | tf_op jit(solution)/shard_map/ppermute | solution.py:428
  4.3 11.4 %copy-start.2 = (f32[22]{0:T(128)S(1)}, f32[22]{0:T(128)}, u32[]{:S(2)}) copy-start(f32[22]{0:T(128)} %diff_ref.1) | copy-start | bytes 268

commit v5 on v4

--- a/solution.py
+++ b/solution.py
@@ -195,10 +195,6 @@
 SMALL = pltpu.CompilerParams(vmem_limit_bytes=LIMIT)
 
 
-def place(s):
-    return s // GROUP * ROWS + s % GROUP
-
-
 def edges_kernel(adj_ref, low_ref, high_ref):
     carried, nx, ny, nz = adj_ref.shape
     mine = lax.axis_index("gy")
@@ -233,17 +229,19 @@
 
 def local_kernel(
     diff_ref, cond_ref, adj_ref, chem_ref, near_ref, low_ref, high_ref, coef_ref, tail_ref,
-    part_ref, msg_ref, band_ref, zz_ref,
+    part_ref, *rest,
 ):
+    send_refs, (msg_ref, band_ref, zz_ref) = rest[:GROUPS], rest[GROUPS:]
     nx, ny, nz = cond_ref.shape
     carried = adj_ref.shape[0]
-    stride = GROUPS * ROWS
-    msg_ref[...] = jnp.zeros(msg_ref.shape, F32)
     at = nx - 2
     face = cond_ref[nx - 1] - THIRD
     for group in range(GROUPS):
         for r, value in ((6, tail_ref[at, 0]), (7, tail_ref[at, 1]), (14, face), (15, tail_ref[at, 2])):
-            msg_ref[pl.ds(group * ROWS + r, ny, stride=stride), :] = value
+            msg_ref[group, r] = value
+    for r in range(carried - GROUP * (GROUPS - 1), GROUP):
+        msg_ref[GROUPS - 1, r] = jnp.zeros((ny, nz), F32)
+        msg_ref[GROUPS - 1, r + 8] = jnp.zeros((ny, nz), F32)
 
     k, z = iota((2 * nz, nz), 0), iota((2 * nz, nz), 1)
     offset = jnp.where(lax.axis_index("gz") == 0, nz, -nz)
@@ -287,8 +285,12 @@
                     carry = coef_ref[1, p] * full
                 else:
                     b_last = b + carry
-            msg_ref[pl.ds(place(s), ny, stride=stride), :] = b_first
-            msg_ref[pl.ds(place(s) + 8, ny, stride=stride), :] = b_last
+            msg_ref[s // GROUP, s % GROUP] = b_first
+            msg_ref[s // GROUP, s % GROUP + 8] = b_last
+
+    mine = lax.axis_index("gx") % GROUPS
+    for turn in range(GROUPS):
+        send_refs[turn][...] = msg_ref[(mine + turn) % GROUPS]
 
 
 def local_part(diffusivity, adjoint, chem, near, low, high, conduct, coef, ends):
@@ -297,86 +299,155 @@
     return pl.pallas_call(
         local_kernel,
         in_specs=[smem] + [WHOLE] * 8,
-        out_specs=[WHOLE] * 2,
-        out_shape=[
-            pltpu.VMEM(adjoint.shape, F32),
-            pltpu.VMEM((GROUPS * ny * ROWS, nz), F32),
-        ],
-        scratch_shapes=[pltpu.VMEM((2 * nz, nz), BF16), pltpu.VMEM((LB, nx * ny, nz), F32)],
+        out_specs=[WHOLE] * (1 + GROUPS),
+        out_shape=[pltpu.VMEM(adjoint.shape, F32)] + [pltpu.VMEM((ROWS, ny, nz), F32)] * GROUPS,
+        scratch_shapes=[
+            pltpu.VMEM((GROUPS, ROWS, ny, nz), F32),
+            pltpu.VMEM((2 * nz, nz), BF16),
+            pltpu.VMEM((LB, nx * ny, nz), F32),
+        ],
         compiler_params=SMALL,
         cost_estimate=pl.CostEstimate(flops=20 * 10**6, bytes_accessed=7 * 10**6, transcendentals=0),
         name="local",
     )(diffusivity, conduct, adjoint, chem, near, low, high, coef, ends)
 
 
-def chain_kernel(in_ref, out_ref):
-    count, _, nz = in_ref.shape
+def reduce_kernel(*refs):
+    got_refs, (msg_ref, part_ref, coef_ref, in_ref) = refs[:GROUPS], refs[GROUPS:]
+    mine = lax.axis_index("gx") % GROUPS
+    for turn in range(GROUPS):
+        in_ref[(mine + GROUPS - turn) % GROUPS] = got_refs[turn][...]
+    gap, mass_first = in_ref[0, 6], in_ref[0, 7]
+    first = [in_ref[0, r] for r in range(GROUP)]
+    mass = in_ref[0, 15]
+    rhs = [in_ref[0, 8 + r] for r in range(GROUP)]
+    for node in range(2 * GROUPS - 2):
+        block, end = (node + 1) // 2, node % 2 == 1
+        after = in_ref[block, 6] if end else in_ref[block, 14]
+        inv = 1.0 / (gap + after + mass)
+        alpha, beta = gap * inv, after * inv
+        coef_ref[0, node], coef_ref[1, node] = alpha, beta
+        base, block = (8, block) if end else (0, block + 1)
+        for r in range(GROUP):
+            part_ref[node, r] = rhs[r] * inv
+            first[r] = first[r] + alpha * rhs[r]
+            rhs[r] = in_ref[block, base + r] + beta * rhs[r]
+        mass_first = mass_first + alpha * mass
+        mass = in_ref[block, base + 7] + beta * mass
+        gap = alpha * after
+    for r, plane in enumerate(first + [gap, mass_first] + rhs + [in_ref[GROUPS - 1, 14], mass]):
+        msg_ref[r] = plane
+
+
+def reduce_blocks(got):
+    plane = got[0].shape[1:]
+    return pl.pallas_call(
+        reduce_kernel,
+        in_specs=[WHOLE] * GROUPS,
+        out_specs=[WHOLE] * 3,
+        out_shape=[
+            pltpu.VMEM((ROWS,) + plane, F32),
+            pltpu.VMEM((2 * GROUPS - 2, GROUP) + plane, F32),
+            pltpu.VMEM((2, 2 * GROUPS - 2) + plane, F32),
+        ],
+        scratch_shapes=[pltpu.VMEM((GROUPS, ROWS) + plane, F32)],
+        compiler_params=SMALL,
+        cost_estimate=pl.CostEstimate(flops=10**6, bytes_accessed=10**6, transcendentals=0),
+        name="reduce",
+    )(*got)
+
+
+def chain_kernel(*refs):
+    count = len(refs) - GROUPS - 5
+    got_refs, (part_ref, coef_ref) = refs[:count], refs[count : count + 2]
+    send_refs, (in_ref, ends_ref, out_ref) = refs[count + 2 : count + 2 + GROUPS], refs[count + 2 + GROUPS :]
+    device = lax.axis_index("gx")
+    mine, home = device % GROUPS, device // GROUPS
+    for turn in range(count):
+        in_ref[(home + count - turn) % count] = got_refs[turn][...]
     h, mass, rhs, ends = [], [], [], []
     passed_m = passed_b = None
     for i in range(count):
-        low, high = in_ref[i, 0:8, :], in_ref[i, 8:16, :]
-        g = jnp.broadcast_to(in_ref[i, 6:7, :], (8, nz))
-        m_f = jnp.broadcast_to(in_ref[i, 7:8, :], (8, nz))
-        face = jnp.broadcast_to(in_ref[i, 14:15, :], (8, nz))
-        m_l = jnp.broadcast_to(in_ref[i, 15:16, :], (8, nz))
+        g, m_f, face, m_l = in_ref[i, 6], in_ref[i, 7], in_ref[i, 14], in_ref[i, 15]
         inv = 1.0 / (g + face + m_l)
         a, c = g * inv, face * inv
-        m, b = m_f + a * m_l, low + a * high
+        m = m_f + a * m_l
+        b = [in_ref[i, r] + a * in_ref[i, 8 + r] for r in range(GROUP)]
         if i > 0:
-            m, b = m + passed_m, b + passed_b
-        passed_m, passed_b = c * m_l, c * high
+            m, b = m + passed_m, [p + q for p, q in zip(b, passed_b)]
+        passed_m, passed_b = c * m_l, [c * in_ref[i, 8 + r] for r in range(GROUP)]
         h.append(a * face)
         mass.append(m)
         rhs.append(b)
-        ends.append((a, c, high * inv))
+        ends.append((a, c, inv))
     half = count // 2
     scale, ratio = [None] * count, [None] * count
-    for i in range(half - 1):
-        inv = 1.0 / (mass[i] + h[i])
-        q = h[i] * inv
-        scale[i], ratio[i] = rhs[i] * inv, q
-        mass[i + 1] = mass[i + 1] + q * mass[i]
-        rhs[i + 1] = rhs[i + 1] + q * rhs[i]
+
+    def pass_on(i, k, link):
+        inv = 1.0 / (mass[i] + link)
+        q = link * inv
+        scale[i], ratio[i] = [v * inv for v in rhs[i]], q
+        mass[k] = mass[k] + q * mass[i]
+        rhs[k] = [v + q * w for v, w in zip(rhs[k], rhs[i])]
+
+    for i in range(half):
+        pass_on(i, i + 1, h[i])
     mass[count - 1] = mass[count - 1] + h[count - 1]
     for i in range(count - 1, half, -1):
-        inv = 1.0 / (mass[i] + h[i - 1])
-        q = h[i - 1] * inv
-        scale[i], ratio[i] = rhs[i] * inv, q
-        mass[i - 1] = mass[i - 1] + q * mass[i]
-        rhs[i - 1] = rhs[i - 1] + q * rhs[i]
-    inv = 1.0 / (mass[half - 1] + h[half - 1])
-    q = h[half - 1] * inv
-    first = [None] * (count + 1)
-    first[half] = (rhs[half] + q * rhs[half - 1]) / (mass[half] + q * mass[half - 1])
-    first[half - 1] = rhs[half - 1] * inv + q * first[half]
-    for i in range(half - 2, -1, -1):
-        first[i] = scale[i] + ratio[i] * first[i + 1]
-    for i in range(half + 1, count):
-        first[i] = scale[i] + ratio[i] * first[i - 1]
+        pass_on(i, i - 1, h[i - 1])
+    first = [None] * count
+    inv = 1.0 / mass[half]
+    first[half] = [v * inv for v in rhs[half]]
+    for i in list(range(half - 1, -1, -1)) + list(range(half + 1, count)):
+        k = i + 1 if i < half else i - 1
+        first[i] = [v + ratio[i] * w for v, w in zip(scale[i], first[k])]
     for i in range(count):
-        a, c, part = ends[i]
-        last = part + a * first[i]
-        if i < count - 1:
-            last = last + c * first[i + 1]
-        out_ref[i, 0:8, :] = first[i]
-        out_ref[i, 8:16, :] = last
-
-
-def chain(message):
+        a, c, inv = ends[i]
+        for r in range(GROUP):
+            last = in_ref[i, 8 + r] * inv + a * first[i][r]
+            if i < count - 1:
+                last = last + c * first[i + 1][r]
+            ends_ref[i, r] = first[i][r]
+            ends_ref[i, GROUP + r] = last
+    for r in range(GROUP):
+        start = ends_ref[home, r]
+        value = ends_ref[home, GROUP + r]
+        out_ref[0, r] = start
+        out_ref[GROUPS - 1, GROUP + r] = value
+        for node in range(2 * GROUPS - 3, -1, -1):
+            value = part_ref[node, r] + coef_ref[0, node] * start + coef_ref[1, node] * value
+            block, end = (node + 1) // 2, node % 2 == 1
+            out_ref[block, r if end else GROUP + r] = value
+    for turn in range(GROUPS):
+        send_refs[turn][...] = out_ref[(mine + turn) % GROUPS]
+
+
+def chain(got, part, coef):
+    plane = part.shape[2:]
+    count = len(got)
     return pl.pallas_call(
         chain_kernel,
-        in_specs=[WHOLE],
-        out_specs=WHOLE,
-        out_shape=pltpu.VMEM(message.shape, F32),
+        in_specs=[WHOLE] * (count + 2),
+        out_specs=[WHOLE] * GROUPS,
+        out_shape=[pltpu.VMEM((2 * GROUP,) + plane, F32)] * GROUPS,
+        scratch_shapes=[
+            pltpu.VMEM((count, ROWS) + plane, F32),
+            pltpu.VMEM((count, 2 * GROUP) + plane, F32),
+            pltpu.VMEM((GROUPS, 2 * GROUP) + plane, F32),
+        ],
         compiler_params=SMALL,
         cost_estimate=pl.CostEstimate(flops=10**6, bytes_accessed=10**6, transcendentals=0),
         name="chain",
-    )(message)
-
-
-def back_kernel(coef_ref, ends_ref, part_ref, out_hbm, out_ref, out_sem):
+    )(*got, part, coef)
+
+
+def back_kernel(coef_ref, part_ref, *refs):
+    got_refs, (out_hbm, ends_ref, out_ref, out_sem) = refs[:GROUPS], refs[GROUPS:]
     carried, nx, ny, _ = part_ref.shape
     groups = carried // SB
+    mine = lax.axis_index("gx") % GROUPS
+    for turn in range(GROUPS):
+        ends_ref[(mine + GROUPS - turn) % GROUPS] = got_refs[turn][...]
 
     def put(g):
         return pltpu.make_async_copy(out_ref.at[pl.ds(g * SB, SB)], out_hbm.at[pl.ds(g * SB, SB)], out_sem.at[g])
@@ -385,8 +456,8 @@
     def _(g):
         for t in range(SB):
             s = g * SB + t
-            first = ends_ref[pl.ds(place(s), ny, stride=GROUPS * ROWS), :]
-            value = ends_ref[pl.ds(place(s) + 8, ny, stride=GROUPS * ROWS), :]
+            first = ends_ref[s // GROUP, s % GROUP]
+            value = ends_ref[s // GROUP, s % GROUP + GROUP]
             out_ref[s, 0] = first
             out_ref[s, nx - 1] = value
             for p in range(nx - 2, 0, -1):
@@ -399,38 +470,52 @@
         put(g).wait()
 
 
-def back(part, coef, ends):
+def back(part, coef, got):
     groups = part.shape[0] // SB
     return pl.pallas_call(
         back_kernel,
-        in_specs=[WHOLE, WHOLE, WHOLE],
+        in_specs=[WHOLE] * (2 + GROUPS),
         out_specs=ANY,
         out_shape=jax.ShapeDtypeStruct(part.shape, F32),
-        scratch_shapes=[pltpu.VMEM(part.shape, F32), pltpu.SemaphoreType.DMA((groups,))],
+        scratch_shapes=[
+            pltpu.VMEM((GROUPS, 2 * GROUP) + part.shape[2:], F32),
+            pltpu.VMEM(part.shape, F32),
+            pltpu.SemaphoreType.DMA((groups,)),
+        ],
         compiler_params=SMALL,
         cost_estimate=pl.CostEstimate(flops=2 * 10**6, bytes_accessed=3 * 10**6, transcendentals=0),
         name="back",
-    )(coef, ends, part)
-
-
-def resident(value):
-    return pltpu.with_memory_space_constraint(value, pltpu.VMEM)
+    )(coef, part, *got)
 
 
 def shards(
     adjoint, log_conc, levels, conduct, orders_fwd, orders_rev, stoich, rate_fwd, rate_rev, diffusivity
 ):
-    carried, nx, ny, nz = adjoint.shape
     rows_y, blocks = lax.axis_size("gy"), lax.axis_size("gx")
+    supers = blocks // GROUPS
     near = lax.ppermute(adjoint, "gz", [(0, 1), (1, 0)])
     tail, head = edges(adjoint)
     low = lax.ppermute(tail, "gy", [(i, (i + 1) % rows_y) for i in range(rows_y)])
     high = lax.ppermute(head, "gy", [((i + 1) % rows_y, i) for i in range(rows_y)])
-    chem, coef, ends_m = chemistry(adjoint, log_conc, levels, conduct, orders_fwd, orders_rev, stoich, rate_fwd, rate_rev)
-    part, message = local_part(diffusivity, adjoint, chem, near, low, high, conduct, coef, ends_m)
-    message = lax.all_to_all(message.reshape(blocks, ROWS, nz), "gx", 0, 0, tiled=True)
-    ends = lax.all_to_all(chain(message), "gx", 0, 0, tiled=True)
-    return back(part, coef, ends.reshape(blocks * ROWS, nz))
+    chem, coef, ends_m = chemistry(
+        adjoint, log_conc, levels, conduct, orders_fwd, orders_rev, stoich, rate_fwd, rate_rev
+    )
+    part, *send = local_part(diffusivity, adjoint, chem, near, low, high, conduct, coef, ends_m)
+
+    def close(value, turn):
+        if turn == 0:
+            return value
+        pairs = [(i, i // GROUPS * GROUPS + (i + turn) % GROUPS) for i in range(blocks)]
+        return lax.ppermute(value, "gx", pairs)
+
+    def far(value, turn):
+        if turn == 0:
+            return value
+        return lax.ppermute(value, "gx", [(i, (i + turn * GROUPS) % blocks) for i in range(blocks)])
+
+    message, inner, links = reduce_blocks([close(value, turn) for turn, value in enumerate(send)])
+    send = chain([far(message, turn) for turn in range(supers)], inner, links)
+    return back(part, coef, [close(value, turn) for turn, value in enumerate(send)])
 
 
 def solution(mesh):

time: 60.3 us -> 60.9 us (level)
  blocking collectives: 40 us -> 0 us
  starting transfers between devices: 2.44 us -> 29.5 us
  waiting for transfers between devices: 0.01 us -> 13.4 us
    all_to_all x2 -> x0, blocking collectives: 40 us -> none  [the longest x1 23.7 us: shards(): lax.all_to_all(message.reshape(blocks, ROWS, nz), 'gx', 0, 0, tiled=True)]
    ppermute x0 -> x13, starting transfers between devices: none -> 27 us  [the longest x7 17.3 us: far(): lax.ppermute(value, 'gx', [(i, (i + turn * GROUPS) % blocks) for i in ran...]
    ppermute x0 -> x13, waiting for transfers between devices: none -> 13.4 us  [the longest x7 7.02 us: far(): lax.ppermute(value, 'gx', [(i, (i + turn * GROUPS) % blocks) for i in ran...]
    pallas_call x2 -> x3, Pallas kernels: 1.6 us -> 1.57 us  [the longest x1 1.26 us: back(): pl.pallas_call(back_kernel, in_specs=[WHOLE] * (2 + GROUPS), out_specs=AN...]
  transfers between devices with their start and end apart: 3 -> 16, of which waited for: 0 -> 9; matrix products, arithmetic and copies ran while one was open for 0% -> 0% of each run, Pallas kernels for 19% -> 19%
where the time goes in v5:
time: 60.9 us; the launch traced here: 60.6 us
  starting transfers between devices  29.5 us (48%)
  Pallas kernels  16 us (26%)
  waiting for transfers between devices  13.4 us (22%)
  local copies, waits for them, and re-layouts  1.4 us (2%)
    ppermute x7, starting transfers between devices, far(): lax.ppermute(value, 'gx', [(i, (i + turn * GROUPS) % blocks) for i in ran...  17.3 us
    pallas_call x1, Pallas kernels, chemistry(): pl.pallas_call(chem_kernel, grid=(nx // XB,), in_specs=[pl.BlockSpec((car...  11.3 us
    ppermute x6, starting transfers between devices, close(): return lax.ppermute(value, 'gx', pairs)  9.79 us
    ppermute x7, waiting for transfers between devices, far(): lax.ppermute(value, 'gx', [(i, (i + turn * GROUPS) % blocks) for i in ran...  7.02 us
    ppermute x6, waiting for transfers between devices, close(): return lax.ppermute(value, 'gx', pairs)  6.42 us
    pallas_call x1, Pallas kernels, local_part(): pl.pallas_call(local_kernel, in_specs=[smem] + [WHOLE] * 8, out_specs=[WH...  2.67 us
    ppermute x1, starting transfers between devices, shards(): lax.ppermute(tail, 'gy', [(i, (i + 1) % rows_y) for i in range(rows_y)])  1.57 us
    unnamed x20, local copies, waits for them, and re-layouts  1.4 us
  transfers between devices with their start and end apart: 16, of which 9 were waited for; matrix products, arithmetic and copies ran while one was open for 0% of the time, Pallas kernels for 19%

profile of v5, /device:TPU:2, one launch (start us, length us, event | category | flops | bytes accessed | tf_op | source)
XLA Modules:
  0.0 60.6 jit_solution(15620534053996020968)
XLA Ops:
  0.0 0.0 collective-permute-start
  0.0 1.4 %copy-done = f32[22,16,8,128]{3,2,1,0:T(8,128)S(1)} copy-done((f32[22,16,8,128]{3,2,1,0:T(8,128)S(1)}, f32[22,16,8,128]{3,2,1,0:T(8,128)}, u32[]{:S(2)}) %copy-start) | copy-done | bytes 1441816
  1.4 0.4 edges.1
  1.8 1.6 %collective-permute-start.1 = (f32[22,16,2,128]{3,2,1,0:T(2,128)S(1)}, f32[22,16,2,128]{3,2,1,0:T(2,128)S(1)}, u32[]{:S(2)}, u32[]{:S(2)}) collective-permute-start(f32[22,16,2,128]{3,2,1,0:T(2,128)S(1)} %get-tuple-element.24), channel_id=1, source_target_pairs={{0,2},{2,4},{4,6},{6,0},{1,3},{3,5},{5,7},{7,1},{8,10},{10,12},{12... | collective-permute-start | bytes 1081352 | tf_op jit(solution)/shard_map/ppermute | solution.py:498
  3.4 0.9 %collective-permute-start.2 = (f32[22,16,2,128]{3,2,1,0:T(2,128)S(1)}, f32[22,16,2,128]{3,2,1,0:T(2,128)S(1)}, u32[]{:S(2)}, u32[]{:S(2)}) collective-permute-start(f32[22,16,2,128]{3,2,1,0:T(2,128)S(1)} %get-tuple-element.25), channel_id=1, source_target_pairs={{2,0},{4,2},{6,4},{0,6},{3,1},{5,3},{7,5},{1,7},{10,8},{12,10},{14... | collective-permute-start | bytes 1081352 | tf_op jit(solution)/shard_map/ppermute | solution.py:499
  4.3 0.0 copy-start.2
  4.3 11.3 %chem.1 = (f32[22,16,8,128]{3,2,1,0:T(8,128)S(1)}, f32[3,17,8,128]{3,2,1,0:T(8,128)S(1)}, f32[17,3,8,128]{3,2,1,0:T(8,128)S(1)}) custom-call(f32[22,16,8,128]{3,2,1,0:T(8,128)S(1)} %copy-done, bf16[32,16,8,128]{3,2,1,0:T(8,128)(2,1)S(1)} %copy-done.3, s32[16,8,128]{2,1,0:T(8,128)S(1)} %copy-done.4, f32[16,8,128]{2,1,0:T(8,128)S(1)} %copy-done.1, ...), custom_call_target="tpu_custom_call" | custom-call | flops 12000000000 | bytes 4000000 | tf_op jit(solution)/shard_map/chem/pallas_call | solution.py:153
  15.7 2.7 %local.1 = (f32[22,16,8,128]{3,2,1,0:T(8,128)S(1)}, f32[16,8,128]{2,1,0:T(8,128)S(1)}, f32[16,8,128]{2,1,0:T(8,128)S(1)}, f32[16,8,128]{2,1,0:T(8,128)S(1)}, f32[16,8,128]{2,1,0:T(8,128)S(1)}) custom-call(f32[22]{0:T(128)S(1)} %copy-done.2, f32[16,8,128]{2,1,0:T(8,128)S(1)} %copy-done.1, f32[22,16,8,128]{3,2,1,0:T(8,128)S(1)} %copy-done, ...), custom_call_target="tpu_custom_call" | custom-call | flops 20000000 | bytes 7000000 | tf_op jit(solution)/shard_map/local/pallas_call | solution.py:299
  18.4 1.3 %collective-permute-start.3 = (f32[16,8,128]{2,1,0:T(8,128)S(1)}, f32[16,8,128]{2,1,0:T(8,128)S(1)}, u32[]{:S(2)}, u32[]{:S(2)}) collective-permute-start(f32[16,8,128]{2,1,0:T(8,128)S(1)} %get-tuple-element.29), channel_id=1, source_target_pairs={{0,8},{8,16},{16,24},{24,0},{32,40},{40,48},{48,56},{56,32},{64,72... | collective-permute-start | bytes 196616 | tf_op jit(solution)/shard_map/ppermute | solution.py:509
  19.7 2.9 %collective-permute-start.4 = (f32[16,8,128]{2,1,0:T(8,128)S(1)}, f32[16,8,128]{2,1,0:T(8,128)S(1)}, u32[]{:S(2)}, u32[]{:S(2)}) collective-permute-start(f32[16,8,128]{2,1,0:T(8,128)S(1)} %get-tuple-element.30), channel_id=1, source_target_pairs={{0,16},{8,24},{16,0},{24,8},{32,48},{40,56},{48,32},{56,40},{64,80... | collective-permute-start | bytes 196616 | tf_op jit(solution)/shard_map/ppermute | solution.py:509
  22.6 1.3 %collective-permute-start.5 = (f32[16,8,128]{2,1,0:T(8,128)S(1)}, f32[16,8,128]{2,1,0:T(8,128)S(1)}, u32[]{:S(2)}, u32[]{:S(2)}) collective-permute-start(f32[16,8,128]{2,1,0:T(8,128)S(1)} %get-tuple-element.31), channel_id=1, source_target_pairs={{0,24},{8,0},{16,8},{24,16},{32,56},{40,32},{48,40},{56,48},{64,88... | collective-permute-start | bytes 196616 | tf_op jit(solution)/shard_map/ppermute | solution.py:509
  23.9 0.4 collective-permute-done.3.refs_1_
  24.4 1.6 %collective-permute-done.4.refs_2_ = f32[16,8,128]{2,1,0:T(8,128)S(1)} collective-permute-done((f32[16,8,128]{2,1,0:T(8,128)S(1)}, f32[16,8,128]{2,1,0:T(8,128)S(1)}, u32[]{:S(2)}, u32[]{:S(2)}) %collective-permute-start.4) | collective-permute-done | bytes 65568 | tf_op jit(solution)/shard_map/ppermute | solution.py:509
  25.9 0.9 %collective-permute-done.5.refs_3_ = f32[16,8,128]{2,1,0:T(8,128)S(1)} collective-permute-done((f32[16,8,128]{2,1,0:T(8,128)S(1)}, f32[16,8,128]{2,1,0:T(8,128)S(1)}, u32[]{:S(2)}, u32[]{:S(2)}) %collective-permute-start.5) | collective-permute-done | bytes 65568 | tf_op jit(solution)/shard_map/ppermute | solution.py:509
  26.9 0.1 reduce.1
  27.0 5.9 %collective-permute-start.12 = (f32[16,8,128]{2,1,0:T(8,128)S(1)}, f32[16,8,128]{2,1,0:T(8,128)S(1)}, u32[]{:S(2)}, u32[]{:S(2)}) collective-permute-start(f32[16,8,128]{2,1,0:T(8,128)S(1)} %get-tuple-element.32.refs_0_), channel_id=1, source_target_pairs={{0,224},{8,232},{16,240},{24,248},{32,0},{40,8},{48,16},{56,24},{6... | collective-permute-start | bytes 196616 | tf_op jit(solution)/shard_map/ppermute | solution.py:514
  32.9 1.5 %collective-permute-start.11 = (f32[16,8,128]{2,1,0:T(8,128)S(1)}, f32[16,8,128]{2,1,0:T(8,128)S(1)}, u32[]{:S(2)}, u32[]{:S(2)}) collective-permute-start(f32[16,8,128]{2,1,0:T(8,128)S(1)} %get-tuple-element.32.refs_0_), channel_id=1, source_target_pairs={{0,192},{8,200},{16,208},{24,216},{32,224},{40,232},{48,240},{56,2... | collective-permute-start | bytes 196616 | tf_op jit(solution)/shard_map/ppermute | solution.py:514
  34.4 0.5 collective-permute-start.10
  34.8 5.0 %collective-permute-start.9 = (f32[16,8,128]{2,1,0:T(8,128)S(1)}, f32[16,8,128]{2,1,0:T(8,128)S(1)}, u32[]{:S(2)}, u32[]{:S(2)}) collective-permute-start(f32[16,8,128]{2,1,0:T(8,128)S(1)} %get-tuple-element.32.refs_0_), channel_id=1, source_target_pairs={{0,128},{8,136},{16,144},{24,152},{32,160},{40,168},{48,176},{56,1... | collective-permute-start | bytes 196616 | tf_op jit(solution)/shard_map/ppermute | solution.py:514
  39.9 2.5 %collective-permute-start.7 = (f32[16,8,128]{2,1,0:T(8,128)S(1)}, f32[16,8,128]{2,1,0:T(8,128)S(1)}, u32[]{:S(2)}, u32[]{:S(2)}) collective-permute-start(f32[16,8,128]{2,1,0:T(8,128)S(1)} %get-tuple-element.32.refs_0_), channel_id=1, source_target_pairs={{0,64},{8,72},{16,80},{24,88},{32,96},{40,104},{48,112},{56,120},{... | collective-permute-start | bytes 196616 | tf_op jit(solution)/shard_map/ppermute | solution.py:514
  42.3 1.9 %collective-permute-start.6 = (f32[16,8,128]{2,1,0:T(8,128)S(1)}, f32[16,8,128]{2,1,0:T(8,128)S(1)}, u32[]{:S(2)}, u32[]{:S(2)}) collective-permute-start(f32[16,8,128]{2,1,0:T(8,128)S(1)} %get-tuple-element.32.refs_0_), channel_id=1, source_target_pairs={{0,32},{8,40},{16,48},{24,56},{32,64},{40,72},{48,80},{56,88},{64,... | collective-permute-start | bytes 196616 | tf_op jit(solution)/shard_map/ppermute | solution.py:514
  44.2 1.0 %collective-permute-done.9.refs_4_ = f32[16,8,128]{2,1,0:T(8,128)S(1)} collective-permute-done((f32[16,8,128]{2,1,0:T(8,128)S(1)}, f32[16,8,128]{2,1,0:T(8,128)S(1)}, u32[]{:S(2)}, u32[]{:S(2)}) %collective-permute-start.9) | collective-permute-done | bytes 65568 | tf_op jit(solution)/shard_map/ppermute | solution.py:514
  45.3 3.9 %collective-permute-done.8.refs_3_ = f32[16,8,128]{2,1,0:T(8,128)S(1)} collective-permute-done((f32[16,8,128]{2,1,0:T(8,128)S(1)}, f32[16,8,128]{2,1,0:T(8,128)S(1)}, u32[]{:S(2)}, u32[]{:S(2)}) %collective-permute-start.8) | collective-permute-done | bytes 65568 | tf_op jit(solution)/shard_map/ppermute | solution.py:514
  49.2 2.1 %collective-permute-done.7.refs_2_ = f32[16,8,128]{2,1,0:T(8,128)S(1)} collective-permute-done((f32[16,8,128]{2,1,0:T(8,128)S(1)}, f32[16,8,128]{2,1,0:T(8,128)S(1)}, u32[]{:S(2)}, u32[]{:S(2)}) %collective-permute-start.7) | collective-permute-done | bytes 65568 | tf_op jit(solution)/shard_map/ppermute | solution.py:514
  51.3 0.2 chain.1
  51.5 0.1 collective-permute-start.13
  51.6 3.5 %collective-permute-start.14 = (f32[12,8,128]{2,1,0:T(8,128)S(1)}, f32[12,8,128]{2,1,0:T(8,128)S(1)}, u32[]{:S(2)}, u32[]{:S(2)}) collective-permute-start(f32[12,8,128]{2,1,0:T(8,128)S(1)} %get-tuple-element.37), channel_id=1, source_target_pairs={{0,16},{8,24},{16,0},{24,8},{32,48},{40,56},{48,32},{56,40},{64,80... | collective-permute-start | bytes 147464 | tf_op jit(solution)/shard_map/ppermute | solution.py:509
  55.1 0.6 collective-permute-start.15
  55.7 1.2 %collective-permute-done.13.refs_1_ = f32[12,8,128]{2,1,0:T(8,128)S(1)} collective-permute-done((f32[12,8,128]{2,1,0:T(8,128)S(1)}, f32[12,8,128]{2,1,0:T(8,128)S(1)}, u32[]{:S(2)}, u32[]{:S(2)}) %collective-permute-start.13) | collective-permute-done | bytes 49184 | tf_op jit(solution)/shard_map/ppermute | solution.py:509
  56.9 0.9 %collective-permute-done.14.refs_2_ = f32[12,8,128]{2,1,0:T(8,128)S(1)} collective-permute-done((f32[12,8,128]{2,1,0:T(8,128)S(1)}, f32[12,8,128]{2,1,0:T(8,128)S(1)}, u32[]{:S(2)}, u32[]{:S(2)}) %collective-permute-start.14) | collective-permute-done | bytes 49184 | tf_op jit(solution)/shard_map/ppermute | solution.py:509
  57.7 1.5 %collective-permute-done.15.refs_3_ = f32[12,8,128]{2,1,0:T(8,128)S(1)} collective-permute-done((f32[12,8,128]{2,1,0:T(8,128)S(1)}, f32[12,8,128]{2,1,0:T(8,128)S(1)}, u32[]{:S(2)}, u32[]{:S(2)}) %collective-permute-start.15) | collective-permute-done | bytes 49184 | tf_op jit(solution)/shard_map/ppermute | solution.py:509
  59.2 1.3 %back.1 = f32[22,16,8,128]{3,2,1,0:T(8,128)} custom-call(f32[3,17,8,128]{3,2,1,0:T(8,128)S(1)} %get-tuple-element.22.coef_ref, f32[22,16,8,128]{3,2,1,0:T(8,128)S(1)} %get-tuple-element.27.part_ref, f32[12,8,128]{2,1,0:T(8,128)S(1)} %get-tuple-element.35.refs_0_, f32[12,8,128]{2,1,0:T(8,128)S(1)} %collective-permute-done.13.refs_1_, ...), custom_call_target="tpu_custom_call" | custom-call | flops 2000000 | bytes 3000000 | tf_op jit(solution)/shard_map/back/pallas_call | solution.py:475
  (26 shorter events, 0.1 us)
Async XLA Ops:
  0.0 15.7 %collective-permute-start = (f32[22,16,8,128]{3,2,1,0:T(8,128)}, f32[22,16,8,128]{3,2,1,0:T(8,128)S(1)}, u32[]{:S(2)}, u32[]{:S(2)}) collective-permute-start(f32[22,16,8,128]{3,2,1,0:T(8,128)} %adj_ref.5), channel_id=1, source_target_pairs={{0,1},{1,0},{2,3},{3,2},{4,5},{5,4},{6,7},{7,6},{8,9},{9,8},{10,11... | collective-permute-start | bytes 4325384 | tf_op jit(solution)/shard_map/ppermute | solution.py:496
  0.0 1.4 %copy-start = (f32[22,16,8,128]{3,2,1,0:T(8,128)S(1)}, f32[22,16,8,128]{3,2,1,0:T(8,128)}, u32[]{:S(2)}) copy-start(f32[22,16,8,128]{3,2,1,0:T(8,128)} %adj_ref.5) | copy-start | bytes 4325380
  1.4 2.9 %copy-start.1 = (f32[16,8,128]{2,1,0:T(8,128)S(1)}, f32[16,8,128]{2,1,0:T(8,128)}, u32[]{:S(2)}) copy-start(f32[16,8,128]{2,1,0:T(8,128)} %cond_ref.3) | copy-start | bytes 196612
  1.4 2.9 %copy-start.3 = (bf16[32,16,8,128]{3,2,1,0:T(8,128)(2,1)S(1)}, bf16[32,16,8,128]{3,2,1,0:T(8,128)(2,1)}, u32[]{:S(2)}) copy-start(bf16[32,16,8,128]{3,2,1,0:T(8,128)(2,1)} %conc_ref.1) | copy-start | bytes 3145732
  1.4 2.9 %copy-start.4 = (s32[16,8,128]{2,1,0:T(8,128)S(1)}, s32[16,8,128]{2,1,0:T(8,128)}, u32[]{:S(2)}) copy-start(s32[16,8,128]{2,1,0:T(8,128)} %lev_ref.1) | copy-start | bytes 196612
  1.4 2.9 %copy-start.5 = (bf16[206,32]{0,1:T(8,128)(2,1)S(1)}, bf16[206,32]{0,1:T(8,128)(2,1)}, u32[]{:S(2)}) copy-start(bf16[206,32]{0,1:T(8,128)(2,1)} %param.14) | copy-start | bytes 39556
  1.4 2.9 %copy-start.6 = (bf16[206,32]{0,1:T(8,128)(2,1)S(1)}, bf16[206,32]{0,1:T(8,128)(2,1)}, u32[]{:S(2)}) copy-start(bf16[206,32]{0,1:T(8,128)(2,1)} %param.15) | copy-start | bytes 39556
  1.4 2.9 %copy-start.7 = (bf16[206,22]{0,1:T(8,128)(2,1)S(1)}, bf16[206,22]{0,1:T(8,128)(2,1)}, u32[]{:S(2)}) copy-start(bf16[206,22]{0,1:T(8,128)(2,1)} %param.16) | copy-start | bytes 27196
  1.4 2.9 %copy-start.8 = (f32[206]{0:T(256)S(1)}, f32[206]{0:T(256)}, u32[]{:S(2)}) copy-start(f32[206]{0:T(256)} %param.17) | copy-start | bytes 2476
  1.4 2.9 %copy-start.9 = (f32[206]{0:T(256)S(1)}, f32[206]{0:T(256)}, u32[]{:S(2)}) copy-start(f32[206]{0:T(256)} %param.18) | copy-start | bytes 2476
  1.8 13.9 %collective-permute-start.1 = (f32[22,16,2,128]{3,2,1,0:T(2,128)S(1)}, f32[22,16,2,128]{3,2,1,0:T(2,128)S(1)}, u32[]{:S(2)}, u32[]{:S(2)}) collective-permute-start(f32[22,16,2,128]{3,2,1,0:T(2,128)S(1)} %get-tuple-element.24), channel_id=1, source_target_pairs={{0,2},{2,4},{4,6},{6,0},{1,3},{3,5},{5,7},{7,1},{8,10},{10,12},{12... | collective-permute-start | bytes 1081352 | tf_op jit(solution)/shard_map/ppermute | solution.py:498
  3.4 12.3 %collective-permute-start.2 = (f32[22,16,2,128]{3,2,1,0:T(2,128)S(1)}, f32[22,16,2,128]{3,2,1,0:T(2,128)S(1)}, u32[]{:S(2)}, u32[]{:S(2)}) collective-permute-start(f32[22,16,2,128]{3,2,1,0:T(2,128)S(1)} %get-tuple-element.25), channel_id=1, source_target_pairs={{2,0},{4,2},{6,4},{0,6},{3,1},{5,3},{7,5},{1,7},{10,8},{12,10},{14... | collective-permute-start | bytes 1081352 | tf_op jit(solution)/shard_map/ppermute | solution.py:499
  4.3 11.4 %copy-start.2 = (f32[22]{0:T(128)S(1)}, f32[22]{0:T(128)}, u32[]{:S(2)}) copy-start(f32[22]{0:T(128)} %diff_ref.1) | copy-start | bytes 268
  18.4 6.0 %collective-permute-start.3 = (f32[16,8,128]{2,1,0:T(8,128)S(1)}, f32[16,8,128]{2,1,0:T(8,128)S(1)}, u32[]{:S(2)}, u32[]{:S(2)}) collective-permute-start(f32[16,8,128]{2,1,0:T(8,128)S(1)} %get-tuple-element.29), channel_id=1, source_target_pairs={{0,8},{8,16},{16,24},{24,0},{32,40},{40,48},{48,56},{56,32},{64,72... | collective-permute-start | bytes 196616 | tf_op jit(solution)/shard_map/ppermute | solution.py:509
  19.7 6.2 %collective-permute-start.4 = (f32[16,8,128]{2,1,0:T(8,128)S(1)}, f32[16,8,128]{2,1,0:T(8,128)S(1)}, u32[]{:S(2)}, u32[]{:S(2)}) collective-permute-start(f32[16,8,128]{2,1,0:T(8,128)S(1)} %get-tuple-element.30), channel_id=1, source_target_pairs={{0,16},{8,24},{16,0},{24,8},{32,48},{40,56},{48,32},{56,40},{64,80... | collective-permute-start | bytes 196616 | tf_op jit(solution)/shard_map/ppermute | solution.py:509
  22.6 4.3 %collective-permute-start.5 = (f32[16,8,128]{2,1,0:T(8,128)S(1)}, f32[16,8,128]{2,1,0:T(8,128)S(1)}, u32[]{:S(2)}, u32[]{:S(2)}) collective-permute-start(f32[16,8,128]{2,1,0:T(8,128)S(1)} %get-tuple-element.31), channel_id=1, source_target_pairs={{0,24},{8,0},{16,8},{24,16},{32,56},{40,32},{48,40},{56,48},{64,88... | collective-permute-start | bytes 196616 | tf_op jit(solution)/shard_map/ppermute | solution.py:509
  27.0 12.9 %collective-permute-start.12 = (f32[16,8,128]{2,1,0:T(8,128)S(1)}, f32[16,8,128]{2,1,0:T(8,128)S(1)}, u32[]{:S(2)}, u32[]{:S(2)}) collective-permute-start(f32[16,8,128]{2,1,0:T(8,128)S(1)} %get-tuple-element.32.refs_0_), channel_id=1, source_target_pairs={{0,224},{8,232},{16,240},{24,248},{32,0},{40,8},{48,16},{56,24},{6... | collective-permute-start | bytes 196616 | tf_op jit(solution)/shard_map/ppermute | solution.py:514
  32.9 9.4 %collective-permute-start.11 = (f32[16,8,128]{2,1,0:T(8,128)S(1)}, f32[16,8,128]{2,1,0:T(8,128)S(1)}, u32[]{:S(2)}, u32[]{:S(2)}) collective-permute-start(f32[16,8,128]{2,1,0:T(8,128)S(1)} %get-tuple-element.32.refs_0_), channel_id=1, source_target_pairs={{0,192},{8,200},{16,208},{24,216},{32,224},{40,232},{48,240},{56,2... | collective-permute-start | bytes 196616 | tf_op jit(solution)/shard_map/ppermute | solution.py:514
  34.4 9.9 %collective-permute-start.10 = (f32[16,8,128]{2,1,0:T(8,128)S(1)}, f32[16,8,128]{2,1,0:T(8,128)S(1)}, u32[]{:S(2)}, u32[]{:S(2)}) collective-permute-start(f32[16,8,128]{2,1,0:T(8,128)S(1)} %get-tuple-element.32.refs_0_), channel_id=1, source_target_pairs={{0,160},{8,168},{16,176},{24,184},{32,192},{40,200},{48,208},{56,2... | collective-permute-start | bytes 196616 | tf_op jit(solution)/shard_map/ppermute | solution.py:514
  34.8 10.5 %collective-permute-start.9 = (f32[16,8,128]{2,1,0:T(8,128)S(1)}, f32[16,8,128]{2,1,0:T(8,128)S(1)}, u32[]{:S(2)}, u32[]{:S(2)}) collective-permute-start(f32[16,8,128]{2,1,0:T(8,128)S(1)} %get-tuple-element.32.refs_0_), channel_id=1, source_target_pairs={{0,128},{8,136},{16,144},{24,152},{32,160},{40,168},{48,176},{56,1... | collective-permute-start | bytes 196616 | tf_op jit(solution)/shard_map/ppermute | solution.py:514
  39.8 9.3 %collective-permute-start.8 = (f32[16,8,128]{2,1,0:T(8,128)S(1)}, f32[16,8,128]{2,1,0:T(8,128)S(1)}, u32[]{:S(2)}, u32[]{:S(2)}) collective-permute-start(f32[16,8,128]{2,1,0:T(8,128)S(1)} %get-tuple-element.32.refs_0_), channel_id=1, source_target_pairs={{0,96},{8,104},{16,112},{24,120},{32,128},{40,136},{48,144},{56,15... | collective-permute-start | bytes 196616 | tf_op jit(solution)/shard_map/ppermute | solution.py:514
  39.9 11.4 %collective-permute-start.7 = (f32[16,8,128]{2,1,0:T(8,128)S(1)}, f32[16,8,128]{2,1,0:T(8,128)S(1)}, u32[]{:S(2)}, u32[]{:S(2)}) collective-permute-start(f32[16,8,128]{2,1,0:T(8,128)S(1)} %get-tuple-element.32.refs_0_), channel_id=1, source_target_pairs={{0,64},{8,72},{16,80},{24,88},{32,96},{40,104},{48,112},{56,120},{... | collective-permute-start | bytes 196616 | tf_op jit(solution)/shard_map/ppermute | solution.py:514
  42.3 8.9 %collective-permute-start.6 = (f32[16,8,128]{2,1,0:T(8,128)S(1)}, f32[16,8,128]{2,1,0:T(8,128)S(1)}, u32[]{:S(2)}, u32[]{:S(2)}) collective-permute-start(f32[16,8,128]{2,1,0:T(8,128)S(1)} %get-tuple-element.32.refs_0_), channel_id=1, source_target_pairs={{0,32},{8,40},{16,48},{24,56},{32,64},{40,72},{48,80},{56,88},{64,... | collective-permute-start | bytes 196616 | tf_op jit(solution)/shard_map/ppermute | solution.py:514
  51.5 5.4 %collective-permute-start.13 = (f32[12,8,128]{2,1,0:T(8,128)S(1)}, f32[12,8,128]{2,1,0:T(8,128)S(1)}, u32[]{:S(2)}, u32[]{:S(2)}) collective-permute-start(f32[12,8,128]{2,1,0:T(8,128)S(1)} %get-tuple-element.36), channel_id=1, source_target_pairs={{0,8},{8,16},{16,24},{24,0},{32,40},{40,48},{48,56},{56,32},{64,72... | collective-permute-start | bytes 147464 | tf_op jit(solution)/shard_map/ppermute | solution.py:509
  51.6 6.1 %collective-permute-start.14 = (f32[12,8,128]{2,1,0:T(8,128)S(1)}, f32[12,8,128]{2,1,0:T(8,128)S(1)}, u32[]{:S(2)}, u32[]{:S(2)}) collective-permute-start(f32[12,8,128]{2,1,0:T(8,128)S(1)} %get-tuple-element.37), channel_id=1, source_target_pairs={{0,16},{8,24},{16,0},{24,8},{32,48},{40,56},{48,32},{56,40},{64,80... | collective-permute-start | bytes 147464 | tf_op jit(solution)/shard_map/ppermute | solution.py:509
  55.1 4.1 %collective-permute-start.15 = (f32[12,8,128]{2,1,0:T(8,128)S(1)}, f32[12,8,128]{2,1,0:T(8,128)S(1)}, u32[]{:S(2)}, u32[]{:S(2)}) collective-permute-start(f32[12,8,128]{2,1,0:T(8,128)S(1)} %get-tuple-element.38), channel_id=1, source_target_pairs={{0,24},{8,0},{16,8},{24,16},{32,56},{40,32},{48,40},{56,48},{64,88... | collective-permute-start | bytes 147464 | tf_op jit(solution)/shard_map/ppermute | solution.py:509

commit v6 on v5

--- a/solution.py
+++ b/solution.py
@@ -188,6 +188,7 @@
 GROUP = 6
 GROUPS = 4
 ROWS = 16
+PAIR = 2
 SB = 2
 LB = 11
 ANY = pl.BlockSpec(memory_space=pl.ANY)
@@ -313,8 +314,11 @@
 
 
 def reduce_kernel(*refs):
-    got_refs, (msg_ref, part_ref, coef_ref, in_ref) = refs[:GROUPS], refs[GROUPS:]
-    mine = lax.axis_index("gx") % GROUPS
+    got_refs, send_refs = refs[:GROUPS], refs[GROUPS : 2 * GROUPS]
+    part_ref, coef_ref, in_ref, msg_ref = refs[2 * GROUPS :]
+    device = lax.axis_index("gx")
+    mine, home = device % GROUPS, device // GROUPS % GROUPS
+    ny = in_ref.shape[2]
     for turn in range(GROUPS):
         in_ref[(mine + GROUPS - turn) % GROUPS] = got_refs[turn][...]
     gap, mass_first = in_ref[0, 6], in_ref[0, 7]
@@ -336,7 +340,10 @@
         mass = in_ref[block, base + 7] + beta * mass
         gap = alpha * after
     for r, plane in enumerate(first + [gap, mass_first] + rhs + [in_ref[GROUPS - 1, 14], mass]):
-        msg_ref[r] = plane
+        msg_ref[pl.ds(r, ny, stride=ROWS), :] = plane
+    size = PAIR * ROWS
+    for turn in range(GROUPS):
+        send_refs[turn][...] = msg_ref[pl.ds(pl.multiple_of((home + turn) % GROUPS * size, size), size), :]
 
 
 def reduce_blocks(got):
@@ -344,74 +351,146 @@
     return pl.pallas_call(
         reduce_kernel,
         in_specs=[WHOLE] * GROUPS,
-        out_specs=[WHOLE] * 3,
-        out_shape=[
-            pltpu.VMEM((ROWS,) + plane, F32),
+        out_specs=[WHOLE] * (GROUPS + 2),
+        out_shape=[pltpu.VMEM((PAIR * ROWS, plane[1]), F32)] * GROUPS
+        + [
             pltpu.VMEM((2 * GROUPS - 2, GROUP) + plane, F32),
             pltpu.VMEM((2, 2 * GROUPS - 2) + plane, F32),
         ],
-        scratch_shapes=[pltpu.VMEM((GROUPS, ROWS) + plane, F32)],
+        scratch_shapes=[
+            pltpu.VMEM((GROUPS, ROWS) + plane, F32),
+            pltpu.VMEM((plane[0] * ROWS, plane[1]), F32),
+        ],
         compiler_params=SMALL,
         cost_estimate=pl.CostEstimate(flops=10**6, bytes_accessed=10**6, transcendentals=0),
         name="reduce",
     )(*got)
 
 
-def chain_kernel(*refs):
-    count = len(refs) - GROUPS - 5
-    got_refs, (part_ref, coef_ref) = refs[:count], refs[count : count + 2]
-    send_refs, (in_ref, ends_ref, out_ref) = refs[count + 2 : count + 2 + GROUPS], refs[count + 2 + GROUPS :]
+def merge_kernel(*refs):
+    got_refs, (msg_ref, part_ref, coef_ref, in_ref) = refs[:GROUPS], refs[GROUPS:]
+    home = lax.axis_index("gx") // GROUPS % GROUPS
+    for turn in range(GROUPS):
+        in_ref[(home + GROUPS - turn) % GROUPS] = got_refs[turn][...]
+    shape = (8, in_ref.shape[2])
+    sub = iota(shape, 0)
+    for pair in range(PAIR):
+        top = pair * ROWS
+
+        def row(block, r):
+            return jnp.broadcast_to(in_ref[block, top + r : top + r + 1, :], shape)
+
+        gap, mass = row(0, 6), row(0, 15)
+        first = in_ref[0, top : top + 8, :]
+        rhs = in_ref[0, top + 8 : top + 16, :]
+        for node in range(2 * GROUPS - 2):
+            block, end = (node + 1) // 2, node % 2 == 1
+            after = row(block, 6 if end else 14)
+            inv = 1.0 / (gap + after + mass)
+            alpha, beta = gap * inv, after * inv
+            coef_ref[0, pair, node], coef_ref[1, pair, node] = alpha, beta
+            part_ref[pair, node] = rhs * inv
+            base, block = (8, block) if end else (0, block + 1)
+            first = first + alpha * rhs
+            rhs = in_ref[block, top + base : top + base + 8, :] + beta * rhs
+            mass = row(block, base + 7) + beta * mass
+            gap = alpha * after
+        msg_ref[top : top + 8, :] = jnp.where(sub == 6, gap, first)
+        msg_ref[top + 8 : top + 16, :] = jnp.where(sub == 6, row(GROUPS - 1, 14), rhs)
+
+
+def merge(got):
+    nz = got[0].shape[1]
+    nodes = 2 * GROUPS - 2
+    return pl.pallas_call(
+        merge_kernel,
+        in_specs=[WHOLE] * GROUPS,
+        out_specs=[WHOLE] * 3,
+        out_shape=[
+            pltpu.VMEM((PAIR * ROWS, nz), F32),
+            pltpu.VMEM((PAIR, nodes, 8, nz), F32),
+            pltpu.VMEM((2, PAIR, nodes, 8, nz), F32),
+        ],
+        scratch_shapes=[pltpu.VMEM((GROUPS, PAIR * ROWS, nz), F32)],
+        compiler_params=SMALL,
+        cost_estimate=pl.CostEstimate(flops=10**6, bytes_accessed=10**6, transcendentals=0),
+        name="merge",
+    )(*got)
+
+
+def chain_kernel(own_ref, other_ref, part_ref, coef_ref, *refs):
+    send_refs, (in_ref, ends_ref, out_ref) = refs[:GROUPS], refs[GROUPS:]
     device = lax.axis_index("gx")
-    mine, home = device % GROUPS, device // GROUPS
-    for turn in range(count):
-        in_ref[(home + count - turn) % count] = got_refs[turn][...]
-    h, mass, rhs, ends = [], [], [], []
-    passed_m = passed_b = None
-    for i in range(count):
-        g, m_f, face, m_l = in_ref[i, 6], in_ref[i, 7], in_ref[i, 14], in_ref[i, 15]
-        inv = 1.0 / (g + face + m_l)
-        a, c = g * inv, face * inv
-        m = m_f + a * m_l
-        b = [in_ref[i, r] + a * in_ref[i, 8 + r] for r in range(GROUP)]
-        if i > 0:
-            m, b = m + passed_m, [p + q for p, q in zip(b, passed_b)]
-        passed_m, passed_b = c * m_l, [c * in_ref[i, 8 + r] for r in range(GROUP)]
-        h.append(a * face)
-        mass.append(m)
-        rhs.append(b)
-        ends.append((a, c, inv))
-    half = count // 2
-    scale, ratio = [None] * count, [None] * count
-
-    def pass_on(i, k, link):
-        inv = 1.0 / (mass[i] + link)
+    home, side = device // GROUPS % GROUPS, device // (GROUPS * GROUPS)
+    in_ref[side] = own_ref[...]
+    in_ref[1 - side] = other_ref[...]
+    shape = (8, in_ref.shape[2])
+    for pair in range(PAIR):
+        top = pair * ROWS
+
+        def row(block, r):
+            return jnp.broadcast_to(in_ref[block, top + r : top + r + 1, :], shape)
+
+        def rows(block, r):
+            return in_ref[block, top + r : top + r + 8, :]
+
+        inv0 = 1.0 / (row(0, 6) + row(0, 14) + row(0, 15))
+        a0, c0 = row(0, 6) * inv0, row(0, 14) * inv0
+        inv1 = 1.0 / (row(1, 6) + row(1, 14) + row(1, 15))
+        a1 = row(1, 6) * inv1
+        link = a0 * row(0, 14)
+        mass0, rhs0 = row(0, 7) + a0 * row(0, 15), rows(0, 0) + a0 * rows(0, 8)
+        mass1 = row(1, 7) + a1 * row(1, 15) + c0 * row(0, 15) + a1 * row(1, 14)
+        rhs1 = rows(1, 0) + a1 * rows(1, 8) + c0 * rows(0, 8)
+        inv = 1.0 / (mass0 + link)
         q = link * inv
-        scale[i], ratio[i] = [v * inv for v in rhs[i]], q
-        mass[k] = mass[k] + q * mass[i]
-        rhs[k] = [v + q * w for v, w in zip(rhs[k], rhs[i])]
-
-    for i in range(half):
-        pass_on(i, i + 1, h[i])
-    mass[count - 1] = mass[count - 1] + h[count - 1]
-    for i in range(count - 1, half, -1):
-        pass_on(i, i - 1, h[i - 1])
-    first = [None] * count
-    inv = 1.0 / mass[half]
-    first[half] = [v * inv for v in rhs[half]]
-    for i in list(range(half - 1, -1, -1)) + list(range(half + 1, count)):
-        k = i + 1 if i < half else i - 1
-        first[i] = [v + ratio[i] * w for v, w in zip(scale[i], first[k])]
-    for i in range(count):
-        a, c, inv = ends[i]
-        for r in range(GROUP):
-            last = in_ref[i, 8 + r] * inv + a * first[i][r]
-            if i < count - 1:
-                last = last + c * first[i + 1][r]
-            ends_ref[i, r] = first[i][r]
-            ends_ref[i, GROUP + r] = last
+        first1 = (rhs1 + q * rhs0) / (mass1 + q * mass0)
+        first0 = rhs0 * inv + q * first1
+        ends_ref[0, pair, 0], ends_ref[0, pair, 1] = first0, rows(0, 8) * inv0 + a0 * first0 + c0 * first1
+        ends_ref[1, pair, 0], ends_ref[1, pair, 1] = first1, rows(1, 8) * inv1 + a1 * first1
+        start, value = ends_ref[side, pair, 0], ends_ref[side, pair, 1]
+        out_ref[0, top : top + 8, :] = start
+        out_ref[GROUPS - 1, top + 8 : top + 16, :] = value
+        for node in range(2 * GROUPS - 3, -1, -1):
+            value = part_ref[pair, node] + coef_ref[0, pair, node] * start + coef_ref[1, pair, node] * value
+            block, end = (node + 1) // 2, node % 2 == 1
+            base = top if end else top + 8
+            out_ref[block, base : base + 8, :] = value
+    for turn in range(GROUPS):
+        send_refs[turn][...] = out_ref[(home + turn) % GROUPS]
+
+
+def chain(own, other, part, coef):
+    nz = own.shape[1]
+    return pl.pallas_call(
+        chain_kernel,
+        in_specs=[WHOLE] * 4,
+        out_specs=[WHOLE] * GROUPS,
+        out_shape=[pltpu.VMEM(own.shape, F32)] * GROUPS,
+        scratch_shapes=[
+            pltpu.VMEM((2, PAIR * ROWS, nz), F32),
+            pltpu.VMEM((2, PAIR, 2, 8, nz), F32),
+            pltpu.VMEM((GROUPS, PAIR * ROWS, nz), F32),
+        ],
+        compiler_params=SMALL,
+        cost_estimate=pl.CostEstimate(flops=10**6, bytes_accessed=10**6, transcendentals=0),
+        name="chain",
+    )(own, other, part, coef)
+
+
+def expand_kernel(*refs):
+    got_refs, (part_ref, coef_ref) = refs[:GROUPS], refs[GROUPS : GROUPS + 2]
+    send_refs, (ends_ref, out_ref) = refs[GROUPS + 2 : 2 * GROUPS + 2], refs[2 * GROUPS + 2 :]
+    device = lax.axis_index("gx")
+    mine, home = device % GROUPS, device // GROUPS % GROUPS
+    ny = out_ref.shape[2]
+    size = PAIR * ROWS
+    for turn in range(GROUPS):
+        at = pl.multiple_of((home + GROUPS - turn) % GROUPS * size, size)
+        ends_ref[pl.ds(at, size), :] = got_refs[turn][...]
     for r in range(GROUP):
-        start = ends_ref[home, r]
-        value = ends_ref[home, GROUP + r]
+        start = ends_ref[pl.ds(r, ny, stride=ROWS), :]
+        value = ends_ref[pl.ds(r + 8, ny, stride=ROWS), :]
         out_ref[0, r] = start
         out_ref[GROUPS - 1, GROUP + r] = value
         for node in range(2 * GROUPS - 3, -1, -1):
@@ -422,22 +501,20 @@
         send_refs[turn][...] = out_ref[(mine + turn) % GROUPS]
 
 
-def chain(got, part, coef):
+def expand(got, part, coef):
     plane = part.shape[2:]
-    count = len(got)
-    return pl.pallas_call(
-        chain_kernel,
-        in_specs=[WHOLE] * (count + 2),
+    return pl.pallas_call(
+        expand_kernel,
+        in_specs=[WHOLE] * (GROUPS + 2),
         out_specs=[WHOLE] * GROUPS,
         out_shape=[pltpu.VMEM((2 * GROUP,) + plane, F32)] * GROUPS,
         scratch_shapes=[
-            pltpu.VMEM((count, ROWS) + plane, F32),
-            pltpu.VMEM((count, 2 * GROUP) + plane, F32),
+            pltpu.VMEM((plane[0] * ROWS, plane[1]), F32),
             pltpu.VMEM((GROUPS, 2 * GROUP) + plane, F32),
         ],
         compiler_params=SMALL,
         cost_estimate=pl.CostEstimate(flops=10**6, bytes_accessed=10**6, transcendentals=0),
-        name="chain",
+        name="expand",
     )(*got, part, coef)
 
 
@@ -492,7 +569,6 @@
     adjoint, log_conc, levels, conduct, orders_fwd, orders_rev, stoich, rate_fwd, rate_rev, diffusivity
 ):
     rows_y, blocks = lax.axis_size("gy"), lax.axis_size("gx")
-    supers = blocks // GROUPS
     near = lax.ppermute(adjoint, "gz", [(0, 1), (1, 0)])
     tail, head = edges(adjoint)
     low = lax.ppermute(tail, "gy", [(i, (i + 1) % rows_y) for i in range(rows_y)])
@@ -502,20 +578,22 @@
     )
     part, *send = local_part(diffusivity, adjoint, chem, near, low, high, conduct, coef, ends_m)
 
-    def close(value, turn):
-        if turn == 0:
-            return value
-        pairs = [(i, i // GROUPS * GROUPS + (i + turn) % GROUPS) for i in range(blocks)]
-        return lax.ppermute(value, "gx", pairs)
-
-    def far(value, turn):
-        if turn == 0:
-            return value
-        return lax.ppermute(value, "gx", [(i, (i + turn * GROUPS) % blocks) for i in range(blocks)])
-
-    message, inner, links = reduce_blocks([close(value, turn) for turn, value in enumerate(send)])
-    send = chain([far(message, turn) for turn in range(supers)], inner, links)
-    return back(part, coef, [close(value, turn) for turn, value in enumerate(send)])
+    def turned(values, inner):
+        span = inner * GROUPS
+
+        def shift(i, turn):
+            return i // span * span + (i % span + turn * inner) % span
+
+        return [
+            value if turn == 0 else lax.ppermute(value, "gx", [(i, shift(i, turn)) for i in range(blocks)])
+            for turn, value in enumerate(values)
+        ]
+
+    *send, close_part, close_coef = reduce_blocks(turned(send, 1))
+    message, far_part, far_coef = merge(turned(send, GROUPS))
+    other = lax.ppermute(message, "gx", [(i, (i + blocks // 2) % blocks) for i in range(blocks)])
+    send = expand(turned(chain(message, other, far_part, far_coef), GROUPS), close_part, close_coef)
+    return back(part, coef, turned(send, 1))
 
 
 def solution(mesh):

time: 60.9 us -> 61.2 us (level)
  waiting for transfers between devices: 13.4 us -> 15.9 us
  starting transfers between devices: 29.5 us -> 27.2 us
    ppermute x13, waiting for transfers between devices: 13.4 us -> 15.9 us  [the longest x12 12.8 us: turned(): lax.ppermute(value, 'gx', [(i, shift(i, turn)) for i in range(blocks)])]
    ppermute x13, starting transfers between devices: 27 us -> 24.7 us  [the longest x12 20 us: turned(): lax.ppermute(value, 'gx', [(i, shift(i, turn)) for i in range(blocks)])]
  transfers between devices with their start and end apart: 16 -> 16, of which waited for: 9 -> 12; matrix products, arithmetic and copies ran while one was open for 0% -> 0% of each run, Pallas kernels for 19% -> 19%
where the time goes in v6:
time: 61.2 us; the launch traced here: 60.7 us
  starting transfers between devices  27.2 us (44%)
  Pallas kernels  16 us (26%)
  waiting for transfers between devices  15.9 us (26%)
  local copies, waits for them, and re-layouts  1.4 us (2%)
    ppermute x12, starting transfers between devices, turned(): lax.ppermute(value, 'gx', [(i, shift(i, turn)) for i in range(blocks)])  20 us
    ppermute x12, waiting for transfers between devices, turned(): lax.ppermute(value, 'gx', [(i, shift(i, turn)) for i in range(blocks)])  12.8 us
    pallas_call x1, Pallas kernels, chemistry(): pl.pallas_call(chem_kernel, grid=(nx // XB,), in_specs=[pl.BlockSpec((car...  11.3 us
    ppermute x1, starting transfers between devices, shards(): lax.ppermute(message, 'gx', [(i, (i + blocks // 2) % blocks) for i in ran...  4.67 us
    ppermute x1, waiting for transfers between devices, shards(): lax.ppermute(message, 'gx', [(i, (i + blocks // 2) % blocks) for i in ran...  3.06 us
    pallas_call x1, Pallas kernels, local_part(): pl.pallas_call(local_kernel, in_specs=[smem] + [WHOLE] * 8, out_specs=[WH...  2.67 us
    ppermute x1, starting transfers between devices, shards(): lax.ppermute(tail, 'gy', [(i, (i + 1) % rows_y) for i in range(rows_y)])  1.57 us
    unnamed x20, local copies, waits for them, and re-layouts  1.4 us
  transfers between devices with their start and end apart: 16, of which 12 were waited for; matrix products, arithmetic and copies ran while one was open for 0% of the time, Pallas kernels for 19%

profile of v6, /device:TPU:2, one launch (start us, length us, event | category | flops | bytes accessed | tf_op | source)
XLA Modules:
  0.0 60.7 jit_solution(18244072469729318294)
XLA Ops:
  0.0 1.4 %copy-done = f32[22,16,8,128]{3,2,1,0:T(8,128)S(1)} copy-done((f32[22,16,8,128]{3,2,1,0:T(8,128)S(1)}, f32[22,16,8,128]{3,2,1,0:T(8,128)}, u32[]{:S(2)}) %copy-start) | copy-done | bytes 1441816
  1.4 0.4 edges.1
  1.8 1.6 %collective-permute-start.1 = (f32[22,16,2,128]{3,2,1,0:T(2,128)S(1)}, f32[22,16,2,128]{3,2,1,0:T(2,128)S(1)}, u32[]{:S(2)}, u32[]{:S(2)}) collective-permute-start(f32[22,16,2,128]{3,2,1,0:T(2,128)S(1)} %get-tuple-element.34), channel_id=1, source_target_pairs={{0,2},{2,4},{4,6},{6,0},{1,3},{3,5},{5,7},{7,1},{8,10},{10,12},{12... | collective-permute-start | bytes 1081352 | tf_op jit(solution)/shard_map/ppermute | solution.py:574
  3.4 0.9 %collective-permute-start.2 = (f32[22,16,2,128]{3,2,1,0:T(2,128)S(1)}, f32[22,16,2,128]{3,2,1,0:T(2,128)S(1)}, u32[]{:S(2)}, u32[]{:S(2)}) collective-permute-start(f32[22,16,2,128]{3,2,1,0:T(2,128)S(1)} %get-tuple-element.35), channel_id=1, source_target_pairs={{2,0},{4,2},{6,4},{0,6},{3,1},{5,3},{7,5},{1,7},{10,8},{12,10},{14... | collective-permute-start | bytes 1081352 | tf_op jit(solution)/shard_map/ppermute | solution.py:575
  4.3 11.3 %chem.1 = (f32[22,16,8,128]{3,2,1,0:T(8,128)S(1)}, f32[3,17,8,128]{3,2,1,0:T(8,128)S(1)}, f32[17,3,8,128]{3,2,1,0:T(8,128)S(1)}) custom-call(f32[22,16,8,128]{3,2,1,0:T(8,128)S(1)} %copy-done, bf16[32,16,8,128]{3,2,1,0:T(8,128)(2,1)S(1)} %copy-done.3, s32[16,8,128]{2,1,0:T(8,128)S(1)} %copy-done.4, f32[16,8,128]{2,1,0:T(8,128)S(1)} %copy-done.1, ...), custom_call_target="tpu_custom_call" | custom-call | flops 12000000000 | bytes 4000000 | tf_op jit(solution)/shard_map/chem/pallas_call | solution.py:153
  15.7 2.7 %local.1 = (f32[22,16,8,128]{3,2,1,0:T(8,128)S(1)}, f32[16,8,128]{2,1,0:T(8,128)S(1)}, f32[16,8,128]{2,1,0:T(8,128)S(1)}, f32[16,8,128]{2,1,0:T(8,128)S(1)}, f32[16,8,128]{2,1,0:T(8,128)S(1)}) custom-call(f32[22]{0:T(128)S(1)} %copy-done.2, f32[16,8,128]{2,1,0:T(8,128)S(1)} %copy-done.1, f32[22,16,8,128]{3,2,1,0:T(8,128)S(1)} %copy-done, ...), custom_call_target="tpu_custom_call" | custom-call | flops 20000000 | bytes 7000000 | tf_op jit(solution)/shard_map/local/pallas_call | solution.py:300
  18.4 1.3 %collective-permute-start.3 = (f32[16,8,128]{2,1,0:T(8,128)S(1)}, f32[16,8,128]{2,1,0:T(8,128)S(1)}, u32[]{:S(2)}, u32[]{:S(2)}) collective-permute-start(f32[16,8,128]{2,1,0:T(8,128)S(1)} %get-tuple-element.39), channel_id=1, source_target_pairs={{0,8},{8,16},{16,24},{24,0},{32,40},{40,48},{48,56},{56,32},{64,72... | collective-permute-start | bytes 196616 | tf_op jit(solution)/shard_map/ppermute | solution.py:588
  19.7 2.9 %collective-permute-start.4 = (f32[16,8,128]{2,1,0:T(8,128)S(1)}, f32[16,8,128]{2,1,0:T(8,128)S(1)}, u32[]{:S(2)}, u32[]{:S(2)}) collective-permute-start(f32[16,8,128]{2,1,0:T(8,128)S(1)} %get-tuple-element.40), channel_id=1, source_target_pairs={{0,16},{8,24},{16,0},{24,8},{32,48},{40,56},{48,32},{56,40},{64,80... | collective-permute-start | bytes 196616 | tf_op jit(solution)/shard_map/ppermute | solution.py:588
  22.6 1.3 %collective-permute-start.5 = (f32[16,8,128]{2,1,0:T(8,128)S(1)}, f32[16,8,128]{2,1,0:T(8,128)S(1)}, u32[]{:S(2)}, u32[]{:S(2)}) collective-permute-start(f32[16,8,128]{2,1,0:T(8,128)S(1)} %get-tuple-element.41), channel_id=1, source_target_pairs={{0,24},{8,0},{16,8},{24,16},{32,56},{40,32},{48,40},{56,48},{64,88... | collective-permute-start | bytes 196616 | tf_op jit(solution)/shard_map/ppermute | solution.py:588
  23.9 0.4 collective-permute-done.3.refs_1_
  24.4 1.6 %collective-permute-done.4.refs_2_ = f32[16,8,128]{2,1,0:T(8,128)S(1)} collective-permute-done((f32[16,8,128]{2,1,0:T(8,128)S(1)}, f32[16,8,128]{2,1,0:T(8,128)S(1)}, u32[]{:S(2)}, u32[]{:S(2)}) %collective-permute-start.4) | collective-permute-done | bytes 65568 | tf_op jit(solution)/shard_map/ppermute | solution.py:588
  25.9 0.9 %collective-permute-done.5.refs_3_ = f32[16,8,128]{2,1,0:T(8,128)S(1)} collective-permute-done((f32[16,8,128]{2,1,0:T(8,128)S(1)}, f32[16,8,128]{2,1,0:T(8,128)S(1)}, u32[]{:S(2)}, u32[]{:S(2)}) %collective-permute-start.5) | collective-permute-done | bytes 65568 | tf_op jit(solution)/shard_map/ppermute | solution.py:588
  27.0 2.0 %collective-permute-start.6 = (f32[32,128]{1,0:T(8,128)S(1)}, f32[32,128]{1,0:T(8,128)S(1)}, u32[]{:S(2)}, u32[]{:S(2)}) collective-permute-start(f32[32,128]{1,0:T(8,128)S(1)} %get-tuple-element.43), channel_id=1, source_target_pairs={{0,32},{8,40},{16,48},{24,56},{32,64},{40,72},{48,80},{56,88},{64,... | collective-permute-start | bytes 49160 | tf_op jit(solution)/shard_map/ppermute | solution.py:588
  29.0 3.3 %collective-permute-start.7 = (f32[32,128]{1,0:T(8,128)S(1)}, f32[32,128]{1,0:T(8,128)S(1)}, u32[]{:S(2)}, u32[]{:S(2)}) collective-permute-start(f32[32,128]{1,0:T(8,128)S(1)} %get-tuple-element.44), channel_id=1, source_target_pairs={{0,64},{8,72},{16,80},{24,88},{32,96},{40,104},{48,112},{56,120},{... | collective-permute-start | bytes 49160 | tf_op jit(solution)/shard_map/ppermute | solution.py:588
  32.3 1.0 %collective-permute-start.8 = (f32[32,128]{1,0:T(8,128)S(1)}, f32[32,128]{1,0:T(8,128)S(1)}, u32[]{:S(2)}, u32[]{:S(2)}) collective-permute-start(f32[32,128]{1,0:T(8,128)S(1)} %get-tuple-element.45), channel_id=1, source_target_pairs={{0,96},{8,104},{16,112},{24,120},{32,0},{40,8},{48,16},{56,24},{64... | collective-permute-start | bytes 49160 | tf_op jit(solution)/shard_map/ppermute | solution.py:588
  33.3 0.1 collective-permute-done.6.refs_1_
  33.4 0.6 collective-permute-done.7.refs_2_
  34.0 2.0 %collective-permute-done.8.refs_3_ = f32[32,128]{1,0:T(8,128)S(1)} collective-permute-done((f32[32,128]{1,0:T(8,128)S(1)}, f32[32,128]{1,0:T(8,128)S(1)}, u32[]{:S(2)}, u32[]{:S(2)}) %collective-permute-start.8) | collective-permute-done | bytes 16416 | tf_op jit(solution)/shard_map/ppermute | solution.py:588
  36.1 4.7 %collective-permute-start.9 = (f32[32,128]{1,0:T(8,128)S(1)}, f32[32,128]{1,0:T(8,128)S(1)}, u32[]{:S(2)}, u32[]{:S(2)}) collective-permute-start(f32[32,128]{1,0:T(8,128)S(1)} %get-tuple-element.46.own_ref), channel_id=1, source_target_pairs={{0,128},{8,136},{16,144},{24,152},{32,160},{40,168},{48,176},{56,1... | collective-permute-start | bytes 49160 | tf_op jit(solution)/shard_map/ppermute | solution.py:594
  40.7 3.1 %collective-permute-done.9.other_ref = f32[32,128]{1,0:T(8,128)S(1)} collective-permute-done((f32[32,128]{1,0:T(8,128)S(1)}, f32[32,128]{1,0:T(8,128)S(1)}, u32[]{:S(2)}, u32[]{:S(2)}) %collective-permute-start.9) | collective-permute-done | bytes 16416 | tf_op jit(solution)/shard_map/ppermute | solution.py:594
  43.9 0.5 collective-permute-start.10
  44.4 2.9 %collective-permute-start.11 = (f32[32,128]{1,0:T(8,128)S(1)}, f32[32,128]{1,0:T(8,128)S(1)}, u32[]{:S(2)}, u32[]{:S(2)}) collective-permute-start(f32[32,128]{1,0:T(8,128)S(1)} %get-tuple-element.51), channel_id=1, source_target_pairs={{0,64},{8,72},{16,80},{24,88},{32,96},{40,104},{48,112},{56,120},{... | collective-permute-start | bytes 49160 | tf_op jit(solution)/shard_map/ppermute | solution.py:588
  47.3 0.5 collective-permute-start.12
  47.8 1.7 %collective-permute-done.10.refs_1_ = f32[32,128]{1,0:T(8,128)S(1)} collective-permute-done((f32[32,128]{1,0:T(8,128)S(1)}, f32[32,128]{1,0:T(8,128)S(1)}, u32[]{:S(2)}, u32[]{:S(2)}) %collective-permute-start.10) | collective-permute-done | bytes 16416 | tf_op jit(solution)/shard_map/ppermute | solution.py:588
  49.5 1.6 %collective-permute-done.12.refs_3_ = f32[32,128]{1,0:T(8,128)S(1)} collective-permute-done((f32[32,128]{1,0:T(8,128)S(1)}, f32[32,128]{1,0:T(8,128)S(1)}, u32[]{:S(2)}, u32[]{:S(2)}) %collective-permute-start.12) | collective-permute-done | bytes 16416 | tf_op jit(solution)/shard_map/ppermute | solution.py:588
  51.1 0.4 collective-permute-start.13
  51.5 3.7 %collective-permute-start.14 = (f32[12,8,128]{2,1,0:T(8,128)S(1)}, f32[12,8,128]{2,1,0:T(8,128)S(1)}, u32[]{:S(2)}, u32[]{:S(2)}) collective-permute-start(f32[12,8,128]{2,1,0:T(8,128)S(1)} %get-tuple-element.57), channel_id=1, source_target_pairs={{0,16},{8,24},{16,0},{24,8},{32,48},{40,56},{48,32},{56,40},{64,80... | collective-permute-start | bytes 147464 | tf_op jit(solution)/shard_map/ppermute | solution.py:588
  55.2 0.2 collective-permute-start.15
  55.4 1.1 %collective-permute-done.13.refs_1_ = f32[12,8,128]{2,1,0:T(8,128)S(1)} collective-permute-done((f32[12,8,128]{2,1,0:T(8,128)S(1)}, f32[12,8,128]{2,1,0:T(8,128)S(1)}, u32[]{:S(2)}, u32[]{:S(2)}) %collective-permute-start.13) | collective-permute-done | bytes 49184 | tf_op jit(solution)/shard_map/ppermute | solution.py:588
  56.5 1.3 %collective-permute-done.14.refs_2_ = f32[12,8,128]{2,1,0:T(8,128)S(1)} collective-permute-done((f32[12,8,128]{2,1,0:T(8,128)S(1)}, f32[12,8,128]{2,1,0:T(8,128)S(1)}, u32[]{:S(2)}, u32[]{:S(2)}) %collective-permute-start.14) | collective-permute-done | bytes 49184 | tf_op jit(solution)/shard_map/ppermute | solution.py:588
  57.8 1.5 %collective-permute-done.15.refs_3_ = f32[12,8,128]{2,1,0:T(8,128)S(1)} collective-permute-done((f32[12,8,128]{2,1,0:T(8,128)S(1)}, f32[12,8,128]{2,1,0:T(8,128)S(1)}, u32[]{:S(2)}, u32[]{:S(2)}) %collective-permute-start.15) | collective-permute-done | bytes 49184 | tf_op jit(solution)/shard_map/ppermute | solution.py:588
  59.3 1.3 %back.1 = f32[22,16,8,128]{3,2,1,0:T(8,128)} custom-call(f32[3,17,8,128]{3,2,1,0:T(8,128)S(1)} %get-tuple-element.32.coef_ref, f32[22,16,8,128]{3,2,1,0:T(8,128)S(1)} %get-tuple-element.37.part_ref, f32[12,8,128]{2,1,0:T(8,128)S(1)} %get-tuple-element.55.refs_0_, f32[12,8,128]{2,1,0:T(8,128)S(1)} %collective-permute-done.13.refs_1_, ...), custom_call_target="tpu_custom_call" | custom-call | flops 2000000 | bytes 3000000 | tf_op jit(solution)/shard_map/back/pallas_call | solution.py:552
  (28 shorter events, 0.4 us)
Async XLA Ops:
  0.0 15.7 %collective-permute-start = (f32[22,16,8,128]{3,2,1,0:T(8,128)}, f32[22,16,8,128]{3,2,1,0:T(8,128)S(1)}, u32[]{:S(2)}, u32[]{:S(2)}) collective-permute-start(f32[22,16,8,128]{3,2,1,0:T(8,128)} %adj_ref.5), channel_id=1, source_target_pairs={{0,1},{1,0},{2,3},{3,2},{4,5},{5,4},{6,7},{7,6},{8,9},{9,8},{10,11... | collective-permute-start | bytes 4325384 | tf_op jit(solution)/shard_map/ppermute | solution.py:572
  0.0 1.4 %copy-start = (f32[22,16,8,128]{3,2,1,0:T(8,128)S(1)}, f32[22,16,8,128]{3,2,1,0:T(8,128)}, u32[]{:S(2)}) copy-start(f32[22,16,8,128]{3,2,1,0:T(8,128)} %adj_ref.5) | copy-start | bytes 4325380
  1.4 2.9 %copy-start.1 = (f32[16,8,128]{2,1,0:T(8,128)S(1)}, f32[16,8,128]{2,1,0:T(8,128)}, u32[]{:S(2)}) copy-start(f32[16,8,128]{2,1,0:T(8,128)} %cond_ref.3) | copy-start | bytes 196612
  1.4 2.9 %copy-start.3 = (bf16[32,16,8,128]{3,2,1,0:T(8,128)(2,1)S(1)}, bf16[32,16,8,128]{3,2,1,0:T(8,128)(2,1)}, u32[]{:S(2)}) copy-start(bf16[32,16,8,128]{3,2,1,0:T(8,128)(2,1)} %conc_ref.1) | copy-start | bytes 3145732
  1.4 2.9 %copy-start.4 = (s32[16,8,128]{2,1,0:T(8,128)S(1)}, s32[16,8,128]{2,1,0:T(8,128)}, u32[]{:S(2)}) copy-start(s32[16,8,128]{2,1,0:T(8,128)} %lev_ref.1) | copy-start | bytes 196612
  1.4 2.9 %copy-start.5 = (bf16[206,32]{0,1:T(8,128)(2,1)S(1)}, bf16[206,32]{0,1:T(8,128)(2,1)}, u32[]{:S(2)}) copy-start(bf16[206,32]{0,1:T(8,128)(2,1)} %param.14) | copy-start | bytes 39556
  1.4 2.9 %copy-start.6 = (bf16[206,32]{0,1:T(8,128)(2,1)S(1)}, bf16[206,32]{0,1:T(8,128)(2,1)}, u32[]{:S(2)}) copy-start(bf16[206,32]{0,1:T(8,128)(2,1)} %param.15) | copy-start | bytes 39556
  1.4 2.9 %copy-start.7 = (bf16[206,22]{0,1:T(8,128)(2,1)S(1)}, bf16[206,22]{0,1:T(8,128)(2,1)}, u32[]{:S(2)}) copy-start(bf16[206,22]{0,1:T(8,128)(2,1)} %param.16) | copy-start | bytes 27196
  1.4 2.9 %copy-start.8 = (f32[206]{0:T(256)S(1)}, f32[206]{0:T(256)}, u32[]{:S(2)}) copy-start(f32[206]{0:T(256)} %param.17) | copy-start | bytes 2476
  1.4 2.9 %copy-start.9 = (f32[206]{0:T(256)S(1)}, f32[206]{0:T(256)}, u32[]{:S(2)}) copy-start(f32[206]{0:T(256)} %param.18) | copy-start | bytes 2476
  1.8 13.9 %collective-permute-start.1 = (f32[22,16,2,128]{3,2,1,0:T(2,128)S(1)}, f32[22,16,2,128]{3,2,1,0:T(2,128)S(1)}, u32[]{:S(2)}, u32[]{:S(2)}) collective-permute-start(f32[22,16,2,128]{3,2,1,0:T(2,128)S(1)} %get-tuple-element.34), channel_id=1, source_target_pairs={{0,2},{2,4},{4,6},{6,0},{1,3},{3,5},{5,7},{7,1},{8,10},{10,12},{12... | collective-permute-start | bytes 1081352 | tf_op jit(solution)/shard_map/ppermute | solution.py:574
  3.4 12.3 %collective-permute-start.2 = (f32[22,16,2,128]{3,2,1,0:T(2,128)S(1)}, f32[22,16,2,128]{3,2,1,0:T(2,128)S(1)}, u32[]{:S(2)}, u32[]{:S(2)}) collective-permute-start(f32[22,16,2,128]{3,2,1,0:T(2,128)S(1)} %get-tuple-element.35), channel_id=1, source_target_pairs={{2,0},{4,2},{6,4},{0,6},{3,1},{5,3},{7,5},{1,7},{10,8},{12,10},{14... | collective-permute-start | bytes 1081352 | tf_op jit(solution)/shard_map/ppermute | solution.py:575
  4.3 11.4 %copy-start.2 = (f32[22]{0:T(128)S(1)}, f32[22]{0:T(128)}, u32[]{:S(2)}) copy-start(f32[22]{0:T(128)} %diff_ref.1) | copy-start | bytes 268
  18.4 6.0 %collective-permute-start.3 = (f32[16,8,128]{2,1,0:T(8,128)S(1)}, f32[16,8,128]{2,1,0:T(8,128)S(1)}, u32[]{:S(2)}, u32[]{:S(2)}) collective-permute-start(f32[16,8,128]{2,1,0:T(8,128)S(1)} %get-tuple-element.39), channel_id=1, source_target_pairs={{0,8},{8,16},{16,24},{24,0},{32,40},{40,48},{48,56},{56,32},{64,72... | collective-permute-start | bytes 196616 | tf_op jit(solution)/shard_map/ppermute | solution.py:588
  19.7 6.2 %collective-permute-start.4 = (f32[16,8,128]{2,1,0:T(8,128)S(1)}, f32[16,8,128]{2,1,0:T(8,128)S(1)}, u32[]{:S(2)}, u32[]{:S(2)}) collective-permute-start(f32[16,8,128]{2,1,0:T(8,128)S(1)} %get-tuple-element.40), channel_id=1, source_target_pairs={{0,16},{8,24},{16,0},{24,8},{32,48},{40,56},{48,32},{56,40},{64,80... | collective-permute-start | bytes 196616 | tf_op jit(solution)/shard_map/ppermute | solution.py:588
  22.6 4.3 %collective-permute-start.5 = (f32[16,8,128]{2,1,0:T(8,128)S(1)}, f32[16,8,128]{2,1,0:T(8,128)S(1)}, u32[]{:S(2)}, u32[]{:S(2)}) collective-permute-start(f32[16,8,128]{2,1,0:T(8,128)S(1)} %get-tuple-element.41), channel_id=1, source_target_pairs={{0,24},{8,0},{16,8},{24,16},{32,56},{40,32},{48,40},{56,48},{64,88... | collective-permute-start | bytes 196616 | tf_op jit(solution)/shard_map/ppermute | solution.py:588
  27.0 6.4 %collective-permute-start.6 = (f32[32,128]{1,0:T(8,128)S(1)}, f32[32,128]{1,0:T(8,128)S(1)}, u32[]{:S(2)}, u32[]{:S(2)}) collective-permute-start(f32[32,128]{1,0:T(8,128)S(1)} %get-tuple-element.43), channel_id=1, source_target_pairs={{0,32},{8,40},{16,48},{24,56},{32,64},{40,72},{48,80},{56,88},{64,... | collective-permute-start | bytes 49160 | tf_op jit(solution)/shard_map/ppermute | solution.py:588
  29.0 5.0 %collective-permute-start.7 = (f32[32,128]{1,0:T(8,128)S(1)}, f32[32,128]{1,0:T(8,128)S(1)}, u32[]{:S(2)}, u32[]{:S(2)}) collective-permute-start(f32[32,128]{1,0:T(8,128)S(1)} %get-tuple-element.44), channel_id=1, source_target_pairs={{0,64},{8,72},{16,80},{24,88},{32,96},{40,104},{48,112},{56,120},{... | collective-permute-start | bytes 49160 | tf_op jit(solution)/shard_map/ppermute | solution.py:588
  32.3 3.7 %collective-permute-start.8 = (f32[32,128]{1,0:T(8,128)S(1)}, f32[32,128]{1,0:T(8,128)S(1)}, u32[]{:S(2)}, u32[]{:S(2)}) collective-permute-start(f32[32,128]{1,0:T(8,128)S(1)} %get-tuple-element.45), channel_id=1, source_target_pairs={{0,96},{8,104},{16,112},{24,120},{32,0},{40,8},{48,16},{56,24},{64... | collective-permute-start | bytes 49160 | tf_op jit(solution)/shard_map/ppermute | solution.py:588
  36.1 7.7 %collective-permute-start.9 = (f32[32,128]{1,0:T(8,128)S(1)}, f32[32,128]{1,0:T(8,128)S(1)}, u32[]{:S(2)}, u32[]{:S(2)}) collective-permute-start(f32[32,128]{1,0:T(8,128)S(1)} %get-tuple-element.46.own_ref), channel_id=1, source_target_pairs={{0,128},{8,136},{16,144},{24,152},{32,160},{40,168},{48,176},{56,1... | collective-permute-start | bytes 49160 | tf_op jit(solution)/shard_map/ppermute | solution.py:594
  43.9 5.6 %collective-permute-start.10 = (f32[32,128]{1,0:T(8,128)S(1)}, f32[32,128]{1,0:T(8,128)S(1)}, u32[]{:S(2)}, u32[]{:S(2)}) collective-permute-start(f32[32,128]{1,0:T(8,128)S(1)} %get-tuple-element.50), channel_id=1, source_target_pairs={{0,32},{8,40},{16,48},{24,56},{32,64},{40,72},{48,80},{56,88},{64,... | collective-permute-start | bytes 49160 | tf_op jit(solution)/shard_map/ppermute | solution.py:588
  44.4 5.1 %collective-permute-start.11 = (f32[32,128]{1,0:T(8,128)S(1)}, f32[32,128]{1,0:T(8,128)S(1)}, u32[]{:S(2)}, u32[]{:S(2)}) collective-permute-start(f32[32,128]{1,0:T(8,128)S(1)} %get-tuple-element.51), channel_id=1, source_target_pairs={{0,64},{8,72},{16,80},{24,88},{32,96},{40,104},{48,112},{56,120},{... | collective-permute-start | bytes 49160 | tf_op jit(solution)/shard_map/ppermute | solution.py:588
  47.3 3.7 %collective-permute-start.12 = (f32[32,128]{1,0:T(8,128)S(1)}, f32[32,128]{1,0:T(8,128)S(1)}, u32[]{:S(2)}, u32[]{:S(2)}) collective-permute-start(f32[32,128]{1,0:T(8,128)S(1)} %get-tuple-element.52), channel_id=1, source_target_pairs={{0,96},{8,104},{16,112},{24,120},{32,0},{40,8},{48,16},{56,24},{64... | collective-permute-start | bytes 49160 | tf_op jit(solution)/shard_map/ppermute | solution.py:588
  51.1 5.4 %collective-permute-start.13 = (f32[12,8,128]{2,1,0:T(8,128)S(1)}, f32[12,8,128]{2,1,0:T(8,128)S(1)}, u32[]{:S(2)}, u32[]{:S(2)}) collective-permute-start(f32[12,8,128]{2,1,0:T(8,128)S(1)} %get-tuple-element.56), channel_id=1, source_target_pairs={{0,8},{8,16},{16,24},{24,0},{32,40},{40,48},{48,56},{56,32},{64,72... | collective-permute-start | bytes 147464 | tf_op jit(solution)/shard_map/ppermute | solution.py:588
  51.5 6.3 %collective-permute-start.14 = (f32[12,8,128]{2,1,0:T(8,128)S(1)}, f32[12,8,128]{2,1,0:T(8,128)S(1)}, u32[]{:S(2)}, u32[]{:S(2)}) collective-permute-start(f32[12,8,128]{2,1,0:T(8,128)S(1)} %get-tuple-element.57), channel_id=1, source_target_pairs={{0,16},{8,24},{16,0},{24,8},{32,48},{40,56},{48,32},{56,40},{64,80... | collective-permute-start | bytes 147464 | tf_op jit(solution)/shard_map/ppermute | solution.py:588
  55.2 4.1 %collective-permute-start.15 = (f32[12,8,128]{2,1,0:T(8,128)S(1)}, f32[12,8,128]{2,1,0:T(8,128)S(1)}, u32[]{:S(2)}, u32[]{:S(2)}) collective-permute-start(f32[12,8,128]{2,1,0:T(8,128)S(1)} %get-tuple-element.58), channel_id=1, source_target_pairs={{0,24},{8,0},{16,8},{24,16},{32,56},{40,32},{48,40},{56,48},{64,88... | collective-permute-start | bytes 147464 | tf_op jit(solution)/shard_map/ppermute | solution.py:588

commit v7 on v5

--- a/solution.py
+++ b/solution.py
@@ -19,7 +19,7 @@
 R_PAD = 208
 STRIP = 16
 CHUNKS = tuple((start, STRIP) for start in range(0, R_PAD, STRIP))
-TILE = 1024
+TILE = 2048
 XB = 4
 LIMIT = 24 * 1024 * 1024
 F32 = jnp.float32
@@ -115,34 +115,32 @@
     for x in range(xb):
         for y in range(ny):
             row = x * ny + y
-            cols = slice(y * nz, (y + 1) * nz)
+            cols = slice(row * nz, (row + 1) * nz)
             conc = jnp.concatenate(
                 [conc32_ref[pl.ds(row + 8 * q * pitch, 8, stride=pitch), :] for q in range(4)], axis=0
             ).astype(BF16)
-            x_ref[x, 0:32, cols] = conc
-            x_ref[x, 32:64, cols] = conc
+            x_ref[0:32, cols] = conc
+            x_ref[32:64, cols] = conc
             lam = [adj_rows[pl.ds(row + first * pitch, 8, stride=pitch), :] for first in (0, 8, carried - 8)]
             level = jnp.broadcast_to(lev_ref[x, y : y + 1, :], (8, nz))
             marks = jnp.where(level <= sub, 1.0, 0.0)
-            x_ref[x, 64:96, cols] = jnp.concatenate(lam + [marks], axis=0).astype(BF16)
+            x_ref[64:96, cols] = jnp.concatenate(lam + [marks], axis=0).astype(BF16)
     per_tile = TILE // nz
-    for x in range(xb):
-        for tile in range(ny // per_tile):
-            slot = (x * (ny // per_tile) + tile) % act_ref.shape[0]
-            data = x_ref[x, :, tile * TILE : (tile + 1) * TILE]
-            every = dot(w_ref[...], data)
-            for start, size in CHUNKS:
-                got = every[3 * start : 3 * (start + size)]
-                weight = got[2 * size :]
-                act_ref[slot, 0, start : start + size, :] = (jnp.exp2(got[:size]) * weight).astype(BF16)
-                act_ref[slot, 1, start : start + size, :] = (jnp.exp2(got[size : 2 * size]) * weight).astype(BF16)
-            chem = dot(c_ref[0], act_ref[slot, 0]) + dot(c_ref[1], act_ref[slot, 1])
-            for part in range(per_tile):
-                row = x * ny + tile * per_tile + part
-                for q, first in enumerate((0, 8, carried - 8)):
-                    out_rows[pl.ds(row + first * pitch, 8, stride=pitch), :] = chem[
-                        8 * q : 8 * q + 8, part * nz : (part + 1) * nz
-                    ]
+    for tile in range(xb * ny // per_tile):
+        slot = tile % act_ref.shape[0]
+        every = dot(w_ref[...], x_ref[:, tile * TILE : (tile + 1) * TILE])
+        for start, size in CHUNKS:
+            got = every[3 * start : 3 * (start + size)]
+            weight = got[2 * size :]
+            act_ref[slot, 0, start : start + size, :] = (jnp.exp2(got[:size]) * weight).astype(BF16)
+            act_ref[slot, 1, start : start + size, :] = (jnp.exp2(got[size : 2 * size]) * weight).astype(BF16)
+        chem = dot(c_ref[0], act_ref[slot, 0]) + dot(c_ref[1], act_ref[slot, 1])
+        for part in range(per_tile):
+            row = tile * per_tile + part
+            for q, first in enumerate((0, 8, carried - 8)):
+                out_rows[pl.ds(row + first * pitch, 8, stride=pitch), :] = chem[
+                    8 * q : 8 * q + 8, part * nz : (part + 1) * nz
+                ]
 
 
 def chemistry(adjoint, log_conc, levels, conduct, orders_fwd, orders_rev, stoich, rate_fwd, rate_rev):
@@ -175,7 +173,7 @@
             pltpu.VMEM((3 * R_PAD, K_ROWS), BF16),
             pltpu.VMEM((2, 32, R_PAD), BF16),
             pltpu.VMEM((species * XB * ny, nz), F32),
-            pltpu.VMEM((XB, K_ROWS, ny * nz), BF16),
+            pltpu.VMEM((K_ROWS, XB * ny * nz), BF16),
             pltpu.VMEM((2, 2, R_PAD, TILE), BF16),
             pltpu.VMEM((3, ny, nz), F32),
         ],
@@ -358,13 +356,11 @@
 
 
 def chain_kernel(*refs):
-    count = len(refs) - GROUPS - 5
-    got_refs, (part_ref, coef_ref) = refs[:count], refs[count : count + 2]
-    send_refs, (in_ref, ends_ref, out_ref) = refs[count + 2 : count + 2 + GROUPS], refs[count + 2 + GROUPS :]
+    in_ref, part_ref, coef_ref = refs[:3]
+    send_refs, (ends_ref, out_ref) = refs[3 : 3 + GROUPS], refs[3 + GROUPS :]
+    count = in_ref.shape[0]
     device = lax.axis_index("gx")
     mine, home = device % GROUPS, device // GROUPS
-    for turn in range(count):
-        in_ref[(home + count - turn) % count] = got_refs[turn][...]
     h, mass, rhs, ends = [], [], [], []
     passed_m = passed_b = None
     for i in range(count):
@@ -424,21 +420,20 @@
 
 def chain(got, part, coef):
     plane = part.shape[2:]
-    count = len(got)
+    count = got.shape[0]
     return pl.pallas_call(
         chain_kernel,
-        in_specs=[WHOLE] * (count + 2),
+        in_specs=[WHOLE] * 3,
         out_specs=[WHOLE] * GROUPS,
         out_shape=[pltpu.VMEM((2 * GROUP,) + plane, F32)] * GROUPS,
         scratch_shapes=[
-            pltpu.VMEM((count, ROWS) + plane, F32),
             pltpu.VMEM((count, 2 * GROUP) + plane, F32),
             pltpu.VMEM((GROUPS, 2 * GROUP) + plane, F32),
         ],
         compiler_params=SMALL,
         cost_estimate=pl.CostEstimate(flops=10**6, bytes_accessed=10**6, transcendentals=0),
         name="chain",
-    )(*got, part, coef)
+    )(got, part, coef)
 
 
 def back_kernel(coef_ref, part_ref, *refs):
@@ -508,13 +503,10 @@
         pairs = [(i, i // GROUPS * GROUPS + (i + turn) % GROUPS) for i in range(blocks)]
         return lax.ppermute(value, "gx", pairs)
 
-    def far(value, turn):
-        if turn == 0:
-            return value
-        return lax.ppermute(value, "gx", [(i, (i + turn * GROUPS) % blocks) for i in range(blocks)])
-
     message, inner, links = reduce_blocks([close(value, turn) for turn, value in enumerate(send)])
-    send = chain([far(message, turn) for turn in range(supers)], inner, links)
+    columns = [[GROUPS * z + y for z in range(supers)] for y in range(GROUPS)]
+    supers_all = lax.all_gather(message, "gx", axis_index_groups=columns)
+    send = chain(supers_all, inner, links)
     return back(part, coef, [close(value, turn) for turn, value in enumerate(send)])
 
 

time: 60.9 us -> 64.9 us (1.066)
  blocking collectives: 0 us -> 28.9 us
  starting transfers between devices: 29.5 us -> 12.3 us
  waiting for transfers between devices: 13.4 us -> 7.01 us
  Pallas kernels: 16 us -> 14.9 us
    all_gather x0 -> x1, blocking collectives: none -> 28.9 us  [shards(): supers_all = lax.all_gather(message, 'gx', axis_index_groups=columns)]
    ppermute x7 -> x0, starting transfers between devices: 17.3 us -> none  [far(): lax.ppermute(value, 'gx', [(i, (i + turn * GROUPS) % blocks) for i in ran...]
    ppermute x7 -> x0, waiting for transfers between devices: 7.02 us -> none  [far(): lax.ppermute(value, 'gx', [(i, (i + turn * GROUPS) % blocks) for i in ran...]
    pallas_call x1, Pallas kernels: 11.3 us -> 10.4 us  [chemistry(): pl.pallas_call(chem_kernel, grid=(nx // XB,), in_specs=[pl.BlockSpec((car...]
  transfers between devices with their start and end apart: 16 -> 9, of which waited for: 9 -> 6; matrix products, arithmetic and copies ran while one was open for 0% -> 0% of each run, Pallas kernels for 19% -> 17%
where the time goes in v7:
time: 64.9 us; the launch traced here: 64.8 us
  blocking collectives  28.9 us (45%)
  Pallas kernels  14.9 us (23%)
  starting transfers between devices  12.3 us (19%)
  waiting for transfers between devices  7.01 us (11%)
  local copies, waits for them, and re-layouts  1.4 us (2%)
    all_gather x1, blocking collectives, shards(): supers_all = lax.all_gather(message, 'gx', axis_index_groups=columns)  28.9 us
    pallas_call x1, Pallas kernels, chemistry(): pl.pallas_call(chem_kernel, grid=(nx // XB,), in_specs=[pl.BlockSpec((car...  10.4 us
    ppermute x6, starting transfers between devices, close(): return lax.ppermute(value, 'gx', pairs)  9.89 us
    ppermute x6, waiting for transfers between devices, close(): return lax.ppermute(value, 'gx', pairs)  7 us
    pallas_call x1, Pallas kernels, local_part(): pl.pallas_call(local_kernel, in_specs=[smem] + [WHOLE] * 8, out_specs=[WH...  2.68 us
    ppermute x1, starting transfers between devices, shards(): lax.ppermute(tail, 'gy', [(i, (i + 1) % rows_y) for i in range(rows_y)])  1.57 us
    unnamed x20, local copies, waits for them, and re-layouts  1.4 us
  transfers between devices with their start and end apart: 9, of which 6 were waited for; matrix products, arithmetic and copies ran while one was open for 0% of the time, Pallas kernels for 17%

profile of v7, /device:TPU:2, one launch (start us, length us, event | category | flops | bytes accessed | tf_op | source)
XLA Modules:
  0.0 64.8 jit_solution(582830748733700260)
XLA Ops:
  0.0 0.0 collective-permute-start
  0.0 1.4 %copy-done = f32[22,16,8,128]{3,2,1,0:T(8,128)S(1)} copy-done((f32[22,16,8,128]{3,2,1,0:T(8,128)S(1)}, f32[22,16,8,128]{3,2,1,0:T(8,128)}, u32[]{:S(2)}) %copy-start) | copy-done | bytes 1441816
  1.4 0.0 copy-start.6
  1.4 0.0 copy-start.7
  1.4 0.0 copy-start.8
  1.4 0.4 edges.1
  1.8 1.6 %collective-permute-start.1 = (f32[22,16,2,128]{3,2,1,0:T(2,128)S(1)}, f32[22,16,2,128]{3,2,1,0:T(2,128)S(1)}, u32[]{:S(2)}, u32[]{:S(2)}) collective-permute-start(f32[22,16,2,128]{3,2,1,0:T(2,128)S(1)} %get-tuple-element.24), channel_id=1, source_target_pairs={{0,2},{2,4},{4,6},{6,0},{1,3},{3,5},{5,7},{7,1},{8,10},{10,12},{12... | collective-permute-start | bytes 1081352 | tf_op jit(solution)/shard_map/ppermute | solution.py:493
  3.4 0.9 %collective-permute-start.2 = (f32[22,16,2,128]{3,2,1,0:T(2,128)S(1)}, f32[22,16,2,128]{3,2,1,0:T(2,128)S(1)}, u32[]{:S(2)}, u32[]{:S(2)}) collective-permute-start(f32[22,16,2,128]{3,2,1,0:T(2,128)S(1)} %get-tuple-element.25), channel_id=1, source_target_pairs={{2,0},{4,2},{6,4},{0,6},{3,1},{5,3},{7,5},{1,7},{10,8},{12,10},{14... | collective-permute-start | bytes 1081352 | tf_op jit(solution)/shard_map/ppermute | solution.py:494
  4.2 0.0 copy-done.4
  4.3 0.0 copy-start.2
  4.3 10.4 %chem.1 = (f32[22,16,8,128]{3,2,1,0:T(8,128)S(1)}, f32[3,17,8,128]{3,2,1,0:T(8,128)S(1)}, f32[17,3,8,128]{3,2,1,0:T(8,128)S(1)}) custom-call(f32[22,16,8,128]{3,2,1,0:T(8,128)S(1)} %copy-done, bf16[32,16,8,128]{3,2,1,0:T(8,128)(2,1)S(1)} %copy-done.3, s32[16,8,128]{2,1,0:T(8,128)S(1)} %copy-done.4, f32[16,8,128]{2,1,0:T(8,128)S(1)} %copy-done.1, ...), custom_call_target="tpu_custom_call" | custom-call | flops 12000000000 | bytes 4000000 | tf_op jit(solution)/shard_map/chem/pallas_call | solution.py:151
  14.7 0.0 collective-permute-done.1.low_ref
  14.7 0.0 collective-permute-done.2.high_ref
  14.7 0.0 collective-permute-done.near_ref
  14.7 0.0 copy-done.2
  14.7 2.7 %local.1 = (f32[22,16,8,128]{3,2,1,0:T(8,128)S(1)}, f32[16,8,128]{2,1,0:T(8,128)S(1)}, f32[16,8,128]{2,1,0:T(8,128)S(1)}, f32[16,8,128]{2,1,0:T(8,128)S(1)}, f32[16,8,128]{2,1,0:T(8,128)S(1)}) custom-call(f32[22]{0:T(128)S(1)} %copy-done.2, f32[16,8,128]{2,1,0:T(8,128)S(1)} %copy-done.1, f32[22,16,8,128]{3,2,1,0:T(8,128)S(1)} %copy-done, ...), custom_call_target="tpu_custom_call" | custom-call | flops 20000000 | bytes 7000000 | tf_op jit(solution)/shard_map/local/pallas_call | solution.py:297
  17.4 1.3 %collective-permute-start.3 = (f32[16,8,128]{2,1,0:T(8,128)S(1)}, f32[16,8,128]{2,1,0:T(8,128)S(1)}, u32[]{:S(2)}, u32[]{:S(2)}) collective-permute-start(f32[16,8,128]{2,1,0:T(8,128)S(1)} %get-tuple-element.29), channel_id=1, source_target_pairs={{0,8},{8,16},{16,24},{24,0},{32,40},{40,48},{48,56},{56,32},{64,72... | collective-permute-start | bytes 196616 | tf_op jit(solution)/shard_map/ppermute | solution.py:504
  18.7 2.9 %collective-permute-start.4 = (f32[16,8,128]{2,1,0:T(8,128)S(1)}, f32[16,8,128]{2,1,0:T(8,128)S(1)}, u32[]{:S(2)}, u32[]{:S(2)}) collective-permute-start(f32[16,8,128]{2,1,0:T(8,128)S(1)} %get-tuple-element.30), channel_id=1, source_target_pairs={{0,16},{8,24},{16,0},{24,8},{32,48},{40,56},{48,32},{56,40},{64,80... | collective-permute-start | bytes 196616 | tf_op jit(solution)/shard_map/ppermute | solution.py:504
  21.6 1.3 %collective-permute-start.5 = (f32[16,8,128]{2,1,0:T(8,128)S(1)}, f32[16,8,128]{2,1,0:T(8,128)S(1)}, u32[]{:S(2)}, u32[]{:S(2)}) collective-permute-start(f32[16,8,128]{2,1,0:T(8,128)S(1)} %get-tuple-element.31), channel_id=1, source_target_pairs={{0,24},{8,0},{16,8},{24,16},{32,56},{40,32},{48,40},{56,48},{64,88... | collective-permute-start | bytes 196616 | tf_op jit(solution)/shard_map/ppermute | solution.py:504
  23.0 0.4 collective-permute-done.3.refs_1_
  23.4 1.6 %collective-permute-done.4.refs_2_ = f32[16,8,128]{2,1,0:T(8,128)S(1)} collective-permute-done((f32[16,8,128]{2,1,0:T(8,128)S(1)}, f32[16,8,128]{2,1,0:T(8,128)S(1)}, u32[]{:S(2)}, u32[]{:S(2)}) %collective-permute-start.4) | collective-permute-done | bytes 65568 | tf_op jit(solution)/shard_map/ppermute | solution.py:504
  24.9 0.9 %collective-permute-done.5.refs_3_ = f32[16,8,128]{2,1,0:T(8,128)S(1)} collective-permute-done((f32[16,8,128]{2,1,0:T(8,128)S(1)}, f32[16,8,128]{2,1,0:T(8,128)S(1)}, u32[]{:S(2)}, u32[]{:S(2)}) %collective-permute-start.5) | collective-permute-done | bytes 65568 | tf_op jit(solution)/shard_map/ppermute | solution.py:504
  25.9 0.1 reduce.1
  26.0 28.9 %all-gather = f32[128,8,128]{2,1,0:T(8,128)S(1)} all-gather(f32[16,8,128]{2,1,0:T(8,128)S(1)} %get-tuple-element.32), channel_id=2, replica_groups={{0,32,64,96,128,160,192,224},{8,40,72,104,136,168,200,232},{16,48,80,11..., dimensions={0}, use_global_device_ids=true | all-gather | bytes 589824 | tf_op jit(solution)/shard_map/all_gather | solution.py:508
  54.9 0.2 chain.1
  55.1 0.4 collective-permute-start.6
  55.5 3.9 %collective-permute-start.7 = (f32[12,8,128]{2,1,0:T(8,128)S(1)}, f32[12,8,128]{2,1,0:T(8,128)S(1)}, u32[]{:S(2)}, u32[]{:S(2)}) collective-permute-start(f32[12,8,128]{2,1,0:T(8,128)S(1)} %get-tuple-element.37), channel_id=1, source_target_pairs={{0,16},{8,24},{16,0},{24,8},{32,48},{40,56},{48,32},{56,40},{64,80... | collective-permute-start | bytes 147464 | tf_op jit(solution)/shard_map/ppermute | solution.py:504
  59.4 0.0 collective-permute-start.8
  59.4 1.1 %collective-permute-done.6.refs_1_ = f32[12,8,128]{2,1,0:T(8,128)S(1)} collective-permute-done((f32[12,8,128]{2,1,0:T(8,128)S(1)}, f32[12,8,128]{2,1,0:T(8,128)S(1)}, u32[]{:S(2)}, u32[]{:S(2)}) %collective-permute-start.6) | collective-permute-done | bytes 49184 | tf_op jit(solution)/shard_map/ppermute | solution.py:504
  60.5 1.5 %collective-permute-done.7.refs_2_ = f32[12,8,128]{2,1,0:T(8,128)S(1)} collective-permute-done((f32[12,8,128]{2,1,0:T(8,128)S(1)}, f32[12,8,128]{2,1,0:T(8,128)S(1)}, u32[]{:S(2)}, u32[]{:S(2)}) %collective-permute-start.7) | collective-permute-done | bytes 49184 | tf_op jit(solution)/shard_map/ppermute | solution.py:504
  62.0 1.5 %collective-permute-done.8.refs_3_ = f32[12,8,128]{2,1,0:T(8,128)S(1)} collective-permute-done((f32[12,8,128]{2,1,0:T(8,128)S(1)}, f32[12,8,128]{2,1,0:T(8,128)S(1)}, u32[]{:S(2)}, u32[]{:S(2)}) %collective-permute-start.8) | collective-permute-done | bytes 49184 | tf_op jit(solution)/shard_map/ppermute | solution.py:504
  63.5 1.3 %back.1 = f32[22,16,8,128]{3,2,1,0:T(8,128)} custom-call(f32[3,17,8,128]{3,2,1,0:T(8,128)S(1)} %get-tuple-element.22.coef_ref, f32[22,16,8,128]{3,2,1,0:T(8,128)S(1)} %get-tuple-element.27.part_ref, f32[12,8,128]{2,1,0:T(8,128)S(1)} %get-tuple-element.35.refs_0_, f32[12,8,128]{2,1,0:T(8,128)S(1)} %collective-permute-done.6.refs_1_, ...), custom_call_target="tpu_custom_call" | custom-call | flops 2000000 | bytes 3000000 | tf_op jit(solution)/shard_map/back/pallas_call | solution.py:470
  (13 shorter events, 0.0 us)
Async XLA Ops:
  0.0 14.7 %collective-permute-start = (f32[22,16,8,128]{3,2,1,0:T(8,128)}, f32[22,16,8,128]{3,2,1,0:T(8,128)S(1)}, u32[]{:S(2)}, u32[]{:S(2)}) collective-permute-start(f32[22,16,8,128]{3,2,1,0:T(8,128)} %adj_ref.5), channel_id=1, source_target_pairs={{0,1},{1,0},{2,3},{3,2},{4,5},{5,4},{6,7},{7,6},{8,9},{9,8},{10,11... | collective-permute-start | bytes 4325384 | tf_op jit(solution)/shard_map/ppermute | solution.py:491
  0.0 1.4 %copy-start = (f32[22,16,8,128]{3,2,1,0:T(8,128)S(1)}, f32[22,16,8,128]{3,2,1,0:T(8,128)}, u32[]{:S(2)}) copy-start(f32[22,16,8,128]{3,2,1,0:T(8,128)} %adj_ref.5) | copy-start | bytes 4325380
  1.4 2.9 %copy-start.1 = (f32[16,8,128]{2,1,0:T(8,128)S(1)}, f32[16,8,128]{2,1,0:T(8,128)}, u32[]{:S(2)}) copy-start(f32[16,8,128]{2,1,0:T(8,128)} %cond_ref.3) | copy-start | bytes 196612
  1.4 2.9 %copy-start.3 = (bf16[32,16,8,128]{3,2,1,0:T(8,128)(2,1)S(1)}, bf16[32,16,8,128]{3,2,1,0:T(8,128)(2,1)}, u32[]{:S(2)}) copy-start(bf16[32,16,8,128]{3,2,1,0:T(8,128)(2,1)} %conc_ref.1) | copy-start | bytes 3145732
  1.4 2.9 %copy-start.4 = (s32[16,8,128]{2,1,0:T(8,128)S(1)}, s32[16,8,128]{2,1,0:T(8,128)}, u32[]{:S(2)}) copy-start(s32[16,8,128]{2,1,0:T(8,128)} %lev_ref.1) | copy-start | bytes 196612
  1.4 2.9 %copy-start.5 = (bf16[206,32]{0,1:T(8,128)(2,1)S(1)}, bf16[206,32]{0,1:T(8,128)(2,1)}, u32[]{:S(2)}) copy-start(bf16[206,32]{0,1:T(8,128)(2,1)} %param.14) | copy-start | bytes 39556
  1.4 2.9 %copy-start.6 = (bf16[206,32]{0,1:T(8,128)(2,1)S(1)}, bf16[206,32]{0,1:T(8,128)(2,1)}, u32[]{:S(2)}) copy-start(bf16[206,32]{0,1:T(8,128)(2,1)} %param.15) | copy-start | bytes 39556
  1.4 2.9 %copy-start.7 = (bf16[206,22]{0,1:T(8,128)(2,1)S(1)}, bf16[206,22]{0,1:T(8,128)(2,1)}, u32[]{:S(2)}) copy-start(bf16[206,22]{0,1:T(8,128)(2,1)} %param.16) | copy-start | bytes 27196
  1.4 2.9 %copy-start.8 = (f32[206]{0:T(256)S(1)}, f32[206]{0:T(256)}, u32[]{:S(2)}) copy-start(f32[206]{0:T(256)} %param.17) | copy-start | bytes 2476
  1.4 2.9 %copy-start.9 = (f32[206]{0:T(256)S(1)}, f32[206]{0:T(256)}, u32[]{:S(2)}) copy-start(f32[206]{0:T(256)} %param.18) | copy-start | bytes 2476
  1.8 12.9 %collective-permute-start.1 = (f32[22,16,2,128]{3,2,1,0:T(2,128)S(1)}, f32[22,16,2,128]{3,2,1,0:T(2,128)S(1)}, u32[]{:S(2)}, u32[]{:S(2)}) collective-permute-start(f32[22,16,2,128]{3,2,1,0:T(2,128)S(1)} %get-tuple-element.24), channel_id=1, source_target_pairs={{0,2},{2,4},{4,6},{6,0},{1,3},{3,5},{5,7},{7,1},{8,10},{10,12},{12... | collective-permute-start | bytes 1081352 | tf_op jit(solution)/shard_map/ppermute | solution.py:493
  3.4 11.3 %collective-permute-start.2 = (f32[22,16,2,128]{3,2,1,0:T(2,128)S(1)}, f32[22,16,2,128]{3,2,1,0:T(2,128)S(1)}, u32[]{:S(2)}, u32[]{:S(2)}) collective-permute-start(f32[22,16,2,128]{3,2,1,0:T(2,128)S(1)} %get-tuple-element.25), channel_id=1, source_target_pairs={{2,0},{4,2},{6,4},{0,6},{3,1},{5,3},{7,5},{1,7},{10,8},{12,10},{14... | collective-permute-start | bytes 1081352 | tf_op jit(solution)/shard_map/ppermute | solution.py:494
  4.3 10.4 %copy-start.2 = (f32[22]{0:T(128)S(1)}, f32[22]{0:T(128)}, u32[]{:S(2)}) copy-start(f32[22]{0:T(128)} %diff_ref.1) | copy-start | bytes 268
  17.4 6.0 %collective-permute-start.3 = (f32[16,8,128]{2,1,0:T(8,128)S(1)}, f32[16,8,128]{2,1,0:T(8,128)S(1)}, u32[]{:S(2)}, u32[]{:S(2)}) collective-permute-start(f32[16,8,128]{2,1,0:T(8,128)S(1)} %get-tuple-element.29), channel_id=1, source_target_pairs={{0,8},{8,16},{16,24},{24,0},{32,40},{40,48},{48,56},{56,32},{64,72... | collective-permute-start | bytes 196616 | tf_op jit(solution)/shard_map/ppermute | solution.py:504
  18.7 6.2 %collective-permute-start.4 = (f32[16,8,128]{2,1,0:T(8,128)S(1)}, f32[16,8,128]{2,1,0:T(8,128)S(1)}, u32[]{:S(2)}, u32[]{:S(2)}) collective-permute-start(f32[16,8,128]{2,1,0:T(8,128)S(1)} %get-tuple-element.30), channel_id=1, source_target_pairs={{0,16},{8,24},{16,0},{24,8},{32,48},{40,56},{48,32},{56,40},{64,80... | collective-permute-start | bytes 196616 | tf_op jit(solution)/shard_map/ppermute | solution.py:504
  21.6 4.3 %collective-permute-start.5 = (f32[16,8,128]{2,1,0:T(8,128)S(1)}, f32[16,8,128]{2,1,0:T(8,128)S(1)}, u32[]{:S(2)}, u32[]{:S(2)}) collective-permute-start(f32[16,8,128]{2,1,0:T(8,128)S(1)} %get-tuple-element.31), channel_id=1, source_target_pairs={{0,24},{8,0},{16,8},{24,16},{32,56},{40,32},{48,40},{56,48},{64,88... | collective-permute-start | bytes 196616 | tf_op jit(solution)/shard_map/ppermute | solution.py:504
  55.1 5.4 %collective-permute-start.6 = (f32[12,8,128]{2,1,0:T(8,128)S(1)}, f32[12,8,128]{2,1,0:T(8,128)S(1)}, u32[]{:S(2)}, u32[]{:S(2)}) collective-permute-start(f32[12,8,128]{2,1,0:T(8,128)S(1)} %get-tuple-element.36), channel_id=1, source_target_pairs={{0,8},{8,16},{16,24},{24,0},{32,40},{40,48},{48,56},{56,32},{64,72... | collective-permute-start | bytes 147464 | tf_op jit(solution)/shard_map/ppermute | solution.py:504
  55.5 6.5 %collective-permute-start.7 = (f32[12,8,128]{2,1,0:T(8,128)S(1)}, f32[12,8,128]{2,1,0:T(8,128)S(1)}, u32[]{:S(2)}, u32[]{:S(2)}) collective-permute-start(f32[12,8,128]{2,1,0:T(8,128)S(1)} %get-tuple-element.37), channel_id=1, source_target_pairs={{0,16},{8,24},{16,0},{24,8},{32,48},{40,56},{48,32},{56,40},{64,80... | collective-permute-start | bytes 147464 | tf_op jit(solution)/shard_map/ppermute | solution.py:504
  59.4 4.1 %collective-permute-start.8 = (f32[12,8,128]{2,1,0:T(8,128)S(1)}, f32[12,8,128]{2,1,0:T(8,128)S(1)}, u32[]{:S(2)}, u32[]{:S(2)}) collective-permute-start(f32[12,8,128]{2,1,0:T(8,128)S(1)} %get-tuple-element.38), channel_id=1, source_target_pairs={{0,24},{8,0},{16,8},{24,16},{32,56},{40,32},{48,40},{56,48},{64,88... | collective-permute-start | bytes 147464 | tf_op jit(solution)/shard_map/ppermute | solution.py:504

commit v8 on v4

--- a/solution.py
+++ b/solution.py
@@ -19,7 +19,7 @@
 R_PAD = 208
 STRIP = 16
 CHUNKS = tuple((start, STRIP) for start in range(0, R_PAD, STRIP))
-TILE = 1024
+TILE = 4096
 XB = 4
 LIMIT = 24 * 1024 * 1024
 F32 = jnp.float32
@@ -115,34 +115,32 @@
     for x in range(xb):
         for y in range(ny):
             row = x * ny + y
-            cols = slice(y * nz, (y + 1) * nz)
+            cols = slice(row * nz, (row + 1) * nz)
             conc = jnp.concatenate(
                 [conc32_ref[pl.ds(row + 8 * q * pitch, 8, stride=pitch), :] for q in range(4)], axis=0
             ).astype(BF16)
-            x_ref[x, 0:32, cols] = conc
-            x_ref[x, 32:64, cols] = conc
+            x_ref[0:32, cols] = conc
+            x_ref[32:64, cols] = conc
             lam = [adj_rows[pl.ds(row + first * pitch, 8, stride=pitch), :] for first in (0, 8, carried - 8)]
             level = jnp.broadcast_to(lev_ref[x, y : y + 1, :], (8, nz))
             marks = jnp.where(level <= sub, 1.0, 0.0)
-            x_ref[x, 64:96, cols] = jnp.concatenate(lam + [marks], axis=0).astype(BF16)
+            x_ref[64:96, cols] = jnp.concatenate(lam + [marks], axis=0).astype(BF16)
     per_tile = TILE // nz
-    for x in range(xb):
-        for tile in range(ny // per_tile):
-            slot = (x * (ny // per_tile) + tile) % act_ref.shape[0]
-            data = x_ref[x, :, tile * TILE : (tile + 1) * TILE]
-            every = dot(w_ref[...], data)
-            for start, size in CHUNKS:
-                got = every[3 * start : 3 * (start + size)]
-                weight = got[2 * size :]
-                act_ref[slot, 0, start : start + size, :] = (jnp.exp2(got[:size]) * weight).astype(BF16)
-                act_ref[slot, 1, start : start + size, :] = (jnp.exp2(got[size : 2 * size]) * weight).astype(BF16)
-            chem = dot(c_ref[0], act_ref[slot, 0]) + dot(c_ref[1], act_ref[slot, 1])
-            for part in range(per_tile):
-                row = x * ny + tile * per_tile + part
-                for q, first in enumerate((0, 8, carried - 8)):
-                    out_rows[pl.ds(row + first * pitch, 8, stride=pitch), :] = chem[
-                        8 * q : 8 * q + 8, part * nz : (part + 1) * nz
-                    ]
+    for tile in range(xb * ny // per_tile):
+        slot = tile % act_ref.shape[0]
+        every = dot(w_ref[...], x_ref[:, tile * TILE : (tile + 1) * TILE])
+        for start, size in CHUNKS:
+            got = every[3 * start : 3 * (start + size)]
+            weight = got[2 * size :]
+            act_ref[slot, 0, start : start + size, :] = (jnp.exp2(got[:size]) * weight).astype(BF16)
+            act_ref[slot, 1, start : start + size, :] = (jnp.exp2(got[size : 2 * size]) * weight).astype(BF16)
+        chem = dot(c_ref[0], act_ref[slot, 0]) + dot(c_ref[1], act_ref[slot, 1])
+        for part in range(per_tile):
+            row = tile * per_tile + part
+            for q, first in enumerate((0, 8, carried - 8)):
+                out_rows[pl.ds(row + first * pitch, 8, stride=pitch), :] = chem[
+                    8 * q : 8 * q + 8, part * nz : (part + 1) * nz
+                ]
 
 
 def chemistry(adjoint, log_conc, levels, conduct, orders_fwd, orders_rev, stoich, rate_fwd, rate_rev):
@@ -175,8 +173,8 @@
             pltpu.VMEM((3 * R_PAD, K_ROWS), BF16),
             pltpu.VMEM((2, 32, R_PAD), BF16),
             pltpu.VMEM((species * XB * ny, nz), F32),
-            pltpu.VMEM((XB, K_ROWS, ny * nz), BF16),
-            pltpu.VMEM((2, 2, R_PAD, TILE), BF16),
+            pltpu.VMEM((K_ROWS, XB * ny * nz), BF16),
+            pltpu.VMEM((1, 2, R_PAD, TILE), BF16),
             pltpu.VMEM((3, ny, nz), F32),
         ],
         compiler_params=pltpu.CompilerParams(dimension_semantics=("arbitrary",), vmem_limit_bytes=LIMIT),
@@ -233,7 +231,7 @@
 
 def local_kernel(
     diff_ref, cond_ref, adj_ref, chem_ref, near_ref, low_ref, high_ref, coef_ref, tail_ref,
-    part_ref, msg_ref, band_ref, zz_ref,
+    part_ref, msg_ref, band_ref, parts_ref, zz_ref,
 ):
     nx, ny, nz = cond_ref.shape
     carried = adj_ref.shape[0]
@@ -246,24 +244,22 @@
             msg_ref[pl.ds(group * ROWS + r, ny, stride=stride), :] = value
 
     k, z = iota((2 * nz, nz), 0), iota((2 * nz, nz), 1)
-    offset = jnp.where(lax.axis_index("gz") == 0, nz, -nz)
-    gap = jnp.abs(jnp.where(k < nz, k, k - nz + offset) - z)
+    gap = jnp.abs(jnp.where(k < nz, k, k - nz) - z)
     band_ref[...] = jnp.where(
         gap == 0, -60.0, jnp.where(gap == 1, 16.0, jnp.where(gap == 2, -1.0, 0.0))
     ).astype(BF16)
-    row = iota((ny, nz), 0)
+    row, lane = iota((ny, nz), 0), iota((ny, nz), 1)
+    low_core = lax.axis_index("gz") == 0
+    turn1, turn2 = jnp.where(low_core, nz - 1, 1), jnp.where(low_core, nz - 2, 2)
+    outer, inner = jnp.where(low_core, nz - 1, 0), jnp.where(low_core, nz - 2, 1)
 
     @pl.loop(0, carried // LB)
     def _(g):
         for t in range(LB):
             s = g * LB + t
             own_hi, own_lo = split(adj_ref[s].reshape(nx * ny, nz))
-            near_hi, near_lo = split(near_ref[s].reshape(nx * ny, nz))
-            sides = jnp.concatenate(
-                [jnp.concatenate([own_hi, near_hi], axis=1), jnp.concatenate([own_lo, near_lo], axis=1)], axis=0
-            )
-            spread_z = dot(sides, band_ref[...])
-            zz_ref[t] = spread_z[: nx * ny] + spread_z[nx * ny :]
+            parts_ref[t * nx * ny : (t + 1) * nx * ny, :] = jnp.concatenate([own_hi, own_lo], axis=1)
+        zz_ref[...] = dot(parts_ref[...], band_ref[...])
         for t in range(LB):
             s = g * LB + t
             scale = diff_ref[s] * (SECTION * STEP / 12.0)
@@ -276,7 +272,11 @@
                 y_up2 = jnp.where(row == ny - 1, high1, jnp.where(row == ny - 2, high0, pltpu.roll(own, ny - 2, 0)))
                 y_dn1 = jnp.where(row == 0, low1, pltpu.roll(own, 1, 0))
                 y_dn2 = jnp.where(row == 0, low0, jnp.where(row == 1, low1, pltpu.roll(own, 2, 0)))
-                spread = 16.0 * (y_up1 + y_dn1) - (y_up2 + y_dn2) + zz_ref[t, p * ny : (p + 1) * ny, :]
+                near = near_ref[s, p]
+                near1, near2 = pltpu.roll(near, turn1, 1), pltpu.roll(near, turn2, 1)
+                edge = jnp.where(lane == outer, 16.0 * near1 - near2, jnp.where(lane == inner, -near2, 0.0))
+                at = (t * nx + p) * ny
+                spread = 16.0 * (y_up1 + y_dn1) - (y_up2 + y_dn2) + (zz_ref[at : at + ny, :] + edge)
                 b = SECTION * own + (SECTION * STEP) * chem_ref[s, p] + scale * spread
                 if p == 0:
                     b_first = b
@@ -302,7 +302,7 @@
             pltpu.VMEM(adjoint.shape, F32),
             pltpu.VMEM((GROUPS * ny * ROWS, nz), F32),
         ],
-        scratch_shapes=[pltpu.VMEM((2 * nz, nz), BF16), pltpu.VMEM((LB, nx * ny, nz), F32)],
+        scratch_shapes=[pltpu.VMEM((2 * nz, nz), BF16), pltpu.VMEM((LB * nx * ny, 2 * nz), BF16), pltpu.VMEM((LB * nx * ny, nz), F32)],
         compiler_params=SMALL,
         cost_estimate=pl.CostEstimate(flops=20 * 10**6, bytes_accessed=7 * 10**6, transcendentals=0),
         name="local",

time: 60.3 us -> 58.7 us (0.973)
  Pallas kernels: 16.1 us -> 14.5 us
    pallas_call x1, Pallas kernels: 11.3 us -> 9.96 us  [chemistry(): pl.pallas_call(chem_kernel, grid=(nx // XB,), in_specs=[pl.BlockSpec((car...]
  transfers between devices with their start and end apart: 3 -> 3, of which waited for: 0 -> 0; matrix products, arithmetic and copies ran while one was open for 0% -> 0% of each run, Pallas kernels for 19% -> 18%
where the time goes in v8:
time: 58.7 us; the launch traced here: 58.5 us
  blocking collectives  40 us (68%)
  Pallas kernels  14.5 us (25%)
  starting transfers between devices  2.44 us (4%)
  local copies, waits for them, and re-layouts  1.4 us (2%)
    all_to_all x1, blocking collectives, shards(): lax.all_to_all(message.reshape(blocks, ROWS, nz), 'gx', 0, 0, tiled=True)  23.7 us
    all_to_all x1, blocking collectives, shards(): ends = lax.all_to_all(chain(message), 'gx', 0, 0, tiled=True)  16.3 us
    pallas_call x1, Pallas kernels, chemistry(): pl.pallas_call(chem_kernel, grid=(nx // XB,), in_specs=[pl.BlockSpec((car...  9.96 us
    pallas_call x1, Pallas kernels, local_part(): pl.pallas_call(local_kernel, in_specs=[smem] + [WHOLE] * 8, out_specs=[WH...  2.56 us
    ppermute x1, starting transfers between devices, shards(): lax.ppermute(tail, 'gy', [(i, (i + 1) % rows_y) for i in range(rows_y)])  1.57 us
    unnamed x20, local copies, waits for them, and re-layouts  1.4 us
    pallas_call x1, Pallas kernels, back(): pl.pallas_call(back_kernel, in_specs=[WHOLE, WHOLE, WHOLE], out_specs=ANY...  1.37 us
  transfers between devices with their start and end apart: 3, of which 0 were waited for; matrix products, arithmetic and copies ran while one was open for 0% of the time, Pallas kernels for 18%

profile of v8, /device:TPU:2, one launch (start us, length us, event | category | flops | bytes accessed | tf_op | source)
XLA Modules:
  0.0 58.5 jit_solution(15086222592994962151)
XLA Ops:
  0.0 0.0 collective-permute-start
  0.0 0.0 copy-start
  0.0 1.4 %copy-done = f32[22,16,8,128]{3,2,1,0:T(8,128)S(1)} copy-done((f32[22,16,8,128]{3,2,1,0:T(8,128)S(1)}, f32[22,16,8,128]{3,2,1,0:T(8,128)}, u32[]{:S(2)}) %copy-start) | copy-done | bytes 1441816
  1.4 0.0 copy-start.1
  1.4 0.0 copy-start.3
  1.4 0.0 copy-start.4
  1.4 0.0 copy-start.6
  1.4 0.0 copy-start.7
  1.4 0.0 copy-start.8
  1.4 0.0 copy-start.9
  1.4 0.4 edges.1
  1.8 1.6 %collective-permute-start.1 = (f32[22,16,2,128]{3,2,1,0:T(2,128)S(1)}, f32[22,16,2,128]{3,2,1,0:T(2,128)S(1)}, u32[]{:S(2)}, u32[]{:S(2)}) collective-permute-start(f32[22,16,2,128]{3,2,1,0:T(2,128)S(1)} %get-tuple-element.14), channel_id=1, source_target_pairs={{0,2},{2,4},{4,6},{6,0},{1,3},{3,5},{5,7},{7,1},{8,10},{10,12},{12... | collective-permute-start | bytes 1081352 | tf_op jit(solution)/shard_map/ppermute | solution.py:427
  3.4 0.9 %collective-permute-start.2 = (f32[22,16,2,128]{3,2,1,0:T(2,128)S(1)}, f32[22,16,2,128]{3,2,1,0:T(2,128)S(1)}, u32[]{:S(2)}, u32[]{:S(2)}) collective-permute-start(f32[22,16,2,128]{3,2,1,0:T(2,128)S(1)} %get-tuple-element.15), channel_id=1, source_target_pairs={{2,0},{4,2},{6,4},{0,6},{3,1},{5,3},{7,5},{1,7},{10,8},{12,10},{14... | collective-permute-start | bytes 1081352 | tf_op jit(solution)/shard_map/ppermute | solution.py:428
  4.2 0.0 copy-done.1
  4.2 0.0 copy-done.3
  4.2 0.0 copy-done.4
  4.2 0.0 copy-done.5
  4.3 0.0 copy-done.6
  4.3 0.0 copy-done.7
  4.3 0.0 copy-done.8
  4.3 0.0 copy-done.9
  4.3 0.0 copy-start.2
  4.3 10.0 %chem.1 = (f32[22,16,8,128]{3,2,1,0:T(8,128)S(1)}, f32[3,17,8,128]{3,2,1,0:T(8,128)S(1)}, f32[17,3,8,128]{3,2,1,0:T(8,128)S(1)}) custom-call(f32[22,16,8,128]{3,2,1,0:T(8,128)S(1)} %copy-done, bf16[32,16,8,128]{3,2,1,0:T(8,128)(2,1)S(1)} %copy-done.3, s32[16,8,128]{2,1,0:T(8,128)S(1)} %copy-done.4, f32[16,8,128]{2,1,0:T(8,128)S(1)} %copy-done.1, ...), custom_call_target="tpu_custom_call" | custom-call | flops 12000000000 | bytes 4000000 | tf_op jit(solution)/shard_map/chem/pallas_call | solution.py:151
  14.3 0.0 collective-permute-done.1.low_ref
  14.3 0.0 collective-permute-done.2.high_ref
  14.3 0.0 collective-permute-done.near_ref
  14.3 0.0 copy-done.2
  14.3 2.6 %local.1 = (f32[22,16,8,128]{3,2,1,0:T(8,128)S(1)}, f32[512,128]{1,0:T(8,128)S(1)}) custom-call(f32[22]{0:T(128)S(1)} %copy-done.2, f32[16,8,128]{2,1,0:T(8,128)S(1)} %copy-done.1, f32[22,16,8,128]{3,2,1,0:T(8,128)S(1)} %copy-done, f32[22,16,8,128]{3,2,1,0:T(8,128)S(1)} %get-tuple-element.13.chem_ref, f32[22,16,8,128]{3,2,1,0:T(8,128)S(1)} %collective-permute-done.near_ref, ...), custom_call_target="tpu_custom_call" | custom-call | flops 20000000 | bytes 7000000 | tf_op jit(solution)/shard_map/local/pallas_call | solution.py:297
  16.9 23.7 %all_to_all.10.in_ref = f32[32,16,128]{2,1,0:T(8,128)S(1)} all-to-all(f32[32,16,128]{2,1,0:T(8,128)S(1)} %bitcast.8), channel_id=1, replica_groups=mesh['gx'=32,'gy'=4,'gz'=2] {'gx'}, dimensions={0} | all-to-all | bytes 524288 | tf_op jit(solution)/shard_map/all_to_all | solution.py:431
  40.6 0.2 chain.1
  40.9 16.3 %all_to_all.11 = f32[32,16,128]{2,1,0:T(8,128)S(1)} all-to-all(f32[32,16,128]{2,1,0:T(8,128)S(1)} %chain.1), channel_id=1, replica_groups=mesh['gx'=32,'gy'=4,'gz'=2] {'gx'}, dimensions={0} | all-to-all | bytes 524288 | tf_op jit(solution)/shard_map/all_to_all | solution.py:432
  57.2 1.4 %back.1 = f32[22,16,8,128]{3,2,1,0:T(8,128)} custom-call(f32[3,17,8,128]{3,2,1,0:T(8,128)S(1)} %get-tuple-element.12.coef_ref, f32[512,128]{1,0:T(8,128)S(1)} %bitcast.7, f32[22,16,8,128]{3,2,1,0:T(8,128)S(1)} %get-tuple-element.18.part_ref), custom_call_target="tpu_custom_call" | custom-call | flops 2000000 | bytes 3000000 | tf_op jit(solution)/shard_map/back/pallas_call | solution.py:404
  (1 shorter events, 0.0 us)
Async XLA Ops:
  0.0 14.3 %collective-permute-start = (f32[22,16,8,128]{3,2,1,0:T(8,128)}, f32[22,16,8,128]{3,2,1,0:T(8,128)S(1)}, u32[]{:S(2)}, u32[]{:S(2)}) collective-permute-start(f32[22,16,8,128]{3,2,1,0:T(8,128)} %adj_ref.5), channel_id=1, source_target_pairs={{0,1},{1,0},{2,3},{3,2},{4,5},{5,4},{6,7},{7,6},{8,9},{9,8},{10,11... | collective-permute-start | bytes 4325384 | tf_op jit(solution)/shard_map/ppermute | solution.py:425
  0.0 1.4 %copy-start = (f32[22,16,8,128]{3,2,1,0:T(8,128)S(1)}, f32[22,16,8,128]{3,2,1,0:T(8,128)}, u32[]{:S(2)}) copy-start(f32[22,16,8,128]{3,2,1,0:T(8,128)} %adj_ref.5) | copy-start | bytes 4325380
  1.4 2.9 %copy-start.1 = (f32[16,8,128]{2,1,0:T(8,128)S(1)}, f32[16,8,128]{2,1,0:T(8,128)}, u32[]{:S(2)}) copy-start(f32[16,8,128]{2,1,0:T(8,128)} %cond_ref.3) | copy-start | bytes 196612
  1.4 2.9 %copy-start.3 = (bf16[32,16,8,128]{3,2,1,0:T(8,128)(2,1)S(1)}, bf16[32,16,8,128]{3,2,1,0:T(8,128)(2,1)}, u32[]{:S(2)}) copy-start(bf16[32,16,8,128]{3,2,1,0:T(8,128)(2,1)} %conc_ref.1) | copy-start | bytes 3145732
  1.4 2.9 %copy-start.4 = (s32[16,8,128]{2,1,0:T(8,128)S(1)}, s32[16,8,128]{2,1,0:T(8,128)}, u32[]{:S(2)}) copy-start(s32[16,8,128]{2,1,0:T(8,128)} %lev_ref.1) | copy-start | bytes 196612
  1.4 2.9 %copy-start.5 = (bf16[206,32]{0,1:T(8,128)(2,1)S(1)}, bf16[206,32]{0,1:T(8,128)(2,1)}, u32[]{:S(2)}) copy-start(bf16[206,32]{0,1:T(8,128)(2,1)} %param.14) | copy-start | bytes 39556
  1.4 2.9 %copy-start.6 = (bf16[206,32]{0,1:T(8,128)(2,1)S(1)}, bf16[206,32]{0,1:T(8,128)(2,1)}, u32[]{:S(2)}) copy-start(bf16[206,32]{0,1:T(8,128)(2,1)} %param.15) | copy-start | bytes 39556
  1.4 2.9 %copy-start.7 = (bf16[206,22]{0,1:T(8,128)(2,1)S(1)}, bf16[206,22]{0,1:T(8,128)(2,1)}, u32[]{:S(2)}) copy-start(bf16[206,22]{0,1:T(8,128)(2,1)} %param.16) | copy-start | bytes 27196
  1.4 2.9 %copy-start.8 = (f32[206]{0:T(256)S(1)}, f32[206]{0:T(256)}, u32[]{:S(2)}) copy-start(f32[206]{0:T(256)} %param.17) | copy-start | bytes 2476
  1.4 2.9 %copy-start.9 = (f32[206]{0:T(256)S(1)}, f32[206]{0:T(256)}, u32[]{:S(2)}) copy-start(f32[206]{0:T(256)} %param.18) | copy-start | bytes 2476
  1.8 12.5 %collective-permute-start.1 = (f32[22,16,2,128]{3,2,1,0:T(2,128)S(1)}, f32[22,16,2,128]{3,2,1,0:T(2,128)S(1)}, u32[]{:S(2)}, u32[]{:S(2)}) collective-permute-start(f32[22,16,2,128]{3,2,1,0:T(2,128)S(1)} %get-tuple-element.14), channel_id=1, source_target_pairs={{0,2},{2,4},{4,6},{6,0},{1,3},{3,5},{5,7},{7,1},{8,10},{10,12},{12... | collective-permute-start | bytes 1081352 | tf_op jit(solution)/shard_map/ppermute | solution.py:427
  3.4 10.9 %collective-permute-start.2 = (f32[22,16,2,128]{3,2,1,0:T(2,128)S(1)}, f32[22,16,2,128]{3,2,1,0:T(2,128)S(1)}, u32[]{:S(2)}, u32[]{:S(2)}) collective-permute-start(f32[22,16,2,128]{3,2,1,0:T(2,128)S(1)} %get-tuple-element.15), channel_id=1, source_target_pairs={{2,0},{4,2},{6,4},{0,6},{3,1},{5,3},{7,5},{1,7},{10,8},{12,10},{14... | collective-permute-start | bytes 1081352 | tf_op jit(solution)/shard_map/ppermute | solution.py:428
  4.3 10.0 %copy-start.2 = (f32[22]{0:T(128)S(1)}, f32[22]{0:T(128)}, u32[]{:S(2)}) copy-start(f32[22]{0:T(128)} %diff_ref.1) | copy-start | bytes 268

commit v9 on v8

--- a/solution.py
+++ b/solution.py
@@ -197,6 +197,13 @@
     return s // GROUP * ROWS + s % GROUP
 
 
+def crossing(adj_ref, s):
+    carried, nx, ny, nz = adj_ref.shape
+    rows = adj_ref.reshape(carried * nx * ny, nz)
+    f0, f1, f6, f7 = [rows[pl.ds(s * nx * ny + r, nx, stride=ny), :] for r in (0, 1, ny - 2, ny - 1)]
+    return (16.0 * f7 - f6, -f7), (-f0, 16.0 * f0 - f1)
+
+
 def edges_kernel(adj_ref, low_ref, high_ref):
     carried, nx, ny, nz = adj_ref.shape
     mine = lax.axis_index("gy")
@@ -205,14 +212,15 @@
 
     @pl.loop(0, carried)
     def _(s):
-        for x in range(nx):
-            low_ref[s, x] = adj_ref[s, x, ny - 2 : ny, :] * to_high
-            high_ref[s, x] = adj_ref[s, x, 0:2, :] * to_low
+        down, up = crossing(adj_ref, s)
+        for k in range(2):
+            low_ref[s, k] = down[k] * to_high
+            high_ref[s, k] = up[k] * to_low
 
 
 def edges(adjoint):
     carried, nx, ny, nz = adjoint.shape
-    shape = pltpu.VMEM((carried, nx, 2, nz), F32)
+    shape = pltpu.VMEM((carried, 2, nx, nz), F32)
     return pl.pallas_call(
         edges_kernel,
         in_specs=[WHOLE],
@@ -248,7 +256,7 @@
     band_ref[...] = jnp.where(
         gap == 0, -60.0, jnp.where(gap == 1, 16.0, jnp.where(gap == 2, -1.0, 0.0))
     ).astype(BF16)
-    row, lane = iota((ny, nz), 0), iota((ny, nz), 1)
+    lane = iota((ny, nz), 1)
     low_core = lax.axis_index("gz") == 0
     turn1, turn2 = jnp.where(low_core, nz - 1, 1), jnp.where(low_core, nz - 2, 2)
     outer, inner = jnp.where(low_core, nz - 1, 0), jnp.where(low_core, nz - 2, 1)
@@ -262,21 +270,28 @@
         zz_ref[...] = dot(parts_ref[...], band_ref[...])
         for t in range(LB):
             s = g * LB + t
+            down, up = crossing(adj_ref, s)
+            for r, own_term, got in (
+                (0, down[0], low_ref[s, 0]),
+                (1, down[1], low_ref[s, 1]),
+                (ny - 2, up[0], high_ref[s, 0]),
+                (ny - 1, up[1], high_ref[s, 1]),
+            ):
+                at = pl.ds(t * nx * ny + r, nx, stride=ny)
+                zz_ref[at, :] = zz_ref[at, :] + (got - own_term)
+        for t in range(LB):
+            s = g * LB + t
             scale = diff_ref[s] * (SECTION * STEP / 12.0)
             b_first, carry = None, None
             for p in range(nx):
                 own = adj_ref[s, p]
-                low0, low1 = low_ref[s, p, 0:1, :], low_ref[s, p, 1:2, :]
-                high0, high1 = high_ref[s, p, 0:1, :], high_ref[s, p, 1:2, :]
-                y_up1 = jnp.where(row == ny - 1, high0, pltpu.roll(own, ny - 1, 0))
-                y_up2 = jnp.where(row == ny - 1, high1, jnp.where(row == ny - 2, high0, pltpu.roll(own, ny - 2, 0)))
-                y_dn1 = jnp.where(row == 0, low1, pltpu.roll(own, 1, 0))
-                y_dn2 = jnp.where(row == 0, low0, jnp.where(row == 1, low1, pltpu.roll(own, 2, 0)))
+                y_near = pltpu.roll(own, ny - 1, 0) + pltpu.roll(own, 1, 0)
+                y_far = pltpu.roll(own, ny - 2, 0) + pltpu.roll(own, 2, 0)
                 near = near_ref[s, p]
                 near1, near2 = pltpu.roll(near, turn1, 1), pltpu.roll(near, turn2, 1)
                 edge = jnp.where(lane == outer, 16.0 * near1 - near2, jnp.where(lane == inner, -near2, 0.0))
                 at = (t * nx + p) * ny
-                spread = 16.0 * (y_up1 + y_dn1) - (y_up2 + y_dn2) + (zz_ref[at : at + ny, :] + edge)
+                spread = 16.0 * y_near - y_far + (zz_ref[at : at + ny, :] + edge)
                 b = SECTION * own + (SECTION * STEP) * chem_ref[s, p] + scale * spread
                 if p == 0:
                     b_first = b
@@ -358,8 +373,10 @@
         last = part + a * first[i]
         if i < count - 1:
             last = last + c * first[i + 1]
-        out_ref[i, 0:8, :] = first[i]
-        out_ref[i, 8:16, :] = last
+        out_ref[i, 0] = first[i][0:4]
+        out_ref[i, 1, 0:2] = first[i][4:6]
+        out_ref[i, 1, 2:4] = last[0:2]
+        out_ref[i, 2] = last[2:6]
 
 
 def chain(message):
@@ -367,16 +384,22 @@
         chain_kernel,
         in_specs=[WHOLE],
         out_specs=WHOLE,
-        out_shape=pltpu.VMEM(message.shape, F32),
+        out_shape=pltpu.VMEM((message.shape[0], 3, 4, message.shape[2]), F32),
         compiler_params=SMALL,
         cost_estimate=pl.CostEstimate(flops=10**6, bytes_accessed=10**6, transcendentals=0),
         name="chain",
     )(message)
 
 
-def back_kernel(coef_ref, ends_ref, part_ref, out_hbm, out_ref, out_sem):
+def back_kernel(coef_ref, got_ref, part_ref, out_hbm, ends_ref, out_ref, out_sem):
     carried, nx, ny, _ = part_ref.shape
     groups = carried // SB
+    for i in range(got_ref.shape[0]):
+        top = i * ROWS
+        ends_ref[top : top + 4, :] = got_ref[i, 0]
+        ends_ref[top + 4 : top + 6, :] = got_ref[i, 1, 0:2]
+        ends_ref[top + 8 : top + 10, :] = got_ref[i, 1, 2:4]
+        ends_ref[top + 10 : top + 14, :] = got_ref[i, 2]
 
     def put(g):
         return pltpu.make_async_copy(out_ref.at[pl.ds(g * SB, SB)], out_hbm.at[pl.ds(g * SB, SB)], out_sem.at[g])
@@ -406,7 +429,11 @@
         in_specs=[WHOLE, WHOLE, WHOLE],
         out_specs=ANY,
         out_shape=jax.ShapeDtypeStruct(part.shape, F32),
-        scratch_shapes=[pltpu.VMEM(part.shape, F32), pltpu.SemaphoreType.DMA((groups,))],
+        scratch_shapes=[
+            pltpu.VMEM((ends.shape[0] * ROWS, part.shape[3]), F32),
+            pltpu.VMEM(part.shape, F32),
+            pltpu.SemaphoreType.DMA((groups,)),
+        ],
         compiler_params=SMALL,
         cost_estimate=pl.CostEstimate(flops=2 * 10**6, bytes_accessed=3 * 10**6, transcendentals=0),
         name="back",
@@ -430,7 +457,7 @@
     part, message = local_part(diffusivity, adjoint, chem, near, low, high, conduct, coef, ends_m)
     message = lax.all_to_all(message.reshape(blocks, ROWS, nz), "gx", 0, 0, tiled=True)
     ends = lax.all_to_all(chain(message), "gx", 0, 0, tiled=True)
-    return back(part, coef, ends.reshape(blocks * ROWS, nz))
+    return back(part, coef, ends)
 
 
 def solution(mesh):

time: 58.7 us -> 57.5 us (0.980)
  blocking collectives: 40 us -> 38.9 us
    all_to_all x1, blocking collectives: 16.3 us -> 15.2 us  [shards(): ends = lax.all_to_all(chain(message), 'gx', 0, 0, tiled=True)]
where the time goes in v9:
time: 57.5 us; the launch traced here: 57.3 us
  blocking collectives  38.9 us (68%)
  Pallas kernels  14.4 us (25%)
  starting transfers between devices  2.44 us (4%)
  local copies, waits for them, and re-layouts  1.4 us (2%)
    all_to_all x1, blocking collectives, shards(): lax.all_to_all(message.reshape(blocks, ROWS, nz), 'gx', 0, 0, tiled=True)  23.7 us
    all_to_all x1, blocking collectives, shards(): ends = lax.all_to_all(chain(message), 'gx', 0, 0, tiled=True)  15.2 us
    pallas_call x1, Pallas kernels, chemistry(): pl.pallas_call(chem_kernel, grid=(nx // XB,), in_specs=[pl.BlockSpec((car...  9.96 us
    pallas_call x1, Pallas kernels, local_part(): pl.pallas_call(local_kernel, in_specs=[smem] + [WHOLE] * 8, out_specs=[WH...  2.55 us
    ppermute x1, starting transfers between devices, shards(): lax.ppermute(tail, 'gy', [(i, (i + 1) % rows_y) for i in range(rows_y)])  1.57 us
    pallas_call x1, Pallas kernels, back(): pl.pallas_call(back_kernel, in_specs=[WHOLE, WHOLE, WHOLE], out_specs=ANY...  1.43 us
    unnamed x20, local copies, waits for them, and re-layouts  1.4 us
  transfers between devices with their start and end apart: 3, of which 0 were waited for; matrix products, arithmetic and copies ran while one was open for 0% of the time, Pallas kernels for 18%

profile of v9, /device:TPU:2, one launch (start us, length us, event | category | flops | bytes accessed | tf_op | source)
XLA Modules:
  0.0 57.3 jit_solution(13945424432390821958)
XLA Ops:
  0.0 0.0 collective-permute-start
  0.0 0.0 copy-start
  0.0 1.4 %copy-done = f32[22,16,8,128]{3,2,1,0:T(8,128)S(1)} copy-done((f32[22,16,8,128]{3,2,1,0:T(8,128)S(1)}, f32[22,16,8,128]{3,2,1,0:T(8,128)}, u32[]{:S(2)}) %copy-start) | copy-done | bytes 1441816
  1.4 0.0 copy-start.1
  1.4 0.0 copy-start.3
  1.4 0.0 copy-start.4
  1.4 0.0 copy-start.6
  1.4 0.0 copy-start.7
  1.4 0.0 copy-start.8
  1.4 0.0 copy-start.9
  1.4 0.2 edges.1
  1.7 1.6 %collective-permute-start.1 = (f32[22,2,16,128]{3,2,1,0:T(8,128)S(1)}, f32[22,2,16,128]{3,2,1,0:T(8,128)S(1)}, u32[]{:S(2)}, u32[]{:S(2)}) collective-permute-start(f32[22,2,16,128]{3,2,1,0:T(8,128)S(1)} %get-tuple-element.14), channel_id=1, source_target_pairs={{0,2},{2,4},{4,6},{6,0},{1,3},{3,5},{5,7},{7,1},{8,10},{10,12},{12... | collective-permute-start | bytes 1081352 | tf_op jit(solution)/shard_map/ppermute | solution.py:454
  3.2 0.9 %collective-permute-start.2 = (f32[22,2,16,128]{3,2,1,0:T(8,128)S(1)}, f32[22,2,16,128]{3,2,1,0:T(8,128)S(1)}, u32[]{:S(2)}, u32[]{:S(2)}) collective-permute-start(f32[22,2,16,128]{3,2,1,0:T(8,128)S(1)} %get-tuple-element.15), channel_id=1, source_target_pairs={{2,0},{4,2},{6,4},{0,6},{3,1},{5,3},{7,5},{1,7},{10,8},{12,10},{14... | collective-permute-start | bytes 1081352 | tf_op jit(solution)/shard_map/ppermute | solution.py:455
  4.1 0.0 copy-done.1
  4.1 0.0 copy-done.3
  4.1 0.0 copy-done.4
  4.1 0.0 copy-done.5
  4.1 0.0 copy-done.6
  4.1 0.0 copy-done.7
  4.1 0.0 copy-done.8
  4.2 0.0 copy-done.9
  4.2 0.0 copy-start.2
  4.2 10.0 %chem.1 = (f32[22,16,8,128]{3,2,1,0:T(8,128)S(1)}, f32[3,17,8,128]{3,2,1,0:T(8,128)S(1)}, f32[17,3,8,128]{3,2,1,0:T(8,128)S(1)}) custom-call(f32[22,16,8,128]{3,2,1,0:T(8,128)S(1)} %copy-done, bf16[32,16,8,128]{3,2,1,0:T(8,128)(2,1)S(1)} %copy-done.3, s32[16,8,128]{2,1,0:T(8,128)S(1)} %copy-done.4, f32[16,8,128]{2,1,0:T(8,128)S(1)} %copy-done.1, ...), custom_call_target="tpu_custom_call" | custom-call | flops 12000000000 | bytes 4000000 | tf_op jit(solution)/shard_map/chem/pallas_call | solution.py:151
  14.1 0.0 collective-permute-done.1.low_ref
  14.2 0.0 collective-permute-done.2.high_ref
  14.2 0.0 collective-permute-done.near_ref
  14.2 0.0 copy-done.2
  14.2 2.6 %local.1 = (f32[22,16,8,128]{3,2,1,0:T(8,128)S(1)}, f32[512,128]{1,0:T(8,128)S(1)}) custom-call(f32[22]{0:T(128)S(1)} %copy-done.2, f32[16,8,128]{2,1,0:T(8,128)S(1)} %copy-done.1, f32[22,16,8,128]{3,2,1,0:T(8,128)S(1)} %copy-done, f32[22,16,8,128]{3,2,1,0:T(8,128)S(1)} %get-tuple-element.13.chem_ref, f32[22,16,8,128]{3,2,1,0:T(8,128)S(1)} %collective-permute-done.near_ref, ...), custom_call_target="tpu_custom_call" | custom-call | flops 20000000 | bytes 7000000 | tf_op jit(solution)/shard_map/local/pallas_call | solution.py:312
  16.7 23.7 %all_to_all.10.in_ref = f32[32,16,128]{2,1,0:T(8,128)S(1)} all-to-all(f32[32,16,128]{2,1,0:T(8,128)S(1)} %bitcast.6), channel_id=1, replica_groups=mesh['gx'=32,'gy'=4,'gz'=2] {'gx'}, dimensions={0} | all-to-all | bytes 524288 | tf_op jit(solution)/shard_map/all_to_all | solution.py:458
  40.5 0.2 chain.1
  40.7 15.2 %all_to_all.11.got_ref = f32[32,3,4,128]{3,2,1,0:T(4,128)S(1)} all-to-all(f32[32,3,4,128]{3,2,1,0:T(4,128)S(1)} %chain.1), channel_id=1, replica_groups=mesh['gx'=32,'gy'=4,'gz'=2] {'gx'}, dimensions={0} | all-to-all | bytes 393216 | tf_op jit(solution)/shard_map/all_to_all | solution.py:459
  55.9 1.4 %back.1 = f32[22,16,8,128]{3,2,1,0:T(8,128)} custom-call(f32[3,17,8,128]{3,2,1,0:T(8,128)S(1)} %get-tuple-element.12.coef_ref, f32[32,3,4,128]{3,2,1,0:T(4,128)S(1)} %all_to_all.11.got_ref, f32[22,16,8,128]{3,2,1,0:T(8,128)S(1)} %get-tuple-element.18.part_ref), custom_call_target="tpu_custom_call" | custom-call | flops 2000000 | bytes 3000000 | tf_op jit(solution)/shard_map/back/pallas_call | solution.py:427
  (1 shorter events, 0.0 us)
Async XLA Ops:
  0.0 14.2 %collective-permute-start = (f32[22,16,8,128]{3,2,1,0:T(8,128)}, f32[22,16,8,128]{3,2,1,0:T(8,128)S(1)}, u32[]{:S(2)}, u32[]{:S(2)}) collective-permute-start(f32[22,16,8,128]{3,2,1,0:T(8,128)} %adj_ref.5), channel_id=1, source_target_pairs={{0,1},{1,0},{2,3},{3,2},{4,5},{5,4},{6,7},{7,6},{8,9},{9,8},{10,11... | collective-permute-start | bytes 4325384 | tf_op jit(solution)/shard_map/ppermute | solution.py:452
  0.0 1.4 %copy-start = (f32[22,16,8,128]{3,2,1,0:T(8,128)S(1)}, f32[22,16,8,128]{3,2,1,0:T(8,128)}, u32[]{:S(2)}) copy-start(f32[22,16,8,128]{3,2,1,0:T(8,128)} %adj_ref.5) | copy-start | bytes 4325380
  1.4 2.7 %copy-start.1 = (f32[16,8,128]{2,1,0:T(8,128)S(1)}, f32[16,8,128]{2,1,0:T(8,128)}, u32[]{:S(2)}) copy-start(f32[16,8,128]{2,1,0:T(8,128)} %cond_ref.3) | copy-start | bytes 196612
  1.4 2.7 %copy-start.3 = (bf16[32,16,8,128]{3,2,1,0:T(8,128)(2,1)S(1)}, bf16[32,16,8,128]{3,2,1,0:T(8,128)(2,1)}, u32[]{:S(2)}) copy-start(bf16[32,16,8,128]{3,2,1,0:T(8,128)(2,1)} %conc_ref.1) | copy-start | bytes 3145732
  1.4 2.7 %copy-start.4 = (s32[16,8,128]{2,1,0:T(8,128)S(1)}, s32[16,8,128]{2,1,0:T(8,128)}, u32[]{:S(2)}) copy-start(s32[16,8,128]{2,1,0:T(8,128)} %lev_ref.1) | copy-start | bytes 196612
  1.4 2.7 %copy-start.5 = (bf16[206,32]{0,1:T(8,128)(2,1)S(1)}, bf16[206,32]{0,1:T(8,128)(2,1)}, u32[]{:S(2)}) copy-start(bf16[206,32]{0,1:T(8,128)(2,1)} %param.14) | copy-start | bytes 39556
  1.4 2.7 %copy-start.6 = (bf16[206,32]{0,1:T(8,128)(2,1)S(1)}, bf16[206,32]{0,1:T(8,128)(2,1)}, u32[]{:S(2)}) copy-start(bf16[206,32]{0,1:T(8,128)(2,1)} %param.15) | copy-start | bytes 39556
  1.4 2.7 %copy-start.7 = (bf16[206,22]{0,1:T(8,128)(2,1)S(1)}, bf16[206,22]{0,1:T(8,128)(2,1)}, u32[]{:S(2)}) copy-start(bf16[206,22]{0,1:T(8,128)(2,1)} %param.16) | copy-start | bytes 27196
  1.4 2.7 %copy-start.8 = (f32[206]{0:T(256)S(1)}, f32[206]{0:T(256)}, u32[]{:S(2)}) copy-start(f32[206]{0:T(256)} %param.17) | copy-start | bytes 2476
  1.4 2.7 %copy-start.9 = (f32[206]{0:T(256)S(1)}, f32[206]{0:T(256)}, u32[]{:S(2)}) copy-start(f32[206]{0:T(256)} %param.18) | copy-start | bytes 2476
  1.7 12.5 %collective-permute-start.1 = (f32[22,2,16,128]{3,2,1,0:T(8,128)S(1)}, f32[22,2,16,128]{3,2,1,0:T(8,128)S(1)}, u32[]{:S(2)}, u32[]{:S(2)}) collective-permute-start(f32[22,2,16,128]{3,2,1,0:T(8,128)S(1)} %get-tuple-element.14), channel_id=1, source_target_pairs={{0,2},{2,4},{4,6},{6,0},{1,3},{3,5},{5,7},{7,1},{8,10},{10,12},{12... | collective-permute-start | bytes 1081352 | tf_op jit(solution)/shard_map/ppermute | solution.py:454
  3.2 10.9 %collective-permute-start.2 = (f32[22,2,16,128]{3,2,1,0:T(8,128)S(1)}, f32[22,2,16,128]{3,2,1,0:T(8,128)S(1)}, u32[]{:S(2)}, u32[]{:S(2)}) collective-permute-start(f32[22,2,16,128]{3,2,1,0:T(8,128)S(1)} %get-tuple-element.15), channel_id=1, source_target_pairs={{2,0},{4,2},{6,4},{0,6},{3,1},{5,3},{7,5},{1,7},{10,8},{12,10},{14... | collective-permute-start | bytes 1081352 | tf_op jit(solution)/shard_map/ppermute | solution.py:455
  4.2 10.0 %copy-start.2 = (f32[22]{0:T(128)S(1)}, f32[22]{0:T(128)}, u32[]{:S(2)}) copy-start(f32[22]{0:T(128)} %diff_ref.1) | copy-start | bytes 268

commit v10 on v9

--- a/solution.py
+++ b/solution.py
@@ -1,5 +1,3 @@
-import math
-
 import jax
 import jax.numpy as jnp
 from jax import lax
@@ -12,10 +10,9 @@
 MASS = 0.001
 THIRD = MASS / 3.0
 BODY = MASS + 2.0 * THIRD
-LOG2E = math.log2(math.e)
 OFF = -1024.0
 
-K_ROWS = 96
+K_ROWS = 64
 R_PAD = 208
 STRIP = 16
 CHUNKS = tuple((start, STRIP) for start in range(0, R_PAD, STRIP))
@@ -47,7 +44,9 @@
     carried = st_ref.shape[0]
     eye = one_hot(iota((R_PAD, 256), 0) == iota((R_PAD, 256), 1))
     pick_row, pick_col = iota((32, 32), 0), iota((32, 32), 1)
-    pick = one_hot(pick_col == jnp.where(pick_row < 16, pick_row, jnp.where(pick_row < 24, pick_row - 2, -1)))
+    pick = one_hot(pick_col == jnp.where(
+        pick_row < 16, pick_row, jnp.where((pick_row > 17) & (pick_row < 24), pick_row - 2, -1)
+    ))
     sub, tier = iota((8, 256), 0), 4 * iota((8, 256), 1) // react
     full = []
     for index, (orders, rate) in enumerate(((of_ref, rf_ref), (or_ref, rr_ref))):
@@ -56,20 +55,16 @@
         plain = wide_ref[0:32, :]
         sign = 1.0 if index == 0 else -1.0
         c_ref[index] = (sign * dot(pick, plain.astype(BF16)))[:, 0:R_PAD].astype(BF16)
-        scaled = plain * LOG2E
-        hi = scaled.astype(BF16).astype(F32)
-        wide_ref[0:32, :] = hi
-        wide_ref[32:64, :] = scaled - hi
-        wide_ref[88:89, 0:react] = jnp.log(rate[...]) * LOG2E
-        r = jnp.broadcast_to(wide_ref[88:89, :], (8, 256))
+        wide_ref[56:57, 0:react] = jnp.log(rate[...])
+        r = jnp.broadcast_to(wide_ref[56:57, :], (8, 256))
         r0 = r.astype(BF16).astype(F32)
         r1 = (r - r0).astype(BF16).astype(F32)
         parts = jnp.where(sub == 3, r0, jnp.where(sub == 4, r1, jnp.where(sub == 5, r - r0 - r1, 0.0)))
-        wide_ref[88:96, :] = jnp.where(sub < 3, jnp.where(tier > sub, OFF, 0.0), parts)
+        wide_ref[56:64, :] = jnp.where(sub < 3, jnp.where(tier > sub, OFF, 0.0), parts)
         full.append(dot_nt(eye, wide_ref[...].astype(BF16)).astype(BF16))
     wide_ref[...] = jnp.zeros(wide_ref.shape, F32)
-    wide_ref[64:80, 0:react] = st_ref[0:16, :].astype(F32)
-    wide_ref[82 : 66 + carried, 0:react] = st_ref[16:carried, :].astype(F32)
+    wide_ref[32:48, 0:react] = st_ref[0:16, :].astype(F32)
+    wide_ref[50 : 34 + carried, 0:react] = st_ref[16:carried, :].astype(F32)
     full.append(dot_nt(eye, wide_ref[...].astype(BF16)).astype(BF16))
     base = 0
     for start, size in CHUNKS:
@@ -80,7 +75,7 @@
 
 def chem_kernel(
     adj_ref, conc_ref, lev_ref, cond_ref, of_ref, or_ref, st_ref, rf_ref, rr_ref,
-    out_ref, coef_ref, tail_ref,
+    out_ref, spread_ref, coef_ref, tail_ref,
     wide_ref, w_ref, c_ref, conc32_ref, x_ref, act_ref, run_ref,
 ):
     step = pl.program_id(0)
@@ -120,11 +115,22 @@
                 [conc32_ref[pl.ds(row + 8 * q * pitch, 8, stride=pitch), :] for q in range(4)], axis=0
             ).astype(BF16)
             x_ref[0:32, cols] = conc
-            x_ref[32:64, cols] = conc
             lam = [adj_rows[pl.ds(row + first * pitch, 8, stride=pitch), :] for first in (0, 8, carried - 8)]
             level = jnp.broadcast_to(lev_ref[x, y : y + 1, :], (8, nz))
             marks = jnp.where(level <= sub, 1.0, 0.0)
-            x_ref[64:96, cols] = jnp.concatenate(lam + [marks], axis=0).astype(BF16)
+            x_ref[32:64, cols] = jnp.concatenate(lam + [marks], axis=0).astype(BF16)
+    lane = iota((ny, nz), 1)
+    for x in range(xb):
+        for k in range(carried):
+            own = adj_ref[k, x]
+            near = pltpu.roll(own, ny - 1, 0) + pltpu.roll(own, 1, 0)
+            near = near + jnp.where(lane == nz - 1, 0.0, pltpu.roll(own, nz - 1, 1))
+            near = near + jnp.where(lane == 0, 0.0, pltpu.roll(own, 1, 1))
+            far = pltpu.roll(own, ny - 2, 0) + pltpu.roll(own, 2, 0)
+            far = far + jnp.where(lane >= nz - 2, 0.0, pltpu.roll(own, nz - 2, 1))
+            far = far + jnp.where(lane < 2, 0.0, pltpu.roll(own, 2, 1))
+            out_ref[k, x] = SECTION * own
+            spread_ref[k, x] = 16.0 * near - far - 60.0 * own
     per_tile = TILE // nz
     for tile in range(xb * ny // per_tile):
         slot = tile % act_ref.shape[0]
@@ -132,15 +138,15 @@
         for start, size in CHUNKS:
             got = every[3 * start : 3 * (start + size)]
             weight = got[2 * size :]
-            act_ref[slot, 0, start : start + size, :] = (jnp.exp2(got[:size]) * weight).astype(BF16)
-            act_ref[slot, 1, start : start + size, :] = (jnp.exp2(got[size : 2 * size]) * weight).astype(BF16)
+            act_ref[slot, 0, start : start + size, :] = (jnp.exp(got[:size]) * weight).astype(BF16)
+            act_ref[slot, 1, start : start + size, :] = (jnp.exp(got[size : 2 * size]) * weight).astype(BF16)
         chem = dot(c_ref[0], act_ref[slot, 0]) + dot(c_ref[1], act_ref[slot, 1])
         for part in range(per_tile):
             row = tile * per_tile + part
             for q, first in enumerate((0, 8, carried - 8)):
-                out_rows[pl.ds(row + first * pitch, 8, stride=pitch), :] = chem[
-                    8 * q : 8 * q + 8, part * nz : (part + 1) * nz
-                ]
+                at = pl.ds(row + first * pitch, 8, stride=pitch)
+                term = chem[8 * q : 8 * q + 8, part * nz : (part + 1) * nz]
+                out_rows[at, :] = out_rows[at, :] + (SECTION * STEP) * term
 
 
 def chemistry(adjoint, log_conc, levels, conduct, orders_fwd, orders_rev, stoich, rate_fwd, rate_rev):
@@ -158,13 +164,13 @@
             whole(conduct),
         ]
         + [whole(a) for a in small],
-        out_specs=[
-            pl.BlockSpec((carried, XB, ny, nz), lambda i: (0, i, 0, 0)),
+        out_specs=[pl.BlockSpec((carried, XB, ny, nz), lambda i: (0, i, 0, 0))] * 2
+        + [
             pl.BlockSpec((3, nx + 1, ny, nz), lambda i: (0, 0, 0, 0)),
             pl.BlockSpec((nx + 1, 3, ny, nz), lambda i: (0, 0, 0, 0)),
         ],
-        out_shape=[
-            jax.ShapeDtypeStruct(adjoint.shape, F32),
+        out_shape=[jax.ShapeDtypeStruct(adjoint.shape, F32)] * 2
+        + [
             jax.ShapeDtypeStruct((3, nx + 1, ny, nz), F32),
             jax.ShapeDtypeStruct((nx + 1, 3, ny, nz), F32),
         ],
@@ -232,14 +238,9 @@
     )(adjoint)
 
 
-def split(value):
-    high = value.astype(BF16)
-    return high, (value - high.astype(F32)).astype(BF16)
-
-
 def local_kernel(
-    diff_ref, cond_ref, adj_ref, chem_ref, near_ref, low_ref, high_ref, coef_ref, tail_ref,
-    part_ref, msg_ref, band_ref, parts_ref, zz_ref,
+    diff_ref, cond_ref, adj_ref, base_ref, spread_ref, near_ref, low_ref, high_ref, coef_ref, tail_ref,
+    part_ref, msg_ref, add_ref,
 ):
     nx, ny, nz = cond_ref.shape
     carried = adj_ref.shape[0]
@@ -251,11 +252,7 @@
         for r, value in ((6, tail_ref[at, 0]), (7, tail_ref[at, 1]), (14, face), (15, tail_ref[at, 2])):
             msg_ref[pl.ds(group * ROWS + r, ny, stride=stride), :] = value
 
-    k, z = iota((2 * nz, nz), 0), iota((2 * nz, nz), 1)
-    gap = jnp.abs(jnp.where(k < nz, k, k - nz) - z)
-    band_ref[...] = jnp.where(
-        gap == 0, -60.0, jnp.where(gap == 1, 16.0, jnp.where(gap == 2, -1.0, 0.0))
-    ).astype(BF16)
+    add_ref[...] = jnp.zeros(add_ref.shape, F32)
     lane = iota((ny, nz), 1)
     low_core = lax.axis_index("gz") == 0
     turn1, turn2 = jnp.where(low_core, nz - 1, 1), jnp.where(low_core, nz - 2, 2)
@@ -263,11 +260,6 @@
 
     @pl.loop(0, carried // LB)
     def _(g):
-        for t in range(LB):
-            s = g * LB + t
-            own_hi, own_lo = split(adj_ref[s].reshape(nx * ny, nz))
-            parts_ref[t * nx * ny : (t + 1) * nx * ny, :] = jnp.concatenate([own_hi, own_lo], axis=1)
-        zz_ref[...] = dot(parts_ref[...], band_ref[...])
         for t in range(LB):
             s = g * LB + t
             down, up = crossing(adj_ref, s)
@@ -277,22 +269,17 @@
                 (ny - 2, up[0], high_ref[s, 0]),
                 (ny - 1, up[1], high_ref[s, 1]),
             ):
-                at = pl.ds(t * nx * ny + r, nx, stride=ny)
-                zz_ref[at, :] = zz_ref[at, :] + (got - own_term)
+                add_ref[pl.ds(t * nx * ny + r, nx, stride=ny), :] = got - own_term
         for t in range(LB):
             s = g * LB + t
             scale = diff_ref[s] * (SECTION * STEP / 12.0)
             b_first, carry = None, None
             for p in range(nx):
-                own = adj_ref[s, p]
-                y_near = pltpu.roll(own, ny - 1, 0) + pltpu.roll(own, 1, 0)
-                y_far = pltpu.roll(own, ny - 2, 0) + pltpu.roll(own, 2, 0)
                 near = near_ref[s, p]
                 near1, near2 = pltpu.roll(near, turn1, 1), pltpu.roll(near, turn2, 1)
                 edge = jnp.where(lane == outer, 16.0 * near1 - near2, jnp.where(lane == inner, -near2, 0.0))
                 at = (t * nx + p) * ny
-                spread = 16.0 * y_near - y_far + (zz_ref[at : at + ny, :] + edge)
-                b = SECTION * own + (SECTION * STEP) * chem_ref[s, p] + scale * spread
+                b = base_ref[s, p] + scale * (spread_ref[s, p] + add_ref[at : at + ny, :] + edge)
                 if p == 0:
                     b_first = b
                 elif p < nx - 1:
@@ -306,22 +293,22 @@
             msg_ref[pl.ds(place(s) + 8, ny, stride=stride), :] = b_last
 
 
-def local_part(diffusivity, adjoint, chem, near, low, high, conduct, coef, ends):
+def local_part(diffusivity, adjoint, chem, spread, near, low, high, conduct, coef, ends):
     carried, nx, ny, nz = adjoint.shape
     smem = pl.BlockSpec(memory_space=pltpu.SMEM)
     return pl.pallas_call(
         local_kernel,
-        in_specs=[smem] + [WHOLE] * 8,
+        in_specs=[smem] + [WHOLE] * 9,
         out_specs=[WHOLE] * 2,
         out_shape=[
             pltpu.VMEM(adjoint.shape, F32),
             pltpu.VMEM((GROUPS * ny * ROWS, nz), F32),
         ],
-        scratch_shapes=[pltpu.VMEM((2 * nz, nz), BF16), pltpu.VMEM((LB * nx * ny, 2 * nz), BF16), pltpu.VMEM((LB * nx * ny, nz), F32)],
+        scratch_shapes=[pltpu.VMEM((LB * nx * ny, nz), F32)],
         compiler_params=SMALL,
         cost_estimate=pl.CostEstimate(flops=20 * 10**6, bytes_accessed=7 * 10**6, transcendentals=0),
         name="local",
-    )(diffusivity, conduct, adjoint, chem, near, low, high, coef, ends)
+    )(diffusivity, conduct, adjoint, chem, spread, near, low, high, coef, ends)
 
 
 def chain_kernel(in_ref, out_ref):
@@ -440,10 +427,6 @@
     )(coef, ends, part)
 
 
-def resident(value):
-    return pltpu.with_memory_space_constraint(value, pltpu.VMEM)
-
-
 def shards(
     adjoint, log_conc, levels, conduct, orders_fwd, orders_rev, stoich, rate_fwd, rate_rev, diffusivity
 ):
@@ -453,8 +436,10 @@
     tail, head = edges(adjoint)
     low = lax.ppermute(tail, "gy", [(i, (i + 1) % rows_y) for i in range(rows_y)])
     high = lax.ppermute(head, "gy", [((i + 1) % rows_y, i) for i in range(rows_y)])
-    chem, coef, ends_m = chemistry(adjoint, log_conc, levels, conduct, orders_fwd, orders_rev, stoich, rate_fwd, rate_rev)
-    part, message = local_part(diffusivity, adjoint, chem, near, low, high, conduct, coef, ends_m)
+    chem, spread, coef, ends_m = chemistry(
+        adjoint, log_conc, levels, conduct, orders_fwd, orders_rev, stoich, rate_fwd, rate_rev
+    )
+    part, message = local_part(diffusivity, adjoint, chem, spread, near, low, high, conduct, coef, ends_m)
     message = lax.all_to_all(message.reshape(blocks, ROWS, nz), "gx", 0, 0, tiled=True)
     ends = lax.all_to_all(chain(message), "gx", 0, 0, tiled=True)
     return back(part, coef, ends)

time: 57.5 us -> 58 us (level)
    pallas_call x1, Pallas kernels: 9.96 us -> 11.2 us  [chemistry(): pl.pallas_call(chem_kernel, grid=(nx // XB,), in_specs=[pl.BlockSpec((car...]
    pallas_call x1, Pallas kernels: 2.55 us -> 1.75 us  [local_part(): pl.pallas_call(local_kernel, in_specs=[smem] + [WHOLE] * 9, out_specs=[WH...]
  transfers between devices with their start and end apart: 3 -> 3, of which waited for: 0 -> 0; matrix products, arithmetic and copies ran while one was open for 0% -> 0% of each run, Pallas kernels for 18% -> 20%
where the time goes in v10:
time: 58 us; the launch traced here: 57.8 us
  blocking collectives  38.9 us (67%)
  Pallas kernels  14.9 us (26%)
  starting transfers between devices  2.44 us (4%)
  local copies, waits for them, and re-layouts  1.4 us (2%)
    all_to_all x1, blocking collectives, shards(): lax.all_to_all(message.reshape(blocks, ROWS, nz), 'gx', 0, 0, tiled=True)  23.7 us
    all_to_all x1, blocking collectives, shards(): ends = lax.all_to_all(chain(message), 'gx', 0, 0, tiled=True)  15.2 us
    pallas_call x1, Pallas kernels, chemistry(): pl.pallas_call(chem_kernel, grid=(nx // XB,), in_specs=[pl.BlockSpec((car...  11.2 us
    pallas_call x1, Pallas kernels, local_part(): pl.pallas_call(local_kernel, in_specs=[smem] + [WHOLE] * 9, out_specs=[WH...  1.75 us
    ppermute x1, starting transfers between devices, shards(): lax.ppermute(tail, 'gy', [(i, (i + 1) % rows_y) for i in range(rows_y)])  1.57 us
    pallas_call x1, Pallas kernels, back(): pl.pallas_call(back_kernel, in_specs=[WHOLE, WHOLE, WHOLE], out_specs=ANY...  1.43 us
    unnamed x20, local copies, waits for them, and re-layouts  1.4 us
  transfers between devices with their start and end apart: 3, of which 0 were waited for; matrix products, arithmetic and copies ran while one was open for 0% of the time, Pallas kernels for 20%

profile of v10, /device:TPU:2, one launch (start us, length us, event | category | flops | bytes accessed | tf_op | source)
XLA Modules:
  0.0 57.8 jit_solution(5800854218245851344)
XLA Ops:
  0.0 0.0 collective-permute-start
  0.0 0.0 copy-start
  0.0 1.4 %copy-done = f32[22,16,8,128]{3,2,1,0:T(8,128)S(1)} copy-done((f32[22,16,8,128]{3,2,1,0:T(8,128)S(1)}, f32[22,16,8,128]{3,2,1,0:T(8,128)}, u32[]{:S(2)}) %copy-start) | copy-done | bytes 1441816
  1.4 0.0 copy-start.1
  1.4 0.0 copy-start.3
  1.4 0.0 copy-start.4
  1.4 0.0 copy-start.6
  1.4 0.0 copy-start.7
  1.4 0.0 copy-start.8
  1.4 0.0 copy-start.9
  1.4 0.2 edges.1
  1.7 1.6 %collective-permute-start.1 = (f32[22,2,16,128]{3,2,1,0:T(8,128)S(1)}, f32[22,2,16,128]{3,2,1,0:T(8,128)S(1)}, u32[]{:S(2)}, u32[]{:S(2)}) collective-permute-start(f32[22,2,16,128]{3,2,1,0:T(8,128)S(1)} %get-tuple-element.16), channel_id=1, source_target_pairs={{0,2},{2,4},{4,6},{6,0},{1,3},{3,5},{5,7},{7,1},{8,10},{10,12},{12... | collective-permute-start | bytes 1081352 | tf_op jit(solution)/shard_map/ppermute | solution.py:437
  3.2 0.9 %collective-permute-start.2 = (f32[22,2,16,128]{3,2,1,0:T(8,128)S(1)}, f32[22,2,16,128]{3,2,1,0:T(8,128)S(1)}, u32[]{:S(2)}, u32[]{:S(2)}) collective-permute-start(f32[22,2,16,128]{3,2,1,0:T(8,128)S(1)} %get-tuple-element.17), channel_id=1, source_target_pairs={{2,0},{4,2},{6,4},{0,6},{3,1},{5,3},{7,5},{1,7},{10,8},{12,10},{14... | collective-permute-start | bytes 1081352 | tf_op jit(solution)/shard_map/ppermute | solution.py:438
  4.1 0.0 copy-done.1
  4.1 0.0 copy-done.3
  4.1 0.0 copy-done.4
  4.1 0.0 copy-done.5
  4.1 0.0 copy-done.6
  4.1 0.0 copy-done.7
  4.1 0.0 copy-done.8
  4.2 0.0 copy-done.9
  4.2 0.0 copy-start.2
  4.2 11.2 %chem.1 = (f32[22,16,8,128]{3,2,1,0:T(8,128)S(1)}, f32[22,16,8,128]{3,2,1,0:T(8,128)S(1)}, f32[3,17,8,128]{3,2,1,0:T(8,128)S(1)}, f32[17,3,8,128]{3,2,1,0:T(8,128)S(1)}) custom-call(f32[22,16,8,128]{3,2,1,0:T(8,128)S(1)} %copy-done, bf16[32,16,8,128]{3,2,1,0:T(8,128)(2,1)S(1)} %copy-done.3, s32[16,8,128]{2,1,0:T(8,128)S(1)} %copy-done.4, ...), custom_call_target="tpu_custom_call" | custom-call | flops 12000000000 | bytes 4000000 | tf_op jit(solution)/shard_map/chem/pallas_call | solution.py:157
  15.4 0.0 collective-permute-done.1.low_ref
  15.4 0.0 collective-permute-done.2.high_ref
  15.4 0.0 collective-permute-done.near_ref
  15.4 0.0 copy-done.2
  15.4 1.7 %local.1 = (f32[22,16,8,128]{3,2,1,0:T(8,128)S(1)}, f32[512,128]{1,0:T(8,128)S(1)}) custom-call(f32[22]{0:T(128)S(1)} %copy-done.2, f32[16,8,128]{2,1,0:T(8,128)S(1)} %copy-done.1, f32[22,16,8,128]{3,2,1,0:T(8,128)S(1)} %copy-done, f32[22,16,8,128]{3,2,1,0:T(8,128)S(1)} %get-tuple-element.14.base_ref, f32[22,16,8,128]{3,2,1,0:T(8,128)S(1)} %get-tuple-element.15.spread_ref, ...), custom_call_target="tpu_custom_call" | custom-call | flops 20000000 | bytes 7000000 | tf_op jit(solution)/shard_map/local/pallas_call | solution.py:299
  17.2 23.7 %all_to_all.10.in_ref = f32[32,16,128]{2,1,0:T(8,128)S(1)} all-to-all(f32[32,16,128]{2,1,0:T(8,128)S(1)} %bitcast.6), channel_id=1, replica_groups=mesh['gx'=32,'gy'=4,'gz'=2] {'gx'}, dimensions={0} | all-to-all | bytes 524288 | tf_op jit(solution)/shard_map/all_to_all | solution.py:443
  40.9 0.2 chain.1
  41.2 15.2 %all_to_all.11.got_ref = f32[32,3,4,128]{3,2,1,0:T(4,128)S(1)} all-to-all(f32[32,3,4,128]{3,2,1,0:T(4,128)S(1)} %chain.1), channel_id=1, replica_groups=mesh['gx'=32,'gy'=4,'gz'=2] {'gx'}, dimensions={0} | all-to-all | bytes 393216 | tf_op jit(solution)/shard_map/all_to_all | solution.py:444
  56.3 1.4 %back.1 = f32[22,16,8,128]{3,2,1,0:T(8,128)} custom-call(f32[3,17,8,128]{3,2,1,0:T(8,128)S(1)} %get-tuple-element.13.coef_ref, f32[32,3,4,128]{3,2,1,0:T(4,128)S(1)} %all_to_all.11.got_ref, f32[22,16,8,128]{3,2,1,0:T(8,128)S(1)} %get-tuple-element.20.part_ref), custom_call_target="tpu_custom_call" | custom-call | flops 2000000 | bytes 3000000 | tf_op jit(solution)/shard_map/back/pallas_call | solution.py:414
  (1 shorter events, 0.0 us)
Async XLA Ops:
  0.0 15.4 %collective-permute-start = (f32[22,16,8,128]{3,2,1,0:T(8,128)}, f32[22,16,8,128]{3,2,1,0:T(8,128)S(1)}, u32[]{:S(2)}, u32[]{:S(2)}) collective-permute-start(f32[22,16,8,128]{3,2,1,0:T(8,128)} %adj_ref.5), channel_id=1, source_target_pairs={{0,1},{1,0},{2,3},{3,2},{4,5},{5,4},{6,7},{7,6},{8,9},{9,8},{10,11... | collective-permute-start | bytes 4325384 | tf_op jit(solution)/shard_map/ppermute | solution.py:435
  0.0 1.4 %copy-start = (f32[22,16,8,128]{3,2,1,0:T(8,128)S(1)}, f32[22,16,8,128]{3,2,1,0:T(8,128)}, u32[]{:S(2)}) copy-start(f32[22,16,8,128]{3,2,1,0:T(8,128)} %adj_ref.5) | copy-start | bytes 4325380
  1.4 2.7 %copy-start.1 = (f32[16,8,128]{2,1,0:T(8,128)S(1)}, f32[16,8,128]{2,1,0:T(8,128)}, u32[]{:S(2)}) copy-start(f32[16,8,128]{2,1,0:T(8,128)} %cond_ref.3) | copy-start | bytes 196612
  1.4 2.7 %copy-start.3 = (bf16[32,16,8,128]{3,2,1,0:T(8,128)(2,1)S(1)}, bf16[32,16,8,128]{3,2,1,0:T(8,128)(2,1)}, u32[]{:S(2)}) copy-start(bf16[32,16,8,128]{3,2,1,0:T(8,128)(2,1)} %conc_ref.1) | copy-start | bytes 3145732
  1.4 2.7 %copy-start.4 = (s32[16,8,128]{2,1,0:T(8,128)S(1)}, s32[16,8,128]{2,1,0:T(8,128)}, u32[]{:S(2)}) copy-start(s32[16,8,128]{2,1,0:T(8,128)} %lev_ref.1) | copy-start | bytes 196612
  1.4 2.7 %copy-start.5 = (bf16[206,32]{0,1:T(8,128)(2,1)S(1)}, bf16[206,32]{0,1:T(8,128)(2,1)}, u32[]{:S(2)}) copy-start(bf16[206,32]{0,1:T(8,128)(2,1)} %param.14) | copy-start | bytes 39556
  1.4 2.7 %copy-start.6 = (bf16[206,32]{0,1:T(8,128)(2,1)S(1)}, bf16[206,32]{0,1:T(8,128)(2,1)}, u32[]{:S(2)}) copy-start(bf16[206,32]{0,1:T(8,128)(2,1)} %param.15) | copy-start | bytes 39556
  1.4 2.7 %copy-start.7 = (bf16[206,22]{0,1:T(8,128)(2,1)S(1)}, bf16[206,22]{0,1:T(8,128)(2,1)}, u32[]{:S(2)}) copy-start(bf16[206,22]{0,1:T(8,128)(2,1)} %param.16) | copy-start | bytes 27196
  1.4 2.7 %copy-start.8 = (f32[206]{0:T(256)S(1)}, f32[206]{0:T(256)}, u32[]{:S(2)}) copy-start(f32[206]{0:T(256)} %param.17) | copy-start | bytes 2476
  1.4 2.7 %copy-start.9 = (f32[206]{0:T(256)S(1)}, f32[206]{0:T(256)}, u32[]{:S(2)}) copy-start(f32[206]{0:T(256)} %param.18) | copy-start | bytes 2476
  1.7 13.7 %collective-permute-start.1 = (f32[22,2,16,128]{3,2,1,0:T(8,128)S(1)}, f32[22,2,16,128]{3,2,1,0:T(8,128)S(1)}, u32[]{:S(2)}, u32[]{:S(2)}) collective-permute-start(f32[22,2,16,128]{3,2,1,0:T(8,128)S(1)} %get-tuple-element.16), channel_id=1, source_target_pairs={{0,2},{2,4},{4,6},{6,0},{1,3},{3,5},{5,7},{7,1},{8,10},{10,12},{12... | collective-permute-start | bytes 1081352 | tf_op jit(solution)/shard_map/ppermute | solution.py:437
  3.2 12.2 %collective-permute-start.2 = (f32[22,2,16,128]{3,2,1,0:T(8,128)S(1)}, f32[22,2,16,128]{3,2,1,0:T(8,128)S(1)}, u32[]{:S(2)}, u32[]{:S(2)}) collective-permute-start(f32[22,2,16,128]{3,2,1,0:T(8,128)S(1)} %get-tuple-element.17), channel_id=1, source_target_pairs={{2,0},{4,2},{6,4},{0,6},{3,1},{5,3},{7,5},{1,7},{10,8},{12,10},{14... | collective-permute-start | bytes 1081352 | tf_op jit(solution)/shard_map/ppermute | solution.py:438
  4.2 11.3 %copy-start.2 = (f32[22]{0:T(128)S(1)}, f32[22]{0:T(128)}, u32[]{:S(2)}) copy-start(f32[22]{0:T(128)} %diff_ref.1) | copy-start | bytes 268

commit v11 on v10

--- a/solution.py
+++ b/solution.py
@@ -45,7 +45,7 @@
     eye = one_hot(iota((R_PAD, 256), 0) == iota((R_PAD, 256), 1))
     pick_row, pick_col = iota((32, 32), 0), iota((32, 32), 1)
     pick = one_hot(pick_col == jnp.where(
-        pick_row < 16, pick_row, jnp.where((pick_row > 17) & (pick_row < 24), pick_row - 2, -1)
+        pick_row < 16, pick_row, jnp.where(pick_row < 24, pick_row - 2, -1)
     ))
     sub, tier = iota((8, 256), 0), 4 * iota((8, 256), 1) // react
     full = []
@@ -75,7 +75,7 @@
 
 def chem_kernel(
     adj_ref, conc_ref, lev_ref, cond_ref, of_ref, or_ref, st_ref, rf_ref, rr_ref,
-    out_ref, spread_ref, coef_ref, tail_ref,
+    out_ref, coef_ref, tail_ref,
     wide_ref, w_ref, c_ref, conc32_ref, x_ref, act_ref, run_ref,
 ):
     step = pl.program_id(0)
@@ -119,18 +119,6 @@
             level = jnp.broadcast_to(lev_ref[x, y : y + 1, :], (8, nz))
             marks = jnp.where(level <= sub, 1.0, 0.0)
             x_ref[32:64, cols] = jnp.concatenate(lam + [marks], axis=0).astype(BF16)
-    lane = iota((ny, nz), 1)
-    for x in range(xb):
-        for k in range(carried):
-            own = adj_ref[k, x]
-            near = pltpu.roll(own, ny - 1, 0) + pltpu.roll(own, 1, 0)
-            near = near + jnp.where(lane == nz - 1, 0.0, pltpu.roll(own, nz - 1, 1))
-            near = near + jnp.where(lane == 0, 0.0, pltpu.roll(own, 1, 1))
-            far = pltpu.roll(own, ny - 2, 0) + pltpu.roll(own, 2, 0)
-            far = far + jnp.where(lane >= nz - 2, 0.0, pltpu.roll(own, nz - 2, 1))
-            far = far + jnp.where(lane < 2, 0.0, pltpu.roll(own, 2, 1))
-            out_ref[k, x] = SECTION * own
-            spread_ref[k, x] = 16.0 * near - far - 60.0 * own
     per_tile = TILE // nz
     for tile in range(xb * ny // per_tile):
         slot = tile % act_ref.shape[0]
@@ -144,9 +132,9 @@
         for part in range(per_tile):
             row = tile * per_tile + part
             for q, first in enumerate((0, 8, carried - 8)):
-                at = pl.ds(row + first * pitch, 8, stride=pitch)
-                term = chem[8 * q : 8 * q + 8, part * nz : (part + 1) * nz]
-                out_rows[at, :] = out_rows[at, :] + (SECTION * STEP) * term
+                out_rows[pl.ds(row + first * pitch, 8, stride=pitch), :] = chem[
+                    8 * q : 8 * q + 8, part * nz : (part + 1) * nz
+                ]
 
 
 def chemistry(adjoint, log_conc, levels, conduct, orders_fwd, orders_rev, stoich, rate_fwd, rate_rev):
@@ -164,13 +152,13 @@
             whole(conduct),
         ]
         + [whole(a) for a in small],
-        out_specs=[pl.BlockSpec((carried, XB, ny, nz), lambda i: (0, i, 0, 0))] * 2
-        + [
+        out_specs=[
+            pl.BlockSpec((carried, XB, ny, nz), lambda i: (0, i, 0, 0)),
             pl.BlockSpec((3, nx + 1, ny, nz), lambda i: (0, 0, 0, 0)),
             pl.BlockSpec((nx + 1, 3, ny, nz), lambda i: (0, 0, 0, 0)),
         ],
-        out_shape=[jax.ShapeDtypeStruct(adjoint.shape, F32)] * 2
-        + [
+        out_shape=[
+            jax.ShapeDtypeStruct(adjoint.shape, F32),
             jax.ShapeDtypeStruct((3, nx + 1, ny, nz), F32),
             jax.ShapeDtypeStruct((nx + 1, 3, ny, nz), F32),
         ],
@@ -239,7 +227,7 @@
 
 
 def local_kernel(
-    diff_ref, cond_ref, adj_ref, base_ref, spread_ref, near_ref, low_ref, high_ref, coef_ref, tail_ref,
+    diff_ref, cond_ref, adj_ref, chem_ref, near_ref, low_ref, high_ref, coef_ref, tail_ref,
     part_ref, msg_ref, add_ref,
 ):
     nx, ny, nz = cond_ref.shape
@@ -254,9 +242,8 @@
 
     add_ref[...] = jnp.zeros(add_ref.shape, F32)
     lane = iota((ny, nz), 1)
-    low_core = lax.axis_index("gz") == 0
-    turn1, turn2 = jnp.where(low_core, nz - 1, 1), jnp.where(low_core, nz - 2, 2)
-    outer, inner = jnp.where(low_core, nz - 1, 0), jnp.where(low_core, nz - 2, 1)
+    keep_low = jnp.where(lax.axis_index("gz") == 0, 1.0, 0.0)
+    keep_high = 1.0 - keep_low
 
     @pl.loop(0, carried // LB)
     def _(g):
@@ -275,11 +262,17 @@
             scale = diff_ref[s] * (SECTION * STEP / 12.0)
             b_first, carry = None, None
             for p in range(nx):
-                near = near_ref[s, p]
-                near1, near2 = pltpu.roll(near, turn1, 1), pltpu.roll(near, turn2, 1)
-                edge = jnp.where(lane == outer, 16.0 * near1 - near2, jnp.where(lane == inner, -near2, 0.0))
+                own, near = adj_ref[s, p], near_ref[s, p]
+                above, below = near * keep_low, near * keep_high
+                close = pltpu.roll(own, ny - 1, 0) + pltpu.roll(own, 1, 0)
+                close = close + pltpu.roll(jnp.where(lane < 1, above, own), nz - 1, 1)
+                close = close + pltpu.roll(jnp.where(lane >= nz - 1, below, own), 1, 1)
+                far = pltpu.roll(own, ny - 2, 0) + pltpu.roll(own, 2, 0)
+                far = far + pltpu.roll(jnp.where(lane < 2, above, own), nz - 2, 1)
+                far = far + pltpu.roll(jnp.where(lane >= nz - 2, below, own), 2, 1)
                 at = (t * nx + p) * ny
-                b = base_ref[s, p] + scale * (spread_ref[s, p] + add_ref[at : at + ny, :] + edge)
+                spread = 16.0 * close - far - 60.0 * own + add_ref[at : at + ny, :]
+                b = SECTION * own + (SECTION * STEP) * chem_ref[s, p] + scale * spread
                 if p == 0:
                     b_first = b
                 elif p < nx - 1:
@@ -293,12 +286,12 @@
             msg_ref[pl.ds(place(s) + 8, ny, stride=stride), :] = b_last
 
 
-def local_part(diffusivity, adjoint, chem, spread, near, low, high, conduct, coef, ends):
+def local_part(diffusivity, adjoint, chem, near, low, high, conduct, coef, ends):
     carried, nx, ny, nz = adjoint.shape
     smem = pl.BlockSpec(memory_space=pltpu.SMEM)
     return pl.pallas_call(
         local_kernel,
-        in_specs=[smem] + [WHOLE] * 9,
+        in_specs=[smem] + [WHOLE] * 8,
         out_specs=[WHOLE] * 2,
         out_shape=[
             pltpu.VMEM(adjoint.shape, F32),
@@ -308,7 +301,7 @@
         compiler_params=SMALL,
         cost_estimate=pl.CostEstimate(flops=20 * 10**6, bytes_accessed=7 * 10**6, transcendentals=0),
         name="local",
-    )(diffusivity, conduct, adjoint, chem, spread, near, low, high, coef, ends)
+    )(diffusivity, conduct, adjoint, chem, near, low, high, coef, ends)
 
 
 def chain_kernel(in_ref, out_ref):
@@ -436,10 +429,10 @@
     tail, head = edges(adjoint)
     low = lax.ppermute(tail, "gy", [(i, (i + 1) % rows_y) for i in range(rows_y)])
     high = lax.ppermute(head, "gy", [((i + 1) % rows_y, i) for i in range(rows_y)])
-    chem, spread, coef, ends_m = chemistry(
+    chem, coef, ends_m = chemistry(
         adjoint, log_conc, levels, conduct, orders_fwd, orders_rev, stoich, rate_fwd, rate_rev
     )
-    part, message = local_part(diffusivity, adjoint, chem, spread, near, low, high, conduct, coef, ends_m)
+    part, message = local_part(diffusivity, adjoint, chem, near, low, high, conduct, coef, ends_m)
     message = lax.all_to_all(message.reshape(blocks, ROWS, nz), "gx", 0, 0, tiled=True)
     ends = lax.all_to_all(chain(message), "gx", 0, 0, tiled=True)
     return back(part, coef, ends)

time: 58 us -> 57.4 us (0.990)
    pallas_call x1, Pallas kernels: 11.2 us -> 10 us  [chemistry(): pl.pallas_call(chem_kernel, grid=(nx // XB,), in_specs=[pl.BlockSpec((car...]
    pallas_call x1, Pallas kernels: 1.75 us -> 2.45 us  [local_part(): pl.pallas_call(local_kernel, in_specs=[smem] + [WHOLE] * 8, out_specs=[WH...]
  transfers between devices with their start and end apart: 3 -> 3, of which waited for: 0 -> 0; matrix products, arithmetic and copies ran while one was open for 0% -> 0% of each run, Pallas kernels for 20% -> 18%
where the time goes in v11:
time: 57.4 us; the launch traced here: 57.3 us
  blocking collectives  38.9 us (68%)
  Pallas kernels  14.4 us (25%)
  starting transfers between devices  2.44 us (4%)
  local copies, waits for them, and re-layouts  1.4 us (2%)
    all_to_all x1, blocking collectives, shards(): lax.all_to_all(message.reshape(blocks, ROWS, nz), 'gx', 0, 0, tiled=True)  23.7 us
    all_to_all x1, blocking collectives, shards(): ends = lax.all_to_all(chain(message), 'gx', 0, 0, tiled=True)  15.2 us
    pallas_call x1, Pallas kernels, chemistry(): pl.pallas_call(chem_kernel, grid=(nx // XB,), in_specs=[pl.BlockSpec((car...  10 us
    pallas_call x1, Pallas kernels, local_part(): pl.pallas_call(local_kernel, in_specs=[smem] + [WHOLE] * 8, out_specs=[WH...  2.45 us
    ppermute x1, starting transfers between devices, shards(): lax.ppermute(tail, 'gy', [(i, (i + 1) % rows_y) for i in range(rows_y)])  1.57 us
    pallas_call x1, Pallas kernels, back(): pl.pallas_call(back_kernel, in_specs=[WHOLE, WHOLE, WHOLE], out_specs=ANY...  1.43 us
    unnamed x20, local copies, waits for them, and re-layouts  1.4 us
  transfers between devices with their start and end apart: 3, of which 0 were waited for; matrix products, arithmetic and copies ran while one was open for 0% of the time, Pallas kernels for 18%

profile of v11, /device:TPU:2, one launch (start us, length us, event | category | flops | bytes accessed | tf_op | source)
XLA Modules:
  0.0 57.3 jit_solution(5853059986704979409)
XLA Ops:
  0.0 0.0 collective-permute-start
  0.0 1.4 %copy-done = f32[22,16,8,128]{3,2,1,0:T(8,128)S(1)} copy-done((f32[22,16,8,128]{3,2,1,0:T(8,128)S(1)}, f32[22,16,8,128]{3,2,1,0:T(8,128)}, u32[]{:S(2)}) %copy-start) | copy-done | bytes 1441816
  1.4 0.0 copy-start.1
  1.4 0.0 copy-start.3
  1.4 0.0 copy-start.4
  1.4 0.0 copy-start.5
  1.4 0.0 copy-start.6
  1.4 0.0 copy-start.7
  1.4 0.0 copy-start.8
  1.4 0.0 copy-start.9
  1.4 0.2 edges.1
  1.7 1.6 %collective-permute-start.1 = (f32[22,2,16,128]{3,2,1,0:T(8,128)S(1)}, f32[22,2,16,128]{3,2,1,0:T(8,128)S(1)}, u32[]{:S(2)}, u32[]{:S(2)}) collective-permute-start(f32[22,2,16,128]{3,2,1,0:T(8,128)S(1)} %get-tuple-element.14), channel_id=1, source_target_pairs={{0,2},{2,4},{4,6},{6,0},{1,3},{3,5},{5,7},{7,1},{8,10},{10,12},{12... | collective-permute-start | bytes 1081352 | tf_op jit(solution)/shard_map/ppermute | solution.py:430
  3.2 0.9 %collective-permute-start.2 = (f32[22,2,16,128]{3,2,1,0:T(8,128)S(1)}, f32[22,2,16,128]{3,2,1,0:T(8,128)S(1)}, u32[]{:S(2)}, u32[]{:S(2)}) collective-permute-start(f32[22,2,16,128]{3,2,1,0:T(8,128)S(1)} %get-tuple-element.15), channel_id=1, source_target_pairs={{2,0},{4,2},{6,4},{0,6},{3,1},{5,3},{7,5},{1,7},{10,8},{12,10},{14... | collective-permute-start | bytes 1081352 | tf_op jit(solution)/shard_map/ppermute | solution.py:431
  4.1 0.0 copy-done.1
  4.1 0.0 copy-done.3
  4.1 0.0 copy-done.4
  4.1 0.0 copy-done.5
  4.1 0.0 copy-done.6
  4.1 0.0 copy-done.7
  4.1 0.0 copy-done.8
  4.2 0.0 copy-done.9
  4.2 0.0 copy-start.2
  4.2 10.0 %chem.1 = (f32[22,16,8,128]{3,2,1,0:T(8,128)S(1)}, f32[3,17,8,128]{3,2,1,0:T(8,128)S(1)}, f32[17,3,8,128]{3,2,1,0:T(8,128)S(1)}) custom-call(f32[22,16,8,128]{3,2,1,0:T(8,128)S(1)} %copy-done, bf16[32,16,8,128]{3,2,1,0:T(8,128)(2,1)S(1)} %copy-done.3, s32[16,8,128]{2,1,0:T(8,128)S(1)} %copy-done.4, f32[16,8,128]{2,1,0:T(8,128)S(1)} %copy-done.1, ...), custom_call_target="tpu_custom_call" | custom-call | flops 12000000000 | bytes 4000000 | tf_op jit(solution)/shard_map/chem/pallas_call | solution.py:145
  14.2 0.0 collective-permute-done.1.low_ref
  14.2 0.0 collective-permute-done.2.high_ref
  14.2 0.0 collective-permute-done.near_ref
  14.2 0.0 copy-done.2
  14.2 2.4 %local.1 = (f32[22,16,8,128]{3,2,1,0:T(8,128)S(1)}, f32[512,128]{1,0:T(8,128)S(1)}) custom-call(f32[22]{0:T(128)S(1)} %copy-done.2, f32[16,8,128]{2,1,0:T(8,128)S(1)} %copy-done.1, f32[22,16,8,128]{3,2,1,0:T(8,128)S(1)} %copy-done, f32[22,16,8,128]{3,2,1,0:T(8,128)S(1)} %get-tuple-element.13.chem_ref, f32[22,16,8,128]{3,2,1,0:T(8,128)S(1)} %collective-permute-done.near_ref, ...), custom_call_target="tpu_custom_call" | custom-call | flops 20000000 | bytes 7000000 | tf_op jit(solution)/shard_map/local/pallas_call | solution.py:292
  16.7 23.7 %all_to_all.10.in_ref = f32[32,16,128]{2,1,0:T(8,128)S(1)} all-to-all(f32[32,16,128]{2,1,0:T(8,128)S(1)} %bitcast.6), channel_id=1, replica_groups=mesh['gx'=32,'gy'=4,'gz'=2] {'gx'}, dimensions={0} | all-to-all | bytes 524288 | tf_op jit(solution)/shard_map/all_to_all | solution.py:436
  40.4 0.2 chain.1
  40.7 15.2 %all_to_all.11.got_ref = f32[32,3,4,128]{3,2,1,0:T(4,128)S(1)} all-to-all(f32[32,3,4,128]{3,2,1,0:T(4,128)S(1)} %chain.1), channel_id=1, replica_groups=mesh['gx'=32,'gy'=4,'gz'=2] {'gx'}, dimensions={0} | all-to-all | bytes 393216 | tf_op jit(solution)/shard_map/all_to_all | solution.py:437
  55.8 1.4 %back.1 = f32[22,16,8,128]{3,2,1,0:T(8,128)} custom-call(f32[3,17,8,128]{3,2,1,0:T(8,128)S(1)} %get-tuple-element.12.coef_ref, f32[32,3,4,128]{3,2,1,0:T(4,128)S(1)} %all_to_all.11.got_ref, f32[22,16,8,128]{3,2,1,0:T(8,128)S(1)} %get-tuple-element.18.part_ref), custom_call_target="tpu_custom_call" | custom-call | flops 2000000 | bytes 3000000 | tf_op jit(solution)/shard_map/back/pallas_call | solution.py:407
  (1 shorter events, 0.0 us)
Async XLA Ops:
  0.0 14.2 %collective-permute-start = (f32[22,16,8,128]{3,2,1,0:T(8,128)}, f32[22,16,8,128]{3,2,1,0:T(8,128)S(1)}, u32[]{:S(2)}, u32[]{:S(2)}) collective-permute-start(f32[22,16,8,128]{3,2,1,0:T(8,128)} %adj_ref.5), channel_id=1, source_target_pairs={{0,1},{1,0},{2,3},{3,2},{4,5},{5,4},{6,7},{7,6},{8,9},{9,8},{10,11... | collective-permute-start | bytes 4325384 | tf_op jit(solution)/shard_map/ppermute | solution.py:428
  0.0 1.4 %copy-start = (f32[22,16,8,128]{3,2,1,0:T(8,128)S(1)}, f32[22,16,8,128]{3,2,1,0:T(8,128)}, u32[]{:S(2)}) copy-start(f32[22,16,8,128]{3,2,1,0:T(8,128)} %adj_ref.5) | copy-start | bytes 4325380
  1.4 2.7 %copy-start.1 = (f32[16,8,128]{2,1,0:T(8,128)S(1)}, f32[16,8,128]{2,1,0:T(8,128)}, u32[]{:S(2)}) copy-start(f32[16,8,128]{2,1,0:T(8,128)} %cond_ref.3) | copy-start | bytes 196612
  1.4 2.7 %copy-start.3 = (bf16[32,16,8,128]{3,2,1,0:T(8,128)(2,1)S(1)}, bf16[32,16,8,128]{3,2,1,0:T(8,128)(2,1)}, u32[]{:S(2)}) copy-start(bf16[32,16,8,128]{3,2,1,0:T(8,128)(2,1)} %conc_ref.1) | copy-start | bytes 3145732
  1.4 2.7 %copy-start.4 = (s32[16,8,128]{2,1,0:T(8,128)S(1)}, s32[16,8,128]{2,1,0:T(8,128)}, u32[]{:S(2)}) copy-start(s32[16,8,128]{2,1,0:T(8,128)} %lev_ref.1) | copy-start | bytes 196612
  1.4 2.7 %copy-start.5 = (bf16[206,32]{0,1:T(8,128)(2,1)S(1)}, bf16[206,32]{0,1:T(8,128)(2,1)}, u32[]{:S(2)}) copy-start(bf16[206,32]{0,1:T(8,128)(2,1)} %param.14) | copy-start | bytes 39556
  1.4 2.7 %copy-start.6 = (bf16[206,32]{0,1:T(8,128)(2,1)S(1)}, bf16[206,32]{0,1:T(8,128)(2,1)}, u32[]{:S(2)}) copy-start(bf16[206,32]{0,1:T(8,128)(2,1)} %param.15) | copy-start | bytes 39556
  1.4 2.7 %copy-start.7 = (bf16[206,22]{0,1:T(8,128)(2,1)S(1)}, bf16[206,22]{0,1:T(8,128)(2,1)}, u32[]{:S(2)}) copy-start(bf16[206,22]{0,1:T(8,128)(2,1)} %param.16) | copy-start | bytes 27196
  1.4 2.7 %copy-start.8 = (f32[206]{0:T(256)S(1)}, f32[206]{0:T(256)}, u32[]{:S(2)}) copy-start(f32[206]{0:T(256)} %param.17) | copy-start | bytes 2476
  1.4 2.7 %copy-start.9 = (f32[206]{0:T(256)S(1)}, f32[206]{0:T(256)}, u32[]{:S(2)}) copy-start(f32[206]{0:T(256)} %param.18) | copy-start | bytes 2476
  1.7 12.5 %collective-permute-start.1 = (f32[22,2,16,128]{3,2,1,0:T(8,128)S(1)}, f32[22,2,16,128]{3,2,1,0:T(8,128)S(1)}, u32[]{:S(2)}, u32[]{:S(2)}) collective-permute-start(f32[22,2,16,128]{3,2,1,0:T(8,128)S(1)} %get-tuple-element.14), channel_id=1, source_target_pairs={{0,2},{2,4},{4,6},{6,0},{1,3},{3,5},{5,7},{7,1},{8,10},{10,12},{12... | collective-permute-start | bytes 1081352 | tf_op jit(solution)/shard_map/ppermute | solution.py:430
  3.2 11.0 %collective-permute-start.2 = (f32[22,2,16,128]{3,2,1,0:T(8,128)S(1)}, f32[22,2,16,128]{3,2,1,0:T(8,128)S(1)}, u32[]{:S(2)}, u32[]{:S(2)}) collective-permute-start(f32[22,2,16,128]{3,2,1,0:T(8,128)S(1)} %get-tuple-element.15), channel_id=1, source_target_pairs={{2,0},{4,2},{6,4},{0,6},{3,1},{5,3},{7,5},{1,7},{10,8},{12,10},{14... | collective-permute-start | bytes 1081352 | tf_op jit(solution)/shard_map/ppermute | solution.py:431
  4.2 10.1 %copy-start.2 = (f32[22]{0:T(128)S(1)}, f32[22]{0:T(128)}, u32[]{:S(2)}) copy-start(f32[22]{0:T(128)} %diff_ref.1) | copy-start | bytes 268

commit v12 on v11

--- a/solution.py
+++ b/solution.py
@@ -1,3 +1,5 @@
+import math
+
 import jax
 import jax.numpy as jnp
 from jax import lax
@@ -10,17 +12,22 @@
 MASS = 0.001
 THIRD = MASS / 3.0
 BODY = MASS + 2.0 * THIRD
+LOG2E = math.log2(math.e)
 OFF = -1024.0
 
-K_ROWS = 64
+K_ROWS = 96
 R_PAD = 208
 STRIP = 16
 CHUNKS = tuple((start, STRIP) for start in range(0, R_PAD, STRIP))
-TILE = 4096
 XB = 4
 LIMIT = 24 * 1024 * 1024
 F32 = jnp.float32
 BF16 = jnp.bfloat16
+
+
+ANY = pl.BlockSpec(memory_space=pl.ANY)
+WHOLE = pl.BlockSpec(memory_space=pltpu.VMEM)
+SMALL = pltpu.CompilerParams(vmem_limit_bytes=LIMIT)
 
 
 def iota(shape, dim):
@@ -44,9 +51,7 @@
     carried = st_ref.shape[0]
     eye = one_hot(iota((R_PAD, 256), 0) == iota((R_PAD, 256), 1))
     pick_row, pick_col = iota((32, 32), 0), iota((32, 32), 1)
-    pick = one_hot(pick_col == jnp.where(
-        pick_row < 16, pick_row, jnp.where(pick_row < 24, pick_row - 2, -1)
-    ))
+    pick = one_hot(pick_col == jnp.where(pick_row < 16, pick_row, jnp.where(pick_row < 24, pick_row - 2, -1)))
     sub, tier = iota((8, 256), 0), 4 * iota((8, 256), 1) // react
     full = []
     for index, (orders, rate) in enumerate(((of_ref, rf_ref), (or_ref, rr_ref))):
@@ -55,16 +60,20 @@
         plain = wide_ref[0:32, :]
         sign = 1.0 if index == 0 else -1.0
         c_ref[index] = (sign * dot(pick, plain.astype(BF16)))[:, 0:R_PAD].astype(BF16)
-        wide_ref[56:57, 0:react] = jnp.log(rate[...])
-        r = jnp.broadcast_to(wide_ref[56:57, :], (8, 256))
+        scaled = plain * LOG2E
+        hi = scaled.astype(BF16).astype(F32)
+        wide_ref[0:32, :] = hi
+        wide_ref[32:64, :] = scaled - hi
+        wide_ref[88:89, 0:react] = jnp.log(rate[...]) * LOG2E
+        r = jnp.broadcast_to(wide_ref[88:89, :], (8, 256))
         r0 = r.astype(BF16).astype(F32)
         r1 = (r - r0).astype(BF16).astype(F32)
         parts = jnp.where(sub == 3, r0, jnp.where(sub == 4, r1, jnp.where(sub == 5, r - r0 - r1, 0.0)))
-        wide_ref[56:64, :] = jnp.where(sub < 3, jnp.where(tier > sub, OFF, 0.0), parts)
+        wide_ref[88:96, :] = jnp.where(sub < 3, jnp.where(tier > sub, OFF, 0.0), parts)
         full.append(dot_nt(eye, wide_ref[...].astype(BF16)).astype(BF16))
     wide_ref[...] = jnp.zeros(wide_ref.shape, F32)
-    wide_ref[32:48, 0:react] = st_ref[0:16, :].astype(F32)
-    wide_ref[50 : 34 + carried, 0:react] = st_ref[16:carried, :].astype(F32)
+    wide_ref[64:80, 0:react] = st_ref[0:16, :].astype(F32)
+    wide_ref[82 : 66 + carried, 0:react] = st_ref[16:carried, :].astype(F32)
     full.append(dot_nt(eye, wide_ref[...].astype(BF16)).astype(BF16))
     base = 0
     for start, size in CHUNKS:
@@ -78,89 +87,76 @@
     out_ref, coef_ref, tail_ref,
     wide_ref, w_ref, c_ref, conc32_ref, x_ref, act_ref, run_ref,
 ):
-    step = pl.program_id(0)
-
-    @pl.when(step == 0)
-    def _():
-        run_ref[0] = cond_ref[0] - THIRD
-        run_ref[1] = jnp.where(lax.axis_index("gx") == 0, MASS + THIRD, BODY) * jnp.ones(run_ref.shape[1:], F32)
-        run_ref[2] = jnp.full(run_ref.shape[1:], BODY, F32)
-        build_weights(of_ref, or_ref, st_ref, rf_ref, rr_ref, wide_ref, w_ref, c_ref)
-
-    gap, mass_first, mass = run_ref[0], run_ref[1], run_ref[2]
-    for q in range(1, XB + 1):
-        p = step * XB + q
-        after = cond_ref[jnp.minimum(p, cond_ref.shape[0] - 1)] - THIRD
-        inv = 1.0 / (gap + after + mass)
-        alpha, beta = gap * inv, after * inv
-        coef_ref[0, p], coef_ref[1, p], coef_ref[2, p] = alpha, beta, inv
-        mass_first = mass_first + alpha * mass
-        mass = BODY + beta * mass
-        gap = alpha * after
-        tail_ref[p, 0], tail_ref[p, 1], tail_ref[p, 2] = gap, mass_first, mass
-    run_ref[0], run_ref[1], run_ref[2] = gap, mass_first, mass
-
-    carried, xb, ny, nz = adj_ref.shape
+    run_ref[0] = cond_ref[0] - THIRD
+    run_ref[1] = jnp.where(lax.axis_index("gx") == 0, MASS + THIRD, BODY) * jnp.ones(run_ref.shape[1:], F32)
+    run_ref[2] = jnp.full(run_ref.shape[1:], BODY, F32)
+    build_weights(of_ref, or_ref, st_ref, rf_ref, rr_ref, wide_ref, w_ref, c_ref)
+
+    carried, nx, ny, nz = adj_ref.shape
     species = conc_ref.shape[0]
-    adj_rows = adj_ref.reshape(carried * xb * ny, nz)
-    out_rows = out_ref.reshape(carried * xb * ny, nz)
-    pitch = xb * ny
-    conc32_ref[...] = conc_ref[...].astype(F32).reshape(species * pitch, nz)
+    pitch = nx * ny
+    adj_rows = adj_ref.reshape(carried * pitch, nz)
+    out_rows = out_ref.reshape(carried * pitch, nz)
     sub = iota((8, nz), 0)
-    for x in range(xb):
-        for y in range(ny):
-            row = x * ny + y
-            cols = slice(row * nz, (row + 1) * nz)
-            conc = jnp.concatenate(
-                [conc32_ref[pl.ds(row + 8 * q * pitch, 8, stride=pitch), :] for q in range(4)], axis=0
-            ).astype(BF16)
-            x_ref[0:32, cols] = conc
-            lam = [adj_rows[pl.ds(row + first * pitch, 8, stride=pitch), :] for first in (0, 8, carried - 8)]
-            level = jnp.broadcast_to(lev_ref[x, y : y + 1, :], (8, nz))
-            marks = jnp.where(level <= sub, 1.0, 0.0)
-            x_ref[32:64, cols] = jnp.concatenate(lam + [marks], axis=0).astype(BF16)
-    per_tile = TILE // nz
-    for tile in range(xb * ny // per_tile):
-        slot = tile % act_ref.shape[0]
-        every = dot(w_ref[...], x_ref[:, tile * TILE : (tile + 1) * TILE])
+
+    @pl.loop(0, nx // XB)
+    def _(step):
+        gap, mass_first, mass = run_ref[0], run_ref[1], run_ref[2]
+        for q in range(1, XB + 1):
+            p = step * XB + q
+            after = cond_ref[jnp.minimum(p, nx - 1)] - THIRD
+            inv = 1.0 / (gap + after + mass)
+            alpha, beta = gap * inv, after * inv
+            coef_ref[0, p], coef_ref[1, p], coef_ref[2, p] = alpha, beta, inv
+            mass_first = mass_first + alpha * mass
+            mass = BODY + beta * mass
+            gap = alpha * after
+            tail_ref[p, 0], tail_ref[p, 1], tail_ref[p, 2] = gap, mass_first, mass
+        run_ref[0], run_ref[1], run_ref[2] = gap, mass_first, mass
+
+        conc32_ref[...] = conc_ref[:, pl.ds(step * XB, XB)].astype(F32).reshape(species * XB * ny, nz)
+        base = step * XB * ny
+        for x in range(XB):
+            for y in range(ny):
+                row = x * ny + y
+                cols = slice(row * nz, (row + 1) * nz)
+                conc = jnp.concatenate(
+                    [conc32_ref[pl.ds(row + 8 * q * XB * ny, 8, stride=XB * ny), :] for q in range(4)], axis=0
+                ).astype(BF16)
+                x_ref[0:32, cols] = conc
+                x_ref[32:64, cols] = conc
+                lam = [
+                    adj_rows[pl.ds(base + row + first * pitch, 8, stride=pitch), :] for first in (0, 8, carried - 8)
+                ]
+                level = jnp.broadcast_to(lev_ref[step * XB + x, y : y + 1, :], (8, nz))
+                marks = jnp.where(level <= sub, 1.0, 0.0)
+                x_ref[64:96, cols] = jnp.concatenate(lam + [marks], axis=0).astype(BF16)
+        every = dot(w_ref[...], x_ref[...])
         for start, size in CHUNKS:
             got = every[3 * start : 3 * (start + size)]
             weight = got[2 * size :]
-            act_ref[slot, 0, start : start + size, :] = (jnp.exp(got[:size]) * weight).astype(BF16)
-            act_ref[slot, 1, start : start + size, :] = (jnp.exp(got[size : 2 * size]) * weight).astype(BF16)
-        chem = dot(c_ref[0], act_ref[slot, 0]) + dot(c_ref[1], act_ref[slot, 1])
-        for part in range(per_tile):
-            row = tile * per_tile + part
+            act_ref[0, start : start + size, :] = (jnp.exp2(got[:size]) * weight).astype(BF16)
+            act_ref[1, start : start + size, :] = (jnp.exp2(got[size : 2 * size]) * weight).astype(BF16)
+        chem = dot(c_ref[0], act_ref[0]) + dot(c_ref[1], act_ref[1])
+        for row in range(XB * ny):
             for q, first in enumerate((0, 8, carried - 8)):
-                out_rows[pl.ds(row + first * pitch, 8, stride=pitch), :] = chem[
-                    8 * q : 8 * q + 8, part * nz : (part + 1) * nz
+                out_rows[pl.ds(base + row + first * pitch, 8, stride=pitch), :] = chem[
+                    8 * q : 8 * q + 8, row * nz : (row + 1) * nz
                 ]
 
 
 def chemistry(adjoint, log_conc, levels, conduct, orders_fwd, orders_rev, stoich, rate_fwd, rate_rev):
     carried, nx, ny, nz = adjoint.shape
     species, react = log_conc.shape[0], orders_fwd.shape[0]
-    whole = lambda a: pl.BlockSpec(a.shape, lambda i: (0,) * len(a.shape))
     small = [orders_fwd.T, orders_rev.T, stoich.T, rate_fwd.reshape(1, react), rate_rev.reshape(1, react)]
     return pl.pallas_call(
         chem_kernel,
-        grid=(nx // XB,),
-        in_specs=[
-            pl.BlockSpec((carried, XB, ny, nz), lambda i: (0, i, 0, 0)),
-            pl.BlockSpec((species, XB, ny, nz), lambda i: (0, i, 0, 0)),
-            pl.BlockSpec((XB, ny, nz), lambda i: (i, 0, 0)),
-            whole(conduct),
-        ]
-        + [whole(a) for a in small],
-        out_specs=[
-            pl.BlockSpec((carried, XB, ny, nz), lambda i: (0, i, 0, 0)),
-            pl.BlockSpec((3, nx + 1, ny, nz), lambda i: (0, 0, 0, 0)),
-            pl.BlockSpec((nx + 1, 3, ny, nz), lambda i: (0, 0, 0, 0)),
-        ],
+        in_specs=[WHOLE] * 9,
+        out_specs=[WHOLE] * 3,
         out_shape=[
-            jax.ShapeDtypeStruct(adjoint.shape, F32),
-            jax.ShapeDtypeStruct((3, nx + 1, ny, nz), F32),
-            jax.ShapeDtypeStruct((nx + 1, 3, ny, nz), F32),
+            pltpu.VMEM(adjoint.shape, F32),
+            pltpu.VMEM((3, nx + 1, ny, nz), F32),
+            pltpu.VMEM((nx + 1, 3, ny, nz), F32),
         ],
         scratch_shapes=[
             pltpu.VMEM((K_ROWS, 256), F32),
@@ -168,10 +164,10 @@
             pltpu.VMEM((2, 32, R_PAD), BF16),
             pltpu.VMEM((species * XB * ny, nz), F32),
             pltpu.VMEM((K_ROWS, XB * ny * nz), BF16),
-            pltpu.VMEM((1, 2, R_PAD, TILE), BF16),
+            pltpu.VMEM((2, R_PAD, XB * ny * nz), BF16),
             pltpu.VMEM((3, ny, nz), F32),
         ],
-        compiler_params=pltpu.CompilerParams(dimension_semantics=("arbitrary",), vmem_limit_bytes=LIMIT),
+        compiler_params=SMALL,
         cost_estimate=pl.CostEstimate(flops=12 * 10**9, bytes_accessed=4 * 10**6, transcendentals=6_750_000),
         name="chem",
     )(adjoint, log_conc, levels, conduct, *small)
@@ -182,11 +178,6 @@
 ROWS = 16
 SB = 2
 LB = 11
-ANY = pl.BlockSpec(memory_space=pl.ANY)
-WHOLE = pl.BlockSpec(memory_space=pltpu.VMEM)
-SMALL = pltpu.CompilerParams(vmem_limit_bytes=LIMIT)
-
-
 def place(s):
     return s // GROUP * ROWS + s % GROUP
 
@@ -395,7 +386,13 @@
             for p in range(nx - 2, 0, -1):
                 value = part_ref[s, p] + coef_ref[0, p] * first + coef_ref[1, p] * value
                 out_ref[s, p] = value
-        put(g).start()
+        @pl.when(g % 2 == 0)
+        def _():
+            put(g).start(priority=0)
+
+        @pl.when(g % 2 == 1)
+        def _():
+            put(g).start(priority=1)
 
     @pl.loop(0, groups)
     def _(g):
@@ -420,6 +417,10 @@
     )(coef, ends, part)
 
 
+def resident(value):
+    return pltpu.with_memory_space_constraint(value, pltpu.VMEM)
+
+
 def shards(
     adjoint, log_conc, levels, conduct, orders_fwd, orders_rev, stoich, rate_fwd, rate_rev, diffusivity
 ):
@@ -429,9 +430,7 @@
     tail, head = edges(adjoint)
     low = lax.ppermute(tail, "gy", [(i, (i + 1) % rows_y) for i in range(rows_y)])
     high = lax.ppermute(head, "gy", [((i + 1) % rows_y, i) for i in range(rows_y)])
-    chem, coef, ends_m = chemistry(
-        adjoint, log_conc, levels, conduct, orders_fwd, orders_rev, stoich, rate_fwd, rate_rev
-    )
+    chem, coef, ends_m = chemistry(adjoint, log_conc, levels, conduct, orders_fwd, orders_rev, stoich, rate_fwd, rate_rev)
     part, message = local_part(diffusivity, adjoint, chem, near, low, high, conduct, coef, ends_m)
     message = lax.all_to_all(message.reshape(blocks, ROWS, nz), "gx", 0, 0, tiled=True)
     ends = lax.all_to_all(chain(message), "gx", 0, 0, tiled=True)

time: 57.4 us -> 57 us (level)
  transfers between devices with their start and end apart: 3 -> 3, of which waited for: 0 -> 0; matrix products, arithmetic and copies ran while one was open for 0% -> 0% of each run, Pallas kernels for 18% -> 17%
where the time goes in v12:
time: 57 us; the launch traced here: 56.8 us
  blocking collectives  38.9 us (68%)
  Pallas kernels  13.9 us (24%)
  starting transfers between devices  2.44 us (4%)
  local copies, waits for them, and re-layouts  1.4 us (2%)
    all_to_all x1, blocking collectives, shards(): lax.all_to_all(message.reshape(blocks, ROWS, nz), 'gx', 0, 0, tiled=True)  23.7 us
    all_to_all x1, blocking collectives, shards(): ends = lax.all_to_all(chain(message), 'gx', 0, 0, tiled=True)  15.2 us
    pallas_call x1, Pallas kernels, chemistry(): pl.pallas_call(chem_kernel, in_specs=[WHOLE] * 9, out_specs=[WHOLE] * 3,...  9.55 us
    pallas_call x1, Pallas kernels, local_part(): pl.pallas_call(local_kernel, in_specs=[smem] + [WHOLE] * 8, out_specs=[WH...  2.45 us
    ppermute x1, starting transfers between devices, shards(): lax.ppermute(tail, 'gy', [(i, (i + 1) % rows_y) for i in range(rows_y)])  1.57 us
    pallas_call x1, Pallas kernels, back(): pl.pallas_call(back_kernel, in_specs=[WHOLE, WHOLE, WHOLE], out_specs=ANY...  1.43 us
    unnamed x20, local copies, waits for them, and re-layouts  1.4 us
  transfers between devices with their start and end apart: 3, of which 0 were waited for; matrix products, arithmetic and copies ran while one was open for 0% of the time, Pallas kernels for 17%

profile of v12, /device:TPU:2, one launch (start us, length us, event | category | flops | bytes accessed | tf_op | source)
XLA Modules:
  0.0 56.8 jit_solution(6492908557862947058)
XLA Ops:
  0.0 0.0 collective-permute-start
  0.0 0.0 copy-start
  0.0 1.4 %copy-done = f32[22,16,8,128]{3,2,1,0:T(8,128)S(1)} copy-done((f32[22,16,8,128]{3,2,1,0:T(8,128)S(1)}, f32[22,16,8,128]{3,2,1,0:T(8,128)}, u32[]{:S(2)}) %copy-start) | copy-done | bytes 1441816
  1.4 0.0 copy-start.1
  1.4 0.0 copy-start.3
  1.4 0.0 copy-start.4
  1.4 0.0 copy-start.6
  1.4 0.0 copy-start.7
  1.4 0.0 copy-start.8
  1.4 0.0 copy-start.9
  1.4 0.2 edges.1
  1.7 1.6 %collective-permute-start.1 = (f32[22,2,16,128]{3,2,1,0:T(8,128)S(1)}, f32[22,2,16,128]{3,2,1,0:T(8,128)S(1)}, u32[]{:S(2)}, u32[]{:S(2)}) collective-permute-start(f32[22,2,16,128]{3,2,1,0:T(8,128)S(1)} %get-tuple-element.14), channel_id=1, source_target_pairs={{0,2},{2,4},{4,6},{6,0},{1,3},{3,5},{5,7},{7,1},{8,10},{10,12},{12... | collective-permute-start | bytes 1081352 | tf_op jit(solution)/shard_map/ppermute | solution.py:431
  3.2 0.9 %collective-permute-start.2 = (f32[22,2,16,128]{3,2,1,0:T(8,128)S(1)}, f32[22,2,16,128]{3,2,1,0:T(8,128)S(1)}, u32[]{:S(2)}, u32[]{:S(2)}) collective-permute-start(f32[22,2,16,128]{3,2,1,0:T(8,128)S(1)} %get-tuple-element.15), channel_id=1, source_target_pairs={{2,0},{4,2},{6,4},{0,6},{3,1},{5,3},{7,5},{1,7},{10,8},{12,10},{14... | collective-permute-start | bytes 1081352 | tf_op jit(solution)/shard_map/ppermute | solution.py:432
  4.1 0.0 copy-done.1
  4.1 0.0 copy-done.3
  4.1 0.0 copy-done.4
  4.1 0.0 copy-done.5
  4.1 0.0 copy-done.6
  4.1 0.0 copy-done.7
  4.1 0.0 copy-done.8
  4.2 0.0 copy-done.9
  4.2 0.0 copy-start.2
  4.2 9.5 %chem.1 = (f32[22,16,8,128]{3,2,1,0:T(8,128)S(1)}, f32[3,17,8,128]{3,2,1,0:T(8,128)S(1)}, f32[17,3,8,128]{3,2,1,0:T(8,128)S(1)}) custom-call(f32[22,16,8,128]{3,2,1,0:T(8,128)S(1)} %copy-done, bf16[32,16,8,128]{3,2,1,0:T(8,128)(2,1)S(1)} %copy-done.3, s32[16,8,128]{2,1,0:T(8,128)S(1)} %copy-done.4, f32[16,8,128]{2,1,0:T(8,128)S(1)} %copy-done.1, ...), custom_call_target="tpu_custom_call" | custom-call | flops 12000000000 | bytes 4000000 | tf_op jit(solution)/shard_map/chem/pallas_call | solution.py:152
  13.7 0.0 collective-permute-done.1.low_ref
  13.7 0.0 collective-permute-done.2.high_ref
  13.8 0.0 collective-permute-done.near_ref
  13.8 0.0 copy-done.2
  13.8 2.4 %local.1 = (f32[22,16,8,128]{3,2,1,0:T(8,128)S(1)}, f32[512,128]{1,0:T(8,128)S(1)}) custom-call(f32[22]{0:T(128)S(1)} %copy-done.2, f32[16,8,128]{2,1,0:T(8,128)S(1)} %copy-done.1, f32[22,16,8,128]{3,2,1,0:T(8,128)S(1)} %copy-done, f32[22,16,8,128]{3,2,1,0:T(8,128)S(1)} %get-tuple-element.13.chem_ref, f32[22,16,8,128]{3,2,1,0:T(8,128)S(1)} %collective-permute-done.near_ref, ...), custom_call_target="tpu_custom_call" | custom-call | flops 20000000 | bytes 7000000 | tf_op jit(solution)/shard_map/local/pallas_call | solution.py:283
  16.2 23.7 %all_to_all.10.in_ref = f32[32,16,128]{2,1,0:T(8,128)S(1)} all-to-all(f32[32,16,128]{2,1,0:T(8,128)S(1)} %bitcast.6), channel_id=1, replica_groups=mesh['gx'=32,'gy'=4,'gz'=2] {'gx'}, dimensions={0} | all-to-all | bytes 524288 | tf_op jit(solution)/shard_map/all_to_all | solution.py:435
  40.0 0.2 chain.1
  40.2 15.2 %all_to_all.11.got_ref = f32[32,3,4,128]{3,2,1,0:T(4,128)S(1)} all-to-all(f32[32,3,4,128]{3,2,1,0:T(4,128)S(1)} %chain.1), channel_id=1, replica_groups=mesh['gx'=32,'gy'=4,'gz'=2] {'gx'}, dimensions={0} | all-to-all | bytes 393216 | tf_op jit(solution)/shard_map/all_to_all | solution.py:436
  55.4 1.4 %back.1 = f32[22,16,8,128]{3,2,1,0:T(8,128)} custom-call(f32[3,17,8,128]{3,2,1,0:T(8,128)S(1)} %get-tuple-element.12.coef_ref, f32[32,3,4,128]{3,2,1,0:T(4,128)S(1)} %all_to_all.11.got_ref, f32[22,16,8,128]{3,2,1,0:T(8,128)S(1)} %get-tuple-element.18.part_ref), custom_call_target="tpu_custom_call" | custom-call | flops 2000000 | bytes 3000000 | tf_op jit(solution)/shard_map/back/pallas_call | solution.py:404
  (1 shorter events, 0.0 us)
Async XLA Ops:
  0.0 13.8 %collective-permute-start = (f32[22,16,8,128]{3,2,1,0:T(8,128)}, f32[22,16,8,128]{3,2,1,0:T(8,128)S(1)}, u32[]{:S(2)}, u32[]{:S(2)}) collective-permute-start(f32[22,16,8,128]{3,2,1,0:T(8,128)} %adj_ref.5), channel_id=1, source_target_pairs={{0,1},{1,0},{2,3},{3,2},{4,5},{5,4},{6,7},{7,6},{8,9},{9,8},{10,11... | collective-permute-start | bytes 4325384 | tf_op jit(solution)/shard_map/ppermute | solution.py:429
  0.0 1.4 %copy-start = (f32[22,16,8,128]{3,2,1,0:T(8,128)S(1)}, f32[22,16,8,128]{3,2,1,0:T(8,128)}, u32[]{:S(2)}) copy-start(f32[22,16,8,128]{3,2,1,0:T(8,128)} %adj_ref.5) | copy-start | bytes 4325380
  1.4 2.7 %copy-start.1 = (f32[16,8,128]{2,1,0:T(8,128)S(1)}, f32[16,8,128]{2,1,0:T(8,128)}, u32[]{:S(2)}) copy-start(f32[16,8,128]{2,1,0:T(8,128)} %cond_ref.3) | copy-start | bytes 196612
  1.4 2.7 %copy-start.3 = (bf16[32,16,8,128]{3,2,1,0:T(8,128)(2,1)S(1)}, bf16[32,16,8,128]{3,2,1,0:T(8,128)(2,1)}, u32[]{:S(2)}) copy-start(bf16[32,16,8,128]{3,2,1,0:T(8,128)(2,1)} %conc_ref.1) | copy-start | bytes 3145732
  1.4 2.7 %copy-start.4 = (s32[16,8,128]{2,1,0:T(8,128)S(1)}, s32[16,8,128]{2,1,0:T(8,128)}, u32[]{:S(2)}) copy-start(s32[16,8,128]{2,1,0:T(8,128)} %lev_ref.1) | copy-start | bytes 196612
  1.4 2.7 %copy-start.5 = (bf16[206,32]{0,1:T(8,128)(2,1)S(1)}, bf16[206,32]{0,1:T(8,128)(2,1)}, u32[]{:S(2)}) copy-start(bf16[206,32]{0,1:T(8,128)(2,1)} %param.14) | copy-start | bytes 39556
  1.4 2.7 %copy-start.6 = (bf16[206,32]{0,1:T(8,128)(2,1)S(1)}, bf16[206,32]{0,1:T(8,128)(2,1)}, u32[]{:S(2)}) copy-start(bf16[206,32]{0,1:T(8,128)(2,1)} %param.15) | copy-start | bytes 39556
  1.4 2.7 %copy-start.7 = (bf16[206,22]{0,1:T(8,128)(2,1)S(1)}, bf16[206,22]{0,1:T(8,128)(2,1)}, u32[]{:S(2)}) copy-start(bf16[206,22]{0,1:T(8,128)(2,1)} %param.16) | copy-start | bytes 27196
  1.4 2.7 %copy-start.8 = (f32[206]{0:T(256)S(1)}, f32[206]{0:T(256)}, u32[]{:S(2)}) copy-start(f32[206]{0:T(256)} %param.17) | copy-start | bytes 2476
  1.4 2.7 %copy-start.9 = (f32[206]{0:T(256)S(1)}, f32[206]{0:T(256)}, u32[]{:S(2)}) copy-start(f32[206]{0:T(256)} %param.18) | copy-start | bytes 2476
  1.7 12.1 %collective-permute-start.1 = (f32[22,2,16,128]{3,2,1,0:T(8,128)S(1)}, f32[22,2,16,128]{3,2,1,0:T(8,128)S(1)}, u32[]{:S(2)}, u32[]{:S(2)}) collective-permute-start(f32[22,2,16,128]{3,2,1,0:T(8,128)S(1)} %get-tuple-element.14), channel_id=1, source_target_pairs={{0,2},{2,4},{4,6},{6,0},{1,3},{3,5},{5,7},{7,1},{8,10},{10,12},{12... | collective-permute-start | bytes 1081352 | tf_op jit(solution)/shard_map/ppermute | solution.py:431
  3.2 10.5 %collective-permute-start.2 = (f32[22,2,16,128]{3,2,1,0:T(8,128)S(1)}, f32[22,2,16,128]{3,2,1,0:T(8,128)S(1)}, u32[]{:S(2)}, u32[]{:S(2)}) collective-permute-start(f32[22,2,16,128]{3,2,1,0:T(8,128)S(1)} %get-tuple-element.15), channel_id=1, source_target_pairs={{2,0},{4,2},{6,4},{0,6},{3,1},{5,3},{7,5},{1,7},{10,8},{12,10},{14... | collective-permute-start | bytes 1081352 | tf_op jit(solution)/shard_map/ppermute | solution.py:432
  4.2 9.6 %copy-start.2 = (f32[22]{0:T(128)S(1)}, f32[22]{0:T(128)}, u32[]{:S(2)}) copy-start(f32[22]{0:T(128)} %diff_ref.1) | copy-start | bytes 268

commit v13 on v12

--- a/solution.py
+++ b/solution.py
@@ -182,10 +182,15 @@
     return s // GROUP * ROWS + s % GROUP
 
 
-def crossing(adj_ref, s):
+def crossing(adj_ref, s, shifted=False):
     carried, nx, ny, nz = adj_ref.shape
     rows = adj_ref.reshape(carried * nx * ny, nz)
     f0, f1, f6, f7 = [rows[pl.ds(s * nx * ny + r, nx, stride=ny), :] for r in (0, 1, ny - 2, ny - 1)]
+    if shifted:
+        x = iota((nx, nz), 0)
+        ends = (x == 0) | (x == nx - 1)
+        f0, f1 = [jnp.where(ends, f, pltpu.roll(f, nx - 1, 0)) for f in (f0, f1)]
+        f6, f7 = [jnp.where(ends, f, pltpu.roll(f, 1, 0)) for f in (f6, f7)]
     return (16.0 * f7 - f6, -f7), (-f0, 16.0 * f0 - f1)
 
 
@@ -233,6 +238,7 @@
 
     add_ref[...] = jnp.zeros(add_ref.shape, F32)
     lane = iota((ny, nz), 1)
+    adj_rows = adj_ref.reshape(carried * nx * ny, nz)
     keep_low = jnp.where(lax.axis_index("gz") == 0, 1.0, 0.0)
     keep_high = 1.0 - keep_low
 
@@ -240,7 +246,7 @@
     def _(g):
         for t in range(LB):
             s = g * LB + t
-            down, up = crossing(adj_ref, s)
+            down, up = crossing(adj_ref, s, shifted=True)
             for r, own_term, got in (
                 (0, down[0], low_ref[s, 0]),
                 (1, down[1], low_ref[s, 1]),
@@ -255,10 +261,15 @@
             for p in range(nx):
                 own, near = adj_ref[s, p], near_ref[s, p]
                 above, below = near * keep_low, near * keep_high
-                close = pltpu.roll(own, ny - 1, 0) + pltpu.roll(own, 1, 0)
+                if 0 < p < nx - 1:
+                    row = (s * nx + p) * ny
+                    up1, down1, up2, down2 = [adj_rows[pl.ds(row + k, ny), :] for k in (1, -1, 2, -2)]
+                else:
+                    up1, down1, up2, down2 = [pltpu.roll(own, k % ny, 0) for k in (-1, 1, -2, 2)]
+                close = up1 + down1
                 close = close + pltpu.roll(jnp.where(lane < 1, above, own), nz - 1, 1)
                 close = close + pltpu.roll(jnp.where(lane >= nz - 1, below, own), 1, 1)
-                far = pltpu.roll(own, ny - 2, 0) + pltpu.roll(own, 2, 0)
+                far = up2 + down2
                 far = far + pltpu.roll(jnp.where(lane < 2, above, own), nz - 2, 1)
                 far = far + pltpu.roll(jnp.where(lane >= nz - 2, below, own), 2, 1)
                 at = (t * nx + p) * ny

time: 57 us -> 57.2 us (level)
  no operation moved by 1% of the time
where the time goes in v13:
time: 57.2 us; the launch traced here: 57 us
  blocking collectives  38.9 us (68%)
  Pallas kernels  14 us (24%)
  starting transfers between devices  2.44 us (4%)
  local copies, waits for them, and re-layouts  1.4 us (2%)
    all_to_all x1, blocking collectives, shards(): lax.all_to_all(message.reshape(blocks, ROWS, nz), 'gx', 0, 0, tiled=True)  23.7 us
    all_to_all x1, blocking collectives, shards(): ends = lax.all_to_all(chain(message), 'gx', 0, 0, tiled=True)  15.2 us
    pallas_call x1, Pallas kernels, chemistry(): pl.pallas_call(chem_kernel, in_specs=[WHOLE] * 9, out_specs=[WHOLE] * 3,...  9.55 us
    pallas_call x1, Pallas kernels, local_part(): pl.pallas_call(local_kernel, in_specs=[smem] + [WHOLE] * 8, out_specs=[WH...  2.59 us
    ppermute x1, starting transfers between devices, shards(): lax.ppermute(tail, 'gy', [(i, (i + 1) % rows_y) for i in range(rows_y)])  1.57 us
    pallas_call x1, Pallas kernels, back(): pl.pallas_call(back_kernel, in_specs=[WHOLE, WHOLE, WHOLE], out_specs=ANY...  1.43 us
    unnamed x20, local copies, waits for them, and re-layouts  1.4 us
  transfers between devices with their start and end apart: 3, of which 0 were waited for; matrix products, arithmetic and copies ran while one was open for 0% of the time, Pallas kernels for 17%

profile of v13, /device:TPU:2, one launch (start us, length us, event | category | flops | bytes accessed | tf_op | source)
XLA Modules:
  0.0 57.0 jit_solution(18232813737094964464)
XLA Ops:
  0.0 0.0 collective-permute-start
  0.0 0.0 copy-start
  0.0 1.4 %copy-done = f32[22,16,8,128]{3,2,1,0:T(8,128)S(1)} copy-done((f32[22,16,8,128]{3,2,1,0:T(8,128)S(1)}, f32[22,16,8,128]{3,2,1,0:T(8,128)}, u32[]{:S(2)}) %copy-start) | copy-done | bytes 1441816
  1.4 0.0 copy-start.1
  1.4 0.0 copy-start.3
  1.4 0.0 copy-start.4
  1.4 0.0 copy-start.6
  1.4 0.0 copy-start.7
  1.4 0.0 copy-start.8
  1.4 0.0 copy-start.9
  1.4 0.2 edges.1
  1.7 1.6 %collective-permute-start.1 = (f32[22,2,16,128]{3,2,1,0:T(8,128)S(1)}, f32[22,2,16,128]{3,2,1,0:T(8,128)S(1)}, u32[]{:S(2)}, u32[]{:S(2)}) collective-permute-start(f32[22,2,16,128]{3,2,1,0:T(8,128)S(1)} %get-tuple-element.14), channel_id=1, source_target_pairs={{0,2},{2,4},{4,6},{6,0},{1,3},{3,5},{5,7},{7,1},{8,10},{10,12},{12... | collective-permute-start | bytes 1081352 | tf_op jit(solution)/shard_map/ppermute | solution.py:442
  3.2 0.9 %collective-permute-start.2 = (f32[22,2,16,128]{3,2,1,0:T(8,128)S(1)}, f32[22,2,16,128]{3,2,1,0:T(8,128)S(1)}, u32[]{:S(2)}, u32[]{:S(2)}) collective-permute-start(f32[22,2,16,128]{3,2,1,0:T(8,128)S(1)} %get-tuple-element.15), channel_id=1, source_target_pairs={{2,0},{4,2},{6,4},{0,6},{3,1},{5,3},{7,5},{1,7},{10,8},{12,10},{14... | collective-permute-start | bytes 1081352 | tf_op jit(solution)/shard_map/ppermute | solution.py:443
  4.1 0.0 copy-done.1
  4.1 0.0 copy-done.3
  4.1 0.0 copy-done.4
  4.1 0.0 copy-done.5
  4.1 0.0 copy-done.6
  4.1 0.0 copy-done.7
  4.1 0.0 copy-done.8
  4.2 0.0 copy-done.9
  4.2 0.0 copy-start.2
  4.2 9.5 %chem.1 = (f32[22,16,8,128]{3,2,1,0:T(8,128)S(1)}, f32[3,17,8,128]{3,2,1,0:T(8,128)S(1)}, f32[17,3,8,128]{3,2,1,0:T(8,128)S(1)}) custom-call(f32[22,16,8,128]{3,2,1,0:T(8,128)S(1)} %copy-done, bf16[32,16,8,128]{3,2,1,0:T(8,128)(2,1)S(1)} %copy-done.3, s32[16,8,128]{2,1,0:T(8,128)S(1)} %copy-done.4, f32[16,8,128]{2,1,0:T(8,128)S(1)} %copy-done.1, ...), custom_call_target="tpu_custom_call" | custom-call | flops 12000000000 | bytes 4000000 | tf_op jit(solution)/shard_map/chem/pallas_call | solution.py:152
  13.7 0.0 collective-permute-done.1.low_ref
  13.7 0.0 collective-permute-done.2.high_ref
  13.8 0.0 collective-permute-done.near_ref
  13.8 0.0 copy-done.2
  13.8 2.6 %local.1 = (f32[22,16,8,128]{3,2,1,0:T(8,128)S(1)}, f32[512,128]{1,0:T(8,128)S(1)}) custom-call(f32[22]{0:T(128)S(1)} %copy-done.2, f32[16,8,128]{2,1,0:T(8,128)S(1)} %copy-done.1, f32[22,16,8,128]{3,2,1,0:T(8,128)S(1)} %copy-done, f32[22,16,8,128]{3,2,1,0:T(8,128)S(1)} %get-tuple-element.13.chem_ref, f32[22,16,8,128]{3,2,1,0:T(8,128)S(1)} %collective-permute-done.near_ref, ...), custom_call_target="tpu_custom_call" | custom-call | flops 20000000 | bytes 7000000 | tf_op jit(solution)/shard_map/local/pallas_call | solution.py:294
  16.4 23.7 %all_to_all.10.in_ref = f32[32,16,128]{2,1,0:T(8,128)S(1)} all-to-all(f32[32,16,128]{2,1,0:T(8,128)S(1)} %bitcast.6), channel_id=1, replica_groups=mesh['gx'=32,'gy'=4,'gz'=2] {'gx'}, dimensions={0} | all-to-all | bytes 524288 | tf_op jit(solution)/shard_map/all_to_all | solution.py:446
  40.1 0.2 chain.1
  40.4 15.2 %all_to_all.11.got_ref = f32[32,3,4,128]{3,2,1,0:T(4,128)S(1)} all-to-all(f32[32,3,4,128]{3,2,1,0:T(4,128)S(1)} %chain.1), channel_id=1, replica_groups=mesh['gx'=32,'gy'=4,'gz'=2] {'gx'}, dimensions={0} | all-to-all | bytes 393216 | tf_op jit(solution)/shard_map/all_to_all | solution.py:447
  55.5 1.4 %back.1 = f32[22,16,8,128]{3,2,1,0:T(8,128)} custom-call(f32[3,17,8,128]{3,2,1,0:T(8,128)S(1)} %get-tuple-element.12.coef_ref, f32[32,3,4,128]{3,2,1,0:T(4,128)S(1)} %all_to_all.11.got_ref, f32[22,16,8,128]{3,2,1,0:T(8,128)S(1)} %get-tuple-element.18.part_ref), custom_call_target="tpu_custom_call" | custom-call | flops 2000000 | bytes 3000000 | tf_op jit(solution)/shard_map/back/pallas_call | solution.py:415
  (1 shorter events, 0.0 us)
Async XLA Ops:
  0.0 13.8 %collective-permute-start = (f32[22,16,8,128]{3,2,1,0:T(8,128)}, f32[22,16,8,128]{3,2,1,0:T(8,128)S(1)}, u32[]{:S(2)}, u32[]{:S(2)}) collective-permute-start(f32[22,16,8,128]{3,2,1,0:T(8,128)} %adj_ref.5), channel_id=1, source_target_pairs={{0,1},{1,0},{2,3},{3,2},{4,5},{5,4},{6,7},{7,6},{8,9},{9,8},{10,11... | collective-permute-start | bytes 4325384 | tf_op jit(solution)/shard_map/ppermute | solution.py:440
  0.0 1.4 %copy-start = (f32[22,16,8,128]{3,2,1,0:T(8,128)S(1)}, f32[22,16,8,128]{3,2,1,0:T(8,128)}, u32[]{:S(2)}) copy-start(f32[22,16,8,128]{3,2,1,0:T(8,128)} %adj_ref.5) | copy-start | bytes 4325380
  1.4 2.7 %copy-start.1 = (f32[16,8,128]{2,1,0:T(8,128)S(1)}, f32[16,8,128]{2,1,0:T(8,128)}, u32[]{:S(2)}) copy-start(f32[16,8,128]{2,1,0:T(8,128)} %cond_ref.3) | copy-start | bytes 196612
  1.4 2.7 %copy-start.3 = (bf16[32,16,8,128]{3,2,1,0:T(8,128)(2,1)S(1)}, bf16[32,16,8,128]{3,2,1,0:T(8,128)(2,1)}, u32[]{:S(2)}) copy-start(bf16[32,16,8,128]{3,2,1,0:T(8,128)(2,1)} %conc_ref.1) | copy-start | bytes 3145732
  1.4 2.7 %copy-start.4 = (s32[16,8,128]{2,1,0:T(8,128)S(1)}, s32[16,8,128]{2,1,0:T(8,128)}, u32[]{:S(2)}) copy-start(s32[16,8,128]{2,1,0:T(8,128)} %lev_ref.1) | copy-start | bytes 196612
  1.4 2.7 %copy-start.5 = (bf16[206,32]{0,1:T(8,128)(2,1)S(1)}, bf16[206,32]{0,1:T(8,128)(2,1)}, u32[]{:S(2)}) copy-start(bf16[206,32]{0,1:T(8,128)(2,1)} %param.14) | copy-start | bytes 39556
  1.4 2.7 %copy-start.6 = (bf16[206,32]{0,1:T(8,128)(2,1)S(1)}, bf16[206,32]{0,1:T(8,128)(2,1)}, u32[]{:S(2)}) copy-start(bf16[206,32]{0,1:T(8,128)(2,1)} %param.15) | copy-start | bytes 39556
  1.4 2.7 %copy-start.7 = (bf16[206,22]{0,1:T(8,128)(2,1)S(1)}, bf16[206,22]{0,1:T(8,128)(2,1)}, u32[]{:S(2)}) copy-start(bf16[206,22]{0,1:T(8,128)(2,1)} %param.16) | copy-start | bytes 27196
  1.4 2.7 %copy-start.8 = (f32[206]{0:T(256)S(1)}, f32[206]{0:T(256)}, u32[]{:S(2)}) copy-start(f32[206]{0:T(256)} %param.17) | copy-start | bytes 2476
  1.4 2.7 %copy-start.9 = (f32[206]{0:T(256)S(1)}, f32[206]{0:T(256)}, u32[]{:S(2)}) copy-start(f32[206]{0:T(256)} %param.18) | copy-start | bytes 2476
  1.7 12.1 %collective-permute-start.1 = (f32[22,2,16,128]{3,2,1,0:T(8,128)S(1)}, f32[22,2,16,128]{3,2,1,0:T(8,128)S(1)}, u32[]{:S(2)}, u32[]{:S(2)}) collective-permute-start(f32[22,2,16,128]{3,2,1,0:T(8,128)S(1)} %get-tuple-element.14), channel_id=1, source_target_pairs={{0,2},{2,4},{4,6},{6,0},{1,3},{3,5},{5,7},{7,1},{8,10},{10,12},{12... | collective-permute-start | bytes 1081352 | tf_op jit(solution)/shard_map/ppermute | solution.py:442
  3.2 10.5 %collective-permute-start.2 = (f32[22,2,16,128]{3,2,1,0:T(8,128)S(1)}, f32[22,2,16,128]{3,2,1,0:T(8,128)S(1)}, u32[]{:S(2)}, u32[]{:S(2)}) collective-permute-start(f32[22,2,16,128]{3,2,1,0:T(8,128)S(1)} %get-tuple-element.15), channel_id=1, source_target_pairs={{2,0},{4,2},{6,4},{0,6},{3,1},{5,3},{7,5},{1,7},{10,8},{12,10},{14... | collective-permute-start | bytes 1081352 | tf_op jit(solution)/shard_map/ppermute | solution.py:443
  4.2 9.6 %copy-start.2 = (f32[22]{0:T(128)S(1)}, f32[22]{0:T(128)}, u32[]{:S(2)}) copy-start(f32[22]{0:T(128)} %diff_ref.1) | copy-start | bytes 268

commit v14 on v12

--- a/solution.py
+++ b/solution.py
@@ -248,11 +248,11 @@
                 (ny - 1, up[1], high_ref[s, 1]),
             ):
                 add_ref[pl.ds(t * nx * ny + r, nx, stride=ny), :] = got - own_term
-        for t in range(LB):
-            s = g * LB + t
-            scale = diff_ref[s] * (SECTION * STEP / 12.0)
-            b_first, carry = None, None
-            for p in range(nx):
+        species = [g * LB + t for t in range(LB)]
+        scales = [diff_ref[s] * (SECTION * STEP / 12.0) for s in species]
+        first, carry = [None] * LB, [None] * LB
+        for p in range(nx):
+            for t, s in enumerate(species):
                 own, near = adj_ref[s, p], near_ref[s, p]
                 above, below = near * keep_low, near * keep_high
                 close = pltpu.roll(own, ny - 1, 0) + pltpu.roll(own, 1, 0)
@@ -263,18 +263,18 @@
                 far = far + pltpu.roll(jnp.where(lane >= nz - 2, below, own), 2, 1)
                 at = (t * nx + p) * ny
                 spread = 16.0 * close - far - 60.0 * own + add_ref[at : at + ny, :]
-                b = SECTION * own + (SECTION * STEP) * chem_ref[s, p] + scale * spread
+                b = SECTION * own + (SECTION * STEP) * chem_ref[s, p] + scales[t] * spread
                 if p == 0:
-                    b_first = b
+                    first[t] = b
                 elif p < nx - 1:
-                    full = b if carry is None else b + carry
+                    full = b if carry[t] is None else b + carry[t]
                     part_ref[s, p] = full * coef_ref[2, p]
-                    b_first = b_first + coef_ref[0, p] * full
-                    carry = coef_ref[1, p] * full
+                    first[t] = first[t] + coef_ref[0, p] * full
+                    carry[t] = coef_ref[1, p] * full
                 else:
-                    b_last = b + carry
-            msg_ref[pl.ds(place(s), ny, stride=stride), :] = b_first
-            msg_ref[pl.ds(place(s) + 8, ny, stride=stride), :] = b_last
+                    msg_ref[pl.ds(place(s) + 8, ny, stride=stride), :] = b + carry[t]
+        for t, s in enumerate(species):
+            msg_ref[pl.ds(place(s), ny, stride=stride), :] = first[t]
 
 
 def local_part(diffusivity, adjoint, chem, near, low, high, conduct, coef, ends):

time: 57 us -> 57.1 us (level)
  no operation moved by 1% of the time
where the time goes in v14:
time: 57.1 us; the launch traced here: 56.9 us
  blocking collectives  38.9 us (68%)
  Pallas kernels  14 us (25%)
  starting transfers between devices  2.44 us (4%)
  local copies, waits for them, and re-layouts  1.4 us (2%)
    all_to_all x1, blocking collectives, shards(): lax.all_to_all(message.reshape(blocks, ROWS, nz), 'gx', 0, 0, tiled=True)  23.7 us
    all_to_all x1, blocking collectives, shards(): ends = lax.all_to_all(chain(message), 'gx', 0, 0, tiled=True)  15.2 us
    pallas_call x1, Pallas kernels, chemistry(): pl.pallas_call(chem_kernel, in_specs=[WHOLE] * 9, out_specs=[WHOLE] * 3,...  9.55 us
    pallas_call x1, Pallas kernels, local_part(): pl.pallas_call(local_kernel, in_specs=[smem] + [WHOLE] * 8, out_specs=[WH...  2.52 us
    ppermute x1, starting transfers between devices, shards(): lax.ppermute(tail, 'gy', [(i, (i + 1) % rows_y) for i in range(rows_y)])  1.57 us
    pallas_call x1, Pallas kernels, back(): pl.pallas_call(back_kernel, in_specs=[WHOLE, WHOLE, WHOLE], out_specs=ANY...  1.43 us
    unnamed x20, local copies, waits for them, and re-layouts  1.4 us
  transfers between devices with their start and end apart: 3, of which 0 were waited for; matrix products, arithmetic and copies ran while one was open for 0% of the time, Pallas kernels for 17%

profile of v14, /device:TPU:2, one launch (start us, length us, event | category | flops | bytes accessed | tf_op | source)
XLA Modules:
  0.0 56.9 jit_solution(3168312896505282775)
XLA Ops:
  0.0 0.0 collective-permute-start
  0.0 0.0 copy-start
  0.0 1.4 %copy-done = f32[22,16,8,128]{3,2,1,0:T(8,128)S(1)} copy-done((f32[22,16,8,128]{3,2,1,0:T(8,128)S(1)}, f32[22,16,8,128]{3,2,1,0:T(8,128)}, u32[]{:S(2)}) %copy-start) | copy-done | bytes 1441816
  1.4 0.0 copy-start.1
  1.4 0.0 copy-start.3
  1.4 0.0 copy-start.4
  1.4 0.0 copy-start.6
  1.4 0.0 copy-start.7
  1.4 0.0 copy-start.8
  1.4 0.0 copy-start.9
  1.4 0.2 edges.1
  1.7 1.6 %collective-permute-start.1 = (f32[22,2,16,128]{3,2,1,0:T(8,128)S(1)}, f32[22,2,16,128]{3,2,1,0:T(8,128)S(1)}, u32[]{:S(2)}, u32[]{:S(2)}) collective-permute-start(f32[22,2,16,128]{3,2,1,0:T(8,128)S(1)} %get-tuple-element.14), channel_id=1, source_target_pairs={{0,2},{2,4},{4,6},{6,0},{1,3},{3,5},{5,7},{7,1},{8,10},{10,12},{12... | collective-permute-start | bytes 1081352 | tf_op jit(solution)/shard_map/ppermute | solution.py:431
  3.2 0.9 %collective-permute-start.2 = (f32[22,2,16,128]{3,2,1,0:T(8,128)S(1)}, f32[22,2,16,128]{3,2,1,0:T(8,128)S(1)}, u32[]{:S(2)}, u32[]{:S(2)}) collective-permute-start(f32[22,2,16,128]{3,2,1,0:T(8,128)S(1)} %get-tuple-element.15), channel_id=1, source_target_pairs={{2,0},{4,2},{6,4},{0,6},{3,1},{5,3},{7,5},{1,7},{10,8},{12,10},{14... | collective-permute-start | bytes 1081352 | tf_op jit(solution)/shard_map/ppermute | solution.py:432
  4.1 0.0 copy-done.1
  4.1 0.0 copy-done.3
  4.1 0.0 copy-done.4
  4.1 0.0 copy-done.5
  4.1 0.0 copy-done.6
  4.1 0.0 copy-done.7
  4.1 0.0 copy-done.8
  4.2 0.0 copy-done.9
  4.2 0.0 copy-start.2
  4.2 9.5 %chem.1 = (f32[22,16,8,128]{3,2,1,0:T(8,128)S(1)}, f32[3,17,8,128]{3,2,1,0:T(8,128)S(1)}, f32[17,3,8,128]{3,2,1,0:T(8,128)S(1)}) custom-call(f32[22,16,8,128]{3,2,1,0:T(8,128)S(1)} %copy-done, bf16[32,16,8,128]{3,2,1,0:T(8,128)(2,1)S(1)} %copy-done.3, s32[16,8,128]{2,1,0:T(8,128)S(1)} %copy-done.4, f32[16,8,128]{2,1,0:T(8,128)S(1)} %copy-done.1, ...), custom_call_target="tpu_custom_call" | custom-call | flops 12000000000 | bytes 4000000 | tf_op jit(solution)/shard_map/chem/pallas_call | solution.py:152
  13.7 0.0 collective-permute-done.1.low_ref
  13.7 0.0 collective-permute-done.2.high_ref
  13.8 0.0 collective-permute-done.near_ref
  13.8 0.0 copy-done.2
  13.8 2.5 %local.1 = (f32[22,16,8,128]{3,2,1,0:T(8,128)S(1)}, f32[512,128]{1,0:T(8,128)S(1)}) custom-call(f32[22]{0:T(128)S(1)} %copy-done.2, f32[16,8,128]{2,1,0:T(8,128)S(1)} %copy-done.1, f32[22,16,8,128]{3,2,1,0:T(8,128)S(1)} %copy-done, f32[22,16,8,128]{3,2,1,0:T(8,128)S(1)} %get-tuple-element.13.chem_ref, f32[22,16,8,128]{3,2,1,0:T(8,128)S(1)} %collective-permute-done.near_ref, ...), custom_call_target="tpu_custom_call" | custom-call | flops 20000000 | bytes 7000000 | tf_op jit(solution)/shard_map/local/pallas_call | solution.py:283
  16.3 23.7 %all_to_all.10.in_ref = f32[32,16,128]{2,1,0:T(8,128)S(1)} all-to-all(f32[32,16,128]{2,1,0:T(8,128)S(1)} %bitcast.6), channel_id=1, replica_groups=mesh['gx'=32,'gy'=4,'gz'=2] {'gx'}, dimensions={0} | all-to-all | bytes 524288 | tf_op jit(solution)/shard_map/all_to_all | solution.py:435
  40.1 0.2 chain.1
  40.3 15.2 %all_to_all.11.got_ref = f32[32,3,4,128]{3,2,1,0:T(4,128)S(1)} all-to-all(f32[32,3,4,128]{3,2,1,0:T(4,128)S(1)} %chain.1), channel_id=1, replica_groups=mesh['gx'=32,'gy'=4,'gz'=2] {'gx'}, dimensions={0} | all-to-all | bytes 393216 | tf_op jit(solution)/shard_map/all_to_all | solution.py:436
  55.5 1.4 %back.1 = f32[22,16,8,128]{3,2,1,0:T(8,128)} custom-call(f32[3,17,8,128]{3,2,1,0:T(8,128)S(1)} %get-tuple-element.12.coef_ref, f32[32,3,4,128]{3,2,1,0:T(4,128)S(1)} %all_to_all.11.got_ref, f32[22,16,8,128]{3,2,1,0:T(8,128)S(1)} %get-tuple-element.18.part_ref), custom_call_target="tpu_custom_call" | custom-call | flops 2000000 | bytes 3000000 | tf_op jit(solution)/shard_map/back/pallas_call | solution.py:404
  (1 shorter events, 0.0 us)
Async XLA Ops:
  0.0 13.8 %collective-permute-start = (f32[22,16,8,128]{3,2,1,0:T(8,128)}, f32[22,16,8,128]{3,2,1,0:T(8,128)S(1)}, u32[]{:S(2)}, u32[]{:S(2)}) collective-permute-start(f32[22,16,8,128]{3,2,1,0:T(8,128)} %adj_ref.5), channel_id=1, source_target_pairs={{0,1},{1,0},{2,3},{3,2},{4,5},{5,4},{6,7},{7,6},{8,9},{9,8},{10,11... | collective-permute-start | bytes 4325384 | tf_op jit(solution)/shard_map/ppermute | solution.py:429
  0.0 1.4 %copy-start = (f32[22,16,8,128]{3,2,1,0:T(8,128)S(1)}, f32[22,16,8,128]{3,2,1,0:T(8,128)}, u32[]{:S(2)}) copy-start(f32[22,16,8,128]{3,2,1,0:T(8,128)} %adj_ref.5) | copy-start | bytes 4325380
  1.4 2.7 %copy-start.1 = (f32[16,8,128]{2,1,0:T(8,128)S(1)}, f32[16,8,128]{2,1,0:T(8,128)}, u32[]{:S(2)}) copy-start(f32[16,8,128]{2,1,0:T(8,128)} %cond_ref.3) | copy-start | bytes 196612
  1.4 2.7 %copy-start.3 = (bf16[32,16,8,128]{3,2,1,0:T(8,128)(2,1)S(1)}, bf16[32,16,8,128]{3,2,1,0:T(8,128)(2,1)}, u32[]{:S(2)}) copy-start(bf16[32,16,8,128]{3,2,1,0:T(8,128)(2,1)} %conc_ref.1) | copy-start | bytes 3145732
  1.4 2.7 %copy-start.4 = (s32[16,8,128]{2,1,0:T(8,128)S(1)}, s32[16,8,128]{2,1,0:T(8,128)}, u32[]{:S(2)}) copy-start(s32[16,8,128]{2,1,0:T(8,128)} %lev_ref.1) | copy-start | bytes 196612
  1.4 2.7 %copy-start.5 = (bf16[206,32]{0,1:T(8,128)(2,1)S(1)}, bf16[206,32]{0,1:T(8,128)(2,1)}, u32[]{:S(2)}) copy-start(bf16[206,32]{0,1:T(8,128)(2,1)} %param.14) | copy-start | bytes 39556
  1.4 2.7 %copy-start.6 = (bf16[206,32]{0,1:T(8,128)(2,1)S(1)}, bf16[206,32]{0,1:T(8,128)(2,1)}, u32[]{:S(2)}) copy-start(bf16[206,32]{0,1:T(8,128)(2,1)} %param.15) | copy-start | bytes 39556
  1.4 2.7 %copy-start.7 = (bf16[206,22]{0,1:T(8,128)(2,1)S(1)}, bf16[206,22]{0,1:T(8,128)(2,1)}, u32[]{:S(2)}) copy-start(bf16[206,22]{0,1:T(8,128)(2,1)} %param.16) | copy-start | bytes 27196
  1.4 2.7 %copy-start.8 = (f32[206]{0:T(256)S(1)}, f32[206]{0:T(256)}, u32[]{:S(2)}) copy-start(f32[206]{0:T(256)} %param.17) | copy-start | bytes 2476
  1.4 2.7 %copy-start.9 = (f32[206]{0:T(256)S(1)}, f32[206]{0:T(256)}, u32[]{:S(2)}) copy-start(f32[206]{0:T(256)} %param.18) | copy-start | bytes 2476
  1.7 12.1 %collective-permute-start.1 = (f32[22,2,16,128]{3,2,1,0:T(8,128)S(1)}, f32[22,2,16,128]{3,2,1,0:T(8,128)S(1)}, u32[]{:S(2)}, u32[]{:S(2)}) collective-permute-start(f32[22,2,16,128]{3,2,1,0:T(8,128)S(1)} %get-tuple-element.14), channel_id=1, source_target_pairs={{0,2},{2,4},{4,6},{6,0},{1,3},{3,5},{5,7},{7,1},{8,10},{10,12},{12... | collective-permute-start | bytes 1081352 | tf_op jit(solution)/shard_map/ppermute | solution.py:431
  3.2 10.5 %collective-permute-start.2 = (f32[22,2,16,128]{3,2,1,0:T(8,128)S(1)}, f32[22,2,16,128]{3,2,1,0:T(8,128)S(1)}, u32[]{:S(2)}, u32[]{:S(2)}) collective-permute-start(f32[22,2,16,128]{3,2,1,0:T(8,128)S(1)} %get-tuple-element.15), channel_id=1, source_target_pairs={{2,0},{4,2},{6,4},{0,6},{3,1},{5,3},{7,5},{1,7},{10,8},{12,10},{14... | collective-permute-start | bytes 1081352 | tf_op jit(solution)/shard_map/ppermute | solution.py:432
  4.2 9.6 %copy-start.2 = (f32[22]{0:T(128)S(1)}, f32[22]{0:T(128)}, u32[]{:S(2)}) copy-start(f32[22]{0:T(128)} %diff_ref.1) | copy-start | bytes 268

commit v15 on v12

--- a/solution.py
+++ b/solution.py
@@ -176,8 +176,8 @@
 GROUP = 6
 GROUPS = 4
 ROWS = 16
-SB = 2
-LB = 11
+SB = 1
+LB = 22
 def place(s):
     return s // GROUP * ROWS + s % GROUP
 

time: 57 us -> 57.4 us (level)
  no operation moved by 1% of the time
where the time goes in v15:
time: 57.4 us; the launch traced here: 57.2 us
  blocking collectives  38.9 us (68%)
  Pallas kernels  14.2 us (25%)
  starting transfers between devices  2.44 us (4%)
  local copies, waits for them, and re-layouts  1.4 us (2%)
    all_to_all x1, blocking collectives, shards(): lax.all_to_all(message.reshape(blocks, ROWS, nz), 'gx', 0, 0, tiled=True)  23.7 us
    all_to_all x1, blocking collectives, shards(): ends = lax.all_to_all(chain(message), 'gx', 0, 0, tiled=True)  15.2 us
    pallas_call x1, Pallas kernels, chemistry(): pl.pallas_call(chem_kernel, in_specs=[WHOLE] * 9, out_specs=[WHOLE] * 3,...  9.55 us
    pallas_call x1, Pallas kernels, local_part(): pl.pallas_call(local_kernel, in_specs=[smem] + [WHOLE] * 8, out_specs=[WH...  2.39 us
    pallas_call x1, Pallas kernels, back(): pl.pallas_call(back_kernel, in_specs=[WHOLE, WHOLE, WHOLE], out_specs=ANY...  1.82 us
    ppermute x1, starting transfers between devices, shards(): lax.ppermute(tail, 'gy', [(i, (i + 1) % rows_y) for i in range(rows_y)])  1.57 us
    unnamed x20, local copies, waits for them, and re-layouts  1.4 us
  transfers between devices with their start and end apart: 3, of which 0 were waited for; matrix products, arithmetic and copies ran while one was open for 0% of the time, Pallas kernels for 17%

profile of v15, /device:TPU:2, one launch (start us, length us, event | category | flops | bytes accessed | tf_op | source)
XLA Modules:
  0.0 57.2 jit_solution(17142109320413123989)
XLA Ops:
  0.0 0.0 collective-permute-start
  0.0 0.0 copy-start
  0.0 1.4 %copy-done = f32[22,16,8,128]{3,2,1,0:T(8,128)S(1)} copy-done((f32[22,16,8,128]{3,2,1,0:T(8,128)S(1)}, f32[22,16,8,128]{3,2,1,0:T(8,128)}, u32[]{:S(2)}) %copy-start) | copy-done | bytes 1441816
  1.4 0.0 copy-start.1
  1.4 0.0 copy-start.3
  1.4 0.0 copy-start.4
  1.4 0.0 copy-start.6
  1.4 0.0 copy-start.7
  1.4 0.0 copy-start.8
  1.4 0.0 copy-start.9
  1.4 0.2 edges.1
  1.7 1.6 %collective-permute-start.1 = (f32[22,2,16,128]{3,2,1,0:T(8,128)S(1)}, f32[22,2,16,128]{3,2,1,0:T(8,128)S(1)}, u32[]{:S(2)}, u32[]{:S(2)}) collective-permute-start(f32[22,2,16,128]{3,2,1,0:T(8,128)S(1)} %get-tuple-element.14), channel_id=1, source_target_pairs={{0,2},{2,4},{4,6},{6,0},{1,3},{3,5},{5,7},{7,1},{8,10},{10,12},{12... | collective-permute-start | bytes 1081352 | tf_op jit(solution)/shard_map/ppermute | solution.py:431
  3.2 0.9 %collective-permute-start.2 = (f32[22,2,16,128]{3,2,1,0:T(8,128)S(1)}, f32[22,2,16,128]{3,2,1,0:T(8,128)S(1)}, u32[]{:S(2)}, u32[]{:S(2)}) collective-permute-start(f32[22,2,16,128]{3,2,1,0:T(8,128)S(1)} %get-tuple-element.15), channel_id=1, source_target_pairs={{2,0},{4,2},{6,4},{0,6},{3,1},{5,3},{7,5},{1,7},{10,8},{12,10},{14... | collective-permute-start | bytes 1081352 | tf_op jit(solution)/shard_map/ppermute | solution.py:432
  4.1 0.0 copy-done.1
  4.1 0.0 copy-done.3
  4.1 0.0 copy-done.4
  4.1 0.0 copy-done.5
  4.1 0.0 copy-done.6
  4.1 0.0 copy-done.7
  4.1 0.0 copy-done.8
  4.2 0.0 copy-done.9
  4.2 0.0 copy-start.2
  4.2 9.5 %chem.1 = (f32[22,16,8,128]{3,2,1,0:T(8,128)S(1)}, f32[3,17,8,128]{3,2,1,0:T(8,128)S(1)}, f32[17,3,8,128]{3,2,1,0:T(8,128)S(1)}) custom-call(f32[22,16,8,128]{3,2,1,0:T(8,128)S(1)} %copy-done, bf16[32,16,8,128]{3,2,1,0:T(8,128)(2,1)S(1)} %copy-done.3, s32[16,8,128]{2,1,0:T(8,128)S(1)} %copy-done.4, f32[16,8,128]{2,1,0:T(8,128)S(1)} %copy-done.1, ...), custom_call_target="tpu_custom_call" | custom-call | flops 12000000000 | bytes 4000000 | tf_op jit(solution)/shard_map/chem/pallas_call | solution.py:152
  13.7 0.0 collective-permute-done.1.low_ref
  13.7 0.0 collective-permute-done.2.high_ref
  13.8 0.0 collective-permute-done.near_ref
  13.8 0.0 copy-done.2
  13.8 2.4 %local.1 = (f32[22,16,8,128]{3,2,1,0:T(8,128)S(1)}, f32[512,128]{1,0:T(8,128)S(1)}) custom-call(f32[22]{0:T(128)S(1)} %copy-done.2, f32[16,8,128]{2,1,0:T(8,128)S(1)} %copy-done.1, f32[22,16,8,128]{3,2,1,0:T(8,128)S(1)} %copy-done, f32[22,16,8,128]{3,2,1,0:T(8,128)S(1)} %get-tuple-element.13.chem_ref, f32[22,16,8,128]{3,2,1,0:T(8,128)S(1)} %collective-permute-done.near_ref, ...), custom_call_target="tpu_custom_call" | custom-call | flops 20000000 | bytes 7000000 | tf_op jit(solution)/shard_map/local/pallas_call | solution.py:283
  16.2 23.7 %all_to_all.10.in_ref = f32[32,16,128]{2,1,0:T(8,128)S(1)} all-to-all(f32[32,16,128]{2,1,0:T(8,128)S(1)} %bitcast.6), channel_id=1, replica_groups=mesh['gx'=32,'gy'=4,'gz'=2] {'gx'}, dimensions={0} | all-to-all | bytes 524288 | tf_op jit(solution)/shard_map/all_to_all | solution.py:435
  39.9 0.2 chain.1
  40.2 15.2 %all_to_all.11.got_ref = f32[32,3,4,128]{3,2,1,0:T(4,128)S(1)} all-to-all(f32[32,3,4,128]{3,2,1,0:T(4,128)S(1)} %chain.1), channel_id=1, replica_groups=mesh['gx'=32,'gy'=4,'gz'=2] {'gx'}, dimensions={0} | all-to-all | bytes 393216 | tf_op jit(solution)/shard_map/all_to_all | solution.py:436
  55.4 1.8 %back.1 = f32[22,16,8,128]{3,2,1,0:T(8,128)} custom-call(f32[3,17,8,128]{3,2,1,0:T(8,128)S(1)} %get-tuple-element.12.coef_ref, f32[32,3,4,128]{3,2,1,0:T(4,128)S(1)} %all_to_all.11.got_ref, f32[22,16,8,128]{3,2,1,0:T(8,128)S(1)} %get-tuple-element.18.part_ref), custom_call_target="tpu_custom_call" | custom-call | flops 2000000 | bytes 3000000 | tf_op jit(solution)/shard_map/back/pallas_call | solution.py:404
  (1 shorter events, 0.0 us)
Async XLA Ops:
  0.0 13.8 %collective-permute-start = (f32[22,16,8,128]{3,2,1,0:T(8,128)}, f32[22,16,8,128]{3,2,1,0:T(8,128)S(1)}, u32[]{:S(2)}, u32[]{:S(2)}) collective-permute-start(f32[22,16,8,128]{3,2,1,0:T(8,128)} %adj_ref.5), channel_id=1, source_target_pairs={{0,1},{1,0},{2,3},{3,2},{4,5},{5,4},{6,7},{7,6},{8,9},{9,8},{10,11... | collective-permute-start | bytes 4325384 | tf_op jit(solution)/shard_map/ppermute | solution.py:429
  0.0 1.4 %copy-start = (f32[22,16,8,128]{3,2,1,0:T(8,128)S(1)}, f32[22,16,8,128]{3,2,1,0:T(8,128)}, u32[]{:S(2)}) copy-start(f32[22,16,8,128]{3,2,1,0:T(8,128)} %adj_ref.5) | copy-start | bytes 4325380
  1.4 2.7 %copy-start.1 = (f32[16,8,128]{2,1,0:T(8,128)S(1)}, f32[16,8,128]{2,1,0:T(8,128)}, u32[]{:S(2)}) copy-start(f32[16,8,128]{2,1,0:T(8,128)} %cond_ref.3) | copy-start | bytes 196612
  1.4 2.7 %copy-start.3 = (bf16[32,16,8,128]{3,2,1,0:T(8,128)(2,1)S(1)}, bf16[32,16,8,128]{3,2,1,0:T(8,128)(2,1)}, u32[]{:S(2)}) copy-start(bf16[32,16,8,128]{3,2,1,0:T(8,128)(2,1)} %conc_ref.1) | copy-start | bytes 3145732
  1.4 2.7 %copy-start.4 = (s32[16,8,128]{2,1,0:T(8,128)S(1)}, s32[16,8,128]{2,1,0:T(8,128)}, u32[]{:S(2)}) copy-start(s32[16,8,128]{2,1,0:T(8,128)} %lev_ref.1) | copy-start | bytes 196612
  1.4 2.7 %copy-start.5 = (bf16[206,32]{0,1:T(8,128)(2,1)S(1)}, bf16[206,32]{0,1:T(8,128)(2,1)}, u32[]{:S(2)}) copy-start(bf16[206,32]{0,1:T(8,128)(2,1)} %param.14) | copy-start | bytes 39556
  1.4 2.7 %copy-start.6 = (bf16[206,32]{0,1:T(8,128)(2,1)S(1)}, bf16[206,32]{0,1:T(8,128)(2,1)}, u32[]{:S(2)}) copy-start(bf16[206,32]{0,1:T(8,128)(2,1)} %param.15) | copy-start | bytes 39556
  1.4 2.7 %copy-start.7 = (bf16[206,22]{0,1:T(8,128)(2,1)S(1)}, bf16[206,22]{0,1:T(8,128)(2,1)}, u32[]{:S(2)}) copy-start(bf16[206,22]{0,1:T(8,128)(2,1)} %param.16) | copy-start | bytes 27196
  1.4 2.7 %copy-start.8 = (f32[206]{0:T(256)S(1)}, f32[206]{0:T(256)}, u32[]{:S(2)}) copy-start(f32[206]{0:T(256)} %param.17) | copy-start | bytes 2476
  1.4 2.7 %copy-start.9 = (f32[206]{0:T(256)S(1)}, f32[206]{0:T(256)}, u32[]{:S(2)}) copy-start(f32[206]{0:T(256)} %param.18) | copy-start | bytes 2476
  1.7 12.1 %collective-permute-start.1 = (f32[22,2,16,128]{3,2,1,0:T(8,128)S(1)}, f32[22,2,16,128]{3,2,1,0:T(8,128)S(1)}, u32[]{:S(2)}, u32[]{:S(2)}) collective-permute-start(f32[22,2,16,128]{3,2,1,0:T(8,128)S(1)} %get-tuple-element.14), channel_id=1, source_target_pairs={{0,2},{2,4},{4,6},{6,0},{1,3},{3,5},{5,7},{7,1},{8,10},{10,12},{12... | collective-permute-start | bytes 1081352 | tf_op jit(solution)/shard_map/ppermute | solution.py:431
  3.2 10.5 %collective-permute-start.2 = (f32[22,2,16,128]{3,2,1,0:T(8,128)S(1)}, f32[22,2,16,128]{3,2,1,0:T(8,128)S(1)}, u32[]{:S(2)}, u32[]{:S(2)}) collective-permute-start(f32[22,2,16,128]{3,2,1,0:T(8,128)S(1)} %get-tuple-element.15), channel_id=1, source_target_pairs={{2,0},{4,2},{6,4},{0,6},{3,1},{5,3},{7,5},{1,7},{10,8},{12,10},{14... | collective-permute-start | bytes 1081352 | tf_op jit(solution)/shard_map/ppermute | solution.py:432
  4.2 9.6 %copy-start.2 = (f32[22]{0:T(128)S(1)}, f32[22]{0:T(128)}, u32[]{:S(2)}) copy-start(f32[22]{0:T(128)} %diff_ref.1) | copy-start | bytes 268
